TPU v7x, 32 devices: a whole 2x2x4 slice. The times are simulated.
32 devices in a mesh: section: 2 (over x), shard: 4 (over z), replica: 4 (over y, core).
Axes of the slice: x: 2, y: 2, z: 4, core: 2. Of those that a mesh axis runs over, the one named last changes fastest.
Arguments:
- edges: bfloat16 [2, 8, 1536, 768], P('section', 'replica', 'shard'), may hold values from -6 to 6
- attn_in: bfloat16 [2, 768, 2304], P('section', 'shard'), may hold values from -0.21875 to 0.21875
- attn_out: bfloat16 [2, 768, 768], P('section', 'shard'), may hold values from -0.625 to 0.625
- mlp_up: bfloat16 [2, 768, 3072], P('section', 'shard'), may hold values from -0.21875 to 0.21875
- mlp_down: bfloat16 [2, 3072, 768], P('section', 'shard'), may hold values from -0.109375 to 0.109375
- vectors: float32 [2, 12, 768], P('section'), may hold values from -0.3 to 1.4
- key_mask: int32 [8, 1536], P('replica'), may hold values from 0 to 1, as said below
Outputs:
- edges_out: bfloat16 [2, 8, 1536, 768], P('section', 'replica', 'shard')
- grad_attn_in: float32 [2, 768, 2304], P('section', 'shard')
- grad_attn_out: float32 [2, 768, 768], P('section', 'shard')
- grad_mlp_up: float32 [2, 768, 3072], P('section', 'shard')
- grad_mlp_down: float32 [2, 3072, 768], P('section', 'shard')
- grad_vectors: float32 [2, 12, 768], P('section', None, 'shard')
Inputs may be any that keep to these rules, and one draw needn't show every extreme that they name: `key_mask`: in each row the ones form a prefix of at least 1440 frames.
All inputs are finite; a program needn't handle non-finite values.
Results may differ from a plain program's by a relative error of at most 0.017.
Values may be sent and summed in bfloat16 or wider, within the bound.
No kernel may reach another device: no remote copies, remote signals or barrier semaphores. Data moves between devices by JAX's collectives and lax.ppermute only.
A program may use at most 320 MiB of HBM per device.

v0:
```python
import math

import jax
import jax.numpy as jnp
from jax import lax
from jax.sharding import PartitionSpec as P

H = 12


EPS = 1e-05
MASKED = -1e30


def passed_along(block, axis, distance):
    devices = range(lax.axis_size(axis))
    route = [(i - distance, i) for i in devices if i - distance in devices]
    return lax.ppermute(block, axis, route)


def layer_norm(values, gain_row, offset):
    center = values - jnp.mean(values, -1, keepdims=True)
    spread = jnp.mean(center * center, -1, keepdims=True)
    return center * lax.rsqrt(spread + EPS) * gain_row + offset


def gelu_exact(values):
    return jax.nn.gelu(values, approximate=False)


def split_heads(values, head_count):
    return values.reshape(values.shape[:-1] + (head_count, values.shape[-1] // head_count))


def body(edges, attn_in, attn_out, mlp_up, mlp_down, vectors, key_mask):
    section_index = lax.axis_index("section")
    is_first = section_index == 0
    inputs_here = edges[0]
    micro_count, frame_count, model_width = inputs_here.shape
    shard_count = lax.axis_size("shard")
    head_count = H
    root_size = math.sqrt(model_width // head_count)
    vector_rows = vectors[0]
    vector_count = vectors.shape[1]
    bias_in = jnp.concatenate([vector_rows[2], jnp.zeros_like(vector_rows[2]), vector_rows[3]])
    last_slot = micro_count - 1
    totals = (
        jnp.zeros(attn_in.shape[1:], jnp.float32),
        jnp.zeros(attn_out.shape[1:], jnp.float32),
        jnp.zeros(mlp_up.shape[1:], jnp.float32),
        jnp.zeros(mlp_down.shape[1:], jnp.float32),
        jnp.zeros((model_width // shard_count, vector_count), jnp.float32),
    )

    def one_tick(tick_index, carry):
        recv_act, recv_grad, out_slots, totals = carry
        w_in, w_out, w_up, w_down = (
            lax.all_gather(attn_in[0], "shard", axis=0, tiled=True),
            lax.all_gather(attn_out[0], "shard", axis=0, tiled=True),
            lax.all_gather(mlp_up[0], "shard", axis=0, tiled=True),
            lax.all_gather(mlp_down[0], "shard", axis=0, tiled=True),
        )
        fwd_slot = jnp.clip(tick_index - section_index, 0, last_slot)
        back_slot = tick_index - 2 + section_index
        is_valid = (back_slot >= 0) & (back_slot < micro_count)
        back_clip = jnp.clip(back_slot, 0, last_slot)
        fwd_pick = lax.dynamic_index_in_dim(inputs_here, fwd_slot, 0, keepdims=False)
        back_pick = lax.dynamic_index_in_dim(inputs_here, back_clip, 0, keepdims=False)
        fwd_frames = jnp.where(is_first, fwd_pick, recv_act)
        back_frames = jnp.where(is_first, back_pick, recv_act)
        back_cot = jnp.where(is_first, recv_grad, back_pick).astype(jnp.float32)
        back_cot = jnp.where(is_valid, back_cot, 0.0)
        frames = jnp.stack([fwd_frames, back_frames]).astype(jnp.float32)
        valid_keys = jnp.stack(
            [
                lax.dynamic_index_in_dim(key_mask, fwd_slot, 0, keepdims=False),
                lax.dynamic_index_in_dim(key_mask, back_clip, 0, keepdims=False),
            ]
        )
        normed = layer_norm(frames, vector_rows[0], vector_rows[1]).astype(jnp.bfloat16)
        projected = (
            jnp.einsum("brd,de->bre", normed, w_in, preferred_element_type=jnp.float32) + bias_in
        ).astype(jnp.bfloat16)
        queries = projected[..., :model_width]
        all_keys, all_values = (
            lax.all_gather(
                projected[..., model_width : 2 * model_width], "shard", axis=1, tiled=True
            ),
            lax.all_gather(projected[..., 2 * model_width :], "shard", axis=1, tiled=True),
        )
        query_heads = split_heads(queries, head_count)
        key_heads = split_heads(all_keys, head_count)
        value_heads = split_heads(all_values, head_count)
        scores = (
            jnp.einsum(
                "bqhd,bkhd->bhqk", query_heads, key_heads, preferred_element_type=jnp.float32
            )
            / root_size
        )
        scores = jnp.where(valid_keys[:, None, None, :] > 0, scores, MASKED)
        exp_scores = jnp.exp(scores - jnp.max(scores, -1, keepdims=True))
        attention_probs = exp_scores / jnp.sum(exp_scores, -1, keepdims=True)
        probs_low = attention_probs.astype(jnp.bfloat16)
        attended = jnp.einsum(
            "bhqk,bkhd->bqhd", probs_low, value_heads, preferred_element_type=jnp.float32
        )
        attended = attended.reshape(2, frame_count, model_width).astype(jnp.bfloat16)
        middle = (
            frames
            + jnp.einsum("brd,de->bre", attended, w_out, preferred_element_type=jnp.float32)
            + vector_rows[4]
        )
        normed_two = layer_norm(middle, vector_rows[5], vector_rows[6]).astype(jnp.bfloat16)
        upward = jnp.einsum(
            "brd,df->brf", normed_two, w_up, preferred_element_type=jnp.float32
        ) + vector_rows[8:].reshape(-1)
        active = gelu_exact(upward).astype(jnp.bfloat16)
        result = (
            middle
            + jnp.einsum("brf,fd->brd", active, w_down, preferred_element_type=jnp.float32)
            + vector_rows[7]
        )
        d_mlp = back_cot.astype(jnp.bfloat16)
        g_down = jnp.einsum("rf,rd->fd", active[1], d_mlp, preferred_element_type=jnp.float32)
        d_active = jnp.einsum("rd,fd->rf", d_mlp, w_down, preferred_element_type=jnp.float32)
        gelu_back = jax.vjp(gelu_exact, upward[1])[1]
        d_upward = gelu_back(d_active)[0].astype(jnp.bfloat16)
        g_up = jnp.einsum("rd,rf->df", normed_two[1], d_upward, preferred_element_type=jnp.float32)
        d_normed_two = jnp.einsum("rf,df->rd", d_upward, w_up, preferred_element_type=jnp.float32)
        norm_back_two = jax.vjp(layer_norm, middle[1], vector_rows[5], vector_rows[6])[1]
        d_middle_part, g_gain_two, g_offset_two = norm_back_two(d_normed_two)
        d_middle = back_cot + d_middle_part
        d_attn = d_middle.astype(jnp.bfloat16)
        g_out = jnp.einsum("rd,re->de", attended[1], d_attn, preferred_element_type=jnp.float32)
        d_attended = jnp.einsum(
            "re,de->rd", d_attn, w_out, preferred_element_type=jnp.float32
        ).astype(jnp.bfloat16)
        d_heads = split_heads(d_attended, head_count)
        probs_back = attention_probs[1]
        d_probs = jnp.einsum(
            "qhd,khd->hqk", d_heads, value_heads[1], preferred_element_type=jnp.float32
        )
        d_scores = (
            probs_back * (d_probs - jnp.sum(probs_back * d_probs, -1, keepdims=True))
        ).astype(jnp.bfloat16)
        d_queries = (
            jnp.einsum(
                "hqk,khd->qhd", d_scores, key_heads[1], preferred_element_type=jnp.float32
            ).reshape(frame_count, model_width)
            / root_size
        )
        d_keys = (
            jnp.einsum(
                "hqk,qhd->khd", d_scores, query_heads[1], preferred_element_type=jnp.float32
            ).reshape(-1, model_width)
            / root_size
        )
        d_values = jnp.einsum(
            "hqk,qhd->khd", probs_low[1], d_heads, preferred_element_type=jnp.float32
        ).reshape(-1, model_width)
        own_keys, own_values = (
            lax.psum_scatter(
                d_keys.astype(jnp.bfloat16), "shard", scatter_dimension=0, tiled=True
            ).astype(jnp.float32),
            lax.psum_scatter(
                d_values.astype(jnp.bfloat16), "shard", scatter_dimension=0, tiled=True
            ).astype(jnp.float32),
        )
        d_project = jnp.concatenate([d_queries, own_keys, own_values], -1).astype(jnp.bfloat16)
        g_in = jnp.einsum("rd,re->de", normed[1], d_project, preferred_element_type=jnp.float32)
        d_normed = jnp.einsum("re,de->rd", d_project, w_in, preferred_element_type=jnp.float32)
        norm_back_one = jax.vjp(layer_norm, frames[1], vector_rows[0], vector_rows[1])[1]
        d_frames_part, g_gain_one, g_offset_one = norm_back_one(d_normed)
        d_frames = (d_middle + d_frames_part).astype(jnp.bfloat16)
        project_sums = jnp.sum(d_project.astype(jnp.float32), 0)
        g_vectors = jnp.concatenate(
            [
                jnp.stack(
                    [
                        g_gain_one,
                        g_offset_one,
                        project_sums[:model_width],
                        project_sums[2 * model_width :],
                        jnp.sum(d_attn.astype(jnp.float32), 0),
                        g_gain_two,
                        g_offset_two,
                        jnp.sum(d_mlp.astype(jnp.float32), 0),
                    ]
                ),
                jnp.sum(d_upward.astype(jnp.float32), 0).reshape(-1, model_width),
            ],
            0,
        )
        weight_grads = (g_in, g_out, g_up, g_down, g_vectors.T)
        owned_part = (
            lax.psum_scatter(
                weight_grads[0].astype(jnp.bfloat16), "shard", scatter_dimension=0, tiled=True
            ).astype(jnp.float32),
            lax.psum_scatter(
                weight_grads[1].astype(jnp.bfloat16), "shard", scatter_dimension=0, tiled=True
            ).astype(jnp.float32),
            lax.psum_scatter(
                weight_grads[2].astype(jnp.bfloat16), "shard", scatter_dimension=0, tiled=True
            ).astype(jnp.float32),
            lax.psum_scatter(
                weight_grads[3].astype(jnp.bfloat16), "shard", scatter_dimension=0, tiled=True
            ).astype(jnp.float32),
            lax.psum_scatter(
                weight_grads[4].astype(jnp.bfloat16), "shard", scatter_dimension=0, tiled=True
            ).astype(jnp.float32),
        )
        totals = tuple((before + added for before, added in zip(totals, owned_part)))
        forward_low = result[0].astype(jnp.bfloat16)
        value_out = jnp.where(is_first, d_frames, forward_low)
        written = lax.dynamic_update_index_in_dim(out_slots, value_out, back_clip, 0)
        out_slots = jnp.where(is_valid, written, out_slots)
        recv_act = passed_along(forward_low, "section", 1)
        recv_grad = passed_along(d_frames, "section", -1)
        return (recv_act, recv_grad, out_slots, totals)

    start_act = jnp.zeros((frame_count, model_width), jnp.bfloat16)
    start_slots = jnp.zeros((micro_count, frame_count, model_width), jnp.bfloat16)
    final_carry = lax.fori_loop(
        0, micro_count + 2, one_tick, (start_act, start_act, start_slots, totals)
    )
    out_slots = final_carry[2]
    totals = final_carry[3]
    grad_in_w, grad_out_w, grad_up_w, grad_down_w, grad_vec = (
        lax.psum(totals[0].astype(jnp.bfloat16), "replica").astype(jnp.float32),
        lax.psum(totals[1].astype(jnp.bfloat16), "replica").astype(jnp.float32),
        lax.psum(totals[2].astype(jnp.bfloat16), "replica").astype(jnp.float32),
        lax.psum(totals[3].astype(jnp.bfloat16), "replica").astype(jnp.float32),
        lax.psum(totals[4].astype(jnp.bfloat16), "replica").astype(jnp.float32),
    )
    return (
        out_slots[None],
        grad_in_w[None],
        grad_out_w[None],
        grad_up_w[None],
        grad_down_w[None],
        grad_vec.T[None],
    )


def solution(mesh):
    placed = (
        P("section", "replica", "shard", None),
        P("section", "shard", None),
        P("section", "shard", None),
        P("section", "shard", None),
        P("section", "shard", None),
        P("section", None, None),
        P("replica", None),
    )
    return jax.shard_map(
        body,
        mesh=mesh,
        in_specs=placed,
        out_specs=(
            P("section", "replica", "shard", None),
            P("section", "shard", None),
            P("section", "shard", None),
            P("section", "shard", None),
            P("section", "shard", None),
            P("section", None, "shard"),
        ),
        check_vma=False,
    )
```

profile of v0, /device:TPU:0, one launch (start us, length us, event | category | flops | bytes accessed | tf_op | source)
XLA Modules:
  0.0 3923.6 jit_solution(6940888632519028779)
XLA Ops:
  13.6 3814.1 %while.30 = (s32[]{:T(128)}, bf16[384,768]{1,0:T(8,128)(2,1)}, bf16[384,768]{1,0:T(8,128)(2,1)}, bf16[2,384,768]{2,1,0:T(8,128)(2,1)}, f32[192,2304]{1,0:T(8,128...) while((s32[]{:T(128)}, bf16[384,768]{1,0:T(8,128)(2,1)}, ...), condition=%wide.region_31.32_spmd.clone, body=%wide.region_0.31_spmd.clone.sunk | while | flops 29469085696 | bytes 953685440 | solution.py:223
  20.7 68.0 %all-gather.23.cloned.1.call-done = bf16[1,768,2304]{2,1,0:T(8,128)(2,1)} async-done(((bf16[1,192,2304]{2,1,0:T(8,128)(2,1)}), bf16[1,768,2304]{2,1,0:T(8,128)(2,1)}) %all-gather.23.cloned.1.call-update) | async-done | bytes 3538960 | tf_op jit(solution)/shard_map/while/body/eval_jaxpr/all_gather | solution.py:58
  104.1 80.4 %all-gather.27.cloned.1.call-done = bf16[2,1536,768]{2,1,0:T(8,128)(2,1)} async-done(((bf16[2,384,768]{2,1,0:T(8,128)(2,1)}), bf16[2,1536,768]{2,1,0:T(8,128)(2,1)}) %all-gather.27.cloned.1.call-update) | async-done | bytes 4718608 | tf_op jit(solution)/shard_map/while/body/eval_jaxpr/all_gather | solution.py:86
  191.2 26.2 fusion.181
  217.4 47.3 %fusion.182 = (bf16[2,12,384,1536]{3,2,1,0:T(8,128)(2,1)}, f32[2,12,384,1536]{3,2,1,0:T(8,128)}) fusion(f32[2,12,384,1536]{3,2,1,0:T(8,128)} %get-tuple-element.782, f32[2,12,384]{2,1,0:T(8,128)S(1)} %get-tuple-element.783), kind=kLoop, calls=%fused_computation.179.clone.1 | loop fusion | flops 28311552 | bytes 141594624 | tf_op jit(solution)/shard_map/while/body/eval_jaxpr/convert_element_type | solution.py:103
  310.2 84.2 %all-gather.33.cloned.1.call-done = bf16[1,768,3072]{2,1,0:T(8,128)(2,1)} async-done(((bf16[1,192,3072]{2,1,0:T(8,128)(2,1)}), bf16[1,768,3072]{2,1,0:T(8,128)(2,1)}) %all-gather.33.cloned.1.call-update) | async-done | bytes 4718608 | tf_op jit(solution)/shard_map/while/body/eval_jaxpr/all_gather | solution.py:60
  409.0 74.7 %all-gather.31.cloned.1.call-done = bf16[1,3072,768]{2,1,0:T(8,128)(2,1)} async-done(((bf16[1,768,768]{2,1,0:T(8,128)(2,1)}), bf16[1,3072,768]{2,1,0:T(8,128)(2,1)}) %all-gather.31.cloned.1.call-update) | async-done | bytes 4718608 | tf_op jit(solution)/shard_map/while/body/eval_jaxpr/all_gather | solution.py:61
  537.0 23.7 multiply_convert_fusion.4
  593.4 23.7 fusion.192
  638.5 32.2 reduce-scatter.20.cloned.1.call-done
  729.6 78.3 %reduce-scatter.30.cloned.1.call-done = bf16[768,768]{1,0:T(8,128)(2,1)} async-done(((bf16[3072,768]{1,0:T(8,128)(2,1)}), bf16[768,768]{1,0:T(8,128)(2,1)}) %reduce-scatter.30.cloned.1.call-update) | async-done | bytes 1179664 | tf_op jit(solution)/shard_map/while/body/eval_jaxpr/reduce_scatter | solution.py:205
  810.8 85.2 %reduce-scatter.28.cloned.1.call-done = bf16[192,3072]{1,0:T(8,128)(2,1)} async-done(((bf16[768,3072]{1,0:T(8,128)(2,1)}), bf16[192,3072]{1,0:T(8,128)(2,1)}) %reduce-scatter.28.cloned.1.call-update) | async-done | bytes 1179664 | tf_op jit(solution)/shard_map/while/body/eval_jaxpr/reduce_scatter | solution.py:202
  898.0 67.3 %reduce-scatter.24.cloned.1.call-done = bf16[192,2304]{1,0:T(8,128)(2,1)} async-done(((bf16[768,2304]{1,0:T(8,128)(2,1)}), bf16[192,2304]{1,0:T(8,128)(2,1)}) %reduce-scatter.24.cloned.1.call-update) | async-done | bytes 884752 | tf_op jit(solution)/shard_map/while/body/eval_jaxpr/reduce_scatter | solution.py:196
  975.2 65.5 %all-gather.23.cloned.1.call-done = bf16[1,768,2304]{2,1,0:T(8,128)(2,1)} async-done(((bf16[1,192,2304]{2,1,0:T(8,128)(2,1)}), bf16[1,768,2304]{2,1,0:T(8,128)(2,1)}) %all-gather.23.cloned.1.call-update) | async-done | bytes 3538960 | tf_op jit(solution)/shard_map/while/body/eval_jaxpr/all_gather | solution.py:58
  1056.1 80.4 %all-gather.27.cloned.1.call-done = bf16[2,1536,768]{2,1,0:T(8,128)(2,1)} async-done(((bf16[2,384,768]{2,1,0:T(8,128)(2,1)}), bf16[2,1536,768]{2,1,0:T(8,128)(2,1)}) %all-gather.27.cloned.1.call-update) | async-done | bytes 4718608 | tf_op jit(solution)/shard_map/while/body/eval_jaxpr/all_gather | solution.py:86
  1143.2 26.2 fusion.181
  1169.4 47.2 %fusion.182 = (bf16[2,12,384,1536]{3,2,1,0:T(8,128)(2,1)}, f32[2,12,384,1536]{3,2,1,0:T(8,128)}) fusion(f32[2,12,384,1536]{3,2,1,0:T(8,128)} %get-tuple-element.782, f32[2,12,384]{2,1,0:T(8,128)S(1)} %get-tuple-element.783), kind=kLoop, calls=%fused_computation.179.clone.1 | loop fusion | flops 28311552 | bytes 141594624 | tf_op jit(solution)/shard_map/while/body/eval_jaxpr/convert_element_type | solution.py:103
  1262.0 84.2 %all-gather.33.cloned.1.call-done = bf16[1,768,3072]{2,1,0:T(8,128)(2,1)} async-done(((bf16[1,192,3072]{2,1,0:T(8,128)(2,1)}), bf16[1,768,3072]{2,1,0:T(8,128)(2,1)}) %all-gather.33.cloned.1.call-update) | async-done | bytes 4718608 | tf_op jit(solution)/shard_map/while/body/eval_jaxpr/all_gather | solution.py:60
  1360.8 74.9 %all-gather.31.cloned.1.call-done = bf16[1,3072,768]{2,1,0:T(8,128)(2,1)} async-done(((bf16[1,768,768]{2,1,0:T(8,128)(2,1)}), bf16[1,3072,768]{2,1,0:T(8,128)(2,1)}) %all-gather.31.cloned.1.call-update) | async-done | bytes 4718608 | tf_op jit(solution)/shard_map/while/body/eval_jaxpr/all_gather | solution.py:61
  1488.9 23.7 multiply_convert_fusion.4
  1545.3 23.7 fusion.192
  1590.5 32.2 reduce-scatter.20.cloned.1.call-done
  1681.7 78.1 %reduce-scatter.30.cloned.1.call-done = bf16[768,768]{1,0:T(8,128)(2,1)} async-done(((bf16[3072,768]{1,0:T(8,128)(2,1)}), bf16[768,768]{1,0:T(8,128)(2,1)}) %reduce-scatter.30.cloned.1.call-update) | async-done | bytes 1179664 | tf_op jit(solution)/shard_map/while/body/eval_jaxpr/reduce_scatter | solution.py:205
  1763.5 84.6 %reduce-scatter.28.cloned.1.call-done = bf16[192,3072]{1,0:T(8,128)(2,1)} async-done(((bf16[768,3072]{1,0:T(8,128)(2,1)}), bf16[192,3072]{1,0:T(8,128)(2,1)}) %reduce-scatter.28.cloned.1.call-update) | async-done | bytes 1179664 | tf_op jit(solution)/shard_map/while/body/eval_jaxpr/reduce_scatter | solution.py:202
  1850.2 67.1 %reduce-scatter.24.cloned.1.call-done = bf16[192,2304]{1,0:T(8,128)(2,1)} async-done(((bf16[768,2304]{1,0:T(8,128)(2,1)}), bf16[192,2304]{1,0:T(8,128)(2,1)}) %reduce-scatter.24.cloned.1.call-update) | async-done | bytes 884752 | tf_op jit(solution)/shard_map/while/body/eval_jaxpr/reduce_scatter | solution.py:196
  1927.7 65.5 %all-gather.23.cloned.1.call-done = bf16[1,768,2304]{2,1,0:T(8,128)(2,1)} async-done(((bf16[1,192,2304]{2,1,0:T(8,128)(2,1)}), bf16[1,768,2304]{2,1,0:T(8,128)(2,1)}) %all-gather.23.cloned.1.call-update) | async-done | bytes 3538960 | tf_op jit(solution)/shard_map/while/body/eval_jaxpr/all_gather | solution.py:58
  2008.9 80.1 %all-gather.27.cloned.1.call-done = bf16[2,1536,768]{2,1,0:T(8,128)(2,1)} async-done(((bf16[2,384,768]{2,1,0:T(8,128)(2,1)}), bf16[2,1536,768]{2,1,0:T(8,128)(2,1)}) %all-gather.27.cloned.1.call-update) | async-done | bytes 4718608 | tf_op jit(solution)/shard_map/while/body/eval_jaxpr/all_gather | solution.py:86
  2095.7 26.2 fusion.181
  2121.9 47.3 %fusion.182 = (bf16[2,12,384,1536]{3,2,1,0:T(8,128)(2,1)}, f32[2,12,384,1536]{3,2,1,0:T(8,128)}) fusion(f32[2,12,384,1536]{3,2,1,0:T(8,128)} %get-tuple-element.782, f32[2,12,384]{2,1,0:T(8,128)S(1)} %get-tuple-element.783), kind=kLoop, calls=%fused_computation.179.clone.1 | loop fusion | flops 28311552 | bytes 141594624 | tf_op jit(solution)/shard_map/while/body/eval_jaxpr/convert_element_type | solution.py:103
  2214.7 84.3 %all-gather.33.cloned.1.call-done = bf16[1,768,3072]{2,1,0:T(8,128)(2,1)} async-done(((bf16[1,192,3072]{2,1,0:T(8,128)(2,1)}), bf16[1,768,3072]{2,1,0:T(8,128)(2,1)}) %all-gather.33.cloned.1.call-update) | async-done | bytes 4718608 | tf_op jit(solution)/shard_map/while/body/eval_jaxpr/all_gather | solution.py:60
  2313.6 74.9 %all-gather.31.cloned.1.call-done = bf16[1,3072,768]{2,1,0:T(8,128)(2,1)} async-done(((bf16[1,768,768]{2,1,0:T(8,128)(2,1)}), bf16[1,3072,768]{2,1,0:T(8,128)(2,1)}) %all-gather.31.cloned.1.call-update) | async-done | bytes 4718608 | tf_op jit(solution)/shard_map/while/body/eval_jaxpr/all_gather | solution.py:61
  2441.7 23.7 multiply_convert_fusion.4
  2543.3 32.2 reduce-scatter.20.cloned.1.call-done
  2634.6 77.9 %reduce-scatter.30.cloned.1.call-done = bf16[768,768]{1,0:T(8,128)(2,1)} async-done(((bf16[3072,768]{1,0:T(8,128)(2,1)}), bf16[768,768]{1,0:T(8,128)(2,1)}) %reduce-scatter.30.cloned.1.call-update) | async-done | bytes 1179664 | tf_op jit(solution)/shard_map/while/body/eval_jaxpr/reduce_scatter | solution.py:205
  2716.1 84.6 %reduce-scatter.28.cloned.1.call-done = bf16[192,3072]{1,0:T(8,128)(2,1)} async-done(((bf16[768,3072]{1,0:T(8,128)(2,1)}), bf16[192,3072]{1,0:T(8,128)(2,1)}) %reduce-scatter.28.cloned.1.call-update) | async-done | bytes 1179664 | tf_op jit(solution)/shard_map/while/body/eval_jaxpr/reduce_scatter | solution.py:202
  2802.8 67.1 %reduce-scatter.24.cloned.1.call-done = bf16[192,2304]{1,0:T(8,128)(2,1)} async-done(((bf16[768,2304]{1,0:T(8,128)(2,1)}), bf16[192,2304]{1,0:T(8,128)(2,1)}) %reduce-scatter.24.cloned.1.call-update) | async-done | bytes 884752 | tf_op jit(solution)/shard_map/while/body/eval_jaxpr/reduce_scatter | solution.py:196
  2880.5 65.6 %all-gather.23.cloned.1.call-done = bf16[1,768,2304]{2,1,0:T(8,128)(2,1)} async-done(((bf16[1,192,2304]{2,1,0:T(8,128)(2,1)}), bf16[1,768,2304]{2,1,0:T(8,128)(2,1)}) %all-gather.23.cloned.1.call-update) | async-done | bytes 3538960 | tf_op jit(solution)/shard_map/while/body/eval_jaxpr/all_gather | solution.py:58
  2961.7 80.2 %all-gather.27.cloned.1.call-done = bf16[2,1536,768]{2,1,0:T(8,128)(2,1)} async-done(((bf16[2,384,768]{2,1,0:T(8,128)(2,1)}), bf16[2,1536,768]{2,1,0:T(8,128)(2,1)}) %all-gather.27.cloned.1.call-update) | async-done | bytes 4718608 | tf_op jit(solution)/shard_map/while/body/eval_jaxpr/all_gather | solution.py:86
  3048.7 26.2 fusion.181
  3074.8 47.2 %fusion.182 = (bf16[2,12,384,1536]{3,2,1,0:T(8,128)(2,1)}, f32[2,12,384,1536]{3,2,1,0:T(8,128)}) fusion(f32[2,12,384,1536]{3,2,1,0:T(8,128)} %get-tuple-element.782, f32[2,12,384]{2,1,0:T(8,128)S(1)} %get-tuple-element.783), kind=kLoop, calls=%fused_computation.179.clone.1 | loop fusion | flops 28311552 | bytes 141594624 | tf_op jit(solution)/shard_map/while/body/eval_jaxpr/convert_element_type | solution.py:103
  3167.6 84.3 %all-gather.33.cloned.1.call-done = bf16[1,768,3072]{2,1,0:T(8,128)(2,1)} async-done(((bf16[1,192,3072]{2,1,0:T(8,128)(2,1)}), bf16[1,768,3072]{2,1,0:T(8,128)(2,1)}) %all-gather.33.cloned.1.call-update) | async-done | bytes 4718608 | tf_op jit(solution)/shard_map/while/body/eval_jaxpr/all_gather | solution.py:60
  3266.5 74.7 %all-gather.31.cloned.1.call-done = bf16[1,3072,768]{2,1,0:T(8,128)(2,1)} async-done(((bf16[1,768,768]{2,1,0:T(8,128)(2,1)}), bf16[1,3072,768]{2,1,0:T(8,128)(2,1)}) %all-gather.31.cloned.1.call-update) | async-done | bytes 4718608 | tf_op jit(solution)/shard_map/while/body/eval_jaxpr/all_gather | solution.py:61
  3394.5 23.7 multiply_convert_fusion.4
  3496.1 32.1 reduce-scatter.20.cloned.1.call-done
  3587.2 78.0 %reduce-scatter.30.cloned.1.call-done = bf16[768,768]{1,0:T(8,128)(2,1)} async-done(((bf16[3072,768]{1,0:T(8,128)(2,1)}), bf16[768,768]{1,0:T(8,128)(2,1)}) %reduce-scatter.30.cloned.1.call-update) | async-done | bytes 1179664 | tf_op jit(solution)/shard_map/while/body/eval_jaxpr/reduce_scatter | solution.py:205
  3668.8 84.5 %reduce-scatter.28.cloned.1.call-done = bf16[192,3072]{1,0:T(8,128)(2,1)} async-done(((bf16[768,3072]{1,0:T(8,128)(2,1)}), bf16[192,3072]{1,0:T(8,128)(2,1)}) %reduce-scatter.28.cloned.1.call-update) | async-done | bytes 1179664 | tf_op jit(solution)/shard_map/while/body/eval_jaxpr/reduce_scatter | solution.py:202
  3755.3 67.3 %reduce-scatter.24.cloned.1.call-done = bf16[192,2304]{1,0:T(8,128)(2,1)} async-done(((bf16[768,2304]{1,0:T(8,128)(2,1)}), bf16[192,2304]{1,0:T(8,128)(2,1)}) %reduce-scatter.24.cloned.1.call-update) | async-done | bytes 884752 | tf_op jit(solution)/shard_map/while/body/eval_jaxpr/reduce_scatter | solution.py:196
  3845.6 63.8 %all-reduce.3.cloned.1.call-done = (bf16[1,192,2304]{2,1,0:T(8,128)(2,1)}, bf16[1,192,768]{2,1,0:T(8,128)(2,1)}, bf16[1,192,3072]{2,1,0:T(8,128)(2,1)}, bf16[1,768,768]{2,1,0:T(8,128)(2,1)}) async-done(((bf16[1,192,2304]{2,1,0:T(8,128)(2,1)}, bf16[1,192,768]{2,1,0:T(8,128)(2,1)}, bf16[1,192,3072]{2,1,0:T(8,128)(2,1)}, bf16[1,768,768]{2,1,0:T(8,128)(2,1)}), (bf16[1,192,2304]{2,1,0:T(8,128)(2,1)}, ...) | async-done | bytes 3538960 | tf_op jit(solution)/shard_map/psum | solution.py:229
  (814 shorter events, 1131.8 us)
Async XLA Ops:
  14.3 170.2 %all-gather.27.cloned.1.call-start = ((), (), s32[]{:S(2)}) async-start(), calls=%async_computation.10 | async-start | bytes 5898240 | tf_op jit(solution)/shard_map/while/body/eval_jaxpr/all_gather | solution.py:86
  96.4 177.6 %all-gather.25.cloned.1.call-start = ((), (), s32[]{:S(2)}) async-start(), calls=%async_computation.9 | async-start | bytes 5898240 | tf_op jit(solution)/shard_map/while/body/eval_jaxpr/all_gather | solution.py:89
  97.1 207.2 %all-gather.29.cloned.1.call-start = ((), (), s32[]{:S(2)}) async-start(), calls=%async_computation.11 | async-start | bytes 1474560 | tf_op jit(solution)/shard_map/while/body/eval_jaxpr/all_gather | solution.py:59
  97.7 296.6 %all-gather.33.cloned.1.call-start = ((), (), s32[]{:S(2)}) async-start(), calls=%async_computation.13 | async-start | bytes 5898240 | tf_op jit(solution)/shard_map/while/body/eval_jaxpr/all_gather | solution.py:60
  98.3 385.4 %all-gather.31.cloned.1.call-start = ((), (), s32[]{:S(2)}) async-start(), calls=%async_computation.12 | async-start | bytes 5898240 | tf_op jit(solution)/shard_map/while/body/eval_jaxpr/all_gather | solution.py:61
  98.9 538.2 %reduce-scatter.22.cloned.1.call-start = ((), (), s32[]{:S(2)}) async-start(), calls=%async_computation.15 | async-start | bytes 2949120 | tf_op jit(solution)/shard_map/while
  588.3 127.0 %reduce-scatter.26.cloned.1.call-start = ((), (), s32[]{:S(2)}) async-start(), calls=%async_computation.17 | async-start | bytes 1474560 | tf_op jit(solution)/shard_map/while/body/eval_jaxpr/reduce_scatter | solution.py:199
  593.3 135.3 %reduce-scatter.32.cloned.1.call-start = ((), (), s32[]{:S(2)}) async-start(), calls=%async_computation.20 | async-start | bytes 245760 | tf_op jit(solution)/shard_map/while
  693.0 202.9 %reduce-scatter.28.cloned.1.call-start = ((), (), s32[]{:S(2)}) async-start(), calls=%async_computation.18 | async-start | bytes 5898240 | tf_op jit(solution)/shard_map/while/body/eval_jaxpr/reduce_scatter | solution.py:202
  700.0 265.3 %reduce-scatter.24.cloned.1.call-start = ((), (), s32[]{:S(2)}) async-start(), calls=%async_computation.16 | async-start | bytes 4423680 | tf_op jit(solution)/shard_map/while/body/eval_jaxpr/reduce_scatter | solution.py:196
  723.0 244.9 %collective-permute-start = (bf16[384,768]{1,0:T(8,128)(2,1)}, bf16[384,768]{1,0:T(8,128)(2,1)}, u32[]{:S(2)}, u32[]{:S(2)}) collective-permute-start(bf16[384,768]{1,0:T(8,128)(2,1)} %get-tuple-element.807), channel_id=1, source_target_pairs={{0,16},{1,17},{2,18},{3,19},{4,20},{5,21},{6,22},{7,23},{8,24},{9,... | collective-permute-start | bytes 1769480 | tf_op jit(solution)/shard_map/while/body/eval_jaxpr/ppermute | solution.py:18
  727.3 240.6 %collective-permute-start.1 = (bf16[384,768]{1,0:T(8,128)(2,1)}, bf16[384,768]{1,0:T(8,128)(2,1)}, u32[]{:S(2)}, u32[]{:S(2)}) collective-permute-start(bf16[384,768]{1,0:T(8,128)(2,1)} %get-tuple-element.808), channel_id=1, source_target_pairs={{16,0},{17,1},{18,2},{19,3},{20,4},{21,5},{22,6},{23,7},{24,8},{25... | collective-permute-start | bytes 1769480 | tf_op jit(solution)/shard_map/while/body/eval_jaxpr/ppermute | solution.py:18
  968.9 167.7 %all-gather.27.cloned.1.call-start = ((), (), s32[]{:S(2)}) async-start(), calls=%async_computation.10 | async-start | bytes 5898240 | tf_op jit(solution)/shard_map/while/body/eval_jaxpr/all_gather | solution.py:86
  1048.4 177.5 %all-gather.25.cloned.1.call-start = ((), (), s32[]{:S(2)}) async-start(), calls=%async_computation.9 | async-start | bytes 5898240 | tf_op jit(solution)/shard_map/while/body/eval_jaxpr/all_gather | solution.py:89
  1049.0 207.2 %all-gather.29.cloned.1.call-start = ((), (), s32[]{:S(2)}) async-start(), calls=%async_computation.11 | async-start | bytes 1474560 | tf_op jit(solution)/shard_map/while/body/eval_jaxpr/all_gather | solution.py:59
  1049.6 296.6 %all-gather.33.cloned.1.call-start = ((), (), s32[]{:S(2)}) async-start(), calls=%async_computation.13 | async-start | bytes 5898240 | tf_op jit(solution)/shard_map/while/body/eval_jaxpr/all_gather | solution.py:60
  1050.1 385.5 %all-gather.31.cloned.1.call-start = ((), (), s32[]{:S(2)}) async-start(), calls=%async_computation.12 | async-start | bytes 5898240 | tf_op jit(solution)/shard_map/while/body/eval_jaxpr/all_gather | solution.py:61
  1050.9 538.2 %reduce-scatter.22.cloned.1.call-start = ((), (), s32[]{:S(2)}) async-start(), calls=%async_computation.15 | async-start | bytes 2949120 | tf_op jit(solution)/shard_map/while
  1540.3 127.0 %reduce-scatter.26.cloned.1.call-start = ((), (), s32[]{:S(2)}) async-start(), calls=%async_computation.17 | async-start | bytes 1474560 | tf_op jit(solution)/shard_map/while/body/eval_jaxpr/reduce_scatter | solution.py:199
  1545.3 135.5 %reduce-scatter.32.cloned.1.call-start = ((), (), s32[]{:S(2)}) async-start(), calls=%async_computation.20 | async-start | bytes 245760 | tf_op jit(solution)/shard_map/while
  1645.0 203.1 %reduce-scatter.28.cloned.1.call-start = ((), (), s32[]{:S(2)}) async-start(), calls=%async_computation.18 | async-start | bytes 5898240 | tf_op jit(solution)/shard_map/while/body/eval_jaxpr/reduce_scatter | solution.py:202
  1651.9 265.3 %reduce-scatter.24.cloned.1.call-start = ((), (), s32[]{:S(2)}) async-start(), calls=%async_computation.16 | async-start | bytes 4423680 | tf_op jit(solution)/shard_map/while/body/eval_jaxpr/reduce_scatter | solution.py:196
  1675.1 245.2 %collective-permute-start = (bf16[384,768]{1,0:T(8,128)(2,1)}, bf16[384,768]{1,0:T(8,128)(2,1)}, u32[]{:S(2)}, u32[]{:S(2)}) collective-permute-start(bf16[384,768]{1,0:T(8,128)(2,1)} %get-tuple-element.807), channel_id=1, source_target_pairs={{0,16},{1,17},{2,18},{3,19},{4,20},{5,21},{6,22},{7,23},{8,24},{9,... | collective-permute-start | bytes 1769480 | tf_op jit(solution)/shard_map/while/body/eval_jaxpr/ppermute | solution.py:18
  1679.5 240.9 %collective-permute-start.1 = (bf16[384,768]{1,0:T(8,128)(2,1)}, bf16[384,768]{1,0:T(8,128)(2,1)}, u32[]{:S(2)}, u32[]{:S(2)}) collective-permute-start(bf16[384,768]{1,0:T(8,128)(2,1)} %get-tuple-element.808), channel_id=1, source_target_pairs={{16,0},{17,1},{18,2},{19,3},{20,4},{21,5},{22,6},{23,7},{24,8},{25... | collective-permute-start | bytes 1769480 | tf_op jit(solution)/shard_map/while/body/eval_jaxpr/ppermute | solution.py:18
  1921.4 167.6 %all-gather.27.cloned.1.call-start = ((), (), s32[]{:S(2)}) async-start(), calls=%async_computation.10 | async-start | bytes 5898240 | tf_op jit(solution)/shard_map/while/body/eval_jaxpr/all_gather | solution.py:86
  2000.9 177.6 %all-gather.25.cloned.1.call-start = ((), (), s32[]{:S(2)}) async-start(), calls=%async_computation.9 | async-start | bytes 5898240 | tf_op jit(solution)/shard_map/while/body/eval_jaxpr/all_gather | solution.py:89
  2001.6 207.2 %all-gather.29.cloned.1.call-start = ((), (), s32[]{:S(2)}) async-start(), calls=%async_computation.11 | async-start | bytes 1474560 | tf_op jit(solution)/shard_map/while/body/eval_jaxpr/all_gather | solution.py:59
  2002.2 296.8 %all-gather.33.cloned.1.call-start = ((), (), s32[]{:S(2)}) async-start(), calls=%async_computation.13 | async-start | bytes 5898240 | tf_op jit(solution)/shard_map/while/body/eval_jaxpr/all_gather | solution.py:60
  2003.0 385.5 %all-gather.31.cloned.1.call-start = ((), (), s32[]{:S(2)}) async-start(), calls=%async_computation.12 | async-start | bytes 5898240 | tf_op jit(solution)/shard_map/while/body/eval_jaxpr/all_gather | solution.py:61
  2003.7 538.2 %reduce-scatter.22.cloned.1.call-start = ((), (), s32[]{:S(2)}) async-start(), calls=%async_computation.15 | async-start | bytes 2949120 | tf_op jit(solution)/shard_map/while
  2493.1 127.0 %reduce-scatter.26.cloned.1.call-start = ((), (), s32[]{:S(2)}) async-start(), calls=%async_computation.17 | async-start | bytes 1474560 | tf_op jit(solution)/shard_map/while/body/eval_jaxpr/reduce_scatter | solution.py:199
  2498.1 135.5 %reduce-scatter.32.cloned.1.call-start = ((), (), s32[]{:S(2)}) async-start(), calls=%async_computation.20 | async-start | bytes 245760 | tf_op jit(solution)/shard_map/while
  2597.8 202.9 %reduce-scatter.28.cloned.1.call-start = ((), (), s32[]{:S(2)}) async-start(), calls=%async_computation.18 | async-start | bytes 5898240 | tf_op jit(solution)/shard_map/while/body/eval_jaxpr/reduce_scatter | solution.py:202
  2604.8 265.2 %reduce-scatter.24.cloned.1.call-start = ((), (), s32[]{:S(2)}) async-start(), calls=%async_computation.16 | async-start | bytes 4423680 | tf_op jit(solution)/shard_map/while/body/eval_jaxpr/reduce_scatter | solution.py:196
  2628.0 245.0 %collective-permute-start = (bf16[384,768]{1,0:T(8,128)(2,1)}, bf16[384,768]{1,0:T(8,128)(2,1)}, u32[]{:S(2)}, u32[]{:S(2)}) collective-permute-start(bf16[384,768]{1,0:T(8,128)(2,1)} %get-tuple-element.807), channel_id=1, source_target_pairs={{0,16},{1,17},{2,18},{3,19},{4,20},{5,21},{6,22},{7,23},{8,24},{9,... | collective-permute-start | bytes 1769480 | tf_op jit(solution)/shard_map/while/body/eval_jaxpr/ppermute | solution.py:18
  2632.3 240.7 %collective-permute-start.1 = (bf16[384,768]{1,0:T(8,128)(2,1)}, bf16[384,768]{1,0:T(8,128)(2,1)}, u32[]{:S(2)}, u32[]{:S(2)}) collective-permute-start(bf16[384,768]{1,0:T(8,128)(2,1)} %get-tuple-element.808), channel_id=1, source_target_pairs={{16,0},{17,1},{18,2},{19,3},{20,4},{21,5},{22,6},{23,7},{24,8},{25... | collective-permute-start | bytes 1769480 | tf_op jit(solution)/shard_map/while/body/eval_jaxpr/ppermute | solution.py:18
  2874.2 167.8 %all-gather.27.cloned.1.call-start = ((), (), s32[]{:S(2)}) async-start(), calls=%async_computation.10 | async-start | bytes 5898240 | tf_op jit(solution)/shard_map/while/body/eval_jaxpr/all_gather | solution.py:86
  2953.8 177.6 %all-gather.25.cloned.1.call-start = ((), (), s32[]{:S(2)}) async-start(), calls=%async_computation.9 | async-start | bytes 5898240 | tf_op jit(solution)/shard_map/while/body/eval_jaxpr/all_gather | solution.py:89
  2954.6 207.2 %all-gather.29.cloned.1.call-start = ((), (), s32[]{:S(2)}) async-start(), calls=%async_computation.11 | async-start | bytes 1474560 | tf_op jit(solution)/shard_map/while/body/eval_jaxpr/all_gather | solution.py:59
  2955.2 296.8 %all-gather.33.cloned.1.call-start = ((), (), s32[]{:S(2)}) async-start(), calls=%async_computation.13 | async-start | bytes 5898240 | tf_op jit(solution)/shard_map/while/body/eval_jaxpr/all_gather | solution.py:60
  2955.9 385.3 %all-gather.31.cloned.1.call-start = ((), (), s32[]{:S(2)}) async-start(), calls=%async_computation.12 | async-start | bytes 5898240 | tf_op jit(solution)/shard_map/while/body/eval_jaxpr/all_gather | solution.py:61
  2956.5 538.2 %reduce-scatter.22.cloned.1.call-start = ((), (), s32[]{:S(2)}) async-start(), calls=%async_computation.15 | async-start | bytes 2949120 | tf_op jit(solution)/shard_map/while
  3445.9 126.9 %reduce-scatter.26.cloned.1.call-start = ((), (), s32[]{:S(2)}) async-start(), calls=%async_computation.17 | async-start | bytes 1474560 | tf_op jit(solution)/shard_map/while/body/eval_jaxpr/reduce_scatter | solution.py:199
  3450.9 135.4 %reduce-scatter.32.cloned.1.call-start = ((), (), s32[]{:S(2)}) async-start(), calls=%async_computation.20 | async-start | bytes 245760 | tf_op jit(solution)/shard_map/while
  3550.4 202.8 %reduce-scatter.28.cloned.1.call-start = ((), (), s32[]{:S(2)}) async-start(), calls=%async_computation.18 | async-start | bytes 5898240 | tf_op jit(solution)/shard_map/while/body/eval_jaxpr/reduce_scatter | solution.py:202
  3557.4 265.2 %reduce-scatter.24.cloned.1.call-start = ((), (), s32[]{:S(2)}) async-start(), calls=%async_computation.16 | async-start | bytes 4423680 | tf_op jit(solution)/shard_map/while/body/eval_jaxpr/reduce_scatter | solution.py:196
  3580.6 245.1 %collective-permute-start = (bf16[384,768]{1,0:T(8,128)(2,1)}, bf16[384,768]{1,0:T(8,128)(2,1)}, u32[]{:S(2)}, u32[]{:S(2)}) collective-permute-start(bf16[384,768]{1,0:T(8,128)(2,1)} %get-tuple-element.807), channel_id=1, source_target_pairs={{0,16},{1,17},{2,18},{3,19},{4,20},{5,21},{6,22},{7,23},{8,24},{9,... | collective-permute-start | bytes 1769480 | tf_op jit(solution)/shard_map/while/body/eval_jaxpr/ppermute | solution.py:18
  3584.9 240.7 %collective-permute-start.1 = (bf16[384,768]{1,0:T(8,128)(2,1)}, bf16[384,768]{1,0:T(8,128)(2,1)}, u32[]{:S(2)}, u32[]{:S(2)}) collective-permute-start(bf16[384,768]{1,0:T(8,128)(2,1)} %get-tuple-element.808), channel_id=1, source_target_pairs={{16,0},{17,1},{18,2},{19,3},{20,4},{21,5},{22,6},{23,7},{24,8},{25... | collective-permute-start | bytes 1769480 | tf_op jit(solution)/shard_map/while/body/eval_jaxpr/ppermute | solution.py:18
  (168 other events, 4862.6 us)
Sparse Core Ops, SparseCore 0:
  16.0 72.6 all-gather.22
  96.5 87.9 all-gather.26
  186.1 87.8 all-gather.24
  275.5 28.8 all-gather.28
  305.8 88.5 all-gather.32
  395.8 87.8 all-gather.30
  574.4 46.4 reduce-scatter.21
  623.2 47.5 reduce-scatter.19
  673.1 28.6 reduce-scatter.25
  724.4 83.4 reduce-scatter.29
  810.2 85.7 reduce-scatter.27
  898.4 66.8 reduce-scatter.23
  970.4 70.2 all-gather.22
  1048.5 87.9 all-gather.26
  1138.0 87.8 all-gather.24
  1227.3 28.8 all-gather.28
  1257.6 88.5 all-gather.32
  1347.8 87.8 all-gather.30
  1526.3 46.4 reduce-scatter.21
  1575.2 47.5 reduce-scatter.19
  1625.0 28.6 reduce-scatter.25
  1676.4 83.4 reduce-scatter.29
  1762.3 85.7 reduce-scatter.27
  1850.4 66.8 reduce-scatter.23
  1922.9 70.2 all-gather.22
  2001.0 87.9 all-gather.26
  2090.6 87.8 all-gather.24
  2179.9 28.8 all-gather.28
  2210.4 88.5 all-gather.32
  2300.6 87.8 all-gather.30
  2479.1 46.4 reduce-scatter.21
  2528.0 47.5 reduce-scatter.19
  2577.9 28.6 reduce-scatter.25
  2629.0 83.4 reduce-scatter.29
  2714.9 85.7 reduce-scatter.27
  2803.0 66.8 reduce-scatter.23
  2875.8 70.2 all-gather.22
  2953.9 87.9 all-gather.26
  3043.6 87.8 all-gather.24
  3132.9 28.8 all-gather.28
  3163.4 88.5 all-gather.32
  3253.3 87.8 all-gather.30
  3431.9 46.4 reduce-scatter.21
  3480.6 47.5 reduce-scatter.19
  3530.3 28.6 reduce-scatter.25
  3581.7 83.4 reduce-scatter.29
  3667.4 85.7 reduce-scatter.27
  3755.7 66.8 reduce-scatter.23
  (4 shorter events, 72.1 us)
Sparse Core Ops, SparseCore 1:
  3833.8 75.5 all-reduce.2
where the time goes:
time: 3930 us; the launch traced here: 3920 us
  waiting for transfers between devices  2420 us (62%)
  matrix products  682 us (17%)
  other arithmetic  501 us (13%)
  local copies, waits for them, and re-layouts  266 us (7%)
    reduce_scatter x4, waiting for transfers between devices, one_tick(): lax.psum_scatter(weight_grads[2].astype(jnp.bfloat16), 'shard', scatter_d...  339 us
    all_gather x4, waiting for transfers between devices, one_tick(): lax.all_gather(mlp_up[0], 'shard', axis=0, tiled=True)  337 us
    all_gather x4, waiting for transfers between devices, one_tick(): lax.all_gather(projected[..., model_width:2 * model_width], 'shard', axis...  321 us
    reduce_scatter x4, waiting for transfers between devices, one_tick(): lax.psum_scatter(weight_grads[3].astype(jnp.bfloat16), 'shard', scatter_d...  312 us
    all_gather x4, waiting for transfers between devices, one_tick(): lax.all_gather(mlp_down[0], 'shard', axis=0, tiled=True)  299 us
    reduce_scatter x4, waiting for transfers between devices, one_tick(): lax.psum_scatter(weight_grads[0].astype(jnp.bfloat16), 'shard', scatter_d...  269 us
    all_gather x4, waiting for transfers between devices, one_tick(): lax.all_gather(attn_in[0], 'shard', axis=0, tiled=True)  265 us
    convert_element_type x4, other arithmetic, one_tick(): probs_low = attention_probs.astype(jnp.bfloat16)  189 us
  transfers between devices with their start and end apart: 61, of which 41 were waited for; matrix products, arithmetic and copies ran while one was open for 26% of the time, Pallas kernels for 0%

commit v1 on v0

v1 whole, which is shorter than its diff:
```python
import functools

import jax
import jax.numpy as jnp
from jax import lax
from jax.experimental import pallas as pl
from jax.experimental.pallas import tpu as pltpu
from jax.sharding import PartitionSpec as P

H = 12
EPS = 1e-05
MASKED = -1e30
QUARTERS = 4
BF16 = jnp.bfloat16
F32 = jnp.float32
AXES = ("section", "shard", "replica")
NN = (((1,), (0,)), ((), ()))
NT = (((1,), (1,)), ((), ()))
TN = (((0,), (0,)), ((), ()))


def dot(a, b, dims=NN):
    return lax.dot_general(a, b, dims, preferred_element_type=F32)


def layer_norm(values, gain, shift):
    center = values - jnp.mean(values, -1, keepdims=True)
    spread = jnp.mean(center * center, -1, keepdims=True)
    return center * lax.rsqrt(spread + EPS) * gain + shift


def key_chunks(sources, size):
    chunks, base = [], 0
    for source in range(len(sources)):
        rows = sources[source].shape[0]
        for start in range(0, rows, size):
            chunks.append((source, start, base + start))
        base += rows
    return chunks


def attend_kernel(own_ref, other_ref, bias_ref, out_ref, exp_ref, inv_ref, score_ref, *, heads, frames, chunk):
    dim = own_ref.shape[1] // (3 * heads)
    wide = heads * dim
    sources = (own_ref, other_ref)
    chunks = key_chunks(sources, chunk)
    outs = []
    for head in range(heads):
        at = head * dim
        query = own_ref[0:frames, at:at + dim] * (dim ** -0.5)
        lane = lax.broadcasted_iota(jnp.int32, (frames, dim), 1)
        query = jnp.concatenate([query.astype(BF16), (lane == 0).astype(BF16)], 1)
        top = None
        for source, start, row in chunks:
            shift = wide if source == 0 else 0
            key = sources[source][start:start + chunk, shift + at:shift + at + dim]
            key = jnp.concatenate([key, bias_ref[row:row + chunk, :]], 1)
            score = dot(key, query, NT)
            score_ref[row:row + chunk, :] = score
            part = jnp.max(score, 0, keepdims=True)
            top = part if top is None else jnp.maximum(top, part)
        total = None
        for source, start, row in chunks:
            shift = 2 * wide if source == 0 else wide
            weight = jnp.exp(score_ref[row:row + chunk, :] - top).astype(BF16)
            exp_ref[head, row:row + chunk, :] = weight
            value = sources[source][start:start + chunk, shift + at:shift + at + dim]
            value = jnp.concatenate([value, jnp.ones_like(value)], 1)
            part = dot(value, weight, TN)
            total = part if total is None else total + part
        inverse = 1.0 / total[dim:dim + 1, :]
        inv_ref[head:head + 1, :] = inverse
        outs.append((total[0:dim, :] * inverse).T)
    out_ref[...] = jnp.concatenate(outs, 1).astype(BF16)


def attend(own, other, bias, heads, frames):
    keys = own.shape[0] + other.shape[0]
    wide = own.shape[1] // 3
    chunk = min(256, frames)
    if own.shape[0] % chunk:
        chunk = frames
    return pl.pallas_call(
        functools.partial(attend_kernel, heads=heads, frames=frames, chunk=chunk),
        out_shape=(
            jax.ShapeDtypeStruct((frames, wide), BF16),
            jax.ShapeDtypeStruct((heads, keys, frames), BF16),
            jax.ShapeDtypeStruct((heads, frames), F32),
        ),
        scratch_shapes=[pltpu.VMEM((keys, frames), F32)],
        compiler_params=pltpu.CompilerParams(vmem_limit_bytes=40 * 2**20),
        cost_estimate=pl.CostEstimate(
            flops=16 * keys * frames * wide, bytes_accessed=2 * heads * keys * frames, transcendentals=heads * keys * frames
        ),
        name="attend",
    )(own, other, bias)


def attend_back_kernel(own_ref, other_ref, exp_ref, inv_ref, dout_ref, dq_ref, dk_ref, dv_ref, prod_ref, *, heads, frames, chunk):
    dim = own_ref.shape[1] // (3 * heads)
    wide = heads * dim
    scale = dim ** -0.5
    sources = (own_ref, other_ref)
    chunks = key_chunks(sources, chunk)
    dqs = []
    dks, dvs = [[] for _ in chunks], [[] for _ in chunks]
    for head in range(heads):
        at = head * dim
        query = (own_ref[0:frames, at:at + dim] * scale).astype(BF16)
        inverse = inv_ref[head:head + 1, :]
        dout_t = dout_ref[:, at:at + dim].astype(F32).T * inverse
        dout = dout_t.T.astype(BF16)
        dout_t = dout_t.astype(BF16)
        delta = None
        for index, (source, start, row) in enumerate(chunks):
            shift = 2 * wide if source == 0 else wide
            value = sources[source][start:start + chunk, shift + at:shift + at + dim]
            weight = exp_ref[head, row:row + chunk, :]
            prod = dot(value, dout_t) * weight.astype(F32)
            prod_ref[row:row + chunk, :] = prod
            part = jnp.sum(prod, 0, keepdims=True)
            delta = part if delta is None else delta + part
            dvs[index].append(dot(weight, dout))
        delta = delta * inverse
        dq_t = None
        for index, (source, start, row) in enumerate(chunks):
            shift = wide if source == 0 else 0
            key = sources[source][start:start + chunk, shift + at:shift + at + dim]
            weight = exp_ref[head, row:row + chunk, :].astype(F32)
            ds = (prod_ref[row:row + chunk, :] - weight * delta).astype(BF16)
            dks[index].append(dot(ds, query))
            part = dot(key, ds, TN)
            dq_t = part if dq_t is None else dq_t + part
        dqs.append(dq_t.T * scale)
    dq_ref[...] = jnp.concatenate(dqs, 1).astype(BF16)
    for index, (source, start, row) in enumerate(chunks):
        dk_ref[row:row + chunk, :] = jnp.concatenate(dks[index], 1).astype(BF16)
        dv_ref[row:row + chunk, :] = jnp.concatenate(dvs[index], 1).astype(BF16)


def attend_back(own, other, weights, inverse, dout, heads, frames):
    keys = own.shape[0] + other.shape[0]
    wide = own.shape[1] // 3
    chunk = min(256, frames)
    if own.shape[0] % chunk:
        chunk = frames
    return pl.pallas_call(
        functools.partial(attend_back_kernel, heads=heads, frames=frames, chunk=chunk),
        out_shape=(
            jax.ShapeDtypeStruct((frames, wide), BF16),
            jax.ShapeDtypeStruct((keys, wide), BF16),
            jax.ShapeDtypeStruct((keys, wide), BF16),
        ),
        scratch_shapes=[pltpu.VMEM((keys, frames), F32)],
        compiler_params=pltpu.CompilerParams(vmem_limit_bytes=40 * 2**20),
        cost_estimate=pl.CostEstimate(
            flops=32 * keys * frames * wide, bytes_accessed=2 * heads * keys * frames, transcendentals=0
        ),
        name="attend_back",
    )(own, other, weights, inverse, dout)


def up_kernel(in_ref, weight_ref, bias_ref, act_ref, slope_ref):
    up = dot(in_ref[...], weight_ref[...]) + bias_ref[...]
    cdf = 0.5 + 0.5 * lax.erf(up * (0.5 ** 0.5))
    pdf = jnp.exp(-0.5 * up * up) * 0.3989422804014327
    act_ref[...] = (up * cdf).astype(BF16)
    slope_ref[...] = (cdf + up * pdf).astype(BF16)


def up_gelu(values, weight, bias):
    rows, depth = values.shape
    columns = weight.shape[1]
    tile = 256 if columns % 256 == 0 else columns
    return pl.pallas_call(
        up_kernel,
        grid=(columns // tile,),
        in_specs=[
            pl.BlockSpec((rows, depth), lambda i: (0, 0)),
            pl.BlockSpec((depth, tile), lambda i: (0, i)),
            pl.BlockSpec((1, tile), lambda i: (0, i)),
        ],
        out_specs=[pl.BlockSpec((rows, tile), lambda i: (0, i))] * 2,
        out_shape=[jax.ShapeDtypeStruct((rows, columns), BF16)] * 2,
        compiler_params=pltpu.CompilerParams(vmem_limit_bytes=32 * 2**20),
        cost_estimate=pl.CostEstimate(
            flops=2 * rows * depth * columns, bytes_accessed=2 * (rows * depth + depth * columns + 2 * rows * columns),
            transcendentals=2 * rows * columns,
        ),
        name="up_gelu",
    )(values, weight, bias)


def across(block, bit):
    count = lax.axis_size("replica")
    return lax.ppermute(block, "replica", [(i, i ^ bit) for i in range(count)])


def swap_sections(block):
    return lax.ppermute(block, "section", [(0, 1), (1, 0)])


def transposed(block, source, target):
    shards, replicas = lax.axis_size("shard"), lax.axis_size("replica")

    def flat(section, shard, replica):
        return (section * shards + shard) * replicas + replica

    route = []
    for shard in range(shards):
        for replica in range(replicas):
            group, place = divmod(replica, shards)
            here, there = (shard, replica), (place, group * shards + shard)
            if source is None:
                route += [(flat(s, *here), flat(s, *there)) for s in range(2)]
            else:
                route.append((flat(source, *here), flat(target, *there)))
    return lax.ppermute(block, AXES, route)


def in_order(pieces, quarter):
    odd, high = (quarter & 1) == 1, (quarter & 2) == 2
    a, b, c, d = pieces
    a, b, c, d = jnp.where(odd, b, a), jnp.where(odd, a, b), jnp.where(odd, d, c), jnp.where(odd, c, d)
    return jnp.where(high, c, a), jnp.where(high, d, b), jnp.where(high, a, c), jnp.where(high, b, d)


def spread(piece):
    far = across(piece, 2)
    return piece, across(piece, 1), far, across(far, 1)


def reduced(pieces):
    near = [across(pieces[1], 1), across(pieces[3], 1)]
    own = (pieces[0].astype(F32) + near[0].astype(F32)).astype(BF16)
    far = (pieces[2].astype(F32) + near[1].astype(F32)).astype(BF16)
    own = (own.astype(F32) + across(far, 2).astype(F32)).astype(BF16)
    bit = QUARTERS
    while bit < lax.axis_size("replica"):
        own = (own.astype(F32) + across(own, bit).astype(F32)).astype(BF16)
        bit *= 2
    return own


def body(edges, attn_in, attn_out, mlp_up, mlp_down, vectors, key_mask):
    section = lax.axis_index("section")
    first = section == 0
    replica = lax.axis_index("replica")
    shards, replicas = lax.axis_size("shard"), lax.axis_size("replica")
    quarter = replica % QUARTERS
    edges_here = edges[0]
    clips, frames, width = edges_here.shape
    hidden = mlp_up.shape[2]
    dim = width // H
    heads = H // QUARTERS
    wide = heads * dim
    unit = hidden // (shards * QUARTERS)
    rows = attn_in.shape[1]
    assert clips == 2 and lax.axis_size("section") == 2 and replicas % shards == 0 and replicas % QUARTERS == 0

    inputs = jnp.where(first, transposed(edges_here[0], 0, 0), transposed(edges_here[1], 0, 1))
    mask_row = transposed(
        lax.dynamic_index_in_dim(key_mask, section, 0, keepdims=False).astype(F32)[None], None, None
    )[0]

    def pick(block, axis):
        return lax.dynamic_index_in_dim(block, quarter, axis, keepdims=False)

    def gathered(block):
        return lax.all_gather(block, "shard", axis=0, tiled=True)

    own_parts = (
        gathered(pick(attn_in[0].reshape(rows, 3, QUARTERS, wide), 2).reshape(rows, 3 * wide)),
        gathered(attn_out[0]),
        gathered(pick(mlp_up[0].reshape(rows, shards, QUARTERS, unit), 2).reshape(rows, shards * unit)),
        gathered(pick(mlp_down[0].reshape(QUARTERS, unit, width), 0)),
    )
    other_parts = tuple(swap_sections(part) for part in own_parts)
    vector_other = swap_sections(vectors[0])
    layers = []
    for layer in range(2):
        mine = first if layer == 0 else ~first
        w_in, w_out, w_up, w_down = (jnp.where(mine, a, b) for a, b in zip(own_parts, other_parts))
        layers.append((spread(w_in), w_out, spread(w_up), spread(w_down), jnp.where(mine, vectors[0], vector_other)))

    members = [0]
    bit = 2
    while bit < shards:
        members = members + [m ^ bit for m in members]
        bit *= 2
    members = members + [m ^ 1 for m in members]
    place = replica % shards
    bias_row = jnp.concatenate(
        [lax.dynamic_slice_in_dim(mask_row, (place ^ m) * frames, frames, 0) for m in members]
    )
    bias_row = jnp.where(bias_row > 0, 0.0, MASKED).astype(BF16)
    lane = jnp.arange(dim)[None, :]
    key_bias = jnp.where(lane == 0, bias_row[:, None], jnp.zeros((), BF16))

    def chips_rows(block):
        bit = 2
        while bit < shards:
            block = jnp.concatenate([block, across(block, bit)], 0)
            bit *= 2
        return block

    def forward(x_low, layer):
        w_in, w_out, w_up, w_down, vec = layers[layer]
        x_set = chips_rows(x_low)
        normed = layer_norm(x_set.astype(F32), vec[0], vec[1]).astype(BF16)
        zeros = jnp.zeros((QUARTERS, wide), F32)
        bias_in = jnp.stack([vec[2].reshape(QUARTERS, wide), zeros, vec[3].reshape(QUARTERS, wide)], 1)
        own_qkv, other_kv = [], [None] * QUARTERS
        for p in range(QUARTERS):
            bias = lax.dynamic_index_in_dim(bias_in, quarter ^ p, 0, keepdims=False).reshape(3 * wide)
            own_qkv.append((dot(normed, w_in[p]) + bias).astype(BF16))
            other_kv[p ^ 1] = across(own_qkv[p][:, wide:], 1)
        outs, weights, inverses = [], [], []
        for p in range(QUARTERS):
            out, weight, inverse = attend(own_qkv[p], other_kv[p], key_bias, heads, frames)
            outs.append(out)
            weights.append(weight)
            inverses.append(inverse)
        attended = jnp.concatenate(in_order(outs, quarter), 1)
        x = x_low.astype(F32)
        middle = x + dot(attended, w_out) + vec[4]
        normed_two = layer_norm(middle, vec[5], vec[6]).astype(BF16)
        bias_up = vec[8:].reshape(shards, QUARTERS, unit)
        acts, slopes = [], []
        result = middle + vec[7]
        for p in range(QUARTERS):
            bias = lax.dynamic_index_in_dim(bias_up, quarter ^ p, 1, keepdims=False).reshape(1, shards * unit)
            act, slope = up_gelu(normed_two, w_up[p], bias)
            acts.append(act)
            slopes.append(slope)
            result = result + dot(act, w_down[p])
        kept = (x, normed, own_qkv, other_kv, weights, inverses, attended, middle, normed_two, acts, slopes)
        return result.astype(BF16), kept

    def norm_back(values, gain, grad):
        center = values - jnp.mean(values, -1, keepdims=True)
        inv = lax.rsqrt(jnp.mean(center * center, -1, keepdims=True) + EPS)
        unit_values = center * inv
        scaled = grad * gain
        back = inv * (
            scaled - jnp.mean(scaled, -1, keepdims=True)
            - unit_values * jnp.mean(scaled * unit_values, -1, keepdims=True)
        )
        return back, jnp.sum(grad * unit_values, 0), jnp.sum(grad, 0)

    def backward(cot, layer, kept):
        w_in, w_out, w_up, w_down, vec = layers[layer]
        x, normed, own_qkv, other_kv, weights, inverses, attended, middle, normed_two, acts, slopes = kept
        d_mlp = cot.astype(BF16)
        g_down, g_up, up_sums = [], [], []
        d_normed_two = None
        for p in range(QUARTERS):
            d_up = (dot(d_mlp, w_down[p], NT) * slopes[p].astype(F32)).astype(BF16)
            part = dot(d_up, w_up[p], NT)
            d_normed_two = part if d_normed_two is None else d_normed_two + part
            g_down.append(dot(acts[p], d_mlp, TN).astype(BF16))
            g_up.append(dot(normed_two, d_up, TN).astype(BF16))
            up_sums.append(jnp.sum(d_up.astype(F32), 0))
        back, g_gain_two, g_shift_two = norm_back(middle, vec[5], d_normed_two)
        d_middle = cot + back
        d_attn = d_middle.astype(BF16)
        d_attn_parts = in_order([d_attn[:, p * wide:(p + 1) * wide] for p in range(QUARTERS)], quarter)
        g_out = [dot(attended, part, TN).astype(BF16) for part in d_attn_parts]
        d_attended = dot(d_attn, w_out, NT).astype(BF16)
        d_heads = in_order([d_attended[:, p * wide:(p + 1) * wide] for p in range(QUARTERS)], quarter)
        half = own_qkv[0].shape[0]
        d_normed, g_in, sums_in = None, [], []
        d_normed_own = None
        results = [
            attend_back(own_qkv[p], other_kv[p], weights[p], inverses[p], d_heads[p], heads, frames)
            for p in range(QUARTERS)
        ]
        for p in range(QUARTERS):
            d_query, d_key, d_value = results[p]
            r_key, r_value = results[p ^ 1][1], results[p ^ 1][2]
            d_key = (d_key[:half].astype(F32) + across(r_key[half:], 1).astype(F32)).astype(BF16)
            d_value = (d_value[:half].astype(F32) + across(r_value[half:], 1).astype(F32)).astype(BF16)
            d_both = jnp.concatenate([d_key, d_value], 1)
            part = dot(d_both, w_in[p][:, wide:], NT)
            d_normed = part if d_normed is None else d_normed + part
            part = dot(d_query, w_in[p][:, :wide], NT)
            d_normed_own = part if d_normed_own is None else d_normed_own + part
            g_in.append(
                jnp.concatenate(
                    [dot(normed[:frames], d_query, TN).astype(BF16), dot(normed, d_both, TN).astype(BF16)], 1
                )
            )
            sums_in.append(
                (jnp.sum(d_query.astype(F32), 0), jnp.sum(d_value.astype(F32), 0))
            )
        block = d_normed
        bit = shards // 2
        while bit >= 2:
            cut = block.shape[0] // 2
            block = block[:cut] + across(block[cut:].astype(BF16), bit).astype(F32)
            bit //= 2
        back, g_gain_one, g_shift_one = norm_back(x, vec[0], block + d_normed_own)
        g_x = d_middle + back
        sum_query = jnp.concatenate(in_order([s[0] for s in sums_in], quarter))
        sum_value = jnp.concatenate(in_order([s[1] for s in sums_in], quarter))
        sum_up = jnp.stack(in_order([s.reshape(shards, unit) for s in up_sums], quarter), 1).reshape(-1, width)
        g_vec = jnp.concatenate(
            [
                jnp.stack(
                    [
                        g_gain_one, g_shift_one, sum_query, sum_value,
                        jnp.sum(d_attn.astype(F32), 0), g_gain_two, g_shift_two,
                        jnp.sum(d_mlp.astype(F32), 0),
                    ]
                ),
                sum_up,
            ]
        )
        return g_x, (g_in, g_out, g_up, g_down), g_vec

    def owned(grads, layer):
        route = [(0, 1)] if layer == 1 else [(1, 0)]
        done = []
        for pieces in grads:
            part = reduced(pieces)
            part = (part.astype(F32) + lax.ppermute(part, "section", route).astype(F32)).astype(BF16)
            done.append(lax.psum_scatter(part, "shard", scatter_dimension=0, tiled=True))
        return done

    x_one, kept_zero = forward(inputs, 0)
    y_one, kept_one = forward(x_one, 1)
    cot = jnp.where(first, transposed(edges_here[0], 1, 0), transposed(edges_here[1], 1, 1))
    out_slots = [transposed(y_one, 0, 1), transposed(y_one, 1, 1)]
    g_one, grads_one, vec_one = backward(cot.astype(F32), 1, kept_one)
    owned_one = owned(grads_one, 1)
    g_zero, grads_zero, vec_zero = backward(g_one.astype(BF16).astype(F32), 0, kept_zero)
    owned_zero = owned(grads_zero, 0)
    g_low = g_zero.astype(BF16)
    back_slots = [transposed(g_low, 0, 0), transposed(g_low, 1, 0)]
    edges_out = jnp.stack([jnp.where(first, b, o) for b, o in zip(back_slots, out_slots)])

    vec_all = lax.psum(jnp.concatenate([vec_zero, vec_one]), AXES)
    vec_all = jnp.where(first, vec_all[:12], vec_all[12:])
    slice_width = width // shards
    g_vectors = lax.dynamic_slice_in_dim(vec_all, lax.axis_index("shard") * slice_width, slice_width, 1)

    finals = []
    for zero, one in zip(owned_zero, owned_one):
        part = jnp.where(first, zero, one)
        finals.append(jnp.stack(in_order(spread(part), quarter)).astype(F32))
    f_in, f_out, f_up, f_down = finals
    f_in = f_in.reshape(QUARTERS, rows, 3, wide).transpose(1, 2, 0, 3).reshape(rows, 3 * width)
    f_out = f_out.transpose(1, 0, 2).reshape(rows, width)
    f_up = f_up.reshape(QUARTERS, rows, shards, unit).transpose(1, 2, 0, 3).reshape(rows, hidden)
    f_down = f_down.reshape(-1, width)
    return edges_out[None], f_in[None], f_out[None], f_up[None], f_down[None], g_vectors[None]


def solution(mesh):
    placed = (
        P("section", "replica", "shard", None),
        P("section", "shard", None),
        P("section", "shard", None),
        P("section", "shard", None),
        P("section", "shard", None),
        P("section", None, None),
        P("replica", None),
    )
    return jax.shard_map(
        body,
        mesh=mesh,
        in_specs=placed,
        out_specs=(
            P("section", "replica", "shard", None),
            P("section", "shard", None),
            P("section", "shard", None),
            P("section", "shard", None),
            P("section", "shard", None),
            P("section", None, "shard"),
        ),
        check_vma=False,
    )
```

time: 3930 us -> 1050 us (0.27)
  waiting for transfers between devices: 2420 us -> 331 us
  matrix products: 682 us -> 129 us
  other arithmetic: 501 us -> 86.2 us
  starting transfers between devices: 26.2 us -> 166 us
  local copies, waits for them, and re-layouts: 266 us -> 137 us
  Pallas kernels: 0 us -> 86.1 us
  blocking collectives: 11.2 us -> 91.2 us
    all_gather x24 -> x3, waiting for transfers between devices: 1290 us -> 0.02 us  [gathered(): return lax.all_gather(block, 'shard', axis=0, tiled=True)]
    reduce_scatter x16 -> x4, waiting for transfers between devices: 920 us -> 49.5 us  [owned(): lax.psum_scatter(part, 'shard', scatter_dimension=0, tiled=True)]
    dot_general x68 -> x92, matrix products: 577 us -> 129 us  [dot(): return lax.dot_general(a, b, dims, preferred_element_type=F32)]
    convert_element_type x24 -> x36, other arithmetic: 387 us -> 39.8 us  [the longest x8 12.6 us: reduced(): own = (own.astype(F32) + across(far, 2).astype(F32)).astype(BF16)]
    ppermute x8 -> x104, waiting for transfers between devices: 0.02 us -> 282 us  [the longest x82 129 us: across(): return lax.ppermute(block, 'replica', [(i, i ^ bit) for i in range(count)])]
    ppermute x8 -> x104, starting transfers between devices: 22.5 us -> 165 us  [the longest x82 108 us: across(): return lax.ppermute(block, 'replica', [(i, i ^ bit) for i in range(count)])]
    while x64 -> x0, waiting for transfers between devices: 141 us -> none
    sub x4 -> x0, matrix products: 105 us -> none  [one_tick(): exp_scores = jnp.exp(scores - jnp.max(scores, -1, keepdims=True))]
  transfers between devices with their start and end apart: 61 -> 116, of which waited for: 41 -> 27; matrix products, arithmetic and copies ran while one was open for 26% -> 26% of each run, Pallas kernels for 0% -> 6%
where the time goes in v1:
time: 1050 us; the launch traced here: 1040 us
  waiting for transfers between devices  331 us (32%)
  starting transfers between devices  166 us (16%)
  local copies, waits for them, and re-layouts  137 us (13%)
  matrix products  129 us (12%)
  blocking collectives  91.2 us (9%)
  other arithmetic  86.2 us (8%)
  Pallas kernels  86.1 us (8%)
  between operations  18.4 us (2%)
    dot_general x92, matrix products, dot(): return lax.dot_general(a, b, dims, preferred_element_type=F32)  129 us
    ppermute x82, waiting for transfers between devices, across(): return lax.ppermute(block, 'replica', [(i, i ^ bit) for i in range(count)])  129 us
    ppermute x8, waiting for transfers between devices, owned(): lax.ppermute(part, 'section', route).astype(F32)  108 us
    ppermute x82, starting transfers between devices, across(): return lax.ppermute(block, 'replica', [(i, i ^ bit) for i in range(count)])  108 us
    all_gather x1, blocking collectives, gathered(): return lax.all_gather(block, 'shard', axis=0, tiled=True)  91.2 us
    unnamed x629, local copies, waits for them, and re-layouts  55.6 us
    reduce_scatter x4, waiting for transfers between devices, owned(): lax.psum_scatter(part, 'shard', scatter_dimension=0, tiled=True)  49.5 us
    pallas_call x8, Pallas kernels, attend_back(): pl.pallas_call(functools.partial(attend_back_kernel, heads=heads, frames=...  42.7 us
  transfers between devices with their start and end apart: 116, of which 27 were waited for; matrix products, arithmetic and copies ran while one was open for 26% of the time, Pallas kernels for 6%

profile of v1, /device:TPU:0, one launch (start us, length us, event | category | flops | bytes accessed | tf_op | source)
XLA Modules:
  0.0 1044.8 jit_solution(11231938940426054421)
XLA Ops:
  7.2 3.8 reshape_squeeze.10
  16.8 5.9 collective-permute-start.2
  24.1 6.2 collective-permute-start.3
  35.3 91.2 %all_gather.12 = bf16[768,576]{1,0:T(8,128)(2,1)S(1)} all-gather(bf16[192,576]{1,0:T(8,128)(2,1)S(1)} %copy.89), channel_id=1, replica_groups=mesh['section'=2,'shard'=4,'replica'=4] {'shard'}, dimensions={0}, use_global_device_ids=true | all-gather | bytes 1105920 | tf_op jit(solution)/shard_map/all_gather | solution.py:270
  127.2 8.1 collective-permute-start.5
  169.1 14.2 %collective-permute-done.7 = bf16[768,576]{0,1:T(8,128)(2,1)} collective-permute-done((bf16[768,576]{0,1:T(8,128)(2,1)}, bf16[768,576]{0,1:T(8,128)(2,1)}, u32[]{:S(2)}, u32[]{:S(2)}) %collective-permute-start.7) | collective-permute-done | bytes 884768 | tf_op jit(solution)/shard_map/ppermute | solution.py:196
  195.9 4.4 attend.10
  205.2 4.4 attend.11
  215.3 5.0 attend.8
  224.2 16.3 %collective-permute-done.17 = bf16[768,768]{1,0:T(8,128)(2,1)} collective-permute-done((bf16[768,768]{1,0:T(8,128)(2,1)}, bf16[768,768]{1,0:T(8,128)(2,1)}, u32[]{:S(2)}, u32[]{:S(2)}) %collective-permute-start.17) | collective-permute-done | bytes 1179680 | tf_op jit(solution)/shard_map/ppermute | solution.py:200
  247.4 17.3 %collective-permute-done.15 = bf16[768,768]{1,0:T(8,128)(2,1)S(1)} collective-permute-done((bf16[768,768]{1,0:T(8,128)(2,1)}, bf16[768,768]{1,0:T(8,128)(2,1)S(1)}, u32[]{:S(2)}, u32[]{:S(2)}) %collective-permute-start.15) | collective-permute-done | bytes 1179680 | tf_op jit(solution)/shard_map/ppermute | solution.py:200
  266.5 10.8 %collective-permute-done.21 = bf16[768,768]{1,0:T(8,128)(2,1)S(1)} collective-permute-done((bf16[768,768]{1,0:T(8,128)(2,1)S(1)}, bf16[768,768]{1,0:T(8,128)(2,1)S(1)}, u32[]{:S(2)}, u32[]{:S(2)}) %collective-permute-start.21) | collective-permute-done | bytes 1179680 | tf_op jit(solution)/shard_map/ppermute | solution.py:196
  294.0 11.4 %collective-permute-done.24 = bf16[384,768]{1,0:T(8,128)(2,1)S(1)} collective-permute-done((bf16[384,768]{1,0:T(8,128)(2,1)S(1)}, bf16[384,768]{1,0:T(8,128)(2,1)S(1)}, u32[]{:S(2)}, u32[]{:S(2)}) %collective-permute-start.24) | collective-permute-done | bytes 589856 | tf_op jit(solution)/shard_map/ppermute | solution.py:196
  320.2 3.7 attend.13
  325.8 4.9 collective-permute-done.35.weight_ref
  330.7 25.0 %collective-permute-done.34 = bf16[768,768]{1,0:T(8,128)(2,1)} collective-permute-done((bf16[768,768]{1,0:T(8,128)(2,1)S(1)}, bf16[768,768]{1,0:T(8,128)(2,1)}, u32[]{:S(2)}, u32[]{:S(2)}) %collective-permute-start.34) | collective-permute-done | bytes 1179680 | tf_op jit(solution)/shard_map/ppermute | solution.py:196
  400.4 5.1 attend_back.11
  409.5 4.6 attend_back.10
  418.8 4.6 attend_back.9
  425.4 5.3 attend_back.8
  476.8 12.7 %collective-permute-done.77 = bf16[768,192]{0,1:T(8,128)(2,1)S(1)} collective-permute-done((bf16[768,192]{0,1:T(8,128)(2,1)S(1)}, bf16[768,192]{0,1:T(8,128)(2,1)S(1)}, u32[]{:S(2)}, u32[]{:S(2)}) %collective-permute-start.77) | collective-permute-done | bytes 294944 | tf_op jit(solution)/shard_map/ppermute | solution.py:196
  501.7 3.6 fusion.49
  526.4 6.2 attend_back.15
  534.3 4.9 attend_back.14
  541.8 6.1 attend_back.13
  552.9 6.0 attend_back.12
  603.8 28.1 %collective-permute-done.73 = bf16[768,192]{0,1:T(8,128)(2,1)S(1)} collective-permute-done((bf16[768,192]{0,1:T(8,128)(2,1)S(1)}, bf16[768,192]{0,1:T(8,128)(2,1)S(1)}, u32[]{:S(2)}, u32[]{:S(2)}) %collective-permute-start.73) | collective-permute-done | bytes 294944 | tf_op jit(solution)/shard_map/ppermute | solution.py:196
  637.2 6.2 collective-permute-start.67
  654.4 7.7 collective-permute-done.67
  669.6 7.0 collective-permute-done.62
  683.7 17.8 %collective-permute-done.63 = bf16[768,576]{0,1:T(8,128)(2,1)S(1)} collective-permute-done((bf16[768,576]{0,1:T(8,128)(2,1)S(1)}, bf16[768,576]{0,1:T(8,128)(2,1)S(1)}, u32[]{:S(2)}, u32[]{:S(2)}) %collective-permute-start.63) | collective-permute-done | bytes 884768 | tf_op jit(solution)/shard_map/ppermute | solution.py:426
  714.0 18.5 %collective-permute-done.89 = bf16[768,768]{1,0:T(8,128)(2,1)S(1)} collective-permute-done((bf16[768,768]{1,0:T(8,128)(2,1)S(1)}, bf16[768,768]{1,0:T(8,128)(2,1)S(1)}, u32[]{:S(2)}, u32[]{:S(2)}) %collective-permute-start.89) | collective-permute-done | bytes 1179680 | tf_op jit(solution)/shard_map/ppermute | solution.py:426
  737.0 5.5 collective-permute-done.84
  752.0 21.7 %collective-permute-done.85 = bf16[768,768]{1,0:T(8,128)(2,1)S(1)} collective-permute-done((bf16[768,768]{1,0:T(8,128)(2,1)S(1)}, bf16[768,768]{1,0:T(8,128)(2,1)S(1)}, u32[]{:S(2)}, u32[]{:S(2)}) %collective-permute-start.85) | collective-permute-done | bytes 1179680 | tf_op jit(solution)/shard_map/ppermute | solution.py:426
  790.9 19.1 %collective-permute-done.100 = bf16[768,768]{1,0:T(8,128)(2,1)S(1)} collective-permute-done((bf16[768,768]{1,0:T(8,128)(2,1)S(1)}, bf16[768,768]{1,0:T(8,128)(2,1)S(1)}, u32[]{:S(2)}, u32[]{:S(2)}) %collective-permute-start.100) | collective-permute-done | bytes 1179680 | tf_op jit(solution)/shard_map/ppermute | solution.py:426
  813.5 3.9 collective-permute-done.95
  829.1 19.9 %collective-permute-done.96 = bf16[768,768]{1,0:T(8,128)(2,1)S(1)} collective-permute-done((bf16[768,768]{1,0:T(8,128)(2,1)S(1)}, bf16[768,768]{1,0:T(8,128)(2,1)S(1)}, u32[]{:S(2)}, u32[]{:S(2)}) %collective-permute-start.96) | collective-permute-done | bytes 1179680 | tf_op jit(solution)/shard_map/ppermute | solution.py:426
  854.9 4.6 collective-permute-start.57
  864.8 6.0 collective-permute-start.79
  870.8 6.8 collective-permute-done.58
  879.6 12.2 %collective-permute-start.80 = (bf16[192,192]{0,1:T(8,128)(2,1)S(1)}, bf16[192,192]{0,1:T(8,128)(2,1)S(1)}, u32[]{:S(2)}, u32[]{:S(2)}) collective-permute-start(bf16[192,192]{0,1:T(8,128)(2,1)S(1)} %collective-permute-done.79), channel_id=1, source_target_pairs={{0,1},{1,0},{2,3},{3,2},{4,5},{5,4},{6,7},{7,6},{8,9},{9,8},{10,11... | collective-permute-start | bytes 221192 | tf_op jit(solution)/shard_map/ppermute | solution.py:196
  895.2 58.4 %collective-permute-start.68 = (bf16[192,576]{0,1:T(8,128)(2,1)S(1)}, bf16[192,576]{0,1:T(8,128)(2,1)S(1)}, u32[]{:S(2)}, u32[]{:S(2)}) collective-permute-start(bf16[192,576]{0,1:T(8,128)(2,1)S(1)} %broadcast_select_fusion.29), channel_id=1, source_target_pairs={{0,2},{1,3},{2,0},{3,1},{4,6},{5,7},{6,4},{7,5},{8,10},{9,11},{10,... | collective-permute-start | bytes 663560 | tf_op jit(solution)/shard_map/ppermute | solution.py:196
  956.7 4.7 collective-permute-done.68
  961.9 19.4 %reduce-scatter.23.cloned.1.call-done = bf16[192,768]{1,0:T(8,128)(2,1)} async-done(((bf16[768,768]{1,0:T(8,128)(2,1)}), bf16[192,768]{1,0:T(8,128)(2,1)}) %reduce-scatter.23.cloned.1.call-update) | async-done | bytes 294928 | tf_op jit(solution)/shard_map/reduce_scatter | solution.py:427
  981.3 30.1 %reduce-scatter.21.cloned.1.call-done = bf16[192,768]{1,0:T(8,128)(2,1)} async-done(((bf16[768,768]{1,0:T(8,128)(2,1)}), bf16[192,768]{1,0:T(8,128)(2,1)}) %reduce-scatter.21.cloned.1.call-update) | async-done | bytes 294928 | tf_op jit(solution)/shard_map/reduce_scatter | solution.py:427
  1017.6 3.7 reshape.540
  1026.2 3.7 copy.119
  1029.9 4.8 reshape.542
  (1175 shorter events, 424.7 us)
Async XLA Ops:
  7.2 178.9 %all-gather.6.cloned.1.call-start = ((), (), s32[]{:S(2)}) async-start(), calls=%async_computation.8 | async-start | bytes 1474560 | tf_op jit(solution)/shard_map/all_gather | solution.py:270
  14.8 175.7 %all-gather.10.cloned.1.call-start = ((), (), s32[]{:S(2)}) async-start(), calls=%async_computation.15 | async-start | bytes 1474560 | tf_op jit(solution)/shard_map/all_gather | solution.py:270
  15.7 196.4 %all-gather.8.cloned.1.call-start = ((), (), s32[]{:S(2)}) async-start(), calls=%async_computation.14 | async-start | bytes 1474560 | tf_op jit(solution)/shard_map/all_gather | solution.py:270
  16.8 133.5 %collective-permute-start.2 = (bf16[384,768]{1,0:T(8,128)(2,1)}, bf16[384,768]{1,0:T(8,128)(2,1)}, u32[]{:S(2)}, u32[]{:S(2)}) collective-permute-start(bf16[384,768]{1,0:T(8,128)(2,1)} %get-tuple-element.257), channel_id=1, source_target_pairs={{0,0},{1,4},{2,8},{3,12},{4,1},{5,5},{6,9},{7,13},{8,2},{9,6},{10,... | collective-permute-start | bytes 1769480 | tf_op jit(solution)/shard_map/ppermute | solution.py:218
  22.8 130.8 %collective-permute-start = (bf16[384,768]{1,0:T(8,128)(2,1)}, bf16[384,768]{1,0:T(8,128)(2,1)}, u32[]{:S(2)}, u32[]{:S(2)}) collective-permute-start(bf16[384,768]{1,0:T(8,128)(2,1)} %get-tuple-element.257), channel_id=1, source_target_pairs={{16,0},{17,4},{18,8},{19,12},{20,1},{21,5},{22,9},{23,13},{24,2},{... | collective-permute-start | bytes 1769480 | tf_op jit(solution)/shard_map/ppermute | solution.py:218
  24.1 126.3 %collective-permute-start.3 = (bf16[384,768]{1,0:T(8,128)(2,1)}, bf16[384,768]{1,0:T(8,128)(2,1)}, u32[]{:S(2)}, u32[]{:S(2)}) collective-permute-start(bf16[384,768]{1,0:T(8,128)(2,1)} %get-tuple-element.256), channel_id=1, source_target_pairs={{0,16},{1,20},{2,24},{3,28},{4,17},{5,21},{6,25},{7,29},{8,18},{9,... | collective-permute-start | bytes 1769480 | tf_op jit(solution)/shard_map/ppermute | solution.py:218
  30.2 123.4 %collective-permute-start.1 = (bf16[384,768]{1,0:T(8,128)(2,1)}, bf16[384,768]{1,0:T(8,128)(2,1)}, u32[]{:S(2)}, u32[]{:S(2)}) collective-permute-start(bf16[384,768]{1,0:T(8,128)(2,1)} %get-tuple-element.256), channel_id=1, source_target_pairs={{16,16},{17,20},{18,24},{19,28},{20,17},{21,21},{22,25},{23,29},{2... | collective-permute-start | bytes 1769480 | tf_op jit(solution)/shard_map/ppermute | solution.py:218
  31.7 95.4 %collective-permute-start.10 = (f32[1,1536]{1,0:T(1,128)S(1)}, f32[1,1536]{1,0:T(1,128)S(1)}, u32[]{:S(2)}, u32[]{:S(2)}) collective-permute-start(f32[1,1536]{1,0:T(1,128)S(1)} %fusion.112), channel_id=1, source_target_pairs={{0,0},{16,16},{1,4},{17,20},{2,8},{18,24},{3,12},{19,28},{4,1},{20... | collective-permute-start | bytes 18440 | tf_op jit(solution)/shard_map/ppermute | solution.py:218
  32.4 827.1 %reduce-scatter.31.cloned.1.call-start = ((), (), s32[]{:S(2)}) async-start(), calls=%async_computation.19 | async-start | bytes 491520
  186.1 36.2 %collective-permute-start.16 = (bf16[768,768]{1,0:T(8,128)(2,1)}, bf16[768,768]{1,0:T(8,128)(2,1)}, u32[]{:S(2)}, u32[]{:S(2)}) collective-permute-start(bf16[768,768]{1,0:T(8,128)(2,1)} %all-gather.6.cloned.1.call-done), channel_id=1, source_target_pairs={{0,16},{16,0},{1,17},{17,1},{2,18},{18,2},{3,19},{19,3},{4,20},{20... | collective-permute-start | bytes 3538952 | tf_op jit(solution)/shard_map/ppermute | solution.py:200
  190.5 50.0 %collective-permute-start.17 = (bf16[768,768]{1,0:T(8,128)(2,1)}, bf16[768,768]{1,0:T(8,128)(2,1)}, u32[]{:S(2)}, u32[]{:S(2)}) collective-permute-start(bf16[768,768]{1,0:T(8,128)(2,1)} %bitcast.204), channel_id=1, source_target_pairs={{0,16},{16,0},{1,17},{17,1},{2,18},{18,2},{3,19},{19,3},{4,20},{20... | collective-permute-start | bytes 3538952 | tf_op jit(solution)/shard_map/ppermute | solution.py:200
  203.5 87.4 %collective-permute-start.25 = (bf16[768,576]{0,1:T(8,128)(2,1)}, bf16[768,576]{0,1:T(8,128)(2,1)}, u32[]{:S(2)}, u32[]{:S(2)}) collective-permute-start(bf16[768,576]{0,1:T(8,128)(2,1)} %copy.104), channel_id=1, source_target_pairs={{0,2},{1,3},{2,0},{3,1},{4,6},{5,7},{6,4},{7,5},{8,10},{9,11},{10,... | collective-permute-start | bytes 2654216 | tf_op jit(solution)/shard_map/ppermute | solution.py:196
  212.1 52.6 %collective-permute-start.15 = (bf16[768,768]{1,0:T(8,128)(2,1)}, bf16[768,768]{1,0:T(8,128)(2,1)S(1)}, u32[]{:S(2)}, u32[]{:S(2)}) collective-permute-start(bf16[768,768]{1,0:T(8,128)(2,1)} %bitcast.211), channel_id=1, source_target_pairs={{0,16},{16,0},{1,17},{17,1},{2,18},{18,2},{3,19},{19,3},{4,20},{20... | collective-permute-start | bytes 3538952 | tf_op jit(solution)/shard_map/ppermute | solution.py:200
  223.8 42.3 %collective-permute-start.20 = (bf16[768,768]{1,0:T(8,128)(2,1)S(1)}, bf16[768,768]{1,0:T(8,128)(2,1)S(1)}, u32[]{:S(2)}, u32[]{:S(2)}) collective-permute-start(bf16[768,768]{1,0:T(8,128)(2,1)S(1)} %get-tuple-element.239.weight_ref), channel_id=1, source_target_pairs={{0,2},{1,3},{2,0},{3,1},{4,6},{5,7},{6,4},{7,5},{8,10},{9,11},{10,... | collective-permute-start | bytes 3538952 | tf_op jit(solution)/shard_map/ppermute | solution.py:196
  240.5 42.4 %collective-permute-start.18 = (bf16[768,768]{1,0:T(8,128)(2,1)S(1)}, bf16[768,768]{1,0:T(8,128)(2,1)S(1)}, u32[]{:S(2)}, u32[]{:S(2)}) collective-permute-start(bf16[768,768]{1,0:T(8,128)(2,1)S(1)} %get-tuple-element.239.weight_ref), channel_id=1, source_target_pairs={{0,1},{1,0},{2,3},{3,2},{4,5},{5,4},{6,7},{7,6},{8,9},{9,8},{10,11... | collective-permute-start | bytes 3538952 | tf_op jit(solution)/shard_map/ppermute | solution.py:196
  242.0 35.4 %collective-permute-start.21 = (bf16[768,768]{1,0:T(8,128)(2,1)S(1)}, bf16[768,768]{1,0:T(8,128)(2,1)S(1)}, u32[]{:S(2)}, u32[]{:S(2)}) collective-permute-start(bf16[768,768]{1,0:T(8,128)(2,1)S(1)} %get-tuple-element.240), channel_id=1, source_target_pairs={{0,2},{1,3},{2,0},{3,1},{4,6},{5,7},{6,4},{7,5},{8,10},{9,11},{10,... | collective-permute-start | bytes 3538952 | tf_op jit(solution)/shard_map/ppermute | solution.py:196
  291.1 39.6 %collective-permute-start.35 = (bf16[768,768]{1,0:T(8,128)(2,1)S(1)}, bf16[768,768]{1,0:T(8,128)(2,1)S(1)}, u32[]{:S(2)}, u32[]{:S(2)}) collective-permute-start(bf16[768,768]{1,0:T(8,128)(2,1)S(1)} %get-tuple-element.238.weight_ref), channel_id=1, source_target_pairs={{0,2},{1,3},{2,0},{3,1},{4,6},{5,7},{6,4},{7,5},{8,10},{9,11},{10,... | collective-permute-start | bytes 3538952 | tf_op jit(solution)/shard_map/ppermute | solution.py:196
  292.5 63.3 %collective-permute-start.34 = (bf16[768,768]{1,0:T(8,128)(2,1)S(1)}, bf16[768,768]{1,0:T(8,128)(2,1)}, u32[]{:S(2)}, u32[]{:S(2)}) collective-permute-start(bf16[768,768]{1,0:T(8,128)(2,1)S(1)} %get-tuple-element.241), channel_id=1, source_target_pairs={{0,2},{1,3},{2,0},{3,1},{4,6},{5,7},{6,4},{7,5},{8,10},{9,11},{10,... | collective-permute-start | bytes 3538952 | tf_op jit(solution)/shard_map/ppermute | solution.py:196
  314.2 41.6 %collective-permute-start.30 = (bf16[768,384]{1,0:T(8,128)(2,1)}, bf16[768,384]{1,0:T(8,128)(2,1)S(1)}, u32[]{:S(2)}, u32[]{:S(2)}) collective-permute-start(bf16[768,384]{1,0:T(8,128)(2,1)} %slice.435), channel_id=1, source_target_pairs={{0,1},{1,0},{2,3},{3,2},{4,5},{5,4},{6,7},{7,6},{8,9},{9,8},{10,11... | collective-permute-start | bytes 1769480 | tf_op jit(solution)/shard_map/ppermute | solution.py:196
  315.6 45.8 %collective-permute-start.31 = (bf16[768,384]{1,0:T(8,128)(2,1)S(1)}, bf16[768,384]{1,0:T(8,128)(2,1)S(1)}, u32[]{:S(2)}, u32[]{:S(2)}) collective-permute-start(bf16[768,384]{1,0:T(8,128)(2,1)S(1)} %slice.436), channel_id=1, source_target_pairs={{0,1},{1,0},{2,3},{3,2},{4,5},{5,4},{6,7},{7,6},{8,9},{9,8},{10,11... | collective-permute-start | bytes 1769480 | tf_op jit(solution)/shard_map/ppermute | solution.py:196
  320.1 53.2 %collective-permute-start.33 = (bf16[768,768]{1,0:T(8,128)(2,1)S(1)}, bf16[768,768]{1,0:T(8,128)(2,1)S(1)}, u32[]{:S(2)}, u32[]{:S(2)}) collective-permute-start(bf16[768,768]{1,0:T(8,128)(2,1)S(1)} %get-tuple-element.238.weight_ref), channel_id=1, source_target_pairs={{0,1},{1,0},{2,3},{3,2},{4,5},{5,4},{6,7},{7,6},{8,9},{9,8},{10,11... | collective-permute-start | bytes 3538952 | tf_op jit(solution)/shard_map/ppermute | solution.py:196
  330.7 50.6 %collective-permute-start.32 = (bf16[768,768]{1,0:T(8,128)(2,1)S(1)}, bf16[768,768]{1,0:T(8,128)(2,1)}, u32[]{:S(2)}, u32[]{:S(2)}) collective-permute-start(bf16[768,768]{1,0:T(8,128)(2,1)S(1)} %get-tuple-element.241), channel_id=1, source_target_pairs={{0,1},{1,0},{2,3},{3,2},{4,5},{5,4},{6,7},{7,6},{8,9},{9,8},{10,11... | collective-permute-start | bytes 3538952 | tf_op jit(solution)/shard_map/ppermute | solution.py:196
  467.5 34.2 %collective-permute-start.46 = (bf16[384,768]{1,0:T(8,128)(2,1)}, bf16[384,768]{1,0:T(8,128)(2,1)}, u32[]{:S(2)}, u32[]{:S(2)}) collective-permute-start(bf16[384,768]{1,0:T(8,128)(2,1)} %slice.765), channel_id=1, source_target_pairs={{0,2},{1,3},{2,0},{3,1},{4,6},{5,7},{6,4},{7,5},{8,10},{9,11},{10,... | collective-permute-start | bytes 1769480 | tf_op jit(solution)/shard_map/ppermute | solution.py:196
  469.1 124.0 %collective-permute-start.65 = (bf16[768,576]{0,1:T(8,128)(2,1)}, bf16[768,576]{0,1:T(8,128)(2,1)}, u32[]{:S(2)}, u32[]{:S(2)}) collective-permute-start(bf16[768,576]{0,1:T(8,128)(2,1)} %pad_maximum_fusion.6), channel_id=1, source_target_pairs={{0,1},{1,0},{2,3},{3,2},{4,5},{5,4},{6,7},{7,6},{8,9},{9,8},{10,11... | collective-permute-start | bytes 2654216 | tf_op jit(solution)/shard_map/ppermute | solution.py:196
  471.3 161.5 %collective-permute-start.64 = (bf16[768,576]{0,1:T(8,128)(2,1)}, bf16[768,576]{0,1:T(8,128)(2,1)}, u32[]{:S(2)}, u32[]{:S(2)}) collective-permute-start(bf16[768,576]{0,1:T(8,128)(2,1)} %pad_maximum_fusion.5), channel_id=1, source_target_pairs={{0,1},{1,0},{2,3},{3,2},{4,5},{5,4},{6,7},{7,6},{8,9},{9,8},{10,11... | collective-permute-start | bytes 2654216 | tf_op jit(solution)/shard_map/ppermute | solution.py:196
  501.6 360.6 %all-reduce.2.cloned.1.call-start = ((), (), s32[]{:S(2)}) async-start(), calls=%async_computation.13 | async-start | bytes 147456 | tf_op jit(solution)/shard_map/psum | solution.py:442
  591.2 46.1 %collective-permute-start.55 = (bf16[384,768]{1,0:T(8,128)(2,1)S(1)}, bf16[384,768]{1,0:T(8,128)(2,1)S(1)}, u32[]{:S(2)}, u32[]{:S(2)}) collective-permute-start(bf16[384,768]{1,0:T(8,128)(2,1)S(1)} %slice.764), channel_id=1, source_target_pairs={{0,2},{1,3},{2,0},{3,1},{4,6},{5,7},{6,4},{7,5},{8,10},{9,11},{10,... | collective-permute-start | bytes 1769480 | tf_op jit(solution)/shard_map/ppermute | solution.py:196
  594.7 38.7 %collective-permute-start.66 = (bf16[768,576]{0,1:T(8,128)(2,1)S(1)}, bf16[768,576]{0,1:T(8,128)(2,1)S(1)}, u32[]{:S(2)}, u32[]{:S(2)}) collective-permute-start(bf16[768,576]{0,1:T(8,128)(2,1)S(1)} %add_convert_fusion.26), channel_id=1, source_target_pairs={{0,2},{1,3},{2,0},{3,1},{4,6},{5,7},{6,4},{7,5},{8,10},{9,11},{10,... | collective-permute-start | bytes 2654216 | tf_op jit(solution)/shard_map/ppermute | solution.py:196
  598.8 33.2 %collective-permute-start.73 = (bf16[768,192]{0,1:T(8,128)(2,1)S(1)}, bf16[768,192]{0,1:T(8,128)(2,1)S(1)}, u32[]{:S(2)}, u32[]{:S(2)}) collective-permute-start(bf16[768,192]{0,1:T(8,128)(2,1)S(1)} %add_convert_fusion.56), channel_id=1, source_target_pairs={{0,2},{1,3},{2,0},{3,1},{4,6},{5,7},{6,4},{7,5},{8,10},{9,11},{10,... | collective-permute-start | bytes 884744 | tf_op jit(solution)/shard_map/ppermute | solution.py:196
  603.7 61.5 %collective-permute-start.87 = (bf16[768,768]{1,0:T(8,128)(2,1)}, bf16[768,768]{1,0:T(8,128)(2,1)}, u32[]{:S(2)}, u32[]{:S(2)}) collective-permute-start(bf16[768,768]{1,0:T(8,128)(2,1)} %convolution_convert_fusion.8), channel_id=1, source_target_pairs={{0,1},{1,0},{2,3},{3,2},{4,5},{5,4},{6,7},{7,6},{8,9},{9,8},{10,11... | collective-permute-start | bytes 3538952 | tf_op jit(solution)/shard_map/ppermute | solution.py:196
  631.9 49.7 %collective-permute-start.86 = (bf16[768,768]{1,0:T(8,128)(2,1)}, bf16[768,768]{1,0:T(8,128)(2,1)}, u32[]{:S(2)}, u32[]{:S(2)}) collective-permute-start(bf16[768,768]{1,0:T(8,128)(2,1)} %convolution_convert_fusion.10), channel_id=1, source_target_pairs={{0,1},{1,0},{2,3},{3,2},{4,5},{5,4},{6,7},{7,6},{8,9},{9,8},{10,11... | collective-permute-start | bytes 3538952 | tf_op jit(solution)/shard_map/ppermute | solution.py:196
  648.9 214.9 %reduce-scatter.29.cloned.1.call-start = ((), (), s32[]{:S(2)}) async-start(), calls=%async_computation.18 | async-start | bytes 491520
  651.1 241.9 %reduce-scatter.27.cloned.1.call-start = ((), (), s32[]{:S(2)}) async-start(), calls=%async_computation.17 | async-start | bytes 1228800
  665.1 229.0 %reduce-scatter.25.cloned.1.call-start = ((), (), s32[]{:S(2)}) async-start(), calls=%async_computation.16 | async-start | bytes 1228800
  668.4 36.5 %collective-permute-start.88 = (bf16[768,768]{1,0:T(8,128)(2,1)}, bf16[768,768]{1,0:T(8,128)(2,1)}, u32[]{:S(2)}, u32[]{:S(2)}) collective-permute-start(bf16[768,768]{1,0:T(8,128)(2,1)} %add_convert_fusion.10), channel_id=1, source_target_pairs={{0,2},{1,3},{2,0},{3,1},{4,6},{5,7},{6,4},{7,5},{8,10},{9,11},{10,... | collective-permute-start | bytes 3538952 | tf_op jit(solution)/shard_map/ppermute | solution.py:196
  704.9 248.7 %reduce-scatter.19.cloned.1.call-start = ((), (), s32[]{:S(2)}) async-start(), calls=%async_computation.10 | async-start | bytes 1474560 | tf_op jit(solution)/shard_map/reduce_scatter | solution.py:427
  733.9 219.7 %reduce-scatter.17.cloned.1.call-start = ((), (), s32[]{:S(2)}) async-start(), calls=%async_computation.9 | async-start | bytes 1474560 | tf_op jit(solution)/shard_map/reduce_scatter | solution.py:427
  747.3 32.7 %collective-permute-start.97 = (bf16[768,768]{1,0:T(8,128)(2,1)}, bf16[768,768]{1,0:T(8,128)(2,1)}, u32[]{:S(2)}, u32[]{:S(2)}) collective-permute-start(bf16[768,768]{1,0:T(8,128)(2,1)} %convolution_convert_fusion.2), channel_id=1, source_target_pairs={{0,1},{1,0},{2,3},{3,2},{4,5},{5,4},{6,7},{7,6},{8,9},{9,8},{10,11... | collective-permute-start | bytes 3538952 | tf_op jit(solution)/shard_map/ppermute | solution.py:196
  749.5 30.5 %collective-permute-start.99 = (bf16[768,768]{1,0:T(8,128)(2,1)}, bf16[768,768]{1,0:T(8,128)(2,1)}, u32[]{:S(2)}, u32[]{:S(2)}) collective-permute-start(bf16[768,768]{1,0:T(8,128)(2,1)} %add_convert_fusion.2), channel_id=1, source_target_pairs={{0,2},{1,3},{2,0},{3,1},{4,6},{5,7},{6,4},{7,5},{8,10},{9,11},{10,... | collective-permute-start | bytes 3538952 | tf_op jit(solution)/shard_map/ppermute | solution.py:196
  751.8 34.2 %collective-permute-start.94 = (bf16[768,768]{1,0:T(8,128)(2,1)}, bf16[768,768]{1,0:T(8,128)(2,1)}, u32[]{:S(2)}, u32[]{:S(2)}) collective-permute-start(bf16[768,768]{1,0:T(8,128)(2,1)} %convolution_convert_fusion.4), channel_id=1, source_target_pairs={{0,1},{1,0},{2,3},{3,2},{4,5},{5,4},{6,7},{7,6},{8,9},{9,8},{10,11... | collective-permute-start | bytes 3538952 | tf_op jit(solution)/shard_map/ppermute | solution.py:196
  775.1 206.2 %reduce-scatter.23.cloned.1.call-start = ((), (), s32[]{:S(2)}) async-start(), calls=%async_computation.12 | async-start | bytes 1474560 | tf_op jit(solution)/shard_map/reduce_scatter | solution.py:427
  811.5 199.9 %reduce-scatter.21.cloned.1.call-start = ((), (), s32[]{:S(2)}) async-start(), calls=%async_computation.11 | async-start | bytes 1474560 | tf_op jit(solution)/shard_map/reduce_scatter | solution.py:427
  827.0 43.8 %collective-permute-start.59 = (bf16[384,768]{1,0:T(8,128)(2,1)S(1)}, bf16[384,768]{1,0:T(8,128)(2,1)}, u32[]{:S(2)}, u32[]{:S(2)}) collective-permute-start(bf16[384,768]{1,0:T(8,128)(2,1)S(1)} %fusion.39), channel_id=1, source_target_pairs={{16,16},{17,20},{18,24},{19,28},{20,17},{21,21},{22,25},{23,29},{2... | collective-permute-start | bytes 1769480 | tf_op jit(solution)/shard_map/ppermute | solution.py:218
  895.2 66.2 %collective-permute-start.68 = (bf16[192,576]{0,1:T(8,128)(2,1)S(1)}, bf16[192,576]{0,1:T(8,128)(2,1)S(1)}, u32[]{:S(2)}, u32[]{:S(2)}) collective-permute-start(bf16[192,576]{0,1:T(8,128)(2,1)S(1)} %broadcast_select_fusion.29), channel_id=1, source_target_pairs={{0,2},{1,3},{2,0},{3,1},{4,6},{5,7},{6,4},{7,5},{8,10},{9,11},{10,... | collective-permute-start | bytes 663560 | tf_op jit(solution)/shard_map/ppermute | solution.py:196
  955.4 59.2 %collective-permute-start.90 = (bf16[192,768]{1,0:T(8,128)(2,1)}, bf16[192,768]{1,0:T(8,128)(2,1)}, u32[]{:S(2)}, u32[]{:S(2)}) collective-permute-start(bf16[192,768]{1,0:T(8,128)(2,1)} %broadcast_select_fusion.16), channel_id=1, source_target_pairs={{0,2},{1,3},{2,0},{3,1},{4,6},{5,7},{6,4},{7,5},{8,10},{9,11},{10,... | collective-permute-start | bytes 884744 | tf_op jit(solution)/shard_map/ppermute | solution.py:196
  956.6 58.0 %collective-permute-start.70 = (bf16[192,576]{0,1:T(8,128)(2,1)S(1)}, bf16[192,576]{0,1:T(8,128)(2,1)S(1)}, u32[]{:S(2)}, u32[]{:S(2)}) collective-permute-start(bf16[192,576]{0,1:T(8,128)(2,1)S(1)} %broadcast_select_fusion.29), channel_id=1, source_target_pairs={{0,1},{1,0},{2,3},{3,2},{4,5},{5,4},{6,7},{7,6},{8,9},{9,8},{10,11... | collective-permute-start | bytes 663560 | tf_op jit(solution)/shard_map/ppermute | solution.py:196
  961.4 53.2 %collective-permute-start.69 = (bf16[192,576]{0,1:T(8,128)(2,1)S(1)}, bf16[192,576]{0,1:T(8,128)(2,1)S(1)}, u32[]{:S(2)}, u32[]{:S(2)}) collective-permute-start(bf16[192,576]{0,1:T(8,128)(2,1)S(1)} %collective-permute-done.68), channel_id=1, source_target_pairs={{0,1},{1,0},{2,3},{3,2},{4,5},{5,4},{6,7},{7,6},{8,9},{9,8},{10,11... | collective-permute-start | bytes 663560 | tf_op jit(solution)/shard_map/ppermute | solution.py:196
  961.4 60.6 %collective-permute-start.92 = (bf16[192,768]{1,0:T(8,128)(2,1)}, bf16[192,768]{1,0:T(8,128)(2,1)}, u32[]{:S(2)}, u32[]{:S(2)}) collective-permute-start(bf16[192,768]{1,0:T(8,128)(2,1)} %broadcast_select_fusion.16), channel_id=1, source_target_pairs={{0,1},{1,0},{2,3},{3,2},{4,5},{5,4},{6,7},{7,6},{8,9},{9,8},{10,11... | collective-permute-start | bytes 884744 | tf_op jit(solution)/shard_map/ppermute | solution.py:196
  (377 other events, 3323.8 us)
Sparse Core Ops, SparseCore 0:
  15.0 72.8 all-gather.5
  89.4 40.8 all-gather.9
  131.8 31.0 all-gather.7
  501.8 19.6 reduce-scatter.30
  649.0 116.0 all-reduce.1
  767.3 22.5 reduce-scatter.28
  792.2 24.3 reduce-scatter.26
  819.0 24.7 reduce-scatter.24
  846.1 68.8 reduce-scatter.18
  917.7 34.7 reduce-scatter.16
  954.9 26.3 reduce-scatter.22
  983.5 27.8 reduce-scatter.20

commit v2 on v1

--- a/solution.py
+++ b/solution.py
@@ -47,13 +47,12 @@
     outs = []
     for head in range(heads):
         at = head * dim
-        query = own_ref[0:frames, at:at + dim] * (dim ** -0.5)
+        query = own_ref[0:frames, 2 * wide + at:2 * wide + at + dim] * (dim ** -0.5)
         lane = lax.broadcasted_iota(jnp.int32, (frames, dim), 1)
         query = jnp.concatenate([query.astype(BF16), (lane == 0).astype(BF16)], 1)
         top = None
         for source, start, row in chunks:
-            shift = wide if source == 0 else 0
-            key = sources[source][start:start + chunk, shift + at:shift + at + dim]
+            key = sources[source][start:start + chunk, at:at + dim]
             key = jnp.concatenate([key, bias_ref[row:row + chunk, :]], 1)
             score = dot(key, query, NT)
             score_ref[row:row + chunk, :] = score
@@ -61,10 +60,9 @@
             top = part if top is None else jnp.maximum(top, part)
         total = None
         for source, start, row in chunks:
-            shift = 2 * wide if source == 0 else wide
             weight = jnp.exp(score_ref[row:row + chunk, :] - top).astype(BF16)
             exp_ref[head, row:row + chunk, :] = weight
-            value = sources[source][start:start + chunk, shift + at:shift + at + dim]
+            value = sources[source][start:start + chunk, wide + at:wide + at + dim]
             value = jnp.concatenate([value, jnp.ones_like(value)], 1)
             part = dot(value, weight, TN)
             total = part if total is None else total + part
@@ -96,7 +94,7 @@
     )(own, other, bias)
 
 
-def attend_back_kernel(own_ref, other_ref, exp_ref, inv_ref, dout_ref, dq_ref, dk_ref, dv_ref, prod_ref, *, heads, frames, chunk):
+def attend_back_kernel(own_ref, other_ref, exp_ref, inv_ref, dout_ref, dq_ref, down_ref, dother_ref, prod_ref, *, heads, frames, chunk):
     dim = own_ref.shape[1] // (3 * heads)
     wide = heads * dim
     scale = dim ** -0.5
@@ -106,15 +104,14 @@
     dks, dvs = [[] for _ in chunks], [[] for _ in chunks]
     for head in range(heads):
         at = head * dim
-        query = (own_ref[0:frames, at:at + dim] * scale).astype(BF16)
+        query = (own_ref[0:frames, 2 * wide + at:2 * wide + at + dim] * scale).astype(BF16)
         inverse = inv_ref[head:head + 1, :]
         dout_t = dout_ref[:, at:at + dim].astype(F32).T * inverse
         dout = dout_t.T.astype(BF16)
         dout_t = dout_t.astype(BF16)
         delta = None
         for index, (source, start, row) in enumerate(chunks):
-            shift = 2 * wide if source == 0 else wide
-            value = sources[source][start:start + chunk, shift + at:shift + at + dim]
+            value = sources[source][start:start + chunk, wide + at:wide + at + dim]
             weight = exp_ref[head, row:row + chunk, :]
             prod = dot(value, dout_t) * weight.astype(F32)
             prod_ref[row:row + chunk, :] = prod
@@ -124,8 +121,7 @@
         delta = delta * inverse
         dq_t = None
         for index, (source, start, row) in enumerate(chunks):
-            shift = wide if source == 0 else 0
-            key = sources[source][start:start + chunk, shift + at:shift + at + dim]
+            key = sources[source][start:start + chunk, at:at + dim]
             weight = exp_ref[head, row:row + chunk, :].astype(F32)
             ds = (prod_ref[row:row + chunk, :] - weight * delta).astype(BF16)
             dks[index].append(dot(ds, query))
@@ -134,8 +130,8 @@
         dqs.append(dq_t.T * scale)
     dq_ref[...] = jnp.concatenate(dqs, 1).astype(BF16)
     for index, (source, start, row) in enumerate(chunks):
-        dk_ref[row:row + chunk, :] = jnp.concatenate(dks[index], 1).astype(BF16)
-        dv_ref[row:row + chunk, :] = jnp.concatenate(dvs[index], 1).astype(BF16)
+        target = down_ref if source == 0 else dother_ref
+        target[start:start + chunk, :] = jnp.concatenate(dks[index] + dvs[index], 1).astype(BF16)
 
 
 def attend_back(own, other, weights, inverse, dout, heads, frames):
@@ -148,8 +144,8 @@
         functools.partial(attend_back_kernel, heads=heads, frames=frames, chunk=chunk),
         out_shape=(
             jax.ShapeDtypeStruct((frames, wide), BF16),
-            jax.ShapeDtypeStruct((keys, wide), BF16),
-            jax.ShapeDtypeStruct((keys, wide), BF16),
+            jax.ShapeDtypeStruct((own.shape[0], 2 * wide), BF16),
+            jax.ShapeDtypeStruct((other.shape[0], 2 * wide), BF16),
         ),
         scratch_shapes=[pltpu.VMEM((keys, frames), F32)],
         compiler_params=pltpu.CompilerParams(vmem_limit_bytes=40 * 2**20),
@@ -225,21 +221,19 @@
     return jnp.where(high, c, a), jnp.where(high, d, b), jnp.where(high, a, c), jnp.where(high, b, d)
 
 
-def spread(piece):
-    far = across(piece, 2)
+def after(value, *others):
+    return lax.optimization_barrier((value, others))[0]
+
+
+def spread(piece, far):
     return piece, across(piece, 1), far, across(far, 1)
 
 
-def reduced(pieces):
-    near = [across(pieces[1], 1), across(pieces[3], 1)]
-    own = (pieces[0].astype(F32) + near[0].astype(F32)).astype(BF16)
-    far = (pieces[2].astype(F32) + near[1].astype(F32)).astype(BF16)
-    own = (own.astype(F32) + across(far, 2).astype(F32)).astype(BF16)
-    bit = QUARTERS
-    while bit < lax.axis_size("replica"):
-        own = (own.astype(F32) + across(own, bit).astype(F32)).astype(BF16)
-        bit *= 2
-    return own
+def low_sum(*parts):
+    total = parts[0].astype(F32)
+    for part in parts[1:]:
+        total = total + part.astype(F32)
+    return total.astype(BF16)
 
 
 def body(edges, attn_in, attn_out, mlp_up, mlp_down, vectors, key_mask):
@@ -269,19 +263,38 @@
     def gathered(block):
         return lax.all_gather(block, "shard", axis=0, tiled=True)
 
-    own_parts = (
-        gathered(pick(attn_in[0].reshape(rows, 3, QUARTERS, wide), 2).reshape(rows, 3 * wide)),
-        gathered(attn_out[0]),
-        gathered(pick(mlp_up[0].reshape(rows, shards, QUARTERS, unit), 2).reshape(rows, shards * unit)),
-        gathered(pick(mlp_down[0].reshape(QUARTERS, unit, width), 0)),
+    def by_layer(own, other):
+        return jnp.where(first, own, other), jnp.where(first, other, own)
+
+    query_in, key_in, value_in = (
+        pick(attn_in[0][:, i * width:(i + 1) * width].reshape(rows, QUARTERS, wide), 1) for i in range(3)
     )
-    other_parts = tuple(swap_sections(part) for part in own_parts)
-    vector_other = swap_sections(vectors[0])
+    own_proj = jnp.concatenate(
+        [key_in, value_in, query_in, pick(attn_out[0].reshape(rows, QUARTERS, width // QUARTERS), 1)], 1
+    )
+    own_up = pick(mlp_up[0].reshape(rows, shards, QUARTERS, unit), 2).reshape(rows, shards * unit)
+    own_down = pick(mlp_down[0].reshape(QUARTERS, unit, width), 0)
+    proj_zero, proj_one = by_layer(own_proj, swap_sections(own_proj))
+    vec_by_layer = by_layer(vectors[0], swap_sections(vectors[0]))
+    proj_zero = gathered(proj_zero)
+    own_up = gathered(after(own_up, proj_zero))
+    own_down = gathered(after(own_down, own_up))
+    proj_one = gathered(after(proj_one, own_down))
+    up_zero, up_one = by_layer(own_up, swap_sections(own_up))
+    down_zero, down_one = by_layer(own_down, swap_sections(own_down))
+    far = [across(proj_zero, 2)]
+    far.append(across(up_zero, 2))
+    far.append(across(after(down_zero, far[1]), 2))
+    far.append(across(after(proj_one, far[2]), 2))
+    far.append(across(after(up_one, far[2]), 2))
+    far.append(across(after(down_one, far[3], far[4]), 2))
+    blocks = (proj_zero, up_zero, down_zero, proj_one, up_one, down_one)
+    blocks = [spread(block, other) for block, other in zip(blocks, far)]
     layers = []
     for layer in range(2):
-        mine = first if layer == 0 else ~first
-        w_in, w_out, w_up, w_down = (jnp.where(mine, a, b) for a, b in zip(own_parts, other_parts))
-        layers.append((spread(w_in), w_out, spread(w_up), spread(w_down), jnp.where(mine, vectors[0], vector_other)))
+        proj, up, down = blocks[3 * layer:3 * layer + 3]
+        w_out = jnp.concatenate(in_order([piece[:, 3 * wide:] for piece in proj], quarter), 1)
+        layers.append((proj, w_out, up, down, vec_by_layer[layer]))
 
     members = [0]
     bit = 2
@@ -305,16 +318,16 @@
         return block
 
     def forward(x_low, layer):
-        w_in, w_out, w_up, w_down, vec = layers[layer]
+        proj, w_out, w_up, w_down, vec = layers[layer]
         x_set = chips_rows(x_low)
         normed = layer_norm(x_set.astype(F32), vec[0], vec[1]).astype(BF16)
         zeros = jnp.zeros((QUARTERS, wide), F32)
-        bias_in = jnp.stack([vec[2].reshape(QUARTERS, wide), zeros, vec[3].reshape(QUARTERS, wide)], 1)
+        bias_in = jnp.stack([zeros, vec[3].reshape(QUARTERS, wide), vec[2].reshape(QUARTERS, wide)], 1)
         own_qkv, other_kv = [], [None] * QUARTERS
         for p in range(QUARTERS):
             bias = lax.dynamic_index_in_dim(bias_in, quarter ^ p, 0, keepdims=False).reshape(3 * wide)
-            own_qkv.append((dot(normed, w_in[p]) + bias).astype(BF16))
-            other_kv[p ^ 1] = across(own_qkv[p][:, wide:], 1)
+            own_qkv.append((dot(normed, proj[p][:, :3 * wide]) + bias).astype(BF16))
+            other_kv[p ^ 1] = across(own_qkv[p][:, :2 * wide], 1)
         outs, weights, inverses = [], [], []
         for p in range(QUARTERS):
             out, weight, inverse = attend(own_qkv[p], other_kv[p], key_bias, heads, frames)
@@ -348,57 +361,89 @@
         )
         return back, jnp.sum(grad * unit_values, 0), jnp.sum(grad, 0)
 
-    def backward(cot, layer, kept):
-        w_in, w_out, w_up, w_down, vec = layers[layer]
+    def scattered(block):
+        bit = QUARTERS
+        while bit < replicas:
+            block = low_sum(block, across(block, bit))
+            bit *= 2
+        return lax.psum_scatter(block, "shard", scatter_dimension=0, tiled=True)
+
+    def half_sum(block):
+        cut = block.shape[1] // 2
+        left, right = block[:, :cut], block[:, cut:]
+        return low_sum(jnp.where(first, left, right), swap_sections(jnp.where(first, right, left)))
+
+    def backward(cot, layer, kept, pending):
+        proj, w_out, w_up, w_down, vec = layers[layer]
         x, normed, own_qkv, other_kv, weights, inverses, attended, middle, normed_two, acts, slopes = kept
         d_mlp = cot.astype(BF16)
-        g_down, g_up, up_sums = [], [], []
+        up_sums, d_ups = [], []
         d_normed_two = None
         for p in range(QUARTERS):
             d_up = (dot(d_mlp, w_down[p], NT) * slopes[p].astype(F32)).astype(BF16)
             part = dot(d_up, w_up[p], NT)
             d_normed_two = part if d_normed_two is None else d_normed_two + part
-            g_down.append(dot(acts[p], d_mlp, TN).astype(BF16))
-            g_up.append(dot(normed_two, d_up, TN).astype(BF16))
+            d_ups.append(d_up)
             up_sums.append(jnp.sum(d_up.astype(F32), 0))
+        near_down = [across(dot(acts[p], d_mlp, TN).astype(BF16), 1) for p in (1, 3)]
+        near_up = [across(dot(normed_two, d_ups[p], TN).astype(BF16), 1) for p in (1, 3)]
+        above = None
         back, g_gain_two, g_shift_two = norm_back(middle, vec[5], d_normed_two)
         d_middle = cot + back
         d_attn = d_middle.astype(BF16)
         d_attn_parts = in_order([d_attn[:, p * wide:(p + 1) * wide] for p in range(QUARTERS)], quarter)
-        g_out = [dot(attended, part, TN).astype(BF16) for part in d_attn_parts]
         d_attended = dot(d_attn, w_out, NT).astype(BF16)
         d_heads = in_order([d_attended[:, p * wide:(p + 1) * wide] for p in range(QUARTERS)], quarter)
-        half = own_qkv[0].shape[0]
-        d_normed, g_in, sums_in = None, [], []
-        d_normed_own = None
-        results = [
-            attend_back(own_qkv[p], other_kv[p], weights[p], inverses[p], d_heads[p], heads, frames)
-            for p in range(QUARTERS)
-        ]
+
+        far_down = low_sum(dot(acts[2], d_mlp, TN), near_down[1])
+        far_down = across(far_down, 2)
+        results = []
         for p in range(QUARTERS):
-            d_query, d_key, d_value = results[p]
-            r_key, r_value = results[p ^ 1][1], results[p ^ 1][2]
-            d_key = (d_key[:half].astype(F32) + across(r_key[half:], 1).astype(F32)).astype(BF16)
-            d_value = (d_value[:half].astype(F32) + across(r_value[half:], 1).astype(F32)).astype(BF16)
-            d_both = jnp.concatenate([d_key, d_value], 1)
-            part = dot(d_both, w_in[p][:, wide:], NT)
+            head = d_heads[p]
+            if p == 0:
+                head = after(head, *near_down)
+            elif p == 1:
+                head = after(head, *near_up)
+            elif pending is not None:
+                head = after(head, pending[p - 2][1])
+            results.append(attend_back(own_qkv[p], other_kv[p], weights[p], inverses[p], head, heads, frames))
+        d_normed, d_normed_own = None, None
+        d_boths, sums_in = [], []
+        for p in range(QUARTERS):
+            d_query = results[p][0]
+            d_both = low_sum(results[p][1], across(results[p ^ 1][2], 1))
+            d_boths.append(d_both)
+            part = dot(d_both, proj[p][:, :2 * wide], NT)
             d_normed = part if d_normed is None else d_normed + part
-            part = dot(d_query, w_in[p][:, :wide], NT)
+            part = dot(d_query, proj[p][:, 2 * wide:3 * wide], NT)
             d_normed_own = part if d_normed_own is None else d_normed_own + part
-            g_in.append(
-                jnp.concatenate(
-                    [dot(normed[:frames], d_query, TN).astype(BF16), dot(normed, d_both, TN).astype(BF16)], 1
-                )
+            sums_in.append((jnp.sum(d_query.astype(F32), 0), jnp.sum(d_both[:, wide:].astype(F32), 0)))
+
+        def g_proj(p):
+            return jnp.concatenate(
+                [
+                    dot(normed, d_boths[p], TN), dot(normed[:frames], results[p][0], TN),
+                    dot(attended, d_attn_parts[p], TN),
+                ],
+                1,
             )
-            sums_in.append(
-                (jnp.sum(d_query.astype(F32), 0), jnp.sum(d_value.astype(F32), 0))
-            )
+
         block = d_normed
+        if pending is not None:
+            halves = [half_sum(make(far)) for make, far in pending]
+            block = after(block, *halves)
+            above = scattered(jnp.concatenate(halves, 1))
         bit = shards // 2
         while bit >= 2:
             cut = block.shape[0] // 2
             block = block[:cut] + across(block[cut:].astype(BF16), bit).astype(F32)
             bit //= 2
+        near_proj = [across(g_proj(p).astype(BF16), 1) for p in (1, 3)]
+        far_up = low_sum(dot(after(normed_two, block), d_ups[2], TN), near_up[1])
+        far_up = across(far_up, 2)
+        block = after(block, far_down)
+        down_done = scattered(half_sum(low_sum(dot(acts[0], d_mlp, TN), near_down[0], far_down)))
+        far_proj = across(low_sum(g_proj(2), near_proj[1]), 2)
         back, g_gain_one, g_shift_one = norm_back(x, vec[0], block + d_normed_own)
         g_x = d_middle + back
         sum_query = jnp.concatenate(in_order([s[0] for s in sums_in], quarter))
@@ -416,43 +461,52 @@
                 sum_up,
             ]
         )
-        return g_x, (g_in, g_out, g_up, g_down), g_vec
-
-    def owned(grads, layer):
-        route = [(0, 1)] if layer == 1 else [(1, 0)]
-        done = []
-        for pieces in grads:
-            part = reduced(pieces)
-            part = (part.astype(F32) + lax.ppermute(part, "section", route).astype(F32)).astype(BF16)
-            done.append(lax.psum_scatter(part, "shard", scatter_dimension=0, tiled=True))
-        return done
+
+        def finish_proj(other):
+            return low_sum(g_proj(0), near_proj[0], other)
+
+        def finish_up(other):
+            return low_sum(dot(normed_two, d_ups[0], TN), near_up[0], other)
+
+        return g_x, down_done, ((finish_up, far_up), (finish_proj, far_proj)), above, g_vec
 
     x_one, kept_zero = forward(inputs, 0)
     y_one, kept_one = forward(x_one, 1)
     cot = jnp.where(first, transposed(edges_here[0], 1, 0), transposed(edges_here[1], 1, 1))
     out_slots = [transposed(y_one, 0, 1), transposed(y_one, 1, 1)]
-    g_one, grads_one, vec_one = backward(cot.astype(F32), 1, kept_one)
-    owned_one = owned(grads_one, 1)
-    g_zero, grads_zero, vec_zero = backward(g_one.astype(BF16).astype(F32), 0, kept_zero)
-    owned_zero = owned(grads_zero, 0)
+    g_one, down_one, pending, _, vec_one = backward(cot.astype(F32), 1, kept_one, None)
+    g_zero, down_zero, pending, rest_one, vec_zero = backward(
+        g_one.astype(BF16).astype(F32), 0, kept_zero, pending
+    )
     g_low = g_zero.astype(BF16)
     back_slots = [transposed(g_low, 0, 0), transposed(g_low, 1, 0)]
     edges_out = jnp.stack([jnp.where(first, b, o) for b, o in zip(back_slots, out_slots)])
-
-    vec_all = lax.psum(jnp.concatenate([vec_zero, vec_one]), AXES)
+    vec_all = lax.psum(after(jnp.concatenate([vec_zero, vec_one]), rest_one, down_one), AXES)
+    rest_zero = jnp.concatenate([half_sum(make(far)) for make, far in pending], 1)
+    rest_zero = scattered(after(rest_zero, down_zero))
     vec_all = jnp.where(first, vec_all[:12], vec_all[12:])
     slice_width = width // shards
     g_vectors = lax.dynamic_slice_in_dim(vec_all, lax.axis_index("shard") * slice_width, slice_width, 1)
 
-    finals = []
-    for zero, one in zip(owned_zero, owned_one):
-        part = jnp.where(first, zero, one)
-        finals.append(jnp.stack(in_order(spread(part), quarter)).astype(F32))
-    f_in, f_out, f_up, f_down = finals
-    f_in = f_in.reshape(QUARTERS, rows, 3, wide).transpose(1, 2, 0, 3).reshape(rows, 3 * width)
-    f_out = f_out.transpose(1, 0, 2).reshape(rows, width)
-    f_up = f_up.reshape(QUARTERS, rows, shards, unit).transpose(1, 2, 0, 3).reshape(rows, hidden)
-    f_down = f_down.reshape(-1, width)
+    def finished(zero, one):
+        own, other = jnp.where(first, zero, one), swap_sections(jnp.where(first, one, zero))
+        cut = width // 2
+        parts = []
+        for start in range(0, own.shape[1], cut):
+            a, b = own[:, start:start + cut], other[:, start:start + cut]
+            parts += [jnp.where(first, a, b), jnp.where(first, b, a)]
+        part = jnp.concatenate(parts, 1)
+        return in_order(spread(part, across(part, 2)), quarter)
+
+    f_down = jnp.stack(finished(down_zero, down_one)).astype(F32).reshape(-1, width)
+    f_rest = finished(rest_zero, rest_one)
+    f_up = jnp.stack([piece[:, :shards * unit].reshape(rows, shards, unit) for piece in f_rest], 2)
+    f_up = f_up.astype(F32).reshape(rows, hidden)
+    f_proj = [piece[:, shards * unit:] for piece in f_rest]
+    f_in = jnp.concatenate(
+        [piece[:, i * wide:(i + 1) * wide] for i in (2, 0, 1) for piece in f_proj], 1
+    ).astype(F32)
+    f_out = jnp.concatenate([piece[:, 3 * wide:] for piece in f_proj], 1).astype(F32)
     return edges_out[None], f_in[None], f_out[None], f_up[None], f_down[None], g_vectors[None]
 
 

time: 1050 us -> 993 us (0.946)
  blocking collectives: 91.2 us -> 0 us
  waiting for transfers between devices: 331 us -> 410 us
  starting transfers between devices: 166 us -> 107 us
  matrix products: 129 us -> 162 us
  local copies, waits for them, and re-layouts: 137 us -> 111 us
    psum x1, waiting for transfers between devices: 0.01 us -> 115 us  [body(): lax.psum(after(jnp.concatenate([vec_zero, vec_one]), rest_one, down_one),...]
    ppermute x8 -> x0, waiting for transfers between devices: 108 us -> none  [owned(): lax.ppermute(part, 'section', route).astype(F32)]
    all_gather x1 -> x0, blocking collectives: 91.2 us -> none  [gathered(): return lax.all_gather(block, 'shard', axis=0, tiled=True)]
    all_gather x3 -> x4, waiting for transfers between devices: 0.02 us -> 59.8 us  [gathered(): return lax.all_gather(block, 'shard', axis=0, tiled=True)]
    ppermute x82 -> x62, starting transfers between devices: 108 us -> 62.7 us  [across(): return lax.ppermute(block, 'replica', [(i, i ^ bit) for i in range(count)])]
    ppermute x82 -> x62, waiting for transfers between devices: 129 us -> 164 us  [across(): return lax.ppermute(block, 'replica', [(i, i ^ bit) for i in range(count)])]
    dot_general x92, matrix products: 129 us -> 162 us  [dot(): return lax.dot_general(a, b, dims, preferred_element_type=F32)]
    reduce_scatter x4, waiting for transfers between devices: 49.5 us -> 20.3 us  [scattered(): return lax.psum_scatter(block, 'shard', scatter_dimension=0, tiled=True)]
  transfers between devices with their start and end apart: 116 -> 92, of which waited for: 27 -> 26; matrix products, arithmetic and copies ran while one was open for 26% -> 30% of each run, Pallas kernels for 6% -> 9%
where the time goes in v2:
time: 993 us; the launch traced here: 980 us
  waiting for transfers between devices  410 us (41%)
  matrix products  162 us (16%)
  local copies, waits for them, and re-layouts  111 us (11%)
  starting transfers between devices  107 us (11%)
  Pallas kernels  88.5 us (9%)
  other arithmetic  83.2 us (8%)
  between operations  17.6 us (2%)
    ppermute x62, waiting for transfers between devices, across(): return lax.ppermute(block, 'replica', [(i, i ^ bit) for i in range(count)])  164 us
    dot_general x92, matrix products, dot(): return lax.dot_general(a, b, dims, preferred_element_type=F32)  162 us
    psum x1, waiting for transfers between devices, body(): lax.psum(after(jnp.concatenate([vec_zero, vec_one]), rest_one, down_one),...  115 us
    ppermute x62, starting transfers between devices, across(): return lax.ppermute(block, 'replica', [(i, i ^ bit) for i in range(count)])  62.7 us
    all_gather x4, waiting for transfers between devices, gathered(): return lax.all_gather(block, 'shard', axis=0, tiled=True)  59.8 us
    pallas_call x8, Pallas kernels, attend_back(): pl.pallas_call(functools.partial(attend_back_kernel, heads=heads, frames=...  43.2 us
    ppermute x12, waiting for transfers between devices, swap_sections(): return lax.ppermute(block, 'section', [(0, 1), (1, 0)])  41.8 us
    unnamed x581, local copies, waits for them, and re-layouts  41.4 us
  transfers between devices with their start and end apart: 92, of which 26 were waited for; matrix products, arithmetic and copies ran while one was open for 30% of the time, Pallas kernels for 9%

profile of v2, /device:TPU:0, one launch (start us, length us, event | category | flops | bytes accessed | tf_op | source)
XLA Modules:
  0.0 980.1 jit_solution(4578290840092035854)
XLA Ops:
  15.1 7.0 collective-permute-done.6
  27.3 6.2 collective-permute-start.3
  35.6 3.8 reshape_squeeze.10
  50.4 34.9 %all-gather.5.cloned.1.call-done = bf16[768,768]{1,0:T(8,128)(2,1)} async-done(((bf16[192,768]{1,0:T(8,128)(2,1)}), bf16[768,768]{1,0:T(8,128)(2,1)}) %all-gather.5.cloned.1.call-update) | async-done | bytes 1179664 | tf_op jit(solution)/shard_map/all_gather | solution.py:264
  93.5 25.5 %collective-permute-start.4 = (bf16[384,768]{1,0:T(8,128)(2,1)S(1)}, bf16[384,768]{1,0:T(8,128)(2,1)S(1)}, u32[]{:S(2)}, u32[]{:S(2)}) collective-permute-start(bf16[384,768]{1,0:T(8,128)(2,1)S(1)} %get-tuple-element.237), channel_id=1, source_target_pairs={{0,2},{1,3},{2,0},{3,1},{4,6},{5,7},{6,4},{7,5},{8,10},{9,11},{10,... | collective-permute-start | bytes 1769480 | tf_op jit(solution)/shard_map/ppermute | solution.py:192
  122.8 4.1 collective-permute-done.4
  127.2 11.5 %all-gather.7.cloned.1.call-done = bf16[768,768]{1,0:T(8,128)(2,1)} async-done(((bf16[192,768]{1,0:T(8,128)(2,1)}), bf16[768,768]{1,0:T(8,128)(2,1)}) %all-gather.7.cloned.1.call-update) | async-done | bytes 1179664 | tf_op jit(solution)/shard_map/all_gather | solution.py:264
  150.5 3.4 attend.10
  157.0 13.4 %all-gather.9.cloned.1.call-done = bf16[768,768]{1,0:T(8,128)(2,1)} async-done(((bf16[192,768]{1,0:T(8,128)(2,1)}), bf16[768,768]{1,0:T(8,128)(2,1)}) %all-gather.9.cloned.1.call-update) | async-done | bytes 1179664 | tf_op jit(solution)/shard_map/all_gather | solution.py:264
  180.4 3.8 attend.11
  186.5 4.4 attend.8
  195.9 3.4 attend.9
  208.3 25.4 %collective-permute-done.20 = bf16[768,768]{1,0:T(8,128)(2,1)} collective-permute-done((bf16[768,768]{1,0:T(8,128)(2,1)}, bf16[768,768]{1,0:T(8,128)(2,1)}, u32[]{:S(2)}, u32[]{:S(2)}) %collective-permute-start.20) | collective-permute-done | bytes 1179680 | tf_op jit(solution)/shard_map/ppermute | solution.py:192
  260.3 14.4 %collective-permute-done.24 = bf16[768,768]{1,0:T(8,128)(2,1)S(1)} collective-permute-done((bf16[768,768]{1,0:T(8,128)(2,1)}, bf16[768,768]{1,0:T(8,128)(2,1)S(1)}, u32[]{:S(2)}, u32[]{:S(2)}) %collective-permute-start.24) | collective-permute-done | bytes 1179680 | tf_op jit(solution)/shard_map/ppermute | solution.py:192
  274.7 25.3 %collective-permute-done.33.weight_ref = bf16[768,768]{1,0:T(8,128)(2,1)S(1)} collective-permute-done((bf16[768,768]{1,0:T(8,128)(2,1)S(1)}, bf16[768,768]{1,0:T(8,128)(2,1)S(1)}, u32[]{:S(2)}, u32[]{:S(2)}) %collective-permute-start.33) | collective-permute-done | bytes 1179680 | tf_op jit(solution)/shard_map/ppermute | solution.py:192
  301.7 10.9 %collective-permute-done.23 = bf16[384,768]{1,0:T(8,128)(2,1)S(1)} collective-permute-done((bf16[384,768]{1,0:T(8,128)(2,1)S(1)}, bf16[384,768]{1,0:T(8,128)(2,1)S(1)}, u32[]{:S(2)}, u32[]{:S(2)}) %collective-permute-start.23) | collective-permute-done | bytes 589856 | tf_op jit(solution)/shard_map/ppermute | solution.py:192
  322.6 3.4 attend.12
  326.5 3.8 attend.14
  332.8 4.7 collective-permute-done.34
  338.1 3.4 attend.15
  343.3 3.4 attend.13
  386.8 5.4 attend_back.11
  393.8 6.0 attend_back.10
  427.7 8.2 collective-permute-start.64
  438.0 5.7 attend_back.8
  458.8 4.8 attend_back.9
  495.2 5.9 collective-permute-done.45
  552.1 11.8 %collective-permute-done.62 = bf16[768,768]{1,0:T(8,128)(2,1)S(1)} collective-permute-done((bf16[768,768]{1,0:T(8,128)(2,1)}, bf16[768,768]{1,0:T(8,128)(2,1)S(1)}, u32[]{:S(2)}, u32[]{:S(2)}) %collective-permute-start.62) | collective-permute-done | bytes 1179680 | tf_op jit(solution)/shard_map/ppermute | solution.py:192
  572.1 9.7 collective-permute-done.73
  590.1 4.5 collective-permute-done.78
  598.9 4.2 fusion.14
  603.1 6.5 attend_back.15
  613.3 5.8 collective-permute-done.53
  621.1 4.6 attend_back.14
  627.6 5.6 attend_back.13
  639.6 4.6 attend_back.12
  662.0 9.1 collective-permute-done.58
  679.2 11.6 %collective-permute-done.61 = bf16[384,768]{1,0:T(8,128)(2,1)S(1)} collective-permute-done((bf16[384,768]{1,0:T(8,128)(2,1)S(1)}, bf16[384,768]{1,0:T(8,128)(2,1)S(1)}, u32[]{:S(2)}, u32[]{:S(2)}) %collective-permute-start.61) | collective-permute-done | bytes 589856 | tf_op jit(solution)/shard_map/ppermute | solution.py:192
  704.0 20.2 %collective-permute-done.67 = bf16[768,768]{1,0:T(8,128)(2,1)} collective-permute-done((bf16[768,768]{1,0:T(8,128)(2,1)}, bf16[768,768]{1,0:T(8,128)(2,1)}, u32[]{:S(2)}, u32[]{:S(2)}) %collective-permute-start.67) | collective-permute-done | bytes 1179680 | tf_op jit(solution)/shard_map/ppermute | solution.py:192
  727.5 19.7 %collective-permute-done.71 = bf16[768,768]{1,0:T(8,128)(2,1)} collective-permute-done((bf16[768,768]{1,0:T(8,128)(2,1)}, bf16[768,768]{1,0:T(8,128)(2,1)}, u32[]{:S(2)}, u32[]{:S(2)}) %collective-permute-start.71) | collective-permute-done | bytes 1179680 | tf_op jit(solution)/shard_map/ppermute | solution.py:192
  753.6 9.3 collective-permute-done.72
  771.6 6.1 collective-permute-start.63
  779.8 9.4 collective-permute-done.65
  790.4 20.2 %reduce-scatter.7.cloned.1.call-done = bf16[192,768]{1,0:T(8,128)(2,1)} async-done(((bf16[768,768]{1,0:T(8,128)(2,1)}), bf16[192,768]{1,0:T(8,128)(2,1)}) %reduce-scatter.7.cloned.1.call-update) | async-done | bytes 294928 | tf_op jit(solution)/shard_map/reduce_scatter | solution.py:369
  814.0 12.1 %collective-permute-start.80 = (bf16[192,768]{1,0:T(8,128)(2,1)}, bf16[192,768]{1,0:T(8,128)(2,1)}, u32[]{:S(2)}, u32[]{:S(2)}) collective-permute-start(bf16[192,768]{1,0:T(8,128)(2,1)} %pad_maximum_fusion.15), channel_id=1, source_target_pairs={{0,2},{1,3},{2,0},{3,1},{4,6},{5,7},{6,4},{7,5},{8,10},{9,11},{10,... | collective-permute-start | bytes 884744 | tf_op jit(solution)/shard_map/ppermute | solution.py:192
  833.0 115.0 %all-reduce.2.cloned.1.call-done = f32[24,768]{1,0:T(8,128)} async-done(((f32[24,768]{1,0:T(8,128)}), f32[24,768]{1,0:T(8,128)}) %all-reduce.2.cloned.1.call-update) | async-done | bytes 73744 | tf_op jit(solution)/shard_map/psum | solution.py:484
  963.8 3.7 copy.159
  967.6 4.9 reshape.755
  (1084 shorter events, 412.0 us)
Async XLA Ops:
  7.2 78.1 %all-gather.5.cloned.1.call-start = ((), (), s32[]{:S(2)}) async-start(), calls=%async_computation.4 | async-start | bytes 1474560 | tf_op jit(solution)/shard_map/all_gather | solution.py:264
  23.1 115.5 %all-gather.7.cloned.1.call-start = ((), (), s32[]{:S(2)}) async-start(), calls=%async_computation.5 | async-start | bytes 1474560 | tf_op jit(solution)/shard_map/all_gather | solution.py:264
  24.3 69.0 %collective-permute-start.2 = (bf16[384,768]{1,0:T(8,128)(2,1)}, bf16[384,768]{1,0:T(8,128)(2,1)S(1)}, u32[]{:S(2)}, u32[]{:S(2)}) collective-permute-start(bf16[384,768]{1,0:T(8,128)(2,1)} %get-tuple-element.258), channel_id=1, source_target_pairs={{0,0},{1,4},{2,8},{3,12},{4,1},{5,5},{6,9},{7,13},{8,2},{9,6},{10,... | collective-permute-start | bytes 1769480 | tf_op jit(solution)/shard_map/ppermute | solution.py:214
  26.0 93.0 %collective-permute-start = (bf16[384,768]{1,0:T(8,128)(2,1)}, bf16[384,768]{1,0:T(8,128)(2,1)}, u32[]{:S(2)}, u32[]{:S(2)}) collective-permute-start(bf16[384,768]{1,0:T(8,128)(2,1)} %get-tuple-element.258), channel_id=1, source_target_pairs={{16,0},{17,4},{18,8},{19,12},{20,1},{21,5},{22,9},{23,13},{24,2},{... | collective-permute-start | bytes 1769480 | tf_op jit(solution)/shard_map/ppermute | solution.py:214
  27.3 66.0 %collective-permute-start.3 = (bf16[384,768]{1,0:T(8,128)(2,1)}, bf16[384,768]{1,0:T(8,128)(2,1)}, u32[]{:S(2)}, u32[]{:S(2)}) collective-permute-start(bf16[384,768]{1,0:T(8,128)(2,1)} %get-tuple-element.257), channel_id=1, source_target_pairs={{0,16},{1,20},{2,24},{3,28},{4,17},{5,21},{6,25},{7,29},{8,18},{9,... | collective-permute-start | bytes 1769480 | tf_op jit(solution)/shard_map/ppermute | solution.py:214
  33.4 85.6 %collective-permute-start.1 = (bf16[384,768]{1,0:T(8,128)(2,1)}, bf16[384,768]{1,0:T(8,128)(2,1)}, u32[]{:S(2)}, u32[]{:S(2)}) collective-permute-start(bf16[384,768]{1,0:T(8,128)(2,1)} %get-tuple-element.257), channel_id=1, source_target_pairs={{16,16},{17,20},{18,24},{19,28},{20,17},{21,21},{22,25},{23,29},{2... | collective-permute-start | bytes 1769480 | tf_op jit(solution)/shard_map/ppermute | solution.py:214
  85.4 85.0 %all-gather.9.cloned.1.call-start = ((), (), s32[]{:S(2)}) async-start(), calls=%async_computation.6 | async-start | bytes 1474560 | tf_op jit(solution)/shard_map/all_gather | solution.py:264
  93.5 33.4 %collective-permute-start.4 = (bf16[384,768]{1,0:T(8,128)(2,1)S(1)}, bf16[384,768]{1,0:T(8,128)(2,1)S(1)}, u32[]{:S(2)}, u32[]{:S(2)}) collective-permute-start(bf16[384,768]{1,0:T(8,128)(2,1)S(1)} %get-tuple-element.237), channel_id=1, source_target_pairs={{0,2},{1,3},{2,0},{3,1},{4,6},{5,7},{6,4},{7,5},{8,10},{9,11},{10,... | collective-permute-start | bytes 1769480 | tf_op jit(solution)/shard_map/ppermute | solution.py:192
  138.7 107.0 %all-gather.11.cloned.1.call-start = ((), (), s32[]{:S(2)}) async-start(), calls=%async_computation.7 | async-start | bytes 1474560 | tf_op jit(solution)/shard_map/all_gather | solution.py:264
  139.4 32.4 %collective-permute-start.15 = (bf16[768,768]{1,0:T(8,128)(2,1)}, bf16[768,768]{1,0:T(8,128)(2,1)}, u32[]{:S(2)}, u32[]{:S(2)}) collective-permute-start(bf16[768,768]{1,0:T(8,128)(2,1)} %all-gather.7.cloned.1.call-done), channel_id=1, source_target_pairs={{0,16},{16,0},{1,17},{17,1},{2,18},{18,2},{3,19},{19,3},{4,20},{20... | collective-permute-start | bytes 3538952 | tf_op jit(solution)/shard_map/ppermute | solution.py:196
  141.5 33.7 %collective-permute-start.8 = (bf16[768,768]{1,0:T(8,128)(2,1)}, bf16[768,768]{1,0:T(8,128)(2,1)}, u32[]{:S(2)}, u32[]{:S(2)}) collective-permute-start(bf16[768,768]{1,0:T(8,128)(2,1)} %collective-permute-done.7), channel_id=1, source_target_pairs={{0,1},{1,0},{2,3},{3,2},{4,5},{5,4},{6,7},{7,6},{8,9},{9,8},{10,11... | collective-permute-start | bytes 3538952 | tf_op jit(solution)/shard_map/ppermute | solution.py:192
  147.8 38.6 %collective-permute-start.9 = (bf16[768,384]{1,0:T(8,128)(2,1)}, bf16[768,384]{1,0:T(8,128)(2,1)}, u32[]{:S(2)}, u32[]{:S(2)}) collective-permute-start(bf16[768,384]{1,0:T(8,128)(2,1)} %slice.569), channel_id=1, source_target_pairs={{0,1},{1,0},{2,3},{3,2},{4,5},{5,4},{6,7},{7,6},{8,9},{9,8},{10,11... | collective-permute-start | bytes 1769480 | tf_op jit(solution)/shard_map/ppermute | solution.py:192
  170.4 31.3 %collective-permute-start.16 = (bf16[768,768]{1,0:T(8,128)(2,1)}, bf16[768,768]{1,0:T(8,128)(2,1)}, u32[]{:S(2)}, u32[]{:S(2)}) collective-permute-start(bf16[768,768]{1,0:T(8,128)(2,1)} %all-gather.9.cloned.1.call-done), channel_id=1, source_target_pairs={{0,16},{16,0},{1,17},{17,1},{2,18},{18,2},{3,19},{19,3},{4,20},{20... | collective-permute-start | bytes 3538952 | tf_op jit(solution)/shard_map/ppermute | solution.py:196
  173.7 31.4 %collective-permute-start.19 = (bf16[768,768]{1,0:T(8,128)(2,1)S(1)}, bf16[768,768]{1,0:T(8,128)(2,1)}, u32[]{:S(2)}, u32[]{:S(2)}) collective-permute-start(bf16[768,768]{1,0:T(8,128)(2,1)S(1)} %get-tuple-element.250.weight_ref), channel_id=1, source_target_pairs={{0,2},{1,3},{2,0},{3,1},{4,6},{5,7},{6,4},{7,5},{8,10},{9,11},{10,... | collective-permute-start | bytes 3538952 | tf_op jit(solution)/shard_map/ppermute | solution.py:192
  195.9 45.3 %collective-permute-start.17 = (bf16[768,768]{1,0:T(8,128)(2,1)S(1)}, bf16[768,768]{1,0:T(8,128)(2,1)}, u32[]{:S(2)}, u32[]{:S(2)}) collective-permute-start(bf16[768,768]{1,0:T(8,128)(2,1)S(1)} %get-tuple-element.250.weight_ref), channel_id=1, source_target_pairs={{0,1},{1,0},{2,3},{3,2},{4,5},{5,4},{6,7},{7,6},{8,9},{9,8},{10,11... | collective-permute-start | bytes 3538952 | tf_op jit(solution)/shard_map/ppermute | solution.py:192
  201.7 562.7 %reduce-scatter.5.cloned.1.call-start = ((), (), s32[]{:S(2)}) async-start(), calls=%async_computation.8 | async-start | bytes 737280 | tf_op jit(solution)/shard_map/reduce_scatter | solution.py:369
  207.4 42.3 %collective-permute-start.21 = (bf16[768,768]{1,0:T(8,128)(2,1)}, bf16[768,768]{1,0:T(8,128)(2,1)}, u32[]{:S(2)}, u32[]{:S(2)}) collective-permute-start(bf16[768,768]{1,0:T(8,128)(2,1)} %collective-permute-done.19.weight_ref), channel_id=1, source_target_pairs={{0,1},{1,0},{2,3},{3,2},{4,5},{5,4},{6,7},{7,6},{8,9},{9,8},{10,11... | collective-permute-start | bytes 3538952 | tf_op jit(solution)/shard_map/ppermute | solution.py:192
  208.2 47.1 %collective-permute-start.18 = (bf16[768,768]{1,0:T(8,128)(2,1)}, bf16[768,768]{1,0:T(8,128)(2,1)}, u32[]{:S(2)}, u32[]{:S(2)}) collective-permute-start(bf16[768,768]{1,0:T(8,128)(2,1)} %get-tuple-element.99), channel_id=1, source_target_pairs={{0,1},{1,0},{2,3},{3,2},{4,5},{5,4},{6,7},{7,6},{8,9},{9,8},{10,11... | collective-permute-start | bytes 3538952 | tf_op jit(solution)/shard_map/ppermute | solution.py:192
  245.7 29.0 %collective-permute-start.24 = (bf16[768,768]{1,0:T(8,128)(2,1)}, bf16[768,768]{1,0:T(8,128)(2,1)S(1)}, u32[]{:S(2)}, u32[]{:S(2)}) collective-permute-start(bf16[768,768]{1,0:T(8,128)(2,1)} %all-gather.11.cloned.1.call-done), channel_id=1, source_target_pairs={{0,2},{1,3},{2,0},{3,1},{4,6},{5,7},{6,4},{7,5},{8,10},{9,11},{10,... | collective-permute-start | bytes 3538952 | tf_op jit(solution)/shard_map/ppermute | solution.py:192
  246.2 53.7 %collective-permute-start.33 = (bf16[768,768]{1,0:T(8,128)(2,1)S(1)}, bf16[768,768]{1,0:T(8,128)(2,1)S(1)}, u32[]{:S(2)}, u32[]{:S(2)}) collective-permute-start(bf16[768,768]{1,0:T(8,128)(2,1)S(1)} %get-tuple-element.109.weight_ref), channel_id=1, source_target_pairs={{0,2},{1,3},{2,0},{3,1},{4,6},{5,7},{6,4},{7,5},{8,10},{9,11},{10,... | collective-permute-start | bytes 3538952 | tf_op jit(solution)/shard_map/ppermute | solution.py:192
  249.7 67.3 %collective-permute-start.28 = (bf16[768,768]{1,0:T(8,128)(2,1)S(1)}, bf16[768,768]{1,0:T(8,128)(2,1)S(1)}, u32[]{:S(2)}, u32[]{:S(2)}) collective-permute-start(bf16[768,768]{1,0:T(8,128)(2,1)S(1)} %copy-done.153), channel_id=1, source_target_pairs={{0,1},{1,0},{2,3},{3,2},{4,5},{5,4},{6,7},{7,6},{8,9},{9,8},{10,11... | collective-permute-start | bytes 3538952 | tf_op jit(solution)/shard_map/ppermute | solution.py:192
  259.7 52.9 %collective-permute-start.23 = (bf16[384,768]{1,0:T(8,128)(2,1)S(1)}, bf16[384,768]{1,0:T(8,128)(2,1)S(1)}, u32[]{:S(2)}, u32[]{:S(2)}) collective-permute-start(bf16[384,768]{1,0:T(8,128)(2,1)S(1)} %get-tuple-element.340), channel_id=1, source_target_pairs={{0,2},{1,3},{2,0},{3,1},{4,6},{5,7},{6,4},{7,5},{8,10},{9,11},{10,... | collective-permute-start | bytes 1769480 | tf_op jit(solution)/shard_map/ppermute | solution.py:192
  299.9 37.6 %collective-permute-start.34 = (bf16[768,768]{1,0:T(8,128)(2,1)S(1)}, bf16[768,768]{1,0:T(8,128)(2,1)}, u32[]{:S(2)}, u32[]{:S(2)}) collective-permute-start(bf16[768,768]{1,0:T(8,128)(2,1)S(1)} %copy-done.122), channel_id=1, source_target_pairs={{0,2},{1,3},{2,0},{3,1},{4,6},{5,7},{6,4},{7,5},{8,10},{9,11},{10,... | collective-permute-start | bytes 3538952 | tf_op jit(solution)/shard_map/ppermute | solution.py:192
  337.6 37.4 %collective-permute-start.35 = (bf16[768,768]{1,0:T(8,128)(2,1)}, bf16[768,768]{1,0:T(8,128)(2,1)}, u32[]{:S(2)}, u32[]{:S(2)}) collective-permute-start(bf16[768,768]{1,0:T(8,128)(2,1)} %collective-permute-done.34), channel_id=1, source_target_pairs={{0,1},{1,0},{2,3},{3,2},{4,5},{5,4},{6,7},{7,6},{8,9},{9,8},{10,11... | collective-permute-start | bytes 3538952 | tf_op jit(solution)/shard_map/ppermute | solution.py:192
  355.6 102.9 %collective-permute-start.39 = (bf16[768,768]{1,0:T(8,128)(2,1)}, bf16[768,768]{1,0:T(8,128)(2,1)}, u32[]{:S(2)}, u32[]{:S(2)}) collective-permute-start(bf16[768,768]{1,0:T(8,128)(2,1)} %convolution_convert_fusion.5), channel_id=1, source_target_pairs={{0,1},{1,0},{2,3},{3,2},{4,5},{5,4},{6,7},{7,6},{8,9},{9,8},{10,11... | collective-permute-start | bytes 3538952 | tf_op jit(solution)/shard_map/ppermute | solution.py:192
  357.5 70.3 %collective-permute-start.37 = (bf16[768,768]{1,0:T(8,128)(2,1)}, bf16[768,768]{1,0:T(8,128)(2,1)}, u32[]{:S(2)}, u32[]{:S(2)}) collective-permute-start(bf16[768,768]{1,0:T(8,128)(2,1)} %convolution_convert_fusion.7), channel_id=1, source_target_pairs={{0,1},{1,0},{2,3},{3,2},{4,5},{5,4},{6,7},{7,6},{8,9},{9,8},{10,11... | collective-permute-start | bytes 3538952 | tf_op jit(solution)/shard_map/ppermute | solution.py:192
  363.4 72.5 %collective-permute-start.38 = (bf16[768,768]{1,0:T(8,128)(2,1)}, bf16[768,768]{1,0:T(8,128)(2,1)}, u32[]{:S(2)}, u32[]{:S(2)}) collective-permute-start(bf16[768,768]{1,0:T(8,128)(2,1)} %convolution_convert_fusion.6), channel_id=1, source_target_pairs={{0,1},{1,0},{2,3},{3,2},{4,5},{5,4},{6,7},{7,6},{8,9},{9,8},{10,11... | collective-permute-start | bytes 3538952 | tf_op jit(solution)/shard_map/ppermute | solution.py:192
  399.8 43.9 %collective-permute-start.44 = (bf16[768,384]{1,0:T(8,128)(2,1)}, bf16[768,384]{1,0:T(8,128)(2,1)}, u32[]{:S(2)}, u32[]{:S(2)}) collective-permute-start(bf16[768,384]{1,0:T(8,128)(2,1)} %get-tuple-element.132), channel_id=1, source_target_pairs={{0,1},{1,0},{2,3},{3,2},{4,5},{5,4},{6,7},{7,6},{8,9},{9,8},{10,11... | collective-permute-start | bytes 1769480 | tf_op jit(solution)/shard_map/ppermute | solution.py:192
  403.1 376.7 %collective-permute-start.66 = (bf16[384,768]{1,0:T(8,128)(2,1)}, bf16[384,768]{1,0:T(8,128)(2,1)}, u32[]{:S(2)}, u32[]{:S(2)}) collective-permute-start(bf16[384,768]{1,0:T(8,128)(2,1)} %fusion.44), channel_id=1, source_target_pairs={{16,16},{17,20},{18,24},{19,28},{20,17},{21,21},{22,25},{23,29},{2... | collective-permute-start | bytes 1769480 | tf_op jit(solution)/shard_map/ppermute | solution.py:214
  427.7 400.9 %collective-permute-start.64 = (bf16[384,768]{1,0:T(8,128)(2,1)}, bf16[384,768]{1,0:T(8,128)(2,1)}, u32[]{:S(2)}, u32[]{:S(2)}) collective-permute-start(bf16[384,768]{1,0:T(8,128)(2,1)} %fusion.44), channel_id=1, source_target_pairs={{0,16},{1,20},{2,24},{3,28},{4,17},{5,21},{6,25},{7,29},{8,18},{9,... | collective-permute-start | bytes 1769480 | tf_op jit(solution)/shard_map/ppermute | solution.py:214
  458.6 33.2 %collective-permute-start.54 = (bf16[768,768]{1,0:T(8,128)(2,1)}, bf16[768,768]{1,0:T(8,128)(2,1)}, u32[]{:S(2)}, u32[]{:S(2)}) collective-permute-start(bf16[768,768]{1,0:T(8,128)(2,1)} %pad_maximum_fusion.4), channel_id=1, source_target_pairs={{0,1},{1,0},{2,3},{3,2},{4,5},{5,4},{6,7},{7,6},{8,9},{9,8},{10,11... | collective-permute-start | bytes 3538952 | tf_op jit(solution)/shard_map/ppermute | solution.py:192
  478.3 120.1 %collective-permute-start.59 = (bf16[768,768]{1,0:T(8,128)(2,1)}, bf16[768,768]{1,0:T(8,128)(2,1)}, u32[]{:S(2)}, u32[]{:S(2)}) collective-permute-start(bf16[768,768]{1,0:T(8,128)(2,1)} %pad_maximum_fusion.5), channel_id=1, source_target_pairs={{0,1},{1,0},{2,3},{3,2},{4,5},{5,4},{6,7},{7,6},{8,9},{9,8},{10,11... | collective-permute-start | bytes 3538952 | tf_op jit(solution)/shard_map/ppermute | solution.py:192
  510.0 41.4 %collective-permute-start.47 = (bf16[768,768]{1,0:T(8,128)(2,1)}, bf16[768,768]{1,0:T(8,128)(2,1)}, u32[]{:S(2)}, u32[]{:S(2)}) collective-permute-start(bf16[768,768]{1,0:T(8,128)(2,1)} %convolution_convert_fusion.3), channel_id=1, source_target_pairs={{0,1},{1,0},{2,3},{3,2},{4,5},{5,4},{6,7},{7,6},{8,9},{9,8},{10,11... | collective-permute-start | bytes 3538952 | tf_op jit(solution)/shard_map/ppermute | solution.py:192
  534.8 29.0 %collective-permute-start.62 = (bf16[768,768]{1,0:T(8,128)(2,1)}, bf16[768,768]{1,0:T(8,128)(2,1)S(1)}, u32[]{:S(2)}, u32[]{:S(2)}) collective-permute-start(bf16[768,768]{1,0:T(8,128)(2,1)} %add_convert_fusion.4), channel_id=1, source_target_pairs={{0,2},{1,3},{2,0},{3,1},{4,6},{5,7},{6,4},{7,5},{8,10},{9,11},{10,... | collective-permute-start | bytes 3538952 | tf_op jit(solution)/shard_map/ppermute | solution.py:192
  551.3 46.9 %collective-permute-start.55 = (bf16[768,768]{1,0:T(8,128)(2,1)}, bf16[768,768]{1,0:T(8,128)(2,1)}, u32[]{:S(2)}, u32[]{:S(2)}) collective-permute-start(bf16[768,768]{1,0:T(8,128)(2,1)} %fusion.12), channel_id=1, source_target_pairs={{0,2},{1,3},{2,0},{3,1},{4,6},{5,7},{6,4},{7,5},{8,10},{9,11},{10,... | collective-permute-start | bytes 3538952 | tf_op jit(solution)/shard_map/ppermute | solution.py:192
  584.2 205.1 %reduce-scatter.11.cloned.1.call-start = ((), (), s32[]{:S(2)}) async-start(), calls=%async_computation.11 | async-start | bytes 737280 | tf_op jit(solution)/shard_map/reduce_scatter | solution.py:369
  598.0 192.4 %reduce-scatter.9.cloned.1.call-start = ((), (), s32[]{:S(2)}) async-start(), calls=%async_computation.10 | async-start | bytes 1474560 | tf_op jit(solution)/shard_map/reduce_scatter | solution.py:369
  598.4 29.2 %collective-permute-start.50 = (bf16[768,768]{1,0:T(8,128)(2,1)}, bf16[768,768]{1,0:T(8,128)(2,1)}, u32[]{:S(2)}, u32[]{:S(2)}) collective-permute-start(bf16[768,768]{1,0:T(8,128)(2,1)} %convolution_convert_fusion), channel_id=1, source_target_pairs={{0,1},{1,0},{2,3},{3,2},{4,5},{5,4},{6,7},{7,6},{8,9},{9,8},{10,11... | collective-permute-start | bytes 3538952 | tf_op jit(solution)/shard_map/ppermute | solution.py:192
  619.1 32.8 %collective-permute-start.56 = (bf16[768,384]{1,0:T(8,128)(2,1)}, bf16[768,384]{1,0:T(8,128)(2,1)}, u32[]{:S(2)}, u32[]{:S(2)}) collective-permute-start(bf16[768,384]{1,0:T(8,128)(2,1)} %get-tuple-element.161), channel_id=1, source_target_pairs={{0,1},{1,0},{2,3},{3,2},{4,5},{5,4},{6,7},{7,6},{8,9},{9,8},{10,11... | collective-permute-start | bytes 1769480 | tf_op jit(solution)/shard_map/ppermute | solution.py:192
  695.0 29.2 %collective-permute-start.67 = (bf16[768,768]{1,0:T(8,128)(2,1)}, bf16[768,768]{1,0:T(8,128)(2,1)}, u32[]{:S(2)}, u32[]{:S(2)}) collective-permute-start(bf16[768,768]{1,0:T(8,128)(2,1)} %add_convert_fusion.3), channel_id=1, source_target_pairs={{0,2},{1,3},{2,0},{3,1},{4,6},{5,7},{6,4},{7,5},{8,10},{9,11},{10,... | collective-permute-start | bytes 3538952 | tf_op jit(solution)/shard_map/ppermute | solution.py:192
  698.3 29.2 %collective-permute-start.69 = (bf16[768,768]{1,0:T(8,128)(2,1)}, bf16[768,768]{1,0:T(8,128)(2,1)}, u32[]{:S(2)}, u32[]{:S(2)}) collective-permute-start(bf16[768,768]{1,0:T(8,128)(2,1)} %pad_maximum_fusion.6), channel_id=1, source_target_pairs={{0,1},{1,0},{2,3},{3,2},{4,5},{5,4},{6,7},{7,6},{8,9},{9,8},{10,11... | collective-permute-start | bytes 3538952 | tf_op jit(solution)/shard_map/ppermute | solution.py:192
  700.4 46.9 %collective-permute-start.71 = (bf16[768,768]{1,0:T(8,128)(2,1)}, bf16[768,768]{1,0:T(8,128)(2,1)}, u32[]{:S(2)}, u32[]{:S(2)}) collective-permute-start(bf16[768,768]{1,0:T(8,128)(2,1)} %fusion.17), channel_id=1, source_target_pairs={{0,2},{1,3},{2,0},{3,1},{4,6},{5,7},{6,4},{7,5},{8,10},{9,11},{10,... | collective-permute-start | bytes 3538952 | tf_op jit(solution)/shard_map/ppermute | solution.py:192
  703.1 107.5 %reduce-scatter.7.cloned.1.call-start = ((), (), s32[]{:S(2)}) async-start(), calls=%async_computation.9 | async-start | bytes 1474560 | tf_op jit(solution)/shard_map/reduce_scatter | solution.py:369
  764.4 183.6 %all-reduce.2.cloned.1.call-start = ((), (), s32[]{:S(2)}) async-start(), calls=%async_computation.12 | async-start | bytes 147456 | tf_op jit(solution)/shard_map/psum | solution.py:484
  771.6 57.0 %collective-permute-start.63 = (bf16[384,768]{1,0:T(8,128)(2,1)}, bf16[384,768]{1,0:T(8,128)(2,1)}, u32[]{:S(2)}, u32[]{:S(2)}) collective-permute-start(bf16[384,768]{1,0:T(8,128)(2,1)} %fusion.56), channel_id=1, source_target_pairs={{0,0},{1,4},{2,8},{3,12},{4,1},{5,5},{6,9},{7,13},{8,2},{9,6},{10,... | collective-permute-start | bytes 1769480 | tf_op jit(solution)/shard_map/ppermute | solution.py:214
  826.2 124.5 %collective-permute-start.75 = (bf16[192,1536]{1,0:T(8,128)(2,1)S(1)}, bf16[192,1536]{1,0:T(8,128)(2,1)S(1)}, u32[]{:S(2)}, u32[]{:S(2)}) collective-permute-start(bf16[192,1536]{1,0:T(8,128)(2,1)S(1)} %pad_maximum_fusion.13), channel_id=1, source_target_pairs={{0,2},{1,3},{2,0},{3,1},{4,6},{5,7},{6,4},{7,5},{8,10},{9,11},{10,... | collective-permute-start | bytes 1769480 | tf_op jit(solution)/shard_map/ppermute | solution.py:192
  830.9 119.8 %collective-permute-start.82 = (bf16[192,768]{1,0:T(8,128)(2,1)}, bf16[192,768]{1,0:T(8,128)(2,1)S(1)}, u32[]{:S(2)}, u32[]{:S(2)}) collective-permute-start(bf16[192,768]{1,0:T(8,128)(2,1)} %pad_maximum_fusion.15), channel_id=1, source_target_pairs={{0,1},{1,0},{2,3},{3,2},{4,5},{5,4},{6,7},{7,6},{8,9},{9,8},{10,11... | collective-permute-start | bytes 884744 | tf_op jit(solution)/shard_map/ppermute | solution.py:192
  833.0 117.8 %collective-permute-start.81 = (bf16[192,768]{1,0:T(8,128)(2,1)}, bf16[192,768]{1,0:T(8,128)(2,1)S(1)}, u32[]{:S(2)}, u32[]{:S(2)}) collective-permute-start(bf16[192,768]{1,0:T(8,128)(2,1)} %collective-permute-done.80), channel_id=1, source_target_pairs={{0,1},{1,0},{2,3},{3,2},{4,5},{5,4},{6,7},{7,6},{8,9},{9,8},{10,11... | collective-permute-start | bytes 884744 | tf_op jit(solution)/shard_map/ppermute | solution.py:192
  (333 other events, 2714.9 us)
Sparse Core Ops, SparseCore 0:
  23.2 62.0 all-gather.4
  87.5 51.1 all-gather.6
  140.8 29.5 all-gather.8
  201.8 30.9 all-gather.10
  584.3 23.1 reduce-scatter.4
  609.6 20.3 reduce-scatter.10
  703.2 29.6 reduce-scatter.8
  764.5 46.1 reduce-scatter.6
  829.9 118.0 all-reduce.1

commit v3 on v2

--- a/solution.py
+++ b/solution.py
@@ -1,4 +1,5 @@
 import functools
+import math
 
 import jax
 import jax.numpy as jnp
@@ -156,35 +157,175 @@
     )(own, other, weights, inverse, dout)
 
 
-def up_kernel(in_ref, weight_ref, bias_ref, act_ref, slope_ref):
-    up = dot(in_ref[...], weight_ref[...]) + bias_ref[...]
+def column_tile(columns):
+    return 256 if columns % 256 == 0 else columns
+
+
+def mlp_kernel(in_ref, up_ref, bias_ref, down_ref, before_ref, act_ref, slope_ref, sum_ref):
+    up = dot(in_ref[...], up_ref[...]) + bias_ref[...]
     cdf = 0.5 + 0.5 * lax.erf(up * (0.5 ** 0.5))
     pdf = jnp.exp(-0.5 * up * up) * 0.3989422804014327
-    act_ref[...] = (up * cdf).astype(BF16)
+    act = (up * cdf).astype(BF16)
+    act_ref[...] = act
     slope_ref[...] = (cdf + up * pdf).astype(BF16)
-
-
-def up_gelu(values, weight, bias):
+    part = dot(act, down_ref[...])
+
+    @pl.when(pl.program_id(0) == 0)
+    def _():
+        sum_ref[...] = before_ref[...] + part
+
+    @pl.when(pl.program_id(0) > 0)
+    def _():
+        sum_ref[...] += part
+
+
+def mlp_part(values, up, bias, down, before):
     rows, depth = values.shape
-    columns = weight.shape[1]
-    tile = 256 if columns % 256 == 0 else columns
+    columns = up.shape[1]
+    tile = column_tile(columns)
+    whole = pl.BlockSpec((rows, depth), lambda i: (0, 0))
+    hidden = pl.BlockSpec((rows, tile), lambda i: (0, i))
     return pl.pallas_call(
-        up_kernel,
+        mlp_kernel,
         grid=(columns // tile,),
         in_specs=[
-            pl.BlockSpec((rows, depth), lambda i: (0, 0)),
+            whole,
             pl.BlockSpec((depth, tile), lambda i: (0, i)),
             pl.BlockSpec((1, tile), lambda i: (0, i)),
+            pl.BlockSpec((tile, depth), lambda i: (i, 0)),
+            whole,
         ],
-        out_specs=[pl.BlockSpec((rows, tile), lambda i: (0, i))] * 2,
-        out_shape=[jax.ShapeDtypeStruct((rows, columns), BF16)] * 2,
+        out_specs=[hidden, hidden, whole],
+        out_shape=[
+            jax.ShapeDtypeStruct((rows, columns), BF16),
+            jax.ShapeDtypeStruct((rows, columns), BF16),
+            jax.ShapeDtypeStruct((rows, depth), F32),
+        ],
         compiler_params=pltpu.CompilerParams(vmem_limit_bytes=32 * 2**20),
         cost_estimate=pl.CostEstimate(
-            flops=2 * rows * depth * columns, bytes_accessed=2 * (rows * depth + depth * columns + 2 * rows * columns),
+            flops=4 * rows * depth * columns, bytes_accessed=4 * (3 * rows * depth + depth * columns + rows * columns),
             transcendentals=2 * rows * columns,
         ),
-        name="up_gelu",
-    )(values, weight, bias)
+        name="mlp_part",
+    )(values, up, bias, down, before)
+
+
+def mlp_back_kernel(grad_ref, in_ref, act_ref, slope_ref, up_ref, down_ref, before_ref, gd_ref, gu_ref, row_ref, sum_ref):
+    grad = grad_ref[...]
+    d_up = (dot(grad, down_ref[...], NT) * slope_ref[...].astype(F32)).astype(BF16)
+    gd_ref[...] = dot(act_ref[...], grad, TN).astype(BF16)
+    gu_ref[...] = dot(in_ref[...], d_up, TN).astype(BF16)
+    row_ref[...] = jnp.sum(d_up.astype(F32), 0, keepdims=True)
+    part = dot(d_up, up_ref[...], NT)
+
+    @pl.when(pl.program_id(0) == 0)
+    def _():
+        sum_ref[...] = before_ref[...] + part
+
+    @pl.when(pl.program_id(0) > 0)
+    def _():
+        sum_ref[...] += part
+
+
+def mlp_back_part(grad, values, act, slope, up, down, before):
+    rows, depth = values.shape
+    columns = up.shape[1]
+    tile = column_tile(columns)
+    whole = pl.BlockSpec((rows, depth), lambda i: (0, 0))
+    hidden = pl.BlockSpec((rows, tile), lambda i: (0, i))
+    up_tile = pl.BlockSpec((depth, tile), lambda i: (0, i))
+    down_tile = pl.BlockSpec((tile, depth), lambda i: (i, 0))
+    return pl.pallas_call(
+        mlp_back_kernel,
+        grid=(columns // tile,),
+        in_specs=[whole, whole, hidden, hidden, up_tile, down_tile, whole],
+        out_specs=[down_tile, up_tile, pl.BlockSpec((1, tile), lambda i: (0, i)), whole],
+        out_shape=[
+            jax.ShapeDtypeStruct((columns, depth), BF16),
+            jax.ShapeDtypeStruct((depth, columns), BF16),
+            jax.ShapeDtypeStruct((1, columns), F32),
+            jax.ShapeDtypeStruct((rows, depth), F32),
+        ],
+        compiler_params=pltpu.CompilerParams(vmem_limit_bytes=40 * 2**20),
+        cost_estimate=pl.CostEstimate(
+            flops=8 * rows * depth * columns, bytes_accessed=4 * (3 * rows * depth + 2 * depth * columns + rows * columns),
+            transcendentals=0,
+        ),
+        name="mlp_back_part",
+    )(grad, values, act, slope, up, down, before)
+
+
+def proj_back_kernel(in_ref, own_ref, other_ref, query_ref, out_ref, grad_ref, weight_ref, before_ref, g_ref, row_ref, sum_ref):
+    frames, wide = query_ref.shape
+    both = (own_ref[...].astype(F32) + other_ref[...].astype(F32)).astype(BF16)
+    query = query_ref[...]
+    values = in_ref[...]
+    g_ref[...] = jnp.concatenate(
+        [dot(values, both, TN), dot(values[:frames], query, TN), dot(out_ref[...], grad_ref[...], TN)], 1
+    ).astype(BF16)
+    row_ref[...] = jnp.concatenate(
+        [jnp.sum(both.astype(F32), 0, keepdims=True), jnp.sum(query.astype(F32), 0, keepdims=True)], 1
+    )
+    total = before_ref[...] + dot(both, weight_ref[:, :2 * wide], NT)
+    own = total[:frames] + dot(query, weight_ref[:, 2 * wide:3 * wide], NT)
+    sum_ref[0:frames, :] = own
+    sum_ref[frames:, :] = total[frames:]
+
+
+def proj_back(values, own, other, query, out, grad, weight, before):
+    rows, depth = values.shape
+    wide = query.shape[1]
+    return pl.pallas_call(
+        proj_back_kernel,
+        out_shape=[
+            jax.ShapeDtypeStruct(weight.shape, BF16),
+            jax.ShapeDtypeStruct((1, 3 * wide), F32),
+            jax.ShapeDtypeStruct((rows, depth), F32),
+        ],
+        compiler_params=pltpu.CompilerParams(vmem_limit_bytes=40 * 2**20),
+        cost_estimate=pl.CostEstimate(
+            flops=8 * rows * depth * 2 * wide, bytes_accessed=12 * rows * depth + 4 * depth * weight.shape[1],
+            transcendentals=0,
+        ),
+        name="proj_back",
+    )(values, own, other, query, out, grad, weight, before)
+
+
+def place_proj_kernel(quarter_ref, in_ref, qkv_ref, out_ref):
+    pieces = [in_ref[place ^ quarter_ref[0]].astype(F32) for place in range(QUARTERS)]
+    wide = pieces[0].shape[1] // 4
+    width = QUARTERS * wide
+    for column, part in ((0, 2), (1, 0), (2, 1)):
+        qkv_ref[:, column * width:(column + 1) * width] = jnp.concatenate(
+            [piece[:, part * wide:(part + 1) * wide] for piece in pieces], 1
+        )
+    out_ref[...] = jnp.concatenate([piece[:, 3 * wide:] for piece in pieces], 1)
+
+
+def place_mlp_kernel(quarter_ref, in_ref, down_ref, up_ref, *, shards):
+    pieces = [in_ref[place ^ quarter_ref[0]].astype(F32) for place in range(QUARTERS)]
+    rows, width = pieces[0].shape[0], pieces[0].shape[1] // 2
+    unit = width // shards
+    for place in range(QUARTERS):
+        down_ref[place * rows:(place + 1) * rows, :] = pieces[place][:, :width]
+    for shard in range(shards):
+        start = width + shard * unit
+        up_ref[:, shard * QUARTERS * unit:(shard + 1) * QUARTERS * unit] = jnp.concatenate(
+            [piece[:, start:start + unit] for piece in pieces], 1
+        )
+
+
+def placed_parts(kernel, quarter, pieces, shapes):
+    stacked = jnp.stack(pieces)
+    size = sum(math.prod(shape) for shape in shapes)
+    return pl.pallas_call(
+        kernel,
+        in_specs=[pl.BlockSpec(memory_space=pltpu.SMEM), pl.BlockSpec(memory_space=pltpu.VMEM)],
+        out_shape=[jax.ShapeDtypeStruct(shape, F32) for shape in shapes],
+        compiler_params=pltpu.CompilerParams(vmem_limit_bytes=32 * 2**20),
+        cost_estimate=pl.CostEstimate(flops=size, bytes_accessed=6 * size, transcendentals=0),
+        name="placed_parts",
+    )(quarter.reshape(1), stacked)
 
 
 def across(block, bit):
@@ -252,19 +393,21 @@
     rows = attn_in.shape[1]
     assert clips == 2 and lax.axis_size("section") == 2 and replicas % shards == 0 and replicas % QUARTERS == 0
 
-    inputs = jnp.where(first, transposed(edges_here[0], 0, 0), transposed(edges_here[1], 0, 1))
+    def by_layer(own, other):
+        return jnp.where(first, own, other), jnp.where(first, other, own)
+
+    vec_by_layer = by_layer(vectors[0], swap_sections(vectors[0]))
     mask_row = transposed(
         lax.dynamic_index_in_dim(key_mask, section, 0, keepdims=False).astype(F32)[None], None, None
     )[0]
+    inputs = after(edges_here, mask_row, *vec_by_layer)
+    inputs = jnp.where(first, transposed(inputs[0], 0, 0), transposed(inputs[1], 0, 1))
 
     def pick(block, axis):
         return lax.dynamic_index_in_dim(block, quarter, axis, keepdims=False)
 
     def gathered(block):
         return lax.all_gather(block, "shard", axis=0, tiled=True)
-
-    def by_layer(own, other):
-        return jnp.where(first, own, other), jnp.where(first, other, own)
 
     query_in, key_in, value_in = (
         pick(attn_in[0][:, i * width:(i + 1) * width].reshape(rows, QUARTERS, wide), 1) for i in range(3)
@@ -275,7 +418,6 @@
     own_up = pick(mlp_up[0].reshape(rows, shards, QUARTERS, unit), 2).reshape(rows, shards * unit)
     own_down = pick(mlp_down[0].reshape(QUARTERS, unit, width), 0)
     proj_zero, proj_one = by_layer(own_proj, swap_sections(own_proj))
-    vec_by_layer = by_layer(vectors[0], swap_sections(vectors[0]))
     proj_zero = gathered(proj_zero)
     own_up = gathered(after(own_up, proj_zero))
     own_down = gathered(after(own_down, own_up))
@@ -343,10 +485,9 @@
         result = middle + vec[7]
         for p in range(QUARTERS):
             bias = lax.dynamic_index_in_dim(bias_up, quarter ^ p, 1, keepdims=False).reshape(1, shards * unit)
-            act, slope = up_gelu(normed_two, w_up[p], bias)
+            act, slope, result = mlp_part(normed_two, w_up[p], bias, w_down[p], result)
             acts.append(act)
             slopes.append(slope)
-            result = result + dot(act, w_down[p])
         kept = (x, normed, own_qkv, other_kv, weights, inverses, attended, middle, normed_two, acts, slopes)
         return result.astype(BF16), kept
 
@@ -376,18 +517,17 @@
     def backward(cot, layer, kept, pending):
         proj, w_out, w_up, w_down, vec = layers[layer]
         x, normed, own_qkv, other_kv, weights, inverses, attended, middle, normed_two, acts, slopes = kept
+        order = (1, 3, 2, 0)
         d_mlp = cot.astype(BF16)
-        up_sums, d_ups = [], []
-        d_normed_two = None
-        for p in range(QUARTERS):
-            d_up = (dot(d_mlp, w_down[p], NT) * slopes[p].astype(F32)).astype(BF16)
-            part = dot(d_up, w_up[p], NT)
-            d_normed_two = part if d_normed_two is None else d_normed_two + part
-            d_ups.append(d_up)
-            up_sums.append(jnp.sum(d_up.astype(F32), 0))
-        near_down = [across(dot(acts[p], d_mlp, TN).astype(BF16), 1) for p in (1, 3)]
-        near_up = [across(dot(normed_two, d_ups[p], TN).astype(BF16), 1) for p in (1, 3)]
-        above = None
+        g_down, g_up, up_sums, near_down, near_up = {}, {}, {}, {}, {}
+        d_normed_two = jnp.zeros((frames, width), F32)
+        for p in order:
+            g_down[p], g_up[p], up_sums[p], d_normed_two = mlp_back_part(
+                d_mlp, normed_two, acts[p], slopes[p], w_up[p], w_down[p], d_normed_two
+            )
+            if p & 1:
+                near_down[p ^ 1] = across(g_down[p], 1)
+                near_up[p ^ 1] = across(g_up[p], 1)
         back, g_gain_two, g_shift_two = norm_back(middle, vec[5], d_normed_two)
         d_middle = cot + back
         d_attn = d_middle.astype(BF16)
@@ -395,65 +535,58 @@
         d_attended = dot(d_attn, w_out, NT).astype(BF16)
         d_heads = in_order([d_attended[:, p * wide:(p + 1) * wide] for p in range(QUARTERS)], quarter)
 
-        far_down = low_sum(dot(acts[2], d_mlp, TN), near_down[1])
-        far_down = across(far_down, 2)
-        results = []
-        for p in range(QUARTERS):
+        far_down = across(low_sum(g_down[2], near_down[2]), 2)
+        far_up = across(low_sum(g_up[2], near_up[2]), 2)
+        above = None
+        results = {}
+        for p in order:
             head = d_heads[p]
-            if p == 0:
-                head = after(head, *near_down)
-            elif p == 1:
-                head = after(head, *near_up)
-            elif pending is not None:
-                head = after(head, pending[p - 2][1])
-            results.append(attend_back(own_qkv[p], other_kv[p], weights[p], inverses[p], head, heads, frames))
-        d_normed, d_normed_own = None, None
-        d_boths, sums_in = [], []
-        for p in range(QUARTERS):
-            d_query = results[p][0]
-            d_both = low_sum(results[p][1], across(results[p ^ 1][2], 1))
-            d_boths.append(d_both)
-            part = dot(d_both, proj[p][:, :2 * wide], NT)
-            d_normed = part if d_normed is None else d_normed + part
-            part = dot(d_query, proj[p][:, 2 * wide:3 * wide], NT)
-            d_normed_own = part if d_normed_own is None else d_normed_own + part
-            sums_in.append((jnp.sum(d_query.astype(F32), 0), jnp.sum(d_both[:, wide:].astype(F32), 0)))
-
-        def g_proj(p):
-            return jnp.concatenate(
-                [
-                    dot(normed, d_boths[p], TN), dot(normed[:frames], results[p][0], TN),
-                    dot(attended, d_attn_parts[p], TN),
-                ],
-                1,
+            if p == 1:
+                head = after(head, *near_down.values())
+                if pending is not None:
+                    head = after(head, pending[1])
+            elif p == 3:
+                head = after(head, *near_up.values())
+            elif p == 2 and pending is not None:
+                make, far = pending[0]
+                above = half_sum(make(far))
+            results[p] = attend_back(own_qkv[p], other_kv[p], weights[p], inverses[p], head, heads, frames)
+        from_other = {p: across(results[p ^ 1][2], 1) for p in range(QUARTERS)}
+        g_proj, sums_in, near_proj = {}, {}, {}
+        d_normed = jnp.zeros(normed.shape, F32)
+        for p in order:
+            g_proj[p], sums_in[p], d_normed = proj_back(
+                normed, results[p][1], from_other[p], results[p][0], attended, d_attn_parts[p], proj[p], d_normed
             )
-
-        block = d_normed
-        if pending is not None:
-            halves = [half_sum(make(far)) for make, far in pending]
-            block = after(block, *halves)
-            above = scattered(jnp.concatenate(halves, 1))
+            if p & 1:
+                near_proj[p ^ 1] = across(g_proj[p], 1)
+        block = after(d_normed, far_down)
+        if above is not None:
+            block = after(block, above)
+            above = scattered(above)
         bit = shards // 2
         while bit >= 2:
             cut = block.shape[0] // 2
             block = block[:cut] + across(block[cut:].astype(BF16), bit).astype(F32)
             bit //= 2
-        near_proj = [across(g_proj(p).astype(BF16), 1) for p in (1, 3)]
-        far_up = low_sum(dot(after(normed_two, block), d_ups[2], TN), near_up[1])
-        far_up = across(far_up, 2)
-        block = after(block, far_down)
-        down_done = scattered(half_sum(low_sum(dot(acts[0], d_mlp, TN), near_down[0], far_down)))
-        far_proj = across(low_sum(g_proj(2), near_proj[1]), 2)
-        back, g_gain_one, g_shift_one = norm_back(x, vec[0], block + d_normed_own)
+        far_proj = across(low_sum(g_proj[2], near_proj[2]), 2)
+        mlp_half = jnp.concatenate(
+            [
+                half_sum(low_sum(g_down[0], near_down[0], far_down)),
+                half_sum(low_sum(g_up[0], near_up[0], far_up)),
+            ],
+            1,
+        )
+        mlp_done = scattered(mlp_half)
+        back, g_gain_one, g_shift_one = norm_back(x, vec[0], block)
         g_x = d_middle + back
-        sum_query = jnp.concatenate(in_order([s[0] for s in sums_in], quarter))
-        sum_value = jnp.concatenate(in_order([s[1] for s in sums_in], quarter))
-        sum_up = jnp.stack(in_order([s.reshape(shards, unit) for s in up_sums], quarter), 1).reshape(-1, width)
+        sums = [jnp.concatenate(in_order([sums_in[p][0, i * wide:(i + 1) * wide] for p in range(4)], quarter)) for i in range(3)]
+        sum_up = jnp.stack(in_order([up_sums[p].reshape(shards, unit) for p in range(4)], quarter), 1).reshape(-1, width)
         g_vec = jnp.concatenate(
             [
                 jnp.stack(
                     [
-                        g_gain_one, g_shift_one, sum_query, sum_value,
+                        g_gain_one, g_shift_one, sums[2], sums[1],
                         jnp.sum(d_attn.astype(F32), 0), g_gain_two, g_shift_two,
                         jnp.sum(d_mlp.astype(F32), 0),
                     ]
@@ -463,30 +596,35 @@
         )
 
         def finish_proj(other):
-            return low_sum(g_proj(0), near_proj[0], other)
-
-        def finish_up(other):
-            return low_sum(dot(normed_two, d_ups[0], TN), near_up[0], other)
-
-        return g_x, down_done, ((finish_up, far_up), (finish_proj, far_proj)), above, g_vec
+            return low_sum(g_proj[0], near_proj[0], other)
+
+        return g_x, mlp_done, ((finish_proj, far_proj), mlp_half), above, g_vec
 
     x_one, kept_zero = forward(inputs, 0)
     y_one, kept_one = forward(x_one, 1)
-    cot = jnp.where(first, transposed(edges_here[0], 1, 0), transposed(edges_here[1], 1, 1))
+    cot = after(edges_here, x_one)
+    cot = jnp.where(first, transposed(cot[0], 1, 0), transposed(cot[1], 1, 1))
     out_slots = [transposed(y_one, 0, 1), transposed(y_one, 1, 1)]
-    g_one, down_one, pending, _, vec_one = backward(cot.astype(F32), 1, kept_one, None)
-    g_zero, down_zero, pending, rest_one, vec_zero = backward(
+    g_one, mlp_one, pending, _, vec_one = backward(cot.astype(F32), 1, kept_one, None)
+    g_zero, mlp_zero, pending, proj_one, vec_zero = backward(
         g_one.astype(BF16).astype(F32), 0, kept_zero, pending
     )
     g_low = g_zero.astype(BF16)
     back_slots = [transposed(g_low, 0, 0), transposed(g_low, 1, 0)]
     edges_out = jnp.stack([jnp.where(first, b, o) for b, o in zip(back_slots, out_slots)])
-    vec_all = lax.psum(after(jnp.concatenate([vec_zero, vec_one]), rest_one, down_one), AXES)
-    rest_zero = jnp.concatenate([half_sum(make(far)) for make, far in pending], 1)
-    rest_zero = scattered(after(rest_zero, down_zero))
-    vec_all = jnp.where(first, vec_all[:12], vec_all[12:])
-    slice_width = width // shards
-    g_vectors = lax.dynamic_slice_in_dim(vec_all, lax.axis_index("shard") * slice_width, slice_width, 1)
+    vec_all = jnp.concatenate([vec_zero, vec_one])
+    bit = 1
+    while bit < replicas:
+        vec_all = vec_all + across(vec_all, bit)
+        bit *= 2
+    vec_all = vec_all + swap_sections(vec_all)
+    vec_all = jnp.pad(vec_all.T, ((0, 0), (0, 128 - vec_all.shape[0]))).astype(BF16)
+    make, far = pending[0]
+    rest = jnp.concatenate([half_sum(make(far)), vec_all], 1)
+    rest = lax.psum_scatter(after(rest, mlp_zero), "shard", scatter_dimension=0, tiled=True)
+    proj_zero = rest[:, :width // 2]
+    g_vectors = rest[:, width // 2:].astype(F32).T
+    g_vectors = jnp.where(first, g_vectors[:12], g_vectors[12:24])
 
     def finished(zero, one):
         own, other = jnp.where(first, zero, one), swap_sections(jnp.where(first, one, zero))
@@ -496,17 +634,15 @@
             a, b = own[:, start:start + cut], other[:, start:start + cut]
             parts += [jnp.where(first, a, b), jnp.where(first, b, a)]
         part = jnp.concatenate(parts, 1)
-        return in_order(spread(part, across(part, 2)), quarter)
-
-    f_down = jnp.stack(finished(down_zero, down_one)).astype(F32).reshape(-1, width)
-    f_rest = finished(rest_zero, rest_one)
-    f_up = jnp.stack([piece[:, :shards * unit].reshape(rows, shards, unit) for piece in f_rest], 2)
-    f_up = f_up.astype(F32).reshape(rows, hidden)
-    f_proj = [piece[:, shards * unit:] for piece in f_rest]
-    f_in = jnp.concatenate(
-        [piece[:, i * wide:(i + 1) * wide] for i in (2, 0, 1) for piece in f_proj], 1
-    ).astype(F32)
-    f_out = jnp.concatenate([piece[:, 3 * wide:] for piece in f_proj], 1).astype(F32)
+        return spread(part, across(part, 2))
+
+    f_down, f_up = placed_parts(
+        functools.partial(place_mlp_kernel, shards=shards), quarter, finished(mlp_zero, mlp_one),
+        [mlp_down.shape[1:], mlp_up.shape[1:]],
+    )
+    f_in, f_out = placed_parts(
+        place_proj_kernel, quarter, finished(proj_zero, proj_one), [attn_in.shape[1:], attn_out.shape[1:]]
+    )
     return edges_out[None], f_in[None], f_out[None], f_up[None], f_down[None], g_vectors[None]
 
 

time: 993 us -> 836 us (0.84)
  waiting for transfers between devices: 410 us -> 242 us
  matrix products: 162 us -> 17.6 us
  starting transfers between devices: 107 us -> 202 us
  Pallas kernels: 88.5 us -> 172 us
  local copies, waits for them, and re-layouts: 111 us -> 94.4 us
    dot_general x92 -> x12, matrix products: 162 us -> 17.6 us  [dot(): return lax.dot_general(a, b, dims, preferred_element_type=F32)]
    psum x1 -> x0, waiting for transfers between devices: 115 us -> none  [body(): lax.psum(after(jnp.concatenate([vec_zero, vec_one]), rest_one, down_one),...]
    pallas_call x8 -> x26, Pallas kernels: 16.5 us -> 97.1 us  [the longest x8 35.7 us: mlp_back_part(): pl.pallas_call(mlp_back_kernel, grid=(columns // tile,), in_specs=[whole,...]
    ppermute x62 -> x64, starting transfers between devices: 62.7 us -> 125 us  [across(): return lax.ppermute(block, 'replica', [(i, i ^ bit) for i in range(count)])]
    ppermute x12 -> x13, starting transfers between devices: 15 us -> 56.6 us  [swap_sections(): return lax.ppermute(block, 'section', [(0, 1), (1, 0)])]
    all_gather x4, waiting for transfers between devices: 59.8 us -> 29.3 us  [gathered(): return lax.all_gather(block, 'shard', axis=0, tiled=True)]
    reduce_scatter x4 -> x3, waiting for transfers between devices: 20.3 us -> 0.04 us  [scattered(): return lax.psum_scatter(block, 'shard', scatter_dimension=0, tiled=True)]
    another operation x32 -> x18, local copies, waits for them, and re-layouts: 24 us -> 7.37 us  [the longest x16 7.14 us: backward(): jnp.stack([g_gain_one, g_shift_one, sums[2], sums[1], jnp.sum(d_attn.asty...]
  transfers between devices with their start and end apart: 92 -> 94, of which waited for: 26 -> 26; matrix products, arithmetic and copies ran while one was open for 30% -> 16% of each run, Pallas kernels for 9% -> 21%
where the time goes in v3:
time: 836 us; the launch traced here: 826 us
  waiting for transfers between devices  242 us (29%)
  starting transfers between devices  202 us (24%)
  Pallas kernels  172 us (21%)
  local copies, waits for them, and re-layouts  94.4 us (11%)
  other arithmetic  80.9 us (10%)
  between operations  17.8 us (2%)
  matrix products  17.6 us (2%)
    ppermute x64, waiting for transfers between devices, across(): return lax.ppermute(block, 'replica', [(i, i ^ bit) for i in range(count)])  163 us
    ppermute x64, starting transfers between devices, across(): return lax.ppermute(block, 'replica', [(i, i ^ bit) for i in range(count)])  125 us
    ppermute x13, starting transfers between devices, swap_sections(): return lax.ppermute(block, 'section', [(0, 1), (1, 0)])  56.6 us
    unnamed x518, local copies, waits for them, and re-layouts  54.7 us
    pallas_call x8, Pallas kernels, attend_back(): pl.pallas_call(functools.partial(attend_back_kernel, heads=heads, frames=...  45.3 us
    ppermute x13, waiting for transfers between devices, swap_sections(): return lax.ppermute(block, 'section', [(0, 1), (1, 0)])  44.3 us
    pallas_call x8, Pallas kernels, mlp_back_part(): pl.pallas_call(mlp_back_kernel, grid=(columns // tile,), in_specs=[whole,...  35.7 us
    pallas_call x8, Pallas kernels, mlp_part(): pl.pallas_call(mlp_kernel, grid=(columns // tile,), in_specs=[whole, pl.B...  30.2 us
  transfers between devices with their start and end apart: 94, of which 26 were waited for; matrix products, arithmetic and copies ran while one was open for 16% of the time, Pallas kernels for 21%

profile of v3, /device:TPU:0, one launch (start us, length us, event | category | flops | bytes accessed | tf_op | source)
XLA Modules:
  0.0 826.0 jit_solution(7962234676137994172)
XLA Ops:
  15.1 7.0 collective-permute-done.4
  25.7 3.8 reshape_squeeze.10
  34.0 21.2 %all-gather.5.cloned.1.call-done.weight_ref = bf16[768,768]{1,0:T(8,128)(2,1)} async-done(((bf16[192,768]{1,0:T(8,128)(2,1)}), bf16[768,768]{1,0:T(8,128)(2,1)}) %all-gather.5.cloned.1.call-update) | async-done | bytes 1179664 | tf_op jit(solution)/shard_map/all_gather | solution.py:410
  68.8 51.7 %collective-permute-start.3 = (bf16[384,768]{1,0:T(8,128)(2,1)S(1)}, bf16[384,768]{1,0:T(8,128)(2,1)S(1)}, u32[]{:S(2)}, u32[]{:S(2)}) collective-permute-start(bf16[384,768]{1,0:T(8,128)(2,1)S(1)} %get-tuple-element.395), channel_id=1, source_target_pairs={{0,2},{1,3},{2,0},{3,1},{4,6},{5,7},{6,4},{7,5},{8,10},{9,11},{10,... | collective-permute-start | bytes 1769480 | tf_op jit(solution)/shard_map/ppermute | solution.py:333
  121.8 12.9 %collective-permute-done.3 = bf16[384,768]{1,0:T(8,128)(2,1)S(1)} collective-permute-done((bf16[384,768]{1,0:T(8,128)(2,1)S(1)}, bf16[384,768]{1,0:T(8,128)(2,1)S(1)}, u32[]{:S(2)}, u32[]{:S(2)}) %collective-permute-start.3) | collective-permute-done | bytes 589856 | tf_op jit(solution)/shard_map/ppermute | solution.py:333
  135.0 7.7 collective-permute-start.13
  143.8 7.4 collective-permute-done.5.weight_ref
  155.9 5.0 all-gather.9.cloned.1.call-done
  182.6 5.8 collective-permute-done.16
  193.6 4.4 attend.11
  200.0 4.5 attend.8
  227.5 4.2 mlp_part.8
  233.4 4.3 mlp_part.9
  239.5 4.3 mlp_part.10
  245.5 4.3 mlp_part.11
  254.4 29.4 %collective-permute-done.31.up_ref = bf16[768,768]{1,0:T(8,128)(2,1)S(1)} collective-permute-done((bf16[768,768]{1,0:T(8,128)(2,1)}, bf16[768,768]{1,0:T(8,128)(2,1)S(1)}, u32[]{:S(2)}, u32[]{:S(2)}) %collective-permute-start.31) | collective-permute-done | bytes 1179680 | tf_op jit(solution)/shard_map/ppermute | solution.py:333
  287.3 15.2 %collective-permute-done.23 = bf16[384,768]{1,0:T(8,128)(2,1)S(1)} collective-permute-done((bf16[384,768]{1,0:T(8,128)(2,1)S(1)}, bf16[384,768]{1,0:T(8,128)(2,1)S(1)}, u32[]{:S(2)}, u32[]{:S(2)}) %collective-permute-start.23) | collective-permute-done | bytes 589856 | tf_op jit(solution)/shard_map/ppermute | solution.py:333
  347.0 4.5 mlp_back_part.8
  359.4 4.5 mlp_back_part.9
  369.6 3.8 mlp_back_part.11
  379.0 5.4 attend_back.10
  400.0 4.6 attend_back.8
  406.6 5.8 attend_back.11
  420.7 5.4 attend_back.9
  448.9 21.2 %collective-permute-done.50 = bf16[768,768]{1,0:T(8,128)(2,1)} collective-permute-done((bf16[768,768]{1,0:T(8,128)(2,1)}, bf16[768,768]{1,0:T(8,128)(2,1)}, u32[]{:S(2)}, u32[]{:S(2)}) %collective-permute-start.50) | collective-permute-done | bytes 1179680 | tf_op jit(solution)/shard_map/ppermute | solution.py:333
  485.2 4.7 mlp_back_part.12
  490.1 4.7 mlp_back_part.13
  495.5 4.8 mlp_back_part.14
  501.0 5.0 mlp_back_part.15
  518.5 6.4 attend_back.12
  528.0 12.1 %collective-permute-done.76 = bf16[768,768]{1,0:T(8,128)(2,1)S(1)} collective-permute-done((bf16[768,768]{1,0:T(8,128)(2,1)S(1)}, bf16[768,768]{1,0:T(8,128)(2,1)S(1)}, u32[]{:S(2)}, u32[]{:S(2)}) %collective-permute-start.76) | collective-permute-done | bytes 1179680 | tf_op jit(solution)/shard_map/ppermute | solution.py:333
  545.6 19.9 %collective-permute-done.58 = bf16[768,768]{1,0:T(8,128)(2,1)S(1)} collective-permute-done((bf16[768,768]{1,0:T(8,128)(2,1)S(1)}, bf16[768,768]{1,0:T(8,128)(2,1)S(1)}, u32[]{:S(2)}, u32[]{:S(2)}) %collective-permute-start.58) | collective-permute-done | bytes 1179680 | tf_op jit(solution)/shard_map/ppermute | solution.py:333
  570.6 5.6 attend_back.14
  577.1 5.7 collective-permute-done.75
  594.8 5.4 attend_back.13
  600.2 3.6 proj_back.12
  605.4 6.7 attend_back.15
  612.2 4.3 proj_back.13
  628.9 8.0 collective-permute-done.62
  653.4 34.2 %collective-permute-done.63 = bf16[384,768]{1,0:T(8,128)(2,1)S(1)} collective-permute-done((bf16[384,768]{1,0:T(8,128)(2,1)S(1)}, bf16[384,768]{1,0:T(8,128)(2,1)S(1)}, u32[]{:S(2)}, u32[]{:S(2)}) %collective-permute-start.63) | collective-permute-done | bytes 589856 | tf_op jit(solution)/shard_map/ppermute | solution.py:333
  696.4 14.6 %collective-permute-start.71 = (bf16[768,384]{1,0:T(8,128)(2,1)S(1)}, bf16[768,384]{1,0:T(8,128)(2,1)S(1)}, u32[]{:S(2)}, u32[]{:S(2)}) collective-permute-start(bf16[768,384]{1,0:T(8,128)(2,1)S(1)} %broadcast_select_fusion.6), channel_id=1, source_target_pairs={{0,16},{16,0},{1,17},{17,1},{2,18},{18,2},{3,19},{19,3},{4,20},{20... | collective-permute-start | bytes 1769480 | tf_op jit(solution)/shard_map/ppermute | solution.py:337
  711.1 5.0 collective-permute-start.74
  716.0 13.0 %collective-permute-done.74 = f32[24,768]{0,1:T(8,128)S(1)} collective-permute-done((f32[24,768]{0,1:T(8,128)S(1)}, f32[24,768]{0,1:T(8,128)S(1)}, u32[]{:S(2)}, u32[]{:S(2)}) %collective-permute-start.74) | collective-permute-done | bytes 73760 | tf_op jit(solution)/shard_map/ppermute | solution.py:337
  741.1 8.1 collective-permute-start.65
  750.6 4.8 collective-permute-done.66
  755.6 11.1 %collective-permute-start.83 = (bf16[192,1536]{1,0:T(8,128)(2,1)}, bf16[192,1536]{1,0:T(8,128)(2,1)S(1)}, u32[]{:S(2)}, u32[]{:S(2)}) collective-permute-start(bf16[192,1536]{1,0:T(8,128)(2,1)} %get-tuple-element.430), channel_id=1, source_target_pairs={{0,1},{1,0},{2,3},{3,2},{4,5},{5,4},{6,7},{7,6},{8,9},{9,8},{10,11... | collective-permute-start | bytes 1769480 | tf_op jit(solution)/shard_map/ppermute | solution.py:333
  767.8 6.0 collective-permute-start.78
  779.9 30.8 %collective-permute-start.80 = (bf16[192,768]{1,0:T(8,128)(2,1)S(1)}, bf16[192,768]{1,0:T(8,128)(2,1)S(1)}, u32[]{:S(2)}, u32[]{:S(2)}) collective-permute-start(bf16[192,768]{1,0:T(8,128)(2,1)S(1)} %get-tuple-element.458), channel_id=1, source_target_pairs={{0,2},{1,3},{2,0},{3,1},{4,6},{5,7},{6,4},{7,5},{8,10},{9,11},{10,... | collective-permute-start | bytes 884744 | tf_op jit(solution)/shard_map/ppermute | solution.py:333
  (922 shorter events, 335.3 us)
Async XLA Ops:
  7.2 48.0 %all-gather.5.cloned.1.call-start = ((), (), s32[]{:S(2)}) async-start(), calls=%async_computation.4 | async-start | bytes 1474560 | tf_op jit(solution)/shard_map/all_gather | solution.py:410
  23.1 97.4 %all-gather.7.cloned.1.call-start = ((), (), s32[]{:S(2)}) async-start(), calls=%async_computation.5 | async-start | bytes 1474560 | tf_op jit(solution)/shard_map/all_gather | solution.py:410
  23.2 32.1 %collective-permute-start = (f32[12,768]{1,0:T(8,128)S(1)}, f32[12,768]{1,0:T(8,128)S(1)}, u32[]{:S(2)}, u32[]{:S(2)}) collective-permute-start(f32[12,768]{1,0:T(8,128)S(1)} %bitcast.105), channel_id=1, source_target_pairs={{0,16},{16,0},{1,17},{17,1},{2,18},{18,2},{3,19},{19,3},{4,20},{20... | collective-permute-start | bytes 110600 | tf_op jit(solution)/shard_map/ppermute | solution.py:337
  55.2 105.7 %all-gather.9.cloned.1.call-start = ((), (), s32[]{:S(2)}) async-start(), calls=%async_computation.6 | async-start | bytes 1474560 | tf_op jit(solution)/shard_map/all_gather | solution.py:410
  68.8 65.9 %collective-permute-start.3 = (bf16[384,768]{1,0:T(8,128)(2,1)S(1)}, bf16[384,768]{1,0:T(8,128)(2,1)S(1)}, u32[]{:S(2)}, u32[]{:S(2)}) collective-permute-start(bf16[384,768]{1,0:T(8,128)(2,1)S(1)} %get-tuple-element.395), channel_id=1, source_target_pairs={{0,2},{1,3},{2,0},{3,1},{4,6},{5,7},{6,4},{7,5},{8,10},{9,11},{10,... | collective-permute-start | bytes 1769480 | tf_op jit(solution)/shard_map/ppermute | solution.py:333
  120.5 103.3 %all-gather.11.cloned.1.call-start = ((), (), s32[]{:S(2)}) async-start(), calls=%async_computation.7 | async-start | bytes 1474560 | tf_op jit(solution)/shard_map/all_gather | solution.py:410
  121.1 30.1 %collective-permute-start.5 = (bf16[768,768]{1,0:T(8,128)(2,1)}, bf16[768,768]{1,0:T(8,128)(2,1)}, u32[]{:S(2)}, u32[]{:S(2)}) collective-permute-start(bf16[768,768]{1,0:T(8,128)(2,1)} %all-gather.5.cloned.1.call-done.weight_ref), channel_id=1, source_target_pairs={{0,2},{1,3},{2,0},{3,1},{4,6},{5,7},{6,4},{7,5},{8,10},{9,11},{10,... | collective-permute-start | bytes 3538952 | tf_op jit(solution)/shard_map/ppermute | solution.py:333
  169.9 30.0 %collective-permute-start.7 = (bf16[768,384]{1,0:T(8,128)(2,1)}, bf16[768,384]{1,0:T(8,128)(2,1)}, u32[]{:S(2)}, u32[]{:S(2)}) collective-permute-start(bf16[768,384]{1,0:T(8,128)(2,1)} %slice.435), channel_id=1, source_target_pairs={{0,1},{1,0},{2,3},{3,2},{4,5},{5,4},{6,7},{7,6},{8,9},{9,8},{10,11... | collective-permute-start | bytes 1769480 | tf_op jit(solution)/shard_map/ppermute | solution.py:333
  182.1 548.3 %reduce-scatter.5.cloned.1.call-start = ((), (), s32[]{:S(2)}) async-start(), calls=%async_computation.8 | async-start | bytes 1474560 | tf_op jit(solution)/shard_map/reduce_scatter | solution.py:510
  214.7 30.7 %collective-permute-start.15 = (bf16[768,768]{1,0:T(8,128)(2,1)}, bf16[768,768]{1,0:T(8,128)(2,1)}, u32[]{:S(2)}, u32[]{:S(2)}) collective-permute-start(bf16[768,768]{1,0:T(8,128)(2,1)} %collective-permute-done.14.up_ref), channel_id=1, source_target_pairs={{0,1},{1,0},{2,3},{3,2},{4,5},{5,4},{6,7},{7,6},{8,9},{9,8},{10,11... | collective-permute-start | bytes 3538952 | tf_op jit(solution)/shard_map/ppermute | solution.py:333
  223.8 29.8 %collective-permute-start.24 = (bf16[768,768]{1,0:T(8,128)(2,1)}, bf16[768,768]{1,0:T(8,128)(2,1)S(1)}, u32[]{:S(2)}, u32[]{:S(2)}) collective-permute-start(bf16[768,768]{1,0:T(8,128)(2,1)} %all-gather.11.cloned.1.call-done.weight_ref), channel_id=1, source_target_pairs={{0,2},{1,3},{2,0},{3,1},{4,6},{5,7},{6,4},{7,5},{8,10},{9,11},{10,... | collective-permute-start | bytes 3538952 | tf_op jit(solution)/shard_map/ppermute | solution.py:333
  225.3 58.4 %collective-permute-start.31 = (bf16[768,768]{1,0:T(8,128)(2,1)}, bf16[768,768]{1,0:T(8,128)(2,1)S(1)}, u32[]{:S(2)}, u32[]{:S(2)}) collective-permute-start(bf16[768,768]{1,0:T(8,128)(2,1)} %get-tuple-element.177.up_ref), channel_id=1, source_target_pairs={{0,2},{1,3},{2,0},{3,1},{4,6},{5,7},{6,4},{7,5},{8,10},{9,11},{10,... | collective-permute-start | bytes 3538952 | tf_op jit(solution)/shard_map/ppermute | solution.py:333
  233.4 72.9 %collective-permute-start.28 = (bf16[768,768]{1,0:T(8,128)(2,1)S(1)}, bf16[768,768]{1,0:T(8,128)(2,1)S(1)}, u32[]{:S(2)}, u32[]{:S(2)}) collective-permute-start(bf16[768,768]{1,0:T(8,128)(2,1)S(1)} %copy-done.13), channel_id=1, source_target_pairs={{0,1},{1,0},{2,3},{3,2},{4,5},{5,4},{6,7},{7,6},{8,9},{9,8},{10,11... | collective-permute-start | bytes 3538952 | tf_op jit(solution)/shard_map/ppermute | solution.py:333
  250.8 51.7 %collective-permute-start.23 = (bf16[384,768]{1,0:T(8,128)(2,1)S(1)}, bf16[384,768]{1,0:T(8,128)(2,1)S(1)}, u32[]{:S(2)}, u32[]{:S(2)}) collective-permute-start(bf16[384,768]{1,0:T(8,128)(2,1)S(1)} %get-tuple-element.397), channel_id=1, source_target_pairs={{0,2},{1,3},{2,0},{3,1},{4,6},{5,7},{6,4},{7,5},{8,10},{9,11},{10,... | collective-permute-start | bytes 1769480 | tf_op jit(solution)/shard_map/ppermute | solution.py:333
  252.4 55.7 %collective-permute-start.21 = (bf16[384,768]{1,0:T(8,128)(2,1)S(1)}, bf16[384,768]{1,0:T(8,128)(2,1)S(1)}, u32[]{:S(2)}, u32[]{:S(2)}) collective-permute-start(bf16[384,768]{1,0:T(8,128)(2,1)S(1)} %get-tuple-element.413), channel_id=1, source_target_pairs={{16,0},{17,4},{18,8},{19,12},{20,1},{21,5},{22,9},{23,13},{24,2},{... | collective-permute-start | bytes 1769480 | tf_op jit(solution)/shard_map/ppermute | solution.py:355
  253.7 54.5 %collective-permute-start.22 = (bf16[384,768]{1,0:T(8,128)(2,1)S(1)}, bf16[384,768]{1,0:T(8,128)(2,1)S(1)}, u32[]{:S(2)}, u32[]{:S(2)}) collective-permute-start(bf16[384,768]{1,0:T(8,128)(2,1)S(1)} %get-tuple-element.412), channel_id=1, source_target_pairs={{16,16},{17,20},{18,24},{19,28},{20,17},{21,21},{22,25},{23,29},{2... | collective-permute-start | bytes 1769480 | tf_op jit(solution)/shard_map/ppermute | solution.py:355
  283.8 42.3 %collective-permute-start.32 = (bf16[768,768]{1,0:T(8,128)(2,1)S(1)}, bf16[768,768]{1,0:T(8,128)(2,1)S(1)}, u32[]{:S(2)}, u32[]{:S(2)}) collective-permute-start(bf16[768,768]{1,0:T(8,128)(2,1)S(1)} %copy-done.9), channel_id=1, source_target_pairs={{0,2},{1,3},{2,0},{3,1},{4,6},{5,7},{6,4},{7,5},{8,10},{9,11},{10,... | collective-permute-start | bytes 3538952 | tf_op jit(solution)/shard_map/ppermute | solution.py:333
  312.4 31.3 %collective-permute-start.33 = (bf16[768,768]{1,0:T(8,128)(2,1)S(1)}, bf16[768,768]{1,0:T(8,128)(2,1)S(1)}, u32[]{:S(2)}, u32[]{:S(2)}) collective-permute-start(bf16[768,768]{1,0:T(8,128)(2,1)S(1)} %copy-done.8), channel_id=1, source_target_pairs={{0,1},{1,0},{2,3},{3,2},{4,5},{5,4},{6,7},{7,6},{8,9},{9,8},{10,11... | collective-permute-start | bytes 3538952 | tf_op jit(solution)/shard_map/ppermute | solution.py:333
  326.0 29.1 %collective-permute-start.36 = (bf16[768,768]{1,0:T(8,128)(2,1)S(1)}, bf16[768,768]{1,0:T(8,128)(2,1)S(1)}, u32[]{:S(2)}, u32[]{:S(2)}) collective-permute-start(bf16[768,768]{1,0:T(8,128)(2,1)S(1)} %collective-permute-done.32.down_ref), channel_id=1, source_target_pairs={{0,1},{1,0},{2,3},{3,2},{4,5},{5,4},{6,7},{7,6},{8,9},{9,8},{10,11... | collective-permute-start | bytes 3538952 | tf_op jit(solution)/shard_map/ppermute | solution.py:333
  351.5 54.5 %collective-permute-start.37 = (bf16[768,768]{1,0:T(8,128)(2,1)}, bf16[768,768]{1,0:T(8,128)(2,1)}, u32[]{:S(2)}, u32[]{:S(2)}) collective-permute-start(bf16[768,768]{1,0:T(8,128)(2,1)} %get-tuple-element.197), channel_id=1, source_target_pairs={{0,1},{1,0},{2,3},{3,2},{4,5},{5,4},{6,7},{7,6},{8,9},{9,8},{10,11... | collective-permute-start | bytes 3538952 | tf_op jit(solution)/shard_map/ppermute | solution.py:333
  351.5 55.0 %collective-permute-start.40 = (bf16[768,768]{1,0:T(8,128)(2,1)}, bf16[768,768]{1,0:T(8,128)(2,1)}, u32[]{:S(2)}, u32[]{:S(2)}) collective-permute-start(bf16[768,768]{1,0:T(8,128)(2,1)} %get-tuple-element.207), channel_id=1, source_target_pairs={{0,1},{1,0},{2,3},{3,2},{4,5},{5,4},{6,7},{7,6},{8,9},{9,8},{10,11... | collective-permute-start | bytes 3538952 | tf_op jit(solution)/shard_map/ppermute | solution.py:333
  377.2 29.3 %collective-permute-start.38 = (bf16[768,768]{1,0:T(8,128)(2,1)}, bf16[768,768]{1,0:T(8,128)(2,1)}, u32[]{:S(2)}, u32[]{:S(2)}) collective-permute-start(bf16[768,768]{1,0:T(8,128)(2,1)} %get-tuple-element.198), channel_id=1, source_target_pairs={{0,1},{1,0},{2,3},{3,2},{4,5},{5,4},{6,7},{7,6},{8,9},{9,8},{10,11... | collective-permute-start | bytes 3538952 | tf_op jit(solution)/shard_map/ppermute | solution.py:333
  377.3 29.2 %collective-permute-start.41 = (bf16[768,768]{1,0:T(8,128)(2,1)}, bf16[768,768]{1,0:T(8,128)(2,1)}, u32[]{:S(2)}, u32[]{:S(2)}) collective-permute-start(bf16[768,768]{1,0:T(8,128)(2,1)} %get-tuple-element.208), channel_id=1, source_target_pairs={{0,1},{1,0},{2,3},{3,2},{4,5},{5,4},{6,7},{7,6},{8,9},{9,8},{10,11... | collective-permute-start | bytes 3538952 | tf_op jit(solution)/shard_map/ppermute | solution.py:333
  385.9 49.7 %collective-permute-start.43 = (bf16[768,384]{1,0:T(8,128)(2,1)}, bf16[768,384]{1,0:T(8,128)(2,1)}, u32[]{:S(2)}, u32[]{:S(2)}) collective-permute-start(bf16[768,384]{1,0:T(8,128)(2,1)} %get-tuple-element.213), channel_id=1, source_target_pairs={{0,1},{1,0},{2,3},{3,2},{4,5},{5,4},{6,7},{7,6},{8,9},{9,8},{10,11... | collective-permute-start | bytes 1769480 | tf_op jit(solution)/shard_map/ppermute | solution.py:333
  415.3 31.5 %collective-permute-start.45 = (bf16[768,768]{1,0:T(8,128)(2,1)}, bf16[768,768]{1,0:T(8,128)(2,1)}, u32[]{:S(2)}, u32[]{:S(2)}) collective-permute-start(bf16[768,768]{1,0:T(8,128)(2,1)} %add_convert_fusion.11), channel_id=1, source_target_pairs={{0,2},{1,3},{2,0},{3,1},{4,6},{5,7},{6,4},{7,5},{8,10},{9,11},{10,... | collective-permute-start | bytes 3538952 | tf_op jit(solution)/shard_map/ppermute | solution.py:333
  420.6 49.6 %collective-permute-start.50 = (bf16[768,768]{1,0:T(8,128)(2,1)}, bf16[768,768]{1,0:T(8,128)(2,1)}, u32[]{:S(2)}, u32[]{:S(2)}) collective-permute-start(bf16[768,768]{1,0:T(8,128)(2,1)} %add_convert_fusion.9), channel_id=1, source_target_pairs={{0,2},{1,3},{2,0},{3,1},{4,6},{5,7},{6,4},{7,5},{8,10},{9,11},{10,... | collective-permute-start | bytes 3538952 | tf_op jit(solution)/shard_map/ppermute | solution.py:333
  439.1 40.0 %collective-permute-start.60 = (bf16[768,768]{1,0:T(8,128)(2,1)S(1)}, bf16[768,768]{1,0:T(8,128)(2,1)S(1)}, u32[]{:S(2)}, u32[]{:S(2)}) collective-permute-start(bf16[768,768]{1,0:T(8,128)(2,1)S(1)} %get-tuple-element.275), channel_id=1, source_target_pairs={{0,1},{1,0},{2,3},{3,2},{4,5},{5,4},{6,7},{7,6},{8,9},{9,8},{10,11... | collective-permute-start | bytes 3538952 | tf_op jit(solution)/shard_map/ppermute | solution.py:333
  439.6 148.6 %collective-permute-start.59 = (bf16[768,768]{1,0:T(8,128)(2,1)}, bf16[768,768]{1,0:T(8,128)(2,1)}, u32[]{:S(2)}, u32[]{:S(2)}) collective-permute-start(bf16[768,768]{1,0:T(8,128)(2,1)} %get-tuple-element.273), channel_id=1, source_target_pairs={{0,1},{1,0},{2,3},{3,2},{4,5},{5,4},{6,7},{7,6},{8,9},{9,8},{10,11... | collective-permute-start | bytes 3538952 | tf_op jit(solution)/shard_map/ppermute | solution.py:333
  446.9 35.5 %collective-permute-start.46 = (bf16[384,768]{1,0:T(8,128)(2,1)S(1)}, bf16[384,768]{1,0:T(8,128)(2,1)S(1)}, u32[]{:S(2)}, u32[]{:S(2)}) collective-permute-start(bf16[384,768]{1,0:T(8,128)(2,1)S(1)} %slice.1013), channel_id=1, source_target_pairs={{0,2},{1,3},{2,0},{3,1},{4,6},{5,7},{6,4},{7,5},{8,10},{9,11},{10,... | collective-permute-start | bytes 1769480 | tf_op jit(solution)/shard_map/ppermute | solution.py:333
  473.1 38.2 %collective-permute-start.51 = (bf16[768,384]{1,0:T(8,128)(2,1)}, bf16[768,384]{1,0:T(8,128)(2,1)}, u32[]{:S(2)}, u32[]{:S(2)}) collective-permute-start(bf16[768,384]{1,0:T(8,128)(2,1)} %broadcast_select_fusion.8), channel_id=1, source_target_pairs={{0,16},{16,0},{1,17},{17,1},{2,18},{18,2},{3,19},{19,3},{4,20},{20... | collective-permute-start | bytes 1769480 | tf_op jit(solution)/shard_map/ppermute | solution.py:337
  490.0 52.6 %collective-permute-start.47 = (bf16[768,768]{1,0:T(8,128)(2,1)S(1)}, bf16[768,768]{1,0:T(8,128)(2,1)}, u32[]{:S(2)}, u32[]{:S(2)}) collective-permute-start(bf16[768,768]{1,0:T(8,128)(2,1)S(1)} %get-tuple-element.241), channel_id=1, source_target_pairs={{0,1},{1,0},{2,3},{3,2},{4,5},{5,4},{6,7},{7,6},{8,9},{9,8},{10,11... | collective-permute-start | bytes 3538952 | tf_op jit(solution)/shard_map/ppermute | solution.py:333
  516.5 49.0 %collective-permute-start.58 = (bf16[768,768]{1,0:T(8,128)(2,1)S(1)}, bf16[768,768]{1,0:T(8,128)(2,1)S(1)}, u32[]{:S(2)}, u32[]{:S(2)}) collective-permute-start(bf16[768,768]{1,0:T(8,128)(2,1)S(1)} %add_convert_fusion.7), channel_id=1, source_target_pairs={{0,2},{1,3},{2,0},{3,1},{4,6},{5,7},{6,4},{7,5},{8,10},{9,11},{10,... | collective-permute-start | bytes 3538952 | tf_op jit(solution)/shard_map/ppermute | solution.py:333
  524.9 59.2 %collective-permute-start.49 = (bf16[768,384]{1,0:T(8,128)(2,1)}, bf16[768,384]{1,0:T(8,128)(2,1)}, u32[]{:S(2)}, u32[]{:S(2)}) collective-permute-start(bf16[768,384]{1,0:T(8,128)(2,1)} %broadcast_select_fusion.9), channel_id=1, source_target_pairs={{0,16},{16,0},{1,17},{17,1},{2,18},{18,2},{3,19},{19,3},{4,20},{20... | collective-permute-start | bytes 1769480 | tf_op jit(solution)/shard_map/ppermute | solution.py:337
  540.2 50.0 %collective-permute-start.61 = (bf16[768,768]{1,0:T(8,128)(2,1)}, bf16[768,768]{1,0:T(8,128)(2,1)}, u32[]{:S(2)}, u32[]{:S(2)}) collective-permute-start(bf16[768,768]{1,0:T(8,128)(2,1)} %add_convert_fusion.6), channel_id=1, source_target_pairs={{0,2},{1,3},{2,0},{3,1},{4,6},{5,7},{6,4},{7,5},{8,10},{9,11},{10,... | collective-permute-start | bytes 3538952 | tf_op jit(solution)/shard_map/ppermute | solution.py:333
  542.5 33.7 %collective-permute-start.77 = (bf16[768,384]{1,0:T(8,128)(2,1)S(1)}, bf16[768,384]{1,0:T(8,128)(2,1)S(1)}, u32[]{:S(2)}, u32[]{:S(2)}) collective-permute-start(bf16[768,384]{1,0:T(8,128)(2,1)S(1)} %broadcast_select_fusion.4), channel_id=1, source_target_pairs={{0,16},{16,0},{1,17},{17,1},{2,18},{18,2},{3,19},{19,3},{4,20},{20... | collective-permute-start | bytes 1769480 | tf_op jit(solution)/shard_map/ppermute | solution.py:337
  576.2 36.0 %collective-permute-start.56 = (bf16[768,384]{1,0:T(8,128)(2,1)}, bf16[768,384]{1,0:T(8,128)(2,1)}, u32[]{:S(2)}, u32[]{:S(2)}) collective-permute-start(bf16[768,384]{1,0:T(8,128)(2,1)} %get-tuple-element.261), channel_id=1, source_target_pairs={{0,1},{1,0},{2,3},{3,2},{4,5},{5,4},{6,7},{7,6},{8,9},{9,8},{10,11... | collective-permute-start | bytes 1769480 | tf_op jit(solution)/shard_map/ppermute | solution.py:333
  584.1 146.3 %reduce-scatter.11.cloned.1.call-start = ((), (), s32[]{:S(2)}) async-start(), calls=%async_computation.11 | async-start | bytes 1474560 | tf_op jit(solution)/shard_map/reduce_scatter | solution.py:510
  622.7 144.2 %reduce-scatter.9.cloned.1.call-start = ((), (), s32[]{:S(2)}) async-start(), calls=%async_computation.10 | async-start | bytes 737280 | tf_op jit(solution)/shard_map/reduce_scatter | solution.py:510
  628.7 65.6 %collective-permute-start.68 = (bf16[768,768]{1,0:T(8,128)(2,1)}, bf16[768,768]{1,0:T(8,128)(2,1)}, u32[]{:S(2)}, u32[]{:S(2)}) collective-permute-start(bf16[768,768]{1,0:T(8,128)(2,1)} %copy-done.106), channel_id=1, source_target_pairs={{0,1},{1,0},{2,3},{3,2},{4,5},{5,4},{6,7},{7,6},{8,9},{9,8},{10,11... | collective-permute-start | bytes 3538952 | tf_op jit(solution)/shard_map/ppermute | solution.py:333
  647.1 47.2 %collective-permute-start.70 = (bf16[768,768]{1,0:T(8,128)(2,1)}, bf16[768,768]{1,0:T(8,128)(2,1)}, u32[]{:S(2)}, u32[]{:S(2)}) collective-permute-start(bf16[768,768]{1,0:T(8,128)(2,1)} %add_convert_fusion.4), channel_id=1, source_target_pairs={{0,2},{1,3},{2,0},{3,1},{4,6},{5,7},{6,4},{7,5},{8,10},{9,11},{10,... | collective-permute-start | bytes 3538952 | tf_op jit(solution)/shard_map/ppermute | solution.py:333
  652.4 35.2 %collective-permute-start.63 = (bf16[384,768]{1,0:T(8,128)(2,1)S(1)}, bf16[384,768]{1,0:T(8,128)(2,1)S(1)}, u32[]{:S(2)}, u32[]{:S(2)}) collective-permute-start(bf16[384,768]{1,0:T(8,128)(2,1)S(1)} %slice.1012), channel_id=1, source_target_pairs={{0,2},{1,3},{2,0},{3,1},{4,6},{5,7},{6,4},{7,5},{8,10},{9,11},{10,... | collective-permute-start | bytes 1769480 | tf_op jit(solution)/shard_map/ppermute | solution.py:333
  689.9 60.8 %collective-permute-start.67 = (bf16[384,768]{1,0:T(8,128)(2,1)}, bf16[384,768]{1,0:T(8,128)(2,1)}, u32[]{:S(2)}, u32[]{:S(2)}) collective-permute-start(bf16[384,768]{1,0:T(8,128)(2,1)} %convert_element_type.353), channel_id=1, source_target_pairs={{16,16},{17,20},{18,24},{19,28},{20,17},{21,21},{22,25},{23,29},{2... | collective-permute-start | bytes 1769480 | tf_op jit(solution)/shard_map/ppermute | solution.py:355
  691.4 75.5 %reduce-scatter.7.cloned.1.call-start = ((), (), s32[]{:S(2)}) async-start(), calls=%async_computation.9 | async-start | bytes 983040 | tf_op jit(solution)/shard_map/reduce_scatter | solution.py:624
  696.4 32.7 %collective-permute-start.71 = (bf16[768,384]{1,0:T(8,128)(2,1)S(1)}, bf16[768,384]{1,0:T(8,128)(2,1)S(1)}, u32[]{:S(2)}, u32[]{:S(2)}) collective-permute-start(bf16[768,384]{1,0:T(8,128)(2,1)S(1)} %broadcast_select_fusion.6), channel_id=1, source_target_pairs={{0,16},{16,0},{1,17},{17,1},{2,18},{18,2},{3,19},{19,3},{4,20},{20... | collective-permute-start | bytes 1769480 | tf_op jit(solution)/shard_map/ppermute | solution.py:337
  741.1 32.7 %collective-permute-start.65 = (bf16[384,768]{1,0:T(8,128)(2,1)}, bf16[384,768]{1,0:T(8,128)(2,1)S(1)}, u32[]{:S(2)}, u32[]{:S(2)}) collective-permute-start(bf16[384,768]{1,0:T(8,128)(2,1)} %convert_element_type.353), channel_id=1, source_target_pairs={{0,16},{1,20},{2,24},{3,28},{4,17},{5,21},{6,25},{7,29},{8,18},{9,... | collective-permute-start | bytes 1769480 | tf_op jit(solution)/shard_map/ppermute | solution.py:355
  755.6 55.1 %collective-permute-start.83 = (bf16[192,1536]{1,0:T(8,128)(2,1)}, bf16[192,1536]{1,0:T(8,128)(2,1)S(1)}, u32[]{:S(2)}, u32[]{:S(2)}) collective-permute-start(bf16[192,1536]{1,0:T(8,128)(2,1)} %get-tuple-element.430), channel_id=1, source_target_pairs={{0,1},{1,0},{2,3},{3,2},{4,5},{5,4},{6,7},{7,6},{8,9},{9,8},{10,11... | collective-permute-start | bytes 1769480 | tf_op jit(solution)/shard_map/ppermute | solution.py:333
  766.7 43.9 %collective-permute-start.85 = (bf16[192,1536]{1,0:T(8,128)(2,1)S(1)}, bf16[192,1536]{1,0:T(8,128)(2,1)}, u32[]{:S(2)}, u32[]{:S(2)}) collective-permute-start(bf16[192,1536]{1,0:T(8,128)(2,1)S(1)} %collective-permute-done.84), channel_id=1, source_target_pairs={{0,1},{1,0},{2,3},{3,2},{4,5},{5,4},{6,7},{7,6},{8,9},{9,8},{10,11... | collective-permute-start | bytes 1769480 | tf_op jit(solution)/shard_map/ppermute | solution.py:333
  779.9 35.5 %collective-permute-start.80 = (bf16[192,768]{1,0:T(8,128)(2,1)S(1)}, bf16[192,768]{1,0:T(8,128)(2,1)S(1)}, u32[]{:S(2)}, u32[]{:S(2)}) collective-permute-start(bf16[192,768]{1,0:T(8,128)(2,1)S(1)} %get-tuple-element.458), channel_id=1, source_target_pairs={{0,2},{1,3},{2,0},{3,1},{4,6},{5,7},{6,4},{7,5},{8,10},{9,11},{10,... | collective-permute-start | bytes 884744 | tf_op jit(solution)/shard_map/ppermute | solution.py:333
  (302 other events, 3057.8 us)
Sparse Core Ops, SparseCore 0:
  23.2 31.9 all-gather.4
  57.3 58.5 all-gather.6
  120.7 40.2 all-gather.8
  182.2 41.6 all-gather.10
  584.2 39.0 reduce-scatter.4
  625.5 35.7 reduce-scatter.10
  691.5 35.8 reduce-scatter.8
  730.5 31.1 reduce-scatter.6

commit v4 on v3

--- a/solution.py
+++ b/solution.py
@@ -45,8 +45,8 @@
     wide = heads * dim
     sources = (own_ref, other_ref)
     chunks = key_chunks(sources, chunk)
-    outs = []
-    for head in range(heads):
+
+    def one_head(head):
         at = head * dim
         query = own_ref[0:frames, 2 * wide + at:2 * wide + at + dim] * (dim ** -0.5)
         lane = lax.broadcasted_iota(jnp.int32, (frames, dim), 1)
@@ -62,25 +62,40 @@
         total = None
         for source, start, row in chunks:
             weight = jnp.exp(score_ref[row:row + chunk, :] - top).astype(BF16)
-            exp_ref[head, row:row + chunk, :] = weight
+            exp_ref[0, row:row + chunk, :] = weight
             value = sources[source][start:start + chunk, wide + at:wide + at + dim]
             value = jnp.concatenate([value, jnp.ones_like(value)], 1)
             part = dot(value, weight, TN)
             total = part if total is None else total + part
         inverse = 1.0 / total[dim:dim + 1, :]
         inv_ref[head:head + 1, :] = inverse
-        outs.append((total[0:dim, :] * inverse).T)
-    out_ref[...] = jnp.concatenate(outs, 1).astype(BF16)
+        out_ref[:, at:at + dim] = (total[0:dim, :] * inverse).T.astype(BF16)
+
+    for head in range(heads):
+        pl.when(pl.program_id(0) == head)(functools.partial(one_head, head))
+
+
+def whole_block(shape):
+    return pl.BlockSpec(shape, lambda i: (0,) * len(shape))
+
+
+def chunk_size(own, frames):
+    chunk = min(256, frames)
+    return frames if own.shape[0] % chunk else chunk
 
 
 def attend(own, other, bias, heads, frames):
     keys = own.shape[0] + other.shape[0]
     wide = own.shape[1] // 3
-    chunk = min(256, frames)
-    if own.shape[0] % chunk:
-        chunk = frames
     return pl.pallas_call(
-        functools.partial(attend_kernel, heads=heads, frames=frames, chunk=chunk),
+        functools.partial(attend_kernel, heads=heads, frames=frames, chunk=chunk_size(own, frames)),
+        grid=(heads,),
+        in_specs=[whole_block(own.shape), whole_block(other.shape), whole_block(bias.shape)],
+        out_specs=[
+            whole_block((frames, wide)),
+            pl.BlockSpec((1, keys, frames), lambda i: (i, 0, 0)),
+            whole_block((heads, frames)),
+        ],
         out_shape=(
             jax.ShapeDtypeStruct((frames, wide), BF16),
             jax.ShapeDtypeStruct((heads, keys, frames), BF16),
@@ -100,10 +115,10 @@
     wide = heads * dim
     scale = dim ** -0.5
     sources = (own_ref, other_ref)
+    targets = (down_ref, dother_ref)
     chunks = key_chunks(sources, chunk)
-    dqs = []
-    dks, dvs = [[] for _ in chunks], [[] for _ in chunks]
-    for head in range(heads):
+
+    def one_head(head):
         at = head * dim
         query = (own_ref[0:frames, 2 * wide + at:2 * wide + at + dim] * scale).astype(BF16)
         inverse = inv_ref[head:head + 1, :]
@@ -111,43 +126,43 @@
         dout = dout_t.T.astype(BF16)
         dout_t = dout_t.astype(BF16)
         delta = None
-        for index, (source, start, row) in enumerate(chunks):
+        for source, start, row in chunks:
             value = sources[source][start:start + chunk, wide + at:wide + at + dim]
-            weight = exp_ref[head, row:row + chunk, :]
+            weight = exp_ref[0, row:row + chunk, :]
             prod = dot(value, dout_t) * weight.astype(F32)
             prod_ref[row:row + chunk, :] = prod
             part = jnp.sum(prod, 0, keepdims=True)
             delta = part if delta is None else delta + part
-            dvs[index].append(dot(weight, dout))
+            targets[source][start:start + chunk, wide + at:wide + at + dim] = dot(weight, dout).astype(BF16)
         delta = delta * inverse
         dq_t = None
-        for index, (source, start, row) in enumerate(chunks):
+        for source, start, row in chunks:
             key = sources[source][start:start + chunk, at:at + dim]
-            weight = exp_ref[head, row:row + chunk, :].astype(F32)
+            weight = exp_ref[0, row:row + chunk, :].astype(F32)
             ds = (prod_ref[row:row + chunk, :] - weight * delta).astype(BF16)
-            dks[index].append(dot(ds, query))
+            targets[source][start:start + chunk, at:at + dim] = dot(ds, query).astype(BF16)
             part = dot(key, ds, TN)
             dq_t = part if dq_t is None else dq_t + part
-        dqs.append(dq_t.T * scale)
-    dq_ref[...] = jnp.concatenate(dqs, 1).astype(BF16)
-    for index, (source, start, row) in enumerate(chunks):
-        target = down_ref if source == 0 else dother_ref
-        target[start:start + chunk, :] = jnp.concatenate(dks[index] + dvs[index], 1).astype(BF16)
+        dq_ref[:, at:at + dim] = (dq_t.T * scale).astype(BF16)
+
+    for head in range(heads):
+        pl.when(pl.program_id(0) == head)(functools.partial(one_head, head))
 
 
 def attend_back(own, other, weights, inverse, dout, heads, frames):
     keys = own.shape[0] + other.shape[0]
     wide = own.shape[1] // 3
-    chunk = min(256, frames)
-    if own.shape[0] % chunk:
-        chunk = frames
+    results = ((frames, wide), (own.shape[0], 2 * wide), (other.shape[0], 2 * wide))
     return pl.pallas_call(
-        functools.partial(attend_back_kernel, heads=heads, frames=frames, chunk=chunk),
-        out_shape=(
-            jax.ShapeDtypeStruct((frames, wide), BF16),
-            jax.ShapeDtypeStruct((own.shape[0], 2 * wide), BF16),
-            jax.ShapeDtypeStruct((other.shape[0], 2 * wide), BF16),
-        ),
+        functools.partial(attend_back_kernel, heads=heads, frames=frames, chunk=chunk_size(own, frames)),
+        grid=(heads,),
+        in_specs=[
+            whole_block(own.shape), whole_block(other.shape),
+            pl.BlockSpec((1, keys, frames), lambda i: (i, 0, 0)),
+            whole_block(inverse.shape), whole_block(dout.shape),
+        ],
+        out_specs=[whole_block(shape) for shape in results],
+        out_shape=[jax.ShapeDtypeStruct(shape, BF16) for shape in results],
         scratch_shapes=[pltpu.VMEM((keys, frames), F32)],
         compiler_params=pltpu.CompilerParams(vmem_limit_bytes=40 * 2**20),
         cost_estimate=pl.CostEstimate(
@@ -155,6 +170,80 @@
         ),
         name="attend_back",
     )(own, other, weights, inverse, dout)
+
+
+def out_kernel(quarter_ref, a_ref, b_ref, c_ref, d_ref, weight_ref, x_ref, vec_ref, att_ref, mid_ref, norm_ref):
+    parts = [ref[...] for ref in (a_ref, b_ref, c_ref, d_ref)]
+    attended = jnp.concatenate(in_order(parts, quarter_ref[0]), 1)
+    att_ref[...] = attended
+    middle = x_ref[...].astype(F32) + dot(attended, weight_ref[...]) + vec_ref[4:5, :]
+    mid_ref[...] = middle
+    norm_ref[...] = layer_norm(middle, vec_ref[5:6, :], vec_ref[6:7, :]).astype(BF16)
+
+
+def scalar_first(count):
+    return [pl.BlockSpec(memory_space=pltpu.SMEM)] + [pl.BlockSpec(memory_space=pltpu.VMEM)] * count
+
+
+def out_part(quarter, outs, weight, x_low, vec):
+    shape = x_low.shape
+    return pl.pallas_call(
+        out_kernel,
+        in_specs=scalar_first(7),
+        out_shape=[jax.ShapeDtypeStruct(shape, kind) for kind in (BF16, F32, BF16)],
+        compiler_params=pltpu.CompilerParams(vmem_limit_bytes=32 * 2**20),
+        cost_estimate=pl.CostEstimate(
+            flops=2 * math.prod(shape) * shape[1], bytes_accessed=14 * math.prod(shape), transcendentals=0
+        ),
+        name="out_part",
+    )(quarter.reshape(1), *outs, weight, x_low, vec)
+
+
+def norm_back(values, gain, grad):
+    center = values - jnp.mean(values, -1, keepdims=True)
+    inv = lax.rsqrt(jnp.mean(center * center, -1, keepdims=True) + EPS)
+    unit_values = center * inv
+    scaled = grad * gain
+    back = inv * (
+        scaled - jnp.mean(scaled, -1, keepdims=True)
+        - unit_values * jnp.mean(scaled * unit_values, -1, keepdims=True)
+    )
+    return back, jnp.sum(grad * unit_values, 0, keepdims=True), jnp.sum(grad, 0, keepdims=True)
+
+
+def middle_back_kernel(quarter_ref, grad_ref, mid_ref, cot_ref, vec_ref, weight_ref, dmid_ref, rows_ref, *part_refs):
+    cot = cot_ref[...].astype(F32)
+    back, gain, shift = norm_back(mid_ref[...], vec_ref[5:6, :], grad_ref[...])
+    d_middle = cot + back
+    dmid_ref[...] = d_middle
+    d_attn = d_middle.astype(BF16)
+    d_low = d_attn.astype(F32)
+    rows_ref[...] = jnp.concatenate(
+        [gain, shift, jnp.sum(d_low, 0, keepdims=True), jnp.sum(cot, 0, keepdims=True)], 0
+    )
+    d_attended = dot(d_attn, weight_ref[...], NT).astype(BF16)
+    for refs, whole in ((part_refs[:QUARTERS], d_attended), (part_refs[QUARTERS:], d_attn)):
+        wide = whole.shape[1] // QUARTERS
+        parts = in_order([whole[:, p * wide:(p + 1) * wide] for p in range(QUARTERS)], quarter_ref[0])
+        for ref, part in zip(refs, parts):
+            ref[...] = part
+
+
+def middle_back(quarter, grad, middle, cot, vec, weight):
+    frames, width = middle.shape
+    part = jax.ShapeDtypeStruct((frames, width // QUARTERS), BF16)
+    results = pl.pallas_call(
+        middle_back_kernel,
+        in_specs=scalar_first(5),
+        out_shape=[jax.ShapeDtypeStruct((frames, width), F32), jax.ShapeDtypeStruct((4, width), F32)]
+        + [part] * (2 * QUARTERS),
+        compiler_params=pltpu.CompilerParams(vmem_limit_bytes=32 * 2**20),
+        cost_estimate=pl.CostEstimate(
+            flops=2 * frames * width * width, bytes_accessed=18 * frames * width, transcendentals=0
+        ),
+        name="middle_back",
+    )(quarter.reshape(1), grad, middle, cot, vec, weight)
+    return results[0], results[1], results[2:2 + QUARTERS], results[2 + QUARTERS:]
 
 
 def column_tile(columns):
@@ -291,10 +380,13 @@
     )(values, own, other, query, out, grad, weight, before)
 
 
-def place_proj_kernel(quarter_ref, in_ref, qkv_ref, out_ref):
-    pieces = [in_ref[place ^ quarter_ref[0]].astype(F32) for place in range(QUARTERS)]
-    wide = pieces[0].shape[1] // 4
-    width = QUARTERS * wide
+def place_proj_kernel(quarter_ref, a_ref, b_ref, c_ref, d_ref, qkv_ref, out_ref, vec_ref):
+    pieces = [ref[...].astype(F32) for ref in (a_ref, b_ref, c_ref, d_ref)]
+    width = out_ref.shape[1]
+    wide = width // QUARTERS
+    total = pieces[0][:, width:] + pieces[1][:, width:] + pieces[2][:, width:] + pieces[3][:, width:]
+    vec_ref[...] = total.T
+    pieces = in_order([piece[:, :width] for piece in pieces], quarter_ref[0])
     for column, part in ((0, 2), (1, 0), (2, 1)):
         qkv_ref[:, column * width:(column + 1) * width] = jnp.concatenate(
             [piece[:, part * wide:(part + 1) * wide] for piece in pieces], 1
@@ -302,8 +394,8 @@
     out_ref[...] = jnp.concatenate([piece[:, 3 * wide:] for piece in pieces], 1)
 
 
-def place_mlp_kernel(quarter_ref, in_ref, down_ref, up_ref, *, shards):
-    pieces = [in_ref[place ^ quarter_ref[0]].astype(F32) for place in range(QUARTERS)]
+def place_mlp_kernel(quarter_ref, a_ref, b_ref, c_ref, d_ref, down_ref, up_ref, *, shards):
+    pieces = in_order([ref[...].astype(F32) for ref in (a_ref, b_ref, c_ref, d_ref)], quarter_ref[0])
     rows, width = pieces[0].shape[0], pieces[0].shape[1] // 2
     unit = width // shards
     for place in range(QUARTERS):
@@ -316,16 +408,15 @@
 
 
 def placed_parts(kernel, quarter, pieces, shapes):
-    stacked = jnp.stack(pieces)
     size = sum(math.prod(shape) for shape in shapes)
     return pl.pallas_call(
         kernel,
-        in_specs=[pl.BlockSpec(memory_space=pltpu.SMEM), pl.BlockSpec(memory_space=pltpu.VMEM)],
+        in_specs=scalar_first(QUARTERS),
         out_shape=[jax.ShapeDtypeStruct(shape, F32) for shape in shapes],
         compiler_params=pltpu.CompilerParams(vmem_limit_bytes=32 * 2**20),
         cost_estimate=pl.CostEstimate(flops=size, bytes_accessed=6 * size, transcendentals=0),
         name="placed_parts",
-    )(quarter.reshape(1), stacked)
+    )(quarter.reshape(1), *pieces)
 
 
 def across(block, bit):
@@ -335,6 +426,14 @@
 
 def swap_sections(block):
     return lax.ppermute(block, "section", [(0, 1), (1, 0)])
+
+
+def reversed_bits(index, count):
+    result, bit = index * 0, 1
+    while bit < count:
+        result = result * 2 + index // bit % 2
+        bit *= 2
+    return result
 
 
 def transposed(block, source, target):
@@ -347,7 +446,8 @@
     for shard in range(shards):
         for replica in range(replicas):
             group, place = divmod(replica, shards)
-            here, there = (shard, replica), (place, group * shards + shard)
+            here = (shard, replica)
+            there = (reversed_bits(place, shards), group * shards + reversed_bits(shard, shards))
             if source is None:
                 route += [(flat(s, *here), flat(s, *there)) for s in range(2)]
             else:
@@ -400,8 +500,7 @@
     mask_row = transposed(
         lax.dynamic_index_in_dim(key_mask, section, 0, keepdims=False).astype(F32)[None], None, None
     )[0]
-    inputs = after(edges_here, mask_row, *vec_by_layer)
-    inputs = jnp.where(first, transposed(inputs[0], 0, 0), transposed(inputs[1], 0, 1))
+    inputs = jnp.where(first, transposed(edges_here[0], 0, 0), transposed(edges_here[1], 0, 1))
 
     def pick(block, axis):
         return lax.dynamic_index_in_dim(block, quarter, axis, keepdims=False)
@@ -424,19 +523,14 @@
     proj_one = gathered(after(proj_one, own_down))
     up_zero, up_one = by_layer(own_up, swap_sections(own_up))
     down_zero, down_one = by_layer(own_down, swap_sections(own_down))
-    far = [across(proj_zero, 2)]
-    far.append(across(up_zero, 2))
-    far.append(across(after(down_zero, far[1]), 2))
-    far.append(across(after(proj_one, far[2]), 2))
-    far.append(across(after(up_one, far[2]), 2))
-    far.append(across(after(down_one, far[3], far[4]), 2))
-    blocks = (proj_zero, up_zero, down_zero, proj_one, up_one, down_one)
-    blocks = [spread(block, other) for block, other in zip(blocks, far)]
+    blocks = [proj_zero, up_zero, down_zero, proj_one, up_one]
+    blocks = [spread(block, across(block, 2)) for block in blocks]
+
     layers = []
     for layer in range(2):
-        proj, up, down = blocks[3 * layer:3 * layer + 3]
+        proj = blocks[3 * layer]
         w_out = jnp.concatenate(in_order([piece[:, 3 * wide:] for piece in proj], quarter), 1)
-        layers.append((proj, w_out, up, down, vec_by_layer[layer]))
+        layers.append([proj, w_out, blocks[3 * layer + 1], blocks[2], vec_by_layer[layer]])
 
     members = [0]
     bit = 2
@@ -446,7 +540,7 @@
     members = members + [m ^ 1 for m in members]
     place = replica % shards
     bias_row = jnp.concatenate(
-        [lax.dynamic_slice_in_dim(mask_row, (place ^ m) * frames, frames, 0) for m in members]
+        [lax.dynamic_slice_in_dim(mask_row, reversed_bits(place ^ m, shards) * frames, frames, 0) for m in members]
     )
     bias_row = jnp.where(bias_row > 0, 0.0, MASKED).astype(BF16)
     lane = jnp.arange(dim)[None, :]
@@ -460,8 +554,11 @@
         return block
 
     def forward(x_low, layer):
+        x_set = chips_rows(x_low)
+        if layer == 1:
+            down = after(down_one, x_set)
+            layers[1][3] = spread(down, across(down, 2))
         proj, w_out, w_up, w_down, vec = layers[layer]
-        x_set = chips_rows(x_low)
         normed = layer_norm(x_set.astype(F32), vec[0], vec[1]).astype(BF16)
         zeros = jnp.zeros((QUARTERS, wide), F32)
         bias_in = jnp.stack([zeros, vec[3].reshape(QUARTERS, wide), vec[2].reshape(QUARTERS, wide)], 1)
@@ -476,10 +573,7 @@
             outs.append(out)
             weights.append(weight)
             inverses.append(inverse)
-        attended = jnp.concatenate(in_order(outs, quarter), 1)
-        x = x_low.astype(F32)
-        middle = x + dot(attended, w_out) + vec[4]
-        normed_two = layer_norm(middle, vec[5], vec[6]).astype(BF16)
+        attended, middle, normed_two = out_part(quarter, outs, w_out, x_low, vec)
         bias_up = vec[8:].reshape(shards, QUARTERS, unit)
         acts, slopes = [], []
         result = middle + vec[7]
@@ -488,19 +582,8 @@
             act, slope, result = mlp_part(normed_two, w_up[p], bias, w_down[p], result)
             acts.append(act)
             slopes.append(slope)
-        kept = (x, normed, own_qkv, other_kv, weights, inverses, attended, middle, normed_two, acts, slopes)
+        kept = (x_low, normed, own_qkv, other_kv, weights, inverses, attended, middle, normed_two, acts, slopes)
         return result.astype(BF16), kept
-
-    def norm_back(values, gain, grad):
-        center = values - jnp.mean(values, -1, keepdims=True)
-        inv = lax.rsqrt(jnp.mean(center * center, -1, keepdims=True) + EPS)
-        unit_values = center * inv
-        scaled = grad * gain
-        back = inv * (
-            scaled - jnp.mean(scaled, -1, keepdims=True)
-            - unit_values * jnp.mean(scaled * unit_values, -1, keepdims=True)
-        )
-        return back, jnp.sum(grad * unit_values, 0), jnp.sum(grad, 0)
 
     def scattered(block):
         bit = QUARTERS
@@ -516,24 +599,18 @@
 
     def backward(cot, layer, kept, pending):
         proj, w_out, w_up, w_down, vec = layers[layer]
-        x, normed, own_qkv, other_kv, weights, inverses, attended, middle, normed_two, acts, slopes = kept
+        x_low, normed, own_qkv, other_kv, weights, inverses, attended, middle, normed_two, acts, slopes = kept
         order = (1, 3, 2, 0)
-        d_mlp = cot.astype(BF16)
         g_down, g_up, up_sums, near_down, near_up = {}, {}, {}, {}, {}
         d_normed_two = jnp.zeros((frames, width), F32)
         for p in order:
             g_down[p], g_up[p], up_sums[p], d_normed_two = mlp_back_part(
-                d_mlp, normed_two, acts[p], slopes[p], w_up[p], w_down[p], d_normed_two
+                cot, normed_two, acts[p], slopes[p], w_up[p], w_down[p], d_normed_two
             )
             if p & 1:
                 near_down[p ^ 1] = across(g_down[p], 1)
                 near_up[p ^ 1] = across(g_up[p], 1)
-        back, g_gain_two, g_shift_two = norm_back(middle, vec[5], d_normed_two)
-        d_middle = cot + back
-        d_attn = d_middle.astype(BF16)
-        d_attn_parts = in_order([d_attn[:, p * wide:(p + 1) * wide] for p in range(QUARTERS)], quarter)
-        d_attended = dot(d_attn, w_out, NT).astype(BF16)
-        d_heads = in_order([d_attended[:, p * wide:(p + 1) * wide] for p in range(QUARTERS)], quarter)
+        d_middle, mid_rows, d_heads, d_attn_parts = middle_back(quarter, d_normed_two, middle, cot, vec, w_out)
 
         far_down = across(low_sum(g_down[2], near_down[2]), 2)
         far_up = across(low_sum(g_up[2], near_up[2]), 2)
@@ -548,10 +625,19 @@
             elif p == 3:
                 head = after(head, *near_up.values())
             elif p == 2 and pending is not None:
-                make, far = pending[0]
+                make, far, vec_block = pending[0]
                 above = half_sum(make(far))
+                head = after(head, above)
+                above = jnp.concatenate([above, vec_block], 1)
+            elif p == 0:
+                head = after(head, far_down)
+                if pending is not None:
+                    head = after(head, pending[2])
             results[p] = attend_back(own_qkv[p], other_kv[p], weights[p], inverses[p], head, heads, frames)
         from_other = {p: across(results[p ^ 1][2], 1) for p in range(QUARTERS)}
+        half_down = half_sum(low_sum(g_down[0], near_down[0], far_down))
+        if above is not None:
+            above = scattered(above)
         g_proj, sums_in, near_proj = {}, {}, {}
         d_normed = jnp.zeros(normed.shape, F32)
         for p in order:
@@ -560,90 +646,84 @@
             )
             if p & 1:
                 near_proj[p ^ 1] = across(g_proj[p], 1)
-        block = after(d_normed, far_down)
+        block = after(d_normed, half_down, far_up)
         if above is not None:
             block = after(block, above)
-            above = scattered(above)
         bit = shards // 2
         while bit >= 2:
             cut = block.shape[0] // 2
             block = block[:cut] + across(block[cut:].astype(BF16), bit).astype(F32)
             bit //= 2
-        far_proj = across(low_sum(g_proj[2], near_proj[2]), 2)
-        mlp_half = jnp.concatenate(
-            [
-                half_sum(low_sum(g_down[0], near_down[0], far_down)),
-                half_sum(low_sum(g_up[0], near_up[0], far_up)),
-            ],
-            1,
-        )
-        mlp_done = scattered(mlp_half)
-        back, g_gain_one, g_shift_one = norm_back(x, vec[0], block)
-        g_x = d_middle + back
-        sums = [jnp.concatenate(in_order([sums_in[p][0, i * wide:(i + 1) * wide] for p in range(4)], quarter)) for i in range(3)]
-        sum_up = jnp.stack(in_order([up_sums[p].reshape(shards, unit) for p in range(4)], quarter), 1).reshape(-1, width)
+        half_up = half_sum(low_sum(g_up[0], near_up[0], far_up))
+        block = after(block, half_up)
+        mlp_done = scattered(jnp.concatenate([half_down, half_up], 1))
+        far_proj = low_sum(g_proj[2], near_proj[2])
+        if layer == 1:
+            far_proj = after(far_proj, block)
+        back, g_gain_one, g_shift_one = norm_back(x_low.astype(F32), vec[0], block)
+        g_low = (d_middle + back).astype(BF16)
+        if layer == 1:
+            g_low = after(g_low, far_proj)
+        far_proj = across(far_proj, 2)
+        sums = [
+            jnp.concatenate(in_order([sums_in[p][:, i * wide:(i + 1) * wide] for p in range(QUARTERS)], quarter), 1)
+            for i in range(1, 3)
+        ]
+        sum_up = jnp.stack(in_order([up_sums[p].reshape(shards, unit) for p in range(QUARTERS)], quarter), 1)
         g_vec = jnp.concatenate(
             [
-                jnp.stack(
-                    [
-                        g_gain_one, g_shift_one, sums[2], sums[1],
-                        jnp.sum(d_attn.astype(F32), 0), g_gain_two, g_shift_two,
-                        jnp.sum(d_mlp.astype(F32), 0),
-                    ]
-                ),
-                sum_up,
+                g_gain_one, g_shift_one, sums[1], sums[0], mid_rows[2:3], mid_rows[0:2], mid_rows[3:4],
+                sum_up.reshape(-1, width),
             ]
         )
+        vec_block = jnp.pad(g_vec.T.astype(BF16), ((0, 0), (0, 128 - g_vec.shape[0])))
 
         def finish_proj(other):
             return low_sum(g_proj[0], near_proj[0], other)
 
-        return g_x, mlp_done, ((finish_proj, far_proj), mlp_half), above, g_vec
+        return g_low, ((finish_proj, far_proj, vec_block), half_up, mlp_done), above
 
     x_one, kept_zero = forward(inputs, 0)
     y_one, kept_one = forward(x_one, 1)
     cot = after(edges_here, x_one)
     cot = jnp.where(first, transposed(cot[0], 1, 0), transposed(cot[1], 1, 1))
+    g_one, pending, _ = backward(cot, 1, kept_one, None)
+    mlp_one = pending[2]
+    g_zero, pending, proj_one = backward(g_one, 0, kept_zero, pending)
+    y_one = after(y_one, g_one)
     out_slots = [transposed(y_one, 0, 1), transposed(y_one, 1, 1)]
-    g_one, mlp_one, pending, _, vec_one = backward(cot.astype(F32), 1, kept_one, None)
-    g_zero, mlp_zero, pending, proj_one, vec_zero = backward(
-        g_one.astype(BF16).astype(F32), 0, kept_zero, pending
-    )
-    g_low = g_zero.astype(BF16)
-    back_slots = [transposed(g_low, 0, 0), transposed(g_low, 1, 0)]
+    back_slots = [transposed(g_zero, 0, 0), transposed(g_zero, 1, 0)]
     edges_out = jnp.stack([jnp.where(first, b, o) for b, o in zip(back_slots, out_slots)])
-    vec_all = jnp.concatenate([vec_zero, vec_one])
-    bit = 1
-    while bit < replicas:
-        vec_all = vec_all + across(vec_all, bit)
-        bit *= 2
-    vec_all = vec_all + swap_sections(vec_all)
-    vec_all = jnp.pad(vec_all.T, ((0, 0), (0, 128 - vec_all.shape[0]))).astype(BF16)
-    make, far = pending[0]
-    rest = jnp.concatenate([half_sum(make(far)), vec_all], 1)
-    rest = lax.psum_scatter(after(rest, mlp_zero), "shard", scatter_dimension=0, tiled=True)
-    proj_zero = rest[:, :width // 2]
-    g_vectors = rest[:, width // 2:].astype(F32).T
-    g_vectors = jnp.where(first, g_vectors[:12], g_vectors[12:24])
-
-    def finished(zero, one):
-        own, other = jnp.where(first, zero, one), swap_sections(jnp.where(first, one, zero))
+    (make, far, vec_block), _, mlp_zero = pending
+    proj_zero = scattered(jnp.concatenate([half_sum(make(far)), vec_block], 1))
+
+    def exchanged(zero, one):
+        return jnp.where(first, zero, one), swap_sections(jnp.where(first, one, zero))
+
+    def joined(own, other):
         cut = width // 2
         parts = []
         for start in range(0, own.shape[1], cut):
             a, b = own[:, start:start + cut], other[:, start:start + cut]
             parts += [jnp.where(first, a, b), jnp.where(first, b, a)]
-        part = jnp.concatenate(parts, 1)
-        return spread(part, across(part, 2))
-
+        return parts
+
+    part = jnp.concatenate(joined(*exchanged(mlp_zero, mlp_one)), 1)
     f_down, f_up = placed_parts(
-        functools.partial(place_mlp_kernel, shards=shards), quarter, finished(mlp_zero, mlp_one),
+        functools.partial(place_mlp_kernel, shards=shards), quarter, spread(part, across(part, 2)),
         [mlp_down.shape[1:], mlp_up.shape[1:]],
     )
-    f_in, f_out = placed_parts(
-        place_proj_kernel, quarter, finished(proj_zero, proj_one), [attn_in.shape[1:], attn_out.shape[1:]]
-    )
-    return edges_out[None], f_in[None], f_out[None], f_up[None], f_down[None], g_vectors[None]
+    own, other = exchanged(proj_zero, proj_one)
+    cut = width // 2
+    part = jnp.concatenate(
+        joined(own[:, :cut], other[:, :cut]) + [low_sum(own[:, cut:], other[:, cut:])], 1
+    )
+    f_in, f_out, f_vec = placed_parts(
+        place_proj_kernel, quarter, spread(part, across(part, 2)),
+        [attn_in.shape[1:], attn_out.shape[1:], (128, rows)],
+    )
+    f_vec = f_vec[:vectors.shape[1]]
+    return edges_out[None], f_in[None], f_out[None], f_up[None], f_down[None], f_vec[None]
 
 
 def solution(mesh):

time: 836 us -> 810 us (0.969)
  starting transfers between devices: 202 us -> 64.1 us
  waiting for transfers between devices: 242 us -> 339 us
  local copies, waits for them, and re-layouts: 94.4 us -> 118 us
  Pallas kernels: 172 us -> 193 us
  other arithmetic: 80.9 us -> 61.1 us
    ppermute x64 -> x62, starting transfers between devices: 125 us -> 35.9 us  [across(): return lax.ppermute(block, 'replica', [(i, i ^ bit) for i in range(count)])]
    all_gather x4, waiting for transfers between devices: 29.3 us -> 83 us  [gathered(): return lax.all_gather(block, 'shard', axis=0, tiled=True)]
    ppermute x13 -> x12, starting transfers between devices: 56.6 us -> 12.8 us  [swap_sections(): return lax.ppermute(block, 'section', [(0, 1), (1, 0)])]
    ppermute x13 -> x12, waiting for transfers between devices: 44.3 us -> 88.1 us  [swap_sections(): return lax.ppermute(block, 'section', [(0, 1), (1, 0)])]
    unnamed x518 -> x490, local copies, waits for them, and re-layouts: 54.7 us -> 85.9 us
    ppermute x64 -> x62, waiting for transfers between devices: 163 us -> 136 us  [across(): return lax.ppermute(block, 'replica', [(i, i ^ bit) for i in range(count)])]
    reduce_scatter x3 -> x4, waiting for transfers between devices: 0.04 us -> 16.6 us  [scattered(): return lax.psum_scatter(block, 'shard', scatter_dimension=0, tiled=True)]
    pallas_call x8, Pallas kernels: 29.3 us -> 43.5 us  [attend(): pl.pallas_call(functools.partial(attend_kernel, heads=heads, frames=frame...]
  transfers between devices with their start and end apart: 94 -> 91, of which waited for: 26 -> 28; matrix products, arithmetic and copies ran while one was open for 16% -> 13% of each run, Pallas kernels for 21% -> 22%
where the time goes in v4:
time: 810 us; the launch traced here: 806 us
  waiting for transfers between devices  339 us (42%)
  Pallas kernels  193 us (24%)
  local copies, waits for them, and re-layouts  118 us (15%)
  starting transfers between devices  64.1 us (8%)
  other arithmetic  61.1 us (8%)
  between operations  17.3 us (2%)
  matrix products  13.1 us (2%)
    ppermute x62, waiting for transfers between devices, across(): return lax.ppermute(block, 'replica', [(i, i ^ bit) for i in range(count)])  136 us
    ppermute x12, waiting for transfers between devices, swap_sections(): return lax.ppermute(block, 'section', [(0, 1), (1, 0)])  88.1 us
    unnamed x490, local copies, waits for them, and re-layouts  85.9 us
    all_gather x4, waiting for transfers between devices, gathered(): return lax.all_gather(block, 'shard', axis=0, tiled=True)  83 us
    pallas_call x8, Pallas kernels, attend_back(): pl.pallas_call(functools.partial(attend_back_kernel, heads=heads, frames=...  47.4 us
    pallas_call x8, Pallas kernels, attend(): pl.pallas_call(functools.partial(attend_kernel, heads=heads, frames=frame...  43.5 us
    pallas_call x8, Pallas kernels, mlp_back_part(): pl.pallas_call(mlp_back_kernel, grid=(columns // tile,), in_specs=[whole,...  36.5 us
    ppermute x62, starting transfers between devices, across(): return lax.ppermute(block, 'replica', [(i, i ^ bit) for i in range(count)])  35.9 us
  transfers between devices with their start and end apart: 91, of which 28 were waited for; matrix products, arithmetic and copies ran while one was open for 13% of the time, Pallas kernels for 22%

profile of v4, /device:TPU:0, one launch (start us, length us, event | category | flops | bytes accessed | tf_op | source)
XLA Modules:
  0.0 805.7 jit_solution(9002283818527764080)
XLA Ops:
  15.1 7.0 collective-permute-done.4
  26.0 4.2 dynamic-slice_reduce_fusion
  31.2 24.0 %all-gather.5.cloned.1.call-done.weight_ref = bf16[768,768]{1,0:T(8,128)(2,1)} async-done(((bf16[192,768]{1,0:T(8,128)(2,1)}), bf16[768,768]{1,0:T(8,128)(2,1)}) %all-gather.5.cloned.1.call-update) | async-done | bytes 1179664 | tf_op jit(solution)/shard_map/all_gather | solution.py:509
  62.7 50.0 %all-gather.7.cloned.1.call-done = bf16[768,768]{1,0:T(8,128)(2,1)} async-done(((bf16[192,768]{1,0:T(8,128)(2,1)}), bf16[768,768]{1,0:T(8,128)(2,1)}) %all-gather.7.cloned.1.call-update) | async-done | bytes 1179664 | tf_op jit(solution)/shard_map/all_gather | solution.py:509
  113.6 9.2 %collective-permute-start.2 = (bf16[384,768]{1,0:T(8,128)(2,1)S(1)}, bf16[384,768]{1,0:T(8,128)(2,1)S(1)}, u32[]{:S(2)}, u32[]{:S(2)}) collective-permute-start(bf16[384,768]{1,0:T(8,128)(2,1)S(1)} %get-tuple-element.433.x_ref), channel_id=1, source_target_pairs={{0,2},{1,3},{2,0},{3,1},{4,6},{5,7},{6,4},{7,5},{8,10},{9,11},{10,... | collective-permute-start | bytes 1769480 | tf_op jit(solution)/shard_map/ppermute | solution.py:424
  127.9 8.6 %collective-permute-done.2 = bf16[384,768]{1,0:T(8,128)(2,1)S(1)} collective-permute-done((bf16[384,768]{1,0:T(8,128)(2,1)S(1)}, bf16[384,768]{1,0:T(8,128)(2,1)S(1)}, u32[]{:S(2)}, u32[]{:S(2)}) %collective-permute-start.2) | collective-permute-done | bytes 589856 | tf_op jit(solution)/shard_map/ppermute | solution.py:424
  139.2 9.0 %all-gather.9.cloned.1.call-done = bf16[768,768]{1,0:T(8,128)(2,1)} async-done(((bf16[192,768]{1,0:T(8,128)(2,1)}), bf16[768,768]{1,0:T(8,128)(2,1)}) %all-gather.9.cloned.1.call-update) | async-done | bytes 1179664 | tf_op jit(solution)/shard_map/all_gather | solution.py:509
  156.0 5.0 collective-permute-done.13
  164.0 17.1 %collective-permute-done.16 = bf16[768,768]{1,0:T(8,128)(2,1)} collective-permute-done((bf16[768,768]{1,0:T(8,128)(2,1)}, bf16[768,768]{1,0:T(8,128)(2,1)}, u32[]{:S(2)}, u32[]{:S(2)}) %collective-permute-start.16) | collective-permute-done | bytes 1179680 | tf_op jit(solution)/shard_map/ppermute | solution.py:428
  190.9 5.1 attend.9
  206.5 6.4 collective-permute-done.17.down_ref
  226.5 14.3 %attend.10 = (bf16[384,192]{1,0:T(8,128)(2,1)S(1)}, bf16[3,1536,384]{2,1,0:T(8,128)(2,1)S(1)}, f32[3,384]{1,0:T(4,128)S(1)}) custom-call(bf16[768,576]{1,0:T(8,128)(2,1)S(1)} %copy-done.75, bf16[768,384]{1,0:T(8,128)(2,1)S(1)} %copy-done.130, bf16[1536,64]{1,0:T(8,128)(2,1)S(1)} %broadcast_select_fusion.28.bias_ref), custom_call_target="tpu_custom_call" | custom-call | flops 1811939328 | bytes 3538944 | tf_op jit(solution)/shard_map/attend/pallas_call | solution.py:90
  245.0 4.3 mlp_part.8
  251.0 4.3 mlp_part.9
  256.1 4.5 mlp_part.10
  262.3 4.5 mlp_part.11
  271.2 12.0 %collective-permute-done.23 = bf16[384,768]{1,0:T(8,128)(2,1)S(1)} collective-permute-done((bf16[384,768]{1,0:T(8,128)(2,1)S(1)}, bf16[384,768]{1,0:T(8,128)(2,1)S(1)}, u32[]{:S(2)}, u32[]{:S(2)}) %collective-permute-start.23) | collective-permute-done | bytes 589856 | tf_op jit(solution)/shard_map/ppermute | solution.py:424
  292.4 15.5 %collective-permute-done.21 = bf16[384,768]{1,0:T(8,128)(2,1)S(1)} collective-permute-done((bf16[384,768]{1,0:T(8,128)(2,1)S(1)}, bf16[384,768]{1,0:T(8,128)(2,1)S(1)}, u32[]{:S(2)}, u32[]{:S(2)}) %collective-permute-start.21) | collective-permute-done | bytes 589856 | tf_op jit(solution)/shard_map/ppermute | solution.py:455
  309.0 4.1 collective-permute-done.31.up_ref
  313.2 30.7 %collective-permute-done.32.down_ref = bf16[768,768]{1,0:T(8,128)(2,1)S(1)} collective-permute-done((bf16[768,768]{1,0:T(8,128)(2,1)S(1)}, bf16[768,768]{1,0:T(8,128)(2,1)S(1)}, u32[]{:S(2)}, u32[]{:S(2)}) %collective-permute-start.32) | collective-permute-done | bytes 1179680 | tf_op jit(solution)/shard_map/ppermute | solution.py:424
  364.6 5.0 attend.15
  387.9 4.5 mlp_back_part.8
  392.4 4.5 mlp_back_part.9
  417.9 5.9 attend_back.10
  438.8 4.9 attend_back.9
  447.9 6.6 attend_back.11
  454.8 8.2 %collective-permute-done.38 = bf16[768,768]{1,0:T(8,128)(2,1)S(1)} collective-permute-done((bf16[768,768]{1,0:T(8,128)(2,1)S(1)}, bf16[768,768]{1,0:T(8,128)(2,1)S(1)}, u32[]{:S(2)}, u32[]{:S(2)}) %collective-permute-start.38) | collective-permute-done | bytes 1179680 | tf_op jit(solution)/shard_map/ppermute | solution.py:424
  463.0 5.2 attend_back.8
  470.2 17.9 %collective-permute-done.47 = bf16[768,768]{1,0:T(8,128)(2,1)} collective-permute-done((bf16[768,768]{1,0:T(8,128)(2,1)S(1)}, bf16[768,768]{1,0:T(8,128)(2,1)}, u32[]{:S(2)}, u32[]{:S(2)}) %collective-permute-start.47) | collective-permute-done | bytes 1179680 | tf_op jit(solution)/shard_map/ppermute | solution.py:424
  511.0 4.8 collective-permute-done.49
  517.3 6.7 collective-permute-done.48
  531.0 5.0 mlp_back_part.12
  538.1 5.4 mlp_back_part.13
  552.3 4.8 mlp_back_part.14
  559.2 4.8 mlp_back_part.15
  579.0 7.2 attend_back.13
  594.2 9.5 %collective-permute-done.52 = bf16[768,768]{1,0:T(8,128)(2,1)S(1)} collective-permute-done((bf16[768,768]{1,0:T(8,128)(2,1)S(1)}, bf16[768,768]{1,0:T(8,128)(2,1)S(1)}, u32[]{:S(2)}, u32[]{:S(2)}) %collective-permute-start.52) | collective-permute-done | bytes 1179680 | tf_op jit(solution)/shard_map/ppermute | solution.py:424
  608.0 5.7 attend_back.12
  615.3 6.1 attend_back.14
  622.5 5.9 attend_back.15
  655.4 5.9 collective-permute-done.63
  661.5 11.5 %collective-permute-done.66 = bf16[768,384]{1,0:T(8,128)(2,1)S(1)} collective-permute-done((bf16[768,384]{1,0:T(8,128)(2,1)S(1)}, bf16[768,384]{1,0:T(8,128)(2,1)S(1)}, u32[]{:S(2)}, u32[]{:S(2)}) %collective-permute-start.66) | collective-permute-done | bytes 589856 | tf_op jit(solution)/shard_map/ppermute | solution.py:428
  692.3 9.7 %collective-permute-done.65 = bf16[384,768]{1,0:T(8,128)(2,1)S(1)} collective-permute-done((bf16[384,768]{1,0:T(8,128)(2,1)S(1)}, bf16[384,768]{1,0:T(8,128)(2,1)S(1)}, u32[]{:S(2)}, u32[]{:S(2)}) %collective-permute-start.65) | collective-permute-done | bytes 589856 | tf_op jit(solution)/shard_map/ppermute | solution.py:424
  720.8 18.4 %collective-permute-done.79 = bf16[192,768]{1,0:T(8,128)(2,1)S(1)} collective-permute-done((bf16[192,768]{1,0:T(8,128)(2,1)S(1)}, bf16[192,768]{1,0:T(8,128)(2,1)S(1)}, u32[]{:S(2)}, u32[]{:S(2)}) %collective-permute-start.79) | collective-permute-done | bytes 294944 | tf_op jit(solution)/shard_map/ppermute | solution.py:428
  739.3 16.5 %reduce-scatter.9.cloned.1.call-done = bf16[192,512]{1,0:T(8,128)(2,1)} async-done(((bf16[768,512]{1,0:T(8,128)(2,1)}), bf16[192,512]{1,0:T(8,128)(2,1)}) %reduce-scatter.9.cloned.1.call-update) | async-done | bytes 196624 | tf_op jit(solution)/shard_map/reduce_scatter | solution.py:593
  757.0 12.2 %collective-permute-done.75 = bf16[192,512]{1,0:T(8,128)(2,1)S(1)} collective-permute-done((bf16[192,512]{1,0:T(8,128)(2,1)S(1)}, bf16[192,512]{1,0:T(8,128)(2,1)S(1)}, u32[]{:S(2)}, u32[]{:S(2)}) %collective-permute-start.75) | collective-permute-done | bytes 196640 | tf_op jit(solution)/shard_map/ppermute | solution.py:428
  771.5 14.0 %collective-permute-done.81.c_ref = bf16[192,1536]{1,0:T(8,128)(2,1)S(1)} collective-permute-done((bf16[192,1536]{1,0:T(8,128)(2,1)S(1)}, bf16[192,1536]{1,0:T(8,128)(2,1)S(1)}, u32[]{:S(2)}, u32[]{:S(2)}) %collective-permute-start.81) | collective-permute-done | bytes 589856 | tf_op jit(solution)/shard_map/ppermute | solution.py:424
  786.1 6.0 collective-permute-done.77.c_ref
  (864 shorter events, 326.1 us)
Async XLA Ops:
  7.2 48.0 %all-gather.5.cloned.1.call-start = ((), (), s32[]{:S(2)}) async-start(), calls=%async_computation.4 | async-start | bytes 1474560 | tf_op jit(solution)/shard_map/all_gather | solution.py:509
  23.1 89.6 %all-gather.7.cloned.1.call-start = ((), (), s32[]{:S(2)}) async-start(), calls=%async_computation.5 | async-start | bytes 1474560 | tf_op jit(solution)/shard_map/all_gather | solution.py:509
  55.2 93.0 %all-gather.9.cloned.1.call-start = ((), (), s32[]{:S(2)}) async-start(), calls=%async_computation.6 | async-start | bytes 1474560 | tf_op jit(solution)/shard_map/all_gather | solution.py:509
  55.3 58.0 %collective-permute-start.3 = (f32[12,768]{1,0:T(8,128)S(1)}, f32[12,768]{1,0:T(8,128)S(1)}, u32[]{:S(2)}, u32[]{:S(2)}) collective-permute-start(f32[12,768]{1,0:T(8,128)S(1)} %bitcast.69), channel_id=1, source_target_pairs={{0,16},{16,0},{1,17},{17,1},{2,18},{18,2},{3,19},{19,3},{4,20},{20... | collective-permute-start | bytes 110600 | tf_op jit(solution)/shard_map/ppermute | solution.py:428
  57.9 55.4 %collective-permute-start = (bf16[384,768]{1,0:T(8,128)(2,1)}, bf16[384,768]{1,0:T(8,128)(2,1)S(1)}, u32[]{:S(2)}, u32[]{:S(2)}) collective-permute-start(bf16[384,768]{1,0:T(8,128)(2,1)} %get-tuple-element.451), channel_id=1, source_target_pairs={{0,0},{1,8},{2,4},{3,12},{4,2},{5,10},{6,6},{7,14},{8,1},{9,9},{10... | collective-permute-start | bytes 1769480 | tf_op jit(solution)/shard_map/ppermute | solution.py:455
  59.6 53.7 %collective-permute-start.1 = (bf16[384,768]{1,0:T(8,128)(2,1)}, bf16[384,768]{1,0:T(8,128)(2,1)S(1)}, u32[]{:S(2)}, u32[]{:S(2)}) collective-permute-start(bf16[384,768]{1,0:T(8,128)(2,1)} %get-tuple-element.450), channel_id=1, source_target_pairs={{0,16},{1,24},{2,20},{3,28},{4,18},{5,26},{6,22},{7,30},{8,17},{9,... | collective-permute-start | bytes 1769480 | tf_op jit(solution)/shard_map/ppermute | solution.py:455
  112.7 110.1 %all-gather.11.cloned.1.call-start = ((), (), s32[]{:S(2)}) async-start(), calls=%async_computation.7 | async-start | bytes 1474560 | tf_op jit(solution)/shard_map/all_gather | solution.py:509
  148.2 32.8 %collective-permute-start.16 = (bf16[768,768]{1,0:T(8,128)(2,1)}, bf16[768,768]{1,0:T(8,128)(2,1)}, u32[]{:S(2)}, u32[]{:S(2)}) collective-permute-start(bf16[768,768]{1,0:T(8,128)(2,1)} %all-gather.9.cloned.1.call-done), channel_id=1, source_target_pairs={{0,16},{16,0},{1,17},{17,1},{2,18},{18,2},{3,19},{19,3},{4,20},{20... | collective-permute-start | bytes 3538952 | tf_op jit(solution)/shard_map/ppermute | solution.py:428
  150.2 34.1 %collective-permute-start.5 = (bf16[768,768]{1,0:T(8,128)(2,1)S(1)}, bf16[768,768]{1,0:T(8,128)(2,1)}, u32[]{:S(2)}, u32[]{:S(2)}) collective-permute-start(bf16[768,768]{1,0:T(8,128)(2,1)S(1)} %copy-done.18), channel_id=1, source_target_pairs={{0,1},{1,0},{2,3},{3,2},{4,5},{5,4},{6,7},{7,6},{8,9},{9,8},{10,11... | collective-permute-start | bytes 3538952 | tf_op jit(solution)/shard_map/ppermute | solution.py:424
  153.8 36.6 %collective-permute-start.8 = (bf16[768,384]{1,0:T(8,128)(2,1)}, bf16[768,384]{1,0:T(8,128)(2,1)}, u32[]{:S(2)}, u32[]{:S(2)}) collective-permute-start(bf16[768,384]{1,0:T(8,128)(2,1)} %slice.382), channel_id=1, source_target_pairs={{0,1},{1,0},{2,3},{3,2},{4,5},{5,4},{6,7},{7,6},{8,9},{9,8},{10,11... | collective-permute-start | bytes 1769480 | tf_op jit(solution)/shard_map/ppermute | solution.py:424
  156.0 46.2 %collective-permute-start.10 = (bf16[768,768]{1,0:T(8,128)(2,1)}, bf16[768,768]{1,0:T(8,128)(2,1)}, u32[]{:S(2)}, u32[]{:S(2)}) collective-permute-start(bf16[768,768]{1,0:T(8,128)(2,1)} %collective-permute-done.9.weight_ref), channel_id=1, source_target_pairs={{0,1},{1,0},{2,3},{3,2},{4,5},{5,4},{6,7},{7,6},{8,9},{9,8},{10,11... | collective-permute-start | bytes 3538952 | tf_op jit(solution)/shard_map/ppermute | solution.py:424
  163.9 42.1 %collective-permute-start.14 = (bf16[768,768]{1,0:T(8,128)(2,1)}, bf16[768,768]{1,0:T(8,128)(2,1)}, u32[]{:S(2)}, u32[]{:S(2)}) collective-permute-start(bf16[768,768]{1,0:T(8,128)(2,1)} %get-tuple-element.447.up_ref), channel_id=1, source_target_pairs={{0,2},{1,3},{2,0},{3,1},{4,6},{5,7},{6,4},{7,5},{8,10},{9,11},{10,... | collective-permute-start | bytes 3538952 | tf_op jit(solution)/shard_map/ppermute | solution.py:424
  163.9 440.8 %reduce-scatter.5.cloned.1.call-start = ((), (), s32[]{:S(2)}) async-start(), calls=%async_computation.8 | async-start | bytes 1474560 | tf_op jit(solution)/shard_map/reduce_scatter | solution.py:593
  205.5 45.5 %collective-permute-start.19 = (bf16[768,768]{1,0:T(8,128)(2,1)}, bf16[768,768]{1,0:T(8,128)(2,1)}, u32[]{:S(2)}, u32[]{:S(2)}) collective-permute-start(bf16[768,768]{1,0:T(8,128)(2,1)} %get-tuple-element.447.up_ref), channel_id=1, source_target_pairs={{0,1},{1,0},{2,3},{3,2},{4,5},{5,4},{6,7},{7,6},{8,9},{9,8},{10,11... | collective-permute-start | bytes 3538952 | tf_op jit(solution)/shard_map/ppermute | solution.py:424
  205.9 56.4 %collective-permute-start.15 = (bf16[768,768]{1,0:T(8,128)(2,1)}, bf16[768,768]{1,0:T(8,128)(2,1)}, u32[]{:S(2)}, u32[]{:S(2)}) collective-permute-start(bf16[768,768]{1,0:T(8,128)(2,1)} %collective-permute-done.14.up_ref), channel_id=1, source_target_pairs={{0,1},{1,0},{2,3},{3,2},{4,5},{5,4},{6,7},{7,6},{8,9},{9,8},{10,11... | collective-permute-start | bytes 3538952 | tf_op jit(solution)/shard_map/ppermute | solution.py:424
  206.0 45.0 %collective-permute-start.20 = (bf16[768,768]{1,0:T(8,128)(2,1)}, bf16[768,768]{1,0:T(8,128)(2,1)}, u32[]{:S(2)}, u32[]{:S(2)}) collective-permute-start(bf16[768,768]{1,0:T(8,128)(2,1)} %get-tuple-element.445.down_ref), channel_id=1, source_target_pairs={{0,1},{1,0},{2,3},{3,2},{4,5},{5,4},{6,7},{7,6},{8,9},{9,8},{10,11... | collective-permute-start | bytes 3538952 | tf_op jit(solution)/shard_map/ppermute | solution.py:424
  212.8 49.5 %collective-permute-start.18 = (bf16[768,768]{1,0:T(8,128)(2,1)}, bf16[768,768]{1,0:T(8,128)(2,1)}, u32[]{:S(2)}, u32[]{:S(2)}) collective-permute-start(bf16[768,768]{1,0:T(8,128)(2,1)} %collective-permute-done.17.down_ref), channel_id=1, source_target_pairs={{0,1},{1,0},{2,3},{3,2},{4,5},{5,4},{6,7},{7,6},{8,9},{9,8},{10,11... | collective-permute-start | bytes 3538952 | tf_op jit(solution)/shard_map/ppermute | solution.py:424
  222.8 47.7 %collective-permute-start.27 = (bf16[768,768]{1,0:T(8,128)(2,1)}, bf16[768,768]{1,0:T(8,128)(2,1)S(1)}, u32[]{:S(2)}, u32[]{:S(2)}) collective-permute-start(bf16[768,768]{1,0:T(8,128)(2,1)} %all-gather.11.cloned.1.call-done.weight_ref), channel_id=1, source_target_pairs={{0,2},{1,3},{2,0},{3,1},{4,6},{5,7},{6,4},{7,5},{8,10},{9,11},{10,... | collective-permute-start | bytes 3538952 | tf_op jit(solution)/shard_map/ppermute | solution.py:424
  268.5 44.6 %collective-permute-start.31 = (bf16[768,768]{1,0:T(8,128)(2,1)S(1)}, bf16[768,768]{1,0:T(8,128)(2,1)S(1)}, u32[]{:S(2)}, u32[]{:S(2)}) collective-permute-start(bf16[768,768]{1,0:T(8,128)(2,1)S(1)} %copy-done.12), channel_id=1, source_target_pairs={{0,2},{1,3},{2,0},{3,1},{4,6},{5,7},{6,4},{7,5},{8,10},{9,11},{10,... | collective-permute-start | bytes 3538952 | tf_op jit(solution)/shard_map/ppermute | solution.py:424
  269.7 74.2 %collective-permute-start.32 = (bf16[768,768]{1,0:T(8,128)(2,1)S(1)}, bf16[768,768]{1,0:T(8,128)(2,1)S(1)}, u32[]{:S(2)}, u32[]{:S(2)}) collective-permute-start(bf16[768,768]{1,0:T(8,128)(2,1)S(1)} %copy-done.13), channel_id=1, source_target_pairs={{0,2},{1,3},{2,0},{3,1},{4,6},{5,7},{6,4},{7,5},{8,10},{9,11},{10,... | collective-permute-start | bytes 3538952 | tf_op jit(solution)/shard_map/ppermute | solution.py:424
  290.1 53.8 %collective-permute-start.25 = (bf16[768,384]{1,0:T(8,128)(2,1)S(1)}, bf16[768,384]{1,0:T(8,128)(2,1)S(1)}, u32[]{:S(2)}, u32[]{:S(2)}) collective-permute-start(bf16[768,384]{1,0:T(8,128)(2,1)S(1)} %slice.399), channel_id=1, source_target_pairs={{0,1},{1,0},{2,3},{3,2},{4,5},{5,4},{6,7},{7,6},{8,9},{9,8},{10,11... | collective-permute-start | bytes 1769480 | tf_op jit(solution)/shard_map/ppermute | solution.py:424
  307.9 37.1 %collective-permute-start.26 = (bf16[768,384]{1,0:T(8,128)(2,1)S(1)}, bf16[768,384]{1,0:T(8,128)(2,1)S(1)}, u32[]{:S(2)}, u32[]{:S(2)}) collective-permute-start(bf16[768,384]{1,0:T(8,128)(2,1)S(1)} %slice.400), channel_id=1, source_target_pairs={{0,1},{1,0},{2,3},{3,2},{4,5},{5,4},{6,7},{7,6},{8,9},{9,8},{10,11... | collective-permute-start | bytes 1769480 | tf_op jit(solution)/shard_map/ppermute | solution.py:424
  307.9 37.2 %collective-permute-start.29 = (bf16[768,384]{1,0:T(8,128)(2,1)S(1)}, bf16[768,384]{1,0:T(8,128)(2,1)S(1)}, u32[]{:S(2)}, u32[]{:S(2)}) collective-permute-start(bf16[768,384]{1,0:T(8,128)(2,1)S(1)} %slice.403), channel_id=1, source_target_pairs={{0,1},{1,0},{2,3},{3,2},{4,5},{5,4},{6,7},{7,6},{8,9},{9,8},{10,11... | collective-permute-start | bytes 1769480 | tf_op jit(solution)/shard_map/ppermute | solution.py:424
  313.2 64.0 %collective-permute-start.33 = (bf16[768,768]{1,0:T(8,128)(2,1)S(1)}, bf16[768,768]{1,0:T(8,128)(2,1)S(1)}, u32[]{:S(2)}, u32[]{:S(2)}) collective-permute-start(bf16[768,768]{1,0:T(8,128)(2,1)S(1)} %copy-done.12), channel_id=1, source_target_pairs={{0,1},{1,0},{2,3},{3,2},{4,5},{5,4},{6,7},{7,6},{8,9},{9,8},{10,11... | collective-permute-start | bytes 3538952 | tf_op jit(solution)/shard_map/ppermute | solution.py:424
  343.9 33.3 %collective-permute-start.34 = (bf16[768,768]{1,0:T(8,128)(2,1)S(1)}, bf16[768,768]{1,0:T(8,128)(2,1)S(1)}, u32[]{:S(2)}, u32[]{:S(2)}) collective-permute-start(bf16[768,768]{1,0:T(8,128)(2,1)S(1)} %copy-done.13), channel_id=1, source_target_pairs={{0,1},{1,0},{2,3},{3,2},{4,5},{5,4},{6,7},{7,6},{8,9},{9,8},{10,11... | collective-permute-start | bytes 3538952 | tf_op jit(solution)/shard_map/ppermute | solution.py:424
  345.0 38.6 %collective-permute-start.35 = (bf16[768,768]{1,0:T(8,128)(2,1)S(1)}, bf16[768,768]{1,0:T(8,128)(2,1)S(1)}, u32[]{:S(2)}, u32[]{:S(2)}) collective-permute-start(bf16[768,768]{1,0:T(8,128)(2,1)S(1)} %collective-permute-done.31.up_ref), channel_id=1, source_target_pairs={{0,1},{1,0},{2,3},{3,2},{4,5},{5,4},{6,7},{7,6},{8,9},{9,8},{10,11... | collective-permute-start | bytes 3538952 | tf_op jit(solution)/shard_map/ppermute | solution.py:424
  346.0 37.6 %collective-permute-start.36 = (bf16[768,768]{1,0:T(8,128)(2,1)S(1)}, bf16[768,768]{1,0:T(8,128)(2,1)S(1)}, u32[]{:S(2)}, u32[]{:S(2)}) collective-permute-start(bf16[768,768]{1,0:T(8,128)(2,1)S(1)} %collective-permute-done.32.down_ref), channel_id=1, source_target_pairs={{0,1},{1,0},{2,3},{3,2},{4,5},{5,4},{6,7},{7,6},{8,9},{9,8},{10,11... | collective-permute-start | bytes 3538952 | tf_op jit(solution)/shard_map/ppermute | solution.py:424
  396.9 34.7 %collective-permute-start.37 = (bf16[768,768]{1,0:T(8,128)(2,1)}, bf16[768,768]{1,0:T(8,128)(2,1)}, u32[]{:S(2)}, u32[]{:S(2)}) collective-permute-start(bf16[768,768]{1,0:T(8,128)(2,1)} %get-tuple-element.228), channel_id=1, source_target_pairs={{0,1},{1,0},{2,3},{3,2},{4,5},{5,4},{6,7},{7,6},{8,9},{9,8},{10,11... | collective-permute-start | bytes 3538952 | tf_op jit(solution)/shard_map/ppermute | solution.py:424
  397.9 38.9 %collective-permute-start.39 = (bf16[768,768]{1,0:T(8,128)(2,1)}, bf16[768,768]{1,0:T(8,128)(2,1)}, u32[]{:S(2)}, u32[]{:S(2)}) collective-permute-start(bf16[768,768]{1,0:T(8,128)(2,1)} %get-tuple-element.234), channel_id=1, source_target_pairs={{0,1},{1,0},{2,3},{3,2},{4,5},{5,4},{6,7},{7,6},{8,9},{9,8},{10,11... | collective-permute-start | bytes 3538952 | tf_op jit(solution)/shard_map/ppermute | solution.py:424
  398.3 45.6 %collective-permute-start.41 = (bf16[768,768]{1,0:T(8,128)(2,1)}, bf16[768,768]{1,0:T(8,128)(2,1)}, u32[]{:S(2)}, u32[]{:S(2)}) collective-permute-start(bf16[768,768]{1,0:T(8,128)(2,1)} %get-tuple-element.247), channel_id=1, source_target_pairs={{0,1},{1,0},{2,3},{3,2},{4,5},{5,4},{6,7},{7,6},{8,9},{9,8},{10,11... | collective-permute-start | bytes 3538952 | tf_op jit(solution)/shard_map/ppermute | solution.py:424
  398.4 45.5 %collective-permute-start.42 = (bf16[768,768]{1,0:T(8,128)(2,1)}, bf16[768,768]{1,0:T(8,128)(2,1)}, u32[]{:S(2)}, u32[]{:S(2)}) collective-permute-start(bf16[768,768]{1,0:T(8,128)(2,1)} %get-tuple-element.248), channel_id=1, source_target_pairs={{0,1},{1,0},{2,3},{3,2},{4,5},{5,4},{6,7},{7,6},{8,9},{9,8},{10,11... | collective-permute-start | bytes 3538952 | tf_op jit(solution)/shard_map/ppermute | solution.py:424
  425.4 71.3 %collective-permute-start.44 = (bf16[768,384]{1,0:T(8,128)(2,1)}, bf16[768,384]{1,0:T(8,128)(2,1)}, u32[]{:S(2)}, u32[]{:S(2)}) collective-permute-start(bf16[768,384]{1,0:T(8,128)(2,1)} %get-tuple-element.254), channel_id=1, source_target_pairs={{0,1},{1,0},{2,3},{3,2},{4,5},{5,4},{6,7},{7,6},{8,9},{9,8},{10,11... | collective-permute-start | bytes 1769480 | tf_op jit(solution)/shard_map/ppermute | solution.py:424
  443.7 60.2 %collective-permute-start.40 = (bf16[768,384]{1,0:T(8,128)(2,1)S(1)}, bf16[768,384]{1,0:T(8,128)(2,1)S(1)}, u32[]{:S(2)}, u32[]{:S(2)}) collective-permute-start(bf16[768,384]{1,0:T(8,128)(2,1)S(1)} %get-tuple-element.236), channel_id=1, source_target_pairs={{0,1},{1,0},{2,3},{3,2},{4,5},{5,4},{6,7},{7,6},{8,9},{9,8},{10,11... | collective-permute-start | bytes 1769480 | tf_op jit(solution)/shard_map/ppermute | solution.py:424
  445.5 42.5 %collective-permute-start.47 = (bf16[768,768]{1,0:T(8,128)(2,1)S(1)}, bf16[768,768]{1,0:T(8,128)(2,1)}, u32[]{:S(2)}, u32[]{:S(2)}) collective-permute-start(bf16[768,768]{1,0:T(8,128)(2,1)S(1)} %add_convert_fusion.9), channel_id=1, source_target_pairs={{0,2},{1,3},{2,0},{3,1},{4,6},{5,7},{6,4},{7,5},{8,10},{9,11},{10,... | collective-permute-start | bytes 3538952 | tf_op jit(solution)/shard_map/ppermute | solution.py:424
  454.5 46.2 %collective-permute-start.43 = (bf16[768,384]{1,0:T(8,128)(2,1)S(1)}, bf16[768,384]{1,0:T(8,128)(2,1)S(1)}, u32[]{:S(2)}, u32[]{:S(2)}) collective-permute-start(bf16[768,384]{1,0:T(8,128)(2,1)S(1)} %get-tuple-element.250), channel_id=1, source_target_pairs={{0,1},{1,0},{2,3},{3,2},{4,5},{5,4},{6,7},{7,6},{8,9},{9,8},{10,11... | collective-permute-start | bytes 1769480 | tf_op jit(solution)/shard_map/ppermute | solution.py:424
  517.1 168.9 %reduce-scatter.7.cloned.1.call-start = ((), (), s32[]{:S(2)}) async-start(), calls=%async_computation.9 | async-start | bytes 983040 | tf_op jit(solution)/shard_map/reduce_scatter | solution.py:593
  517.2 57.7 %collective-permute-start.55 = (bf16[768,768]{1,0:T(8,128)(2,1)}, bf16[768,768]{1,0:T(8,128)(2,1)}, u32[]{:S(2)}, u32[]{:S(2)}) collective-permute-start(bf16[768,768]{1,0:T(8,128)(2,1)} %get-tuple-element.309), channel_id=1, source_target_pairs={{0,1},{1,0},{2,3},{3,2},{4,5},{5,4},{6,7},{7,6},{8,9},{9,8},{10,11... | collective-permute-start | bytes 3538952 | tf_op jit(solution)/shard_map/ppermute | solution.py:424
  548.6 37.6 %collective-permute-start.58 = (bf16[768,768]{1,0:T(8,128)(2,1)}, bf16[768,768]{1,0:T(8,128)(2,1)}, u32[]{:S(2)}, u32[]{:S(2)}) collective-permute-start(bf16[768,768]{1,0:T(8,128)(2,1)} %copy-done.122), channel_id=1, source_target_pairs={{0,1},{1,0},{2,3},{3,2},{4,5},{5,4},{6,7},{7,6},{8,9},{9,8},{10,11... | collective-permute-start | bytes 3538952 | tf_op jit(solution)/shard_map/ppermute | solution.py:424
  586.2 88.5 %collective-permute-start.54 = (bf16[768,384]{1,0:T(8,128)(2,1)}, bf16[768,384]{1,0:T(8,128)(2,1)}, u32[]{:S(2)}, u32[]{:S(2)}) collective-permute-start(bf16[768,384]{1,0:T(8,128)(2,1)} %get-tuple-element.301), channel_id=1, source_target_pairs={{0,1},{1,0},{2,3},{3,2},{4,5},{5,4},{6,7},{7,6},{8,9},{9,8},{10,11... | collective-permute-start | bytes 1769480 | tf_op jit(solution)/shard_map/ppermute | solution.py:424
  587.5 58.6 %collective-permute-start.64 = (bf16[768,768]{1,0:T(8,128)(2,1)}, bf16[768,768]{1,0:T(8,128)(2,1)}, u32[]{:S(2)}, u32[]{:S(2)}) collective-permute-start(bf16[768,768]{1,0:T(8,128)(2,1)} %add_convert_fusion.3), channel_id=1, source_target_pairs={{0,2},{1,3},{2,0},{3,1},{4,6},{5,7},{6,4},{7,5},{8,10},{9,11},{10,... | collective-permute-start | bytes 3538952 | tf_op jit(solution)/shard_map/ppermute | solution.py:424
  631.0 84.2 %reduce-scatter.11.cloned.1.call-start = ((), (), s32[]{:S(2)}) async-start(), calls=%async_computation.11 | async-start | bytes 1474560 | tf_op jit(solution)/shard_map/reduce_scatter | solution.py:593
  649.5 38.5 %collective-permute-start.71 = (bf16[768,768]{1,0:T(8,128)(2,1)}, bf16[768,768]{1,0:T(8,128)(2,1)}, u32[]{:S(2)}, u32[]{:S(2)}) collective-permute-start(bf16[768,768]{1,0:T(8,128)(2,1)} %get-tuple-element.351), channel_id=1, source_target_pairs={{0,1},{1,0},{2,3},{3,2},{4,5},{5,4},{6,7},{7,6},{8,9},{9,8},{10,11... | collective-permute-start | bytes 3538952 | tf_op jit(solution)/shard_map/ppermute | solution.py:424
  654.8 33.2 %collective-permute-start.73 = (bf16[768,768]{1,0:T(8,128)(2,1)}, bf16[768,768]{1,0:T(8,128)(2,1)}, u32[]{:S(2)}, u32[]{:S(2)}) collective-permute-start(bf16[768,768]{1,0:T(8,128)(2,1)} %add_convert_fusion.1), channel_id=1, source_target_pairs={{0,2},{1,3},{2,0},{3,1},{4,6},{5,7},{6,4},{7,5},{8,10},{9,11},{10,... | collective-permute-start | bytes 3538952 | tf_op jit(solution)/shard_map/ppermute | solution.py:424
  674.4 81.5 %reduce-scatter.9.cloned.1.call-start = ((), (), s32[]{:S(2)}) async-start(), calls=%async_computation.10 | async-start | bytes 983040 | tf_op jit(solution)/shard_map/reduce_scatter | solution.py:593
  708.6 60.7 %collective-permute-start.70 = (bf16[384,768]{1,0:T(8,128)(2,1)S(1)}, bf16[384,768]{1,0:T(8,128)(2,1)}, u32[]{:S(2)}, u32[]{:S(2)}) collective-permute-start(bf16[384,768]{1,0:T(8,128)(2,1)S(1)} %convert_element_type.345), channel_id=1, source_target_pairs={{16,16},{17,24},{18,20},{19,28},{20,18},{21,26},{22,22},{23,30},{2... | collective-permute-start | bytes 1769480 | tf_op jit(solution)/shard_map/ppermute | solution.py:455
  710.3 75.3 %collective-permute-start.68 = (bf16[384,768]{1,0:T(8,128)(2,1)S(1)}, bf16[384,768]{1,0:T(8,128)(2,1)}, u32[]{:S(2)}, u32[]{:S(2)}) collective-permute-start(bf16[384,768]{1,0:T(8,128)(2,1)S(1)} %convert_element_type.345), channel_id=1, source_target_pairs={{0,16},{1,24},{2,20},{3,28},{4,18},{5,26},{6,22},{7,30},{8,17},{9,... | collective-permute-start | bytes 1769480 | tf_op jit(solution)/shard_map/ppermute | solution.py:455
  717.7 53.8 %collective-permute-start.69 = (bf16[384,768]{1,0:T(8,128)(2,1)}, bf16[384,768]{1,0:T(8,128)(2,1)S(1)}, u32[]{:S(2)}, u32[]{:S(2)}) collective-permute-start(bf16[384,768]{1,0:T(8,128)(2,1)} %fusion.28), channel_id=1, source_target_pairs={{16,0},{17,8},{18,4},{19,12},{20,2},{21,10},{22,6},{23,14},{24,1},... | collective-permute-start | bytes 1769480 | tf_op jit(solution)/shard_map/ppermute | solution.py:455
  719.1 73.0 %collective-permute-start.67 = (bf16[384,768]{1,0:T(8,128)(2,1)}, bf16[384,768]{1,0:T(8,128)(2,1)S(1)}, u32[]{:S(2)}, u32[]{:S(2)}) collective-permute-start(bf16[384,768]{1,0:T(8,128)(2,1)} %fusion.28), channel_id=1, source_target_pairs={{0,0},{1,8},{2,4},{3,12},{4,2},{5,10},{6,6},{7,14},{8,1},{9,9},{10... | collective-permute-start | bytes 1769480 | tf_op jit(solution)/shard_map/ppermute | solution.py:455
  (287 other events, 2662.0 us)
Sparse Core Ops, SparseCore 0:
  23.2 31.9 all-gather.4
  57.3 55.3 all-gather.6
  114.8 33.3 all-gather.8
  164.0 30.2 all-gather.10
  517.2 29.8 reduce-scatter.4
  631.1 24.0 reduce-scatter.6
  674.5 29.8 reduce-scatter.10
  708.1 47.6 reduce-scatter.8

commit v5 on v4

--- a/solution.py
+++ b/solution.py
@@ -12,6 +12,7 @@
 EPS = 1e-05
 MASKED = -1e30
 QUARTERS = 4
+ATTEND_VMEM = 58 * 2**20
 BF16 = jnp.bfloat16
 F32 = jnp.float32
 AXES = ("section", "shard", "replica")
@@ -102,7 +103,7 @@
             jax.ShapeDtypeStruct((heads, frames), F32),
         ),
         scratch_shapes=[pltpu.VMEM((keys, frames), F32)],
-        compiler_params=pltpu.CompilerParams(vmem_limit_bytes=40 * 2**20),
+        compiler_params=pltpu.CompilerParams(vmem_limit_bytes=ATTEND_VMEM),
         cost_estimate=pl.CostEstimate(
             flops=16 * keys * frames * wide, bytes_accessed=2 * heads * keys * frames, transcendentals=heads * keys * frames
         ),
@@ -164,7 +165,7 @@
         out_specs=[whole_block(shape) for shape in results],
         out_shape=[jax.ShapeDtypeStruct(shape, BF16) for shape in results],
         scratch_shapes=[pltpu.VMEM((keys, frames), F32)],
-        compiler_params=pltpu.CompilerParams(vmem_limit_bytes=40 * 2**20),
+        compiler_params=pltpu.CompilerParams(vmem_limit_bytes=ATTEND_VMEM),
         cost_estimate=pl.CostEstimate(
             flops=32 * keys * frames * wide, bytes_accessed=2 * heads * keys * frames, transcendentals=0
         ),
@@ -244,6 +245,38 @@
         name="middle_back",
     )(quarter.reshape(1), grad, middle, cot, vec, weight)
     return results[0], results[1], results[2:2 + QUARTERS], results[2 + QUARTERS:]
+
+
+def vector_kernel(quarter_ref, *refs, shards):
+    ins, up_ins = refs[:QUARTERS], refs[QUARTERS:2 * QUARTERS]
+    gain_ref, shift_ref, mid_ref, out_ref = refs[2 * QUARTERS:]
+    width = out_ref.shape[0]
+    wide, unit = width // QUARTERS, width // shards
+    ins = in_order([ref[...] for ref in ins], quarter_ref[0])
+    value_row, query_row = (
+        jnp.concatenate([piece[:, i * wide:(i + 1) * wide] for piece in ins], 1) for i in range(1, 3)
+    )
+    ups = in_order([ref[...] for ref in up_ins], quarter_ref[0])
+    up_row = jnp.concatenate(
+        [piece[:, shard * unit:(shard + 1) * unit] for shard in range(shards) for piece in ups], 1
+    )
+    rows = [gain_ref[...], shift_ref[...], query_row, value_row, mid_ref[2:3, :], mid_ref[0:2, :], mid_ref[3:4, :]]
+    rows += [up_row[:, start:start + width] for start in range(0, up_row.shape[1], width)]
+    rows = jnp.concatenate(rows, 0)
+    rows = jnp.concatenate([rows, jnp.zeros((128 - rows.shape[0], width), F32)], 0)
+    out_ref[...] = rows.T.astype(BF16)
+
+
+def vector_block(quarter, sums_in, up_sums, gain, shift, mid_rows, shards):
+    width = gain.shape[1]
+    return pl.pallas_call(
+        functools.partial(vector_kernel, shards=shards),
+        in_specs=scalar_first(2 * QUARTERS + 3),
+        out_shape=jax.ShapeDtypeStruct((width, 128), BF16),
+        compiler_params=pltpu.CompilerParams(vmem_limit_bytes=32 * 2**20),
+        cost_estimate=pl.CostEstimate(flops=128 * width, bytes_accessed=512 * width, transcendentals=0),
+        name="vector_block",
+    )(quarter.reshape(1), *sums_in, *up_sums, gain, shift, mid_rows)
 
 
 def column_tile(columns):
@@ -518,19 +551,18 @@
     own_down = pick(mlp_down[0].reshape(QUARTERS, unit, width), 0)
     proj_zero, proj_one = by_layer(own_proj, swap_sections(own_proj))
     proj_zero = gathered(proj_zero)
-    own_up = gathered(after(own_up, proj_zero))
-    own_down = gathered(after(own_down, own_up))
-    proj_one = gathered(after(proj_one, own_down))
-    up_zero, up_one = by_layer(own_up, swap_sections(own_up))
-    down_zero, down_one = by_layer(own_down, swap_sections(own_down))
-    blocks = [proj_zero, up_zero, down_zero, proj_one, up_one]
-    blocks = [spread(block, across(block, 2)) for block in blocks]
-
-    layers = []
-    for layer in range(2):
-        proj = blocks[3 * layer]
-        w_out = jnp.concatenate(in_order([piece[:, 3 * wide:] for piece in proj], quarter), 1)
-        layers.append([proj, w_out, blocks[3 * layer + 1], blocks[2], vec_by_layer[layer]])
+    own_up = after(own_up, inputs)
+    own_down = after(own_down, own_up)
+    proj_one = after(proj_one, own_down)
+    own_up, own_down, proj_one = gathered(own_up), gathered(own_down), gathered(proj_one)
+    other_up, other_down = swap_sections(own_up), swap_sections(own_down)
+
+    def head_weights(block):
+        pieces = spread(block, across(block, 2))
+        return pieces, jnp.concatenate(in_order([piece[:, 3 * wide:] for piece in pieces], quarter), 1)
+
+    heads_by_layer = [head_weights(proj_zero), None]
+    hidden_by_layer = [None, None]
 
     members = [0]
     bit = 2
@@ -554,26 +586,48 @@
         return block
 
     def forward(x_low, layer):
+        vec = vec_by_layer[layer]
         x_set = chips_rows(x_low)
-        if layer == 1:
-            down = after(down_one, x_set)
-            layers[1][3] = spread(down, across(down, 2))
-        proj, w_out, w_up, w_down, vec = layers[layer]
+        proj, w_out = heads_by_layer[layer]
         normed = layer_norm(x_set.astype(F32), vec[0], vec[1]).astype(BF16)
         zeros = jnp.zeros((QUARTERS, wide), F32)
         bias_in = jnp.stack([zeros, vec[3].reshape(QUARTERS, wide), vec[2].reshape(QUARTERS, wide)], 1)
-        own_qkv, other_kv = [], [None] * QUARTERS
-        for p in range(QUARTERS):
+        own_qkv, other_kv = {}, {}
+        order = (0, 1, 2, 3)
+        for p in order:
             bias = lax.dynamic_index_in_dim(bias_in, quarter ^ p, 0, keepdims=False).reshape(3 * wide)
-            own_qkv.append((dot(normed, proj[p][:, :3 * wide]) + bias).astype(BF16))
+            own_qkv[p] = (dot(normed, proj[p][:, :3 * wide]) + bias).astype(BF16)
             other_kv[p ^ 1] = across(own_qkv[p][:, :2 * wide], 1)
-        outs, weights, inverses = [], [], []
-        for p in range(QUARTERS):
-            out, weight, inverse = attend(own_qkv[p], other_kv[p], key_bias, heads, frames)
-            outs.append(out)
-            weights.append(weight)
-            inverses.append(inverse)
-        attended, middle, normed_two = out_part(quarter, outs, w_out, x_low, vec)
+        outs, weights, inverses = {}, {}, {}
+        late = {}
+        for step, p in enumerate(order):
+            own = own_qkv[p]
+            if layer == 0 and step == 3:
+                own = after(own, proj_one)
+            outs[p], weights[p], inverses[p] = attend(own, other_kv[p], key_bias, heads, frames)
+            if layer == 0 and step == 0:
+                late["up"] = by_layer(own_up, after(other_up, outs[p]))
+                late["up_far"] = across(late["up"][0], 2)
+            elif layer == 0 and step == 1:
+                late["down"] = by_layer(own_down, after(other_down, outs[p]))
+                late["down_far"] = across(late["down"][0], 2)
+            elif layer == 0 and step == 2:
+                w_up = spread(late["up"][0], after(late["up_far"], outs[p]))
+                late["one_far"] = across(after(proj_one, outs[p]), 2)
+            elif layer == 0 and step == 3:
+                w_down = spread(late["down"][0], after(late["down_far"], outs[p]))
+                hidden_by_layer[0] = (w_up, w_down)
+            elif layer == 1 and step == 0:
+                late["down_far"] = across(after(pending_one["down"], outs[p]), 2)
+            elif layer == 1 and step == 1:
+                cot = after(edges_here, outs[p])
+                pending_one["cot"] = [transposed(cot[0], 1, 0), transposed(cot[1], 1, 1)]
+                w_up = spread(pending_one["up"], after(pending_one["up_far"], outs[p]))
+            elif layer == 1 and step == 3:
+                w_down = spread(pending_one["down"], after(late["down_far"], outs[p]))
+                hidden_by_layer[1] = (w_up, w_down)
+        attended, middle, normed_two = out_part(quarter, [outs[p] for p in range(QUARTERS)], w_out, x_low, vec)
+        w_up, w_down = hidden_by_layer[layer]
         bias_up = vec[8:].reshape(shards, QUARTERS, unit)
         acts, slopes = [], []
         result = middle + vec[7]
@@ -582,8 +636,17 @@
             act, slope, result = mlp_part(normed_two, w_up[p], bias, w_down[p], result)
             acts.append(act)
             slopes.append(slope)
+            if layer == 0 and p == 0:
+                far = after(late["one_far"], act)
+                pieces = spread(proj_one, far)
+                w_out_one = jnp.concatenate(in_order([piece[:, 3 * wide:] for piece in pieces], quarter), 1)
+                heads_by_layer[1] = (pieces, w_out_one)
+                pending_one["up"], pending_one["down"] = late["up"][1], late["down"][1]
+                pending_one["up_far"] = across(after(pending_one["up"], far), 2)
         kept = (x_low, normed, own_qkv, other_kv, weights, inverses, attended, middle, normed_two, acts, slopes)
         return result.astype(BF16), kept
+
+    pending_one = {}
 
     def scattered(block):
         bit = QUARTERS
@@ -597,47 +660,47 @@
         left, right = block[:, :cut], block[:, cut:]
         return low_sum(jnp.where(first, left, right), swap_sections(jnp.where(first, right, left)))
 
-    def backward(cot, layer, kept, pending):
-        proj, w_out, w_up, w_down, vec = layers[layer]
+    def backward(cot, layer, kept, above):
+        (proj, w_out), (w_up, w_down), vec = heads_by_layer[layer], hidden_by_layer[layer], vec_by_layer[layer]
         x_low, normed, own_qkv, other_kv, weights, inverses, attended, middle, normed_two, acts, slopes = kept
-        order = (1, 3, 2, 0)
+        order = (3, 1, 2, 0)
         g_down, g_up, up_sums, near_down, near_up = {}, {}, {}, {}, {}
         d_normed_two = jnp.zeros((frames, width), F32)
-        for p in order:
+        for step, p in enumerate(order):
             g_down[p], g_up[p], up_sums[p], d_normed_two = mlp_back_part(
                 cot, normed_two, acts[p], slopes[p], w_up[p], w_down[p], d_normed_two
             )
             if p & 1:
                 near_down[p ^ 1] = across(g_down[p], 1)
                 near_up[p ^ 1] = across(g_up[p], 1)
+            if above is not None and step == 1:
+                halves = [after(half, g_up[p]) for half in above["halves"]]
+                above["mlp"] = scattered(jnp.concatenate(halves, 1))
         d_middle, mid_rows, d_heads, d_attn_parts = middle_back(quarter, d_normed_two, middle, cot, vec, w_out)
-
-        far_down = across(low_sum(g_down[2], near_down[2]), 2)
-        far_up = across(low_sum(g_up[2], near_up[2]), 2)
-        above = None
+        if above is not None:
+            far = after(above["far_proj"], mid_rows)
+            above["half"] = half_sum(above["finish"](far))
+        far_down = low_sum(g_down[2], after(near_down[2], mid_rows))
         results = {}
-        for p in order:
+        for step, p in enumerate(order):
             head = d_heads[p]
-            if p == 1:
-                head = after(head, *near_down.values())
-                if pending is not None:
-                    head = after(head, pending[1])
-            elif p == 3:
-                head = after(head, *near_up.values())
-            elif p == 2 and pending is not None:
-                make, far, vec_block = pending[0]
-                above = half_sum(make(far))
-                head = after(head, above)
-                above = jnp.concatenate([above, vec_block], 1)
-            elif p == 0:
+            if step == 1:
                 head = after(head, far_down)
-                if pending is not None:
-                    head = after(head, pending[2])
+                far_down = across(far_down, 2)
+            elif step == 2:
+                head = after(head, far_up)
+                far_up = across(far_up, 2)
+                if above is not None:
+                    half = after(above["half"], results[order[1]][0])
+                    above["proj"] = scattered(jnp.concatenate([half, above["vec"]], 1))
+            elif step == 3 and above is not None:
+                head = after(head, above["mlp"])
             results[p] = attend_back(own_qkv[p], other_kv[p], weights[p], inverses[p], head, heads, frames)
+            if step == 0:
+                far_up = low_sum(g_up[2], after(near_up[2], results[p][0]))
+        last = results[order[3]][0]
         from_other = {p: across(results[p ^ 1][2], 1) for p in range(QUARTERS)}
-        half_down = half_sum(low_sum(g_down[0], near_down[0], far_down))
-        if above is not None:
-            above = scattered(above)
+        half_down = half_sum(low_sum(g_down[0], near_down[0], after(far_down, last)))
         g_proj, sums_in, near_proj = {}, {}, {}
         d_normed = jnp.zeros(normed.shape, F32)
         for p in order:
@@ -646,56 +709,46 @@
             )
             if p & 1:
                 near_proj[p ^ 1] = across(g_proj[p], 1)
-        block = after(d_normed, half_down, far_up)
-        if above is not None:
-            block = after(block, above)
+        block = d_normed
         bit = shards // 2
         while bit >= 2:
             cut = block.shape[0] // 2
             block = block[:cut] + across(block[cut:].astype(BF16), bit).astype(F32)
             bit //= 2
-        half_up = half_sum(low_sum(g_up[0], near_up[0], far_up))
-        block = after(block, half_up)
-        mlp_done = scattered(jnp.concatenate([half_down, half_up], 1))
-        far_proj = low_sum(g_proj[2], near_proj[2])
+        half_up = half_sum(low_sum(g_up[0], near_up[0], after(far_up, d_normed)))
         if layer == 1:
-            far_proj = after(far_proj, block)
+            far_proj = low_sum(g_proj[2], after(near_proj[2], block))
+        else:
+            far_proj = low_sum(g_proj[2], after(near_proj[2], d_normed))
         back, g_gain_one, g_shift_one = norm_back(x_low.astype(F32), vec[0], block)
         g_low = (d_middle + back).astype(BF16)
-        if layer == 1:
-            g_low = after(g_low, far_proj)
+        g_low = after(g_low, far_proj)
         far_proj = across(far_proj, 2)
-        sums = [
-            jnp.concatenate(in_order([sums_in[p][:, i * wide:(i + 1) * wide] for p in range(QUARTERS)], quarter), 1)
-            for i in range(1, 3)
-        ]
-        sum_up = jnp.stack(in_order([up_sums[p].reshape(shards, unit) for p in range(QUARTERS)], quarter), 1)
-        g_vec = jnp.concatenate(
-            [
-                g_gain_one, g_shift_one, sums[1], sums[0], mid_rows[2:3], mid_rows[0:2], mid_rows[3:4],
-                sum_up.reshape(-1, width),
-            ]
+        vec_block = vector_block(
+            quarter, [sums_in[p] for p in range(QUARTERS)], [up_sums[p] for p in range(QUARTERS)],
+            g_gain_one, g_shift_one, mid_rows, shards,
         )
-        vec_block = jnp.pad(g_vec.T.astype(BF16), ((0, 0), (0, 128 - g_vec.shape[0])))
+        if above is not None:
+            g_low = after(g_low, above["proj"])
 
         def finish_proj(other):
             return low_sum(g_proj[0], near_proj[0], other)
 
-        return g_low, ((finish_proj, far_proj, vec_block), half_up, mlp_done), above
+        return g_low, {"halves": [half_down, half_up], "far_proj": far_proj, "finish": finish_proj, "vec": vec_block}
 
     x_one, kept_zero = forward(inputs, 0)
     y_one, kept_one = forward(x_one, 1)
-    cot = after(edges_here, x_one)
-    cot = jnp.where(first, transposed(cot[0], 1, 0), transposed(cot[1], 1, 1))
-    g_one, pending, _ = backward(cot, 1, kept_one, None)
-    mlp_one = pending[2]
-    g_zero, pending, proj_one = backward(g_one, 0, kept_zero, pending)
+    cot = [after(part, y_one) for part in pending_one["cot"]]
+    g_one, one = backward(jnp.where(first, cot[0], cot[1]), 1, kept_one, None)
+    g_zero, zero = backward(g_one, 0, kept_zero, one)
     y_one = after(y_one, g_one)
     out_slots = [transposed(y_one, 0, 1), transposed(y_one, 1, 1)]
     back_slots = [transposed(g_zero, 0, 0), transposed(g_zero, 1, 0)]
     edges_out = jnp.stack([jnp.where(first, b, o) for b, o in zip(back_slots, out_slots)])
-    (make, far, vec_block), _, mlp_zero = pending
-    proj_zero = scattered(jnp.concatenate([half_sum(make(far)), vec_block], 1))
+    mlp_one, proj_one = one["mlp"], one["proj"]
+    mlp_zero = scattered(jnp.concatenate([after(half, g_zero) for half in zero["halves"]], 1))
+    far = after(zero["far_proj"], g_zero)
+    proj_zero = scattered(jnp.concatenate([half_sum(zero["finish"](far)), zero["vec"]], 1))
 
     def exchanged(zero, one):
         return jnp.where(first, zero, one), swap_sections(jnp.where(first, one, zero))

time: 810 us -> 792 us (0.978)
  waiting for transfers between devices: 339 us -> 242 us
  starting transfers between devices: 64.1 us -> 135 us
  local copies, waits for them, and re-layouts: 118 us -> 75.3 us
  Pallas kernels: 193 us -> 229 us
    ppermute x62, starting transfers between devices: 35.9 us -> 93.5 us  [across(): return lax.ppermute(block, 'replica', [(i, i ^ bit) for i in range(count)])]
    ppermute x12, waiting for transfers between devices: 88.1 us -> 33.1 us  [swap_sections(): return lax.ppermute(block, 'section', [(0, 1), (1, 0)])]
    all_gather x4, waiting for transfers between devices: 83 us -> 33.5 us  [gathered(): return lax.all_gather(block, 'shard', axis=0, tiled=True)]
    unnamed x490 -> x340, local copies, waits for them, and re-layouts: 85.9 us -> 44.2 us
    reduce_scatter x4, waiting for transfers between devices: 16.6 us -> 34.5 us  [scattered(): return lax.psum_scatter(block, 'shard', scatter_dimension=0, tiled=True)]
    pallas_call x8, Pallas kernels: 47.4 us -> 63.9 us  [attend_back(): pl.pallas_call(functools.partial(attend_back_kernel, heads=heads, frames=...]
    ppermute x9, waiting for transfers between devices: 15.5 us -> 0.02 us  [transposed(): return lax.ppermute(block, AXES, route)]
    ppermute x12, starting transfers between devices: 12.8 us -> 21.7 us  [swap_sections(): return lax.ppermute(block, 'section', [(0, 1), (1, 0)])]
  transfers between devices with their start and end apart: 91 -> 91, of which waited for: 28 -> 23; matrix products, arithmetic and copies ran while one was open for 13% -> 14% of each run, Pallas kernels for 22% -> 28%
where the time goes in v5:
time: 792 us; the launch traced here: 781 us
  waiting for transfers between devices  242 us (31%)
  Pallas kernels  229 us (29%)
  starting transfers between devices  135 us (17%)
  local copies, waits for them, and re-layouts  75.3 us (10%)
  other arithmetic  68.2 us (9%)
  between operations  16.9 us (2%)
  matrix products  14.5 us (2%)
    ppermute x62, waiting for transfers between devices, across(): return lax.ppermute(block, 'replica', [(i, i ^ bit) for i in range(count)])  141 us
    ppermute x62, starting transfers between devices, across(): return lax.ppermute(block, 'replica', [(i, i ^ bit) for i in range(count)])  93.5 us
    pallas_call x8, Pallas kernels, attend_back(): pl.pallas_call(functools.partial(attend_back_kernel, heads=heads, frames=...  63.9 us
    pallas_call x8, Pallas kernels, attend(): pl.pallas_call(functools.partial(attend_kernel, heads=heads, frames=frame...  51.4 us
    unnamed x340, local copies, waits for them, and re-layouts  44.2 us
    pallas_call x8, Pallas kernels, mlp_back_part(): pl.pallas_call(mlp_back_kernel, grid=(columns // tile,), in_specs=[whole,...  41.8 us
    pallas_call x8, Pallas kernels, mlp_part(): pl.pallas_call(mlp_kernel, grid=(columns // tile,), in_specs=[whole, pl.B...  34.9 us
    reduce_scatter x4, waiting for transfers between devices, scattered(): return lax.psum_scatter(block, 'shard', scatter_dimension=0, tiled=True)  34.5 us
  transfers between devices with their start and end apart: 91, of which 23 were waited for; matrix products, arithmetic and copies ran while one was open for 14% of the time, Pallas kernels for 28%

profile of v5, /device:TPU:0, one launch (start us, length us, event | category | flops | bytes accessed | tf_op | source)
XLA Modules:
  0.0 781.0 jit_solution(15353773857712381673)
XLA Ops:
  15.1 7.0 collective-permute-done.4
  24.2 6.0 collective-permute-start
  44.8 54.6 %collective-permute-start.2 = (bf16[384,768]{1,0:T(8,128)(2,1)S(1)}, bf16[384,768]{1,0:T(8,128)(2,1)S(1)}, u32[]{:S(2)}, u32[]{:S(2)}) collective-permute-start(bf16[384,768]{1,0:T(8,128)(2,1)S(1)} %get-tuple-element.455.x_ref), channel_id=1, source_target_pairs={{0,2},{1,3},{2,0},{3,1},{4,6},{5,7},{6,4},{7,5},{8,10},{9,11},{10,... | collective-permute-start | bytes 1769480 | tf_op jit(solution)/shard_map/ppermute | solution.py:457
  101.6 5.6 collective-permute-done.2
  112.4 6.2 all-gather.11.cloned.1.call-done
  122.9 27.4 %all-gather.9.cloned.1.call-done = bf16[768,768]{1,0:T(8,128)(2,1)} async-done(((bf16[192,768]{1,0:T(8,128)(2,1)}), bf16[768,768]{1,0:T(8,128)(2,1)}) %all-gather.9.cloned.1.call-update) | async-done | bytes 1179664 | tf_op jit(solution)/shard_map/all_gather | solution.py:542
  157.7 6.3 attend.9
  168.4 6.3 attend.8
  188.6 6.3 attend.11
  196.0 6.8 attend.10
  202.8 17.7 %collective-permute-done.14.up_ref = bf16[768,768]{1,0:T(8,128)(2,1)} collective-permute-done((bf16[768,768]{1,0:T(8,128)(2,1)}, bf16[768,768]{1,0:T(8,128)(2,1)}, u32[]{:S(2)}, u32[]{:S(2)}) %collective-permute-start.14) | collective-permute-done | bytes 1179680 | tf_op jit(solution)/shard_map/ppermute | solution.py:457
  244.9 4.5 mlp_part.11
  259.1 7.6 collective-permute-done.21
  273.8 17.8 %collective-permute-done.26.weight_ref = bf16[768,768]{1,0:T(8,128)(2,1)} collective-permute-done((bf16[768,768]{1,0:T(8,128)(2,1)}, bf16[768,768]{1,0:T(8,128)(2,1)}, u32[]{:S(2)}, u32[]{:S(2)}) %collective-permute-start.26) | collective-permute-done | bytes 1179680 | tf_op jit(solution)/shard_map/ppermute | solution.py:457
  295.7 6.4 attend.13
  312.8 6.5 attend.12
  321.7 6.3 attend.15
  328.0 18.1 %collective-permute-done.32.down_ref = bf16[768,768]{1,0:T(8,128)(2,1)} collective-permute-done((bf16[768,768]{1,0:T(8,128)(2,1)}, bf16[768,768]{1,0:T(8,128)(2,1)}, u32[]{:S(2)}, u32[]{:S(2)}) %collective-permute-start.32) | collective-permute-done | bytes 1179680 | tf_op jit(solution)/shard_map/ppermute | solution.py:457
  351.7 6.4 attend.14
  362.8 4.7 mlp_part.12
  382.5 6.1 mlp_back_part.8
  389.2 5.4 mlp_back_part.9
  395.6 4.6 mlp_back_part.10
  402.3 4.6 mlp_back_part.11
  414.5 8.0 %attend_back.10 = (bf16[384,192]{1,0:T(8,128)(2,1)}, bf16[768,384]{1,0:T(8,128)(2,1)}, bf16[768,384]{1,0:T(8,128)(2,1)}) custom-call(bf16[768,576]{1,0:T(8,128)(2,1)} %copy-done.145, bf16[768,384]{1,0:T(8,128)(2,1)} %collective-permute-done.29.other_ref, bf16[3,1536,384]{2,1,0:T(8,128)(2,1)} %get-tuple-element.280.exp_ref, ...), custom_call_target="tpu_custom_call" | custom-call | flops 3623878656 | bytes 3538944 | tf_op jit(solution)/shard_map/attend_back/pallas_call | solution.py:157
  422.9 7.9 %attend_back.8 = (bf16[384,192]{1,0:T(8,128)(2,1)}, bf16[768,384]{1,0:T(8,128)(2,1)}, bf16[768,384]{1,0:T(8,128)(2,1)}) custom-call(bf16[768,576]{1,0:T(8,128)(2,1)} %add_convert_fusion.14.own_ref, bf16[768,384]{1,0:T(8,128)(2,1)} %collective-permute-done.25.other_ref, bf16[3,1536,384]{2,1,0:T(8,128)(2,1)} %get-tuple-element.259.exp_ref, ...), custom_call_target="tpu_custom_call" | custom-call | flops 3623878656 | bytes 3538944 | tf_op jit(solution)/shard_map/attend_back/pallas_call | solution.py:157
  433.9 9.4 %collective-permute-start.49 = (bf16[768,768]{1,0:T(8,128)(2,1)}, bf16[768,768]{1,0:T(8,128)(2,1)}, u32[]{:S(2)}, u32[]{:S(2)}) collective-permute-start(bf16[768,768]{1,0:T(8,128)(2,1)} %add_convert_fusion.10), channel_id=1, source_target_pairs={{0,2},{1,3},{2,0},{3,1},{4,6},{5,7},{6,4},{7,5},{8,10},{9,11},{10,... | collective-permute-start | bytes 3538952 | tf_op jit(solution)/shard_map/ppermute | solution.py:457
  443.3 8.1 %attend_back.11 = (bf16[384,192]{1,0:T(8,128)(2,1)}, bf16[768,384]{1,0:T(8,128)(2,1)}, bf16[768,384]{1,0:T(8,128)(2,1)}) custom-call(bf16[768,576]{1,0:T(8,128)(2,1)} %copy-done.144, bf16[768,384]{1,0:T(8,128)(2,1)} %collective-permute-done.28.other_ref, bf16[3,1536,384]{2,1,0:T(8,128)(2,1)} %get-tuple-element.275.exp_ref, ...), custom_call_target="tpu_custom_call" | custom-call | flops 3623878656 | bytes 3538944 | tf_op jit(solution)/shard_map/attend_back/pallas_call | solution.py:157
  454.2 8.3 %attend_back.9 = (bf16[384,192]{1,0:T(8,128)(2,1)}, bf16[768,384]{1,0:T(8,128)(2,1)}, bf16[768,384]{1,0:T(8,128)(2,1)}) custom-call(bf16[768,576]{1,0:T(8,128)(2,1)} %copy-done.143, bf16[768,384]{1,0:T(8,128)(2,1)} %copy-done.164, bf16[3,1536,384]{2,1,0:T(8,128)(2,1)} %get-tuple-element.263.exp_ref, f32[3,384]{1,0:T(4,128)} %get-tuple-element.264.inv_ref, ...), custom_call_target="tpu_custom_call" | custom-call | flops 3623878656 | bytes 3538944 | tf_op jit(solution)/shard_map/attend_back/pallas_call | solution.py:157
  464.8 4.4 proj_back.8
  483.6 12.0 %collective-permute-done.46 = bf16[768,768]{1,0:T(8,128)(2,1)S(1)} collective-permute-done((bf16[768,768]{1,0:T(8,128)(2,1)}, bf16[768,768]{1,0:T(8,128)(2,1)S(1)}, u32[]{:S(2)}, u32[]{:S(2)}) %collective-permute-start.46) | collective-permute-done | bytes 1179680 | tf_op jit(solution)/shard_map/ppermute | solution.py:457
  495.6 5.7 collective-permute-start.50
  501.9 6.1 collective-permute-done.43
  512.5 5.9 mlp_back_part.12
  519.6 5.7 mlp_back_part.13
  532.9 4.7 mlp_back_part.14
  537.7 4.7 mlp_back_part.15
  551.3 7.8 attend_back.14
  572.9 8.2 %attend_back.15 = (bf16[384,192]{1,0:T(8,128)(2,1)}, bf16[768,384]{1,0:T(8,128)(2,1)}, bf16[768,384]{1,0:T(8,128)(2,1)}) custom-call(bf16[768,576]{1,0:T(8,128)(2,1)} %copy-done.141, bf16[768,384]{1,0:T(8,128)(2,1)} %collective-permute-done.11.other_ref, bf16[3,1536,384]{2,1,0:T(8,128)(2,1)} %get-tuple-element.343.exp_ref, ...), custom_call_target="tpu_custom_call" | custom-call | flops 3623878656 | bytes 3538944 | tf_op jit(solution)/shard_map/attend_back/pallas_call | solution.py:157
  581.1 7.8 %attend_back.13 = (bf16[384,192]{1,0:T(8,128)(2,1)}, bf16[768,384]{1,0:T(8,128)(2,1)}, bf16[768,384]{1,0:T(8,128)(2,1)}) custom-call(bf16[768,576]{1,0:T(8,128)(2,1)} %copy-done.140, bf16[768,384]{1,0:T(8,128)(2,1)} %collective-permute-done.8.other_ref, bf16[3,1536,384]{2,1,0:T(8,128)(2,1)} %get-tuple-element.331.exp_ref, ...), custom_call_target="tpu_custom_call" | custom-call | flops 3623878656 | bytes 3538944 | tf_op jit(solution)/shard_map/attend_back/pallas_call | solution.py:157
  589.9 7.8 %attend_back.12 = (bf16[384,192]{1,0:T(8,128)(2,1)}, bf16[768,384]{1,0:T(8,128)(2,1)}, bf16[768,384]{1,0:T(8,128)(2,1)}) custom-call(bf16[768,576]{1,0:T(8,128)(2,1)} %copy-done.139, bf16[768,384]{1,0:T(8,128)(2,1)} %collective-permute-done.6.other_ref, bf16[3,1536,384]{2,1,0:T(8,128)(2,1)} %get-tuple-element.317.exp_ref, ...), custom_call_target="tpu_custom_call" | custom-call | flops 3623878656 | bytes 3538944 | tf_op jit(solution)/shard_map/attend_back/pallas_call | solution.py:157
  623.4 5.2 collective-permute-done.77
  634.3 7.0 collective-permute-done.57
  650.5 15.2 %collective-permute-done.67 = bf16[768,768]{1,0:T(8,128)(2,1)} collective-permute-done((bf16[768,768]{1,0:T(8,128)(2,1)}, bf16[768,768]{1,0:T(8,128)(2,1)}, u32[]{:S(2)}, u32[]{:S(2)}) %collective-permute-start.67) | collective-permute-done | bytes 1179680 | tf_op jit(solution)/shard_map/ppermute | solution.py:457
  668.8 13.7 %collective-permute-done.68 = bf16[768,384]{1,0:T(8,128)(2,1)S(1)} collective-permute-done((bf16[768,384]{1,0:T(8,128)(2,1)S(1)}, bf16[768,384]{1,0:T(8,128)(2,1)S(1)}, u32[]{:S(2)}, u32[]{:S(2)}) %collective-permute-start.68) | collective-permute-done | bytes 589856 | tf_op jit(solution)/shard_map/ppermute | solution.py:461
  693.2 34.5 %reduce-scatter.9.cloned.1.call-done = bf16[192,512]{1,0:T(8,128)(2,1)} async-done(((bf16[768,512]{1,0:T(8,128)(2,1)}), bf16[192,512]{1,0:T(8,128)(2,1)}) %reduce-scatter.9.cloned.1.call-update) | async-done | bytes 196624 | tf_op jit(solution)/shard_map/reduce_scatter | solution.py:656
  741.2 17.9 %collective-permute-done.81.c_ref = bf16[192,1536]{1,0:T(8,128)(2,1)S(1)} collective-permute-done((bf16[192,1536]{1,0:T(8,128)(2,1)S(1)}, bf16[192,1536]{1,0:T(8,128)(2,1)S(1)}, u32[]{:S(2)}, u32[]{:S(2)}) %collective-permute-start.81) | collective-permute-done | bytes 589856 | tf_op jit(solution)/shard_map/ppermute | solution.py:457
  759.1 7.3 collective-permute-done.71.c_ref
  (680 shorter events, 291.6 us)
Async XLA Ops:
  7.2 100.3 %all-gather.5.cloned.1.call-start = ((), (), s32[]{:S(2)}) async-start(), calls=%async_computation.4 | async-start | bytes 1474560 | tf_op jit(solution)/shard_map/all_gather | solution.py:542
  23.1 95.4 %all-gather.11.cloned.1.call-start = ((), (), s32[]{:S(2)}) async-start(), calls=%async_computation.7 | async-start | bytes 1474560 | tf_op jit(solution)/shard_map/all_gather | solution.py:542
  42.5 107.7 %all-gather.9.cloned.1.call-start = ((), (), s32[]{:S(2)}) async-start(), calls=%async_computation.6 | async-start | bytes 1474560 | tf_op jit(solution)/shard_map/all_gather | solution.py:542
  42.6 57.1 %collective-permute-start.3 = (f32[12,768]{1,0:T(8,128)S(1)}, f32[12,768]{1,0:T(8,128)S(1)}, u32[]{:S(2)}, u32[]{:S(2)}) collective-permute-start(f32[12,768]{1,0:T(8,128)S(1)} %bitcast.65), channel_id=1, source_target_pairs={{0,16},{16,0},{1,17},{17,1},{2,18},{18,2},{3,19},{19,3},{4,20},{20... | collective-permute-start | bytes 110600 | tf_op jit(solution)/shard_map/ppermute | solution.py:461
  44.8 62.5 %collective-permute-start.2 = (bf16[384,768]{1,0:T(8,128)(2,1)S(1)}, bf16[384,768]{1,0:T(8,128)(2,1)S(1)}, u32[]{:S(2)}, u32[]{:S(2)}) collective-permute-start(bf16[384,768]{1,0:T(8,128)(2,1)S(1)} %get-tuple-element.455.x_ref), channel_id=1, source_target_pairs={{0,2},{1,3},{2,0},{3,1},{4,6},{5,7},{6,4},{7,5},{8,10},{9,11},{10,... | collective-permute-start | bytes 1769480 | tf_op jit(solution)/shard_map/ppermute | solution.py:457
  99.4 88.7 %all-gather.7.cloned.1.call-start = ((), (), s32[]{:S(2)}) async-start(), calls=%async_computation.5 | async-start | bytes 1474560 | tf_op jit(solution)/shard_map/all_gather | solution.py:542
  107.5 44.2 %collective-permute-start.5 = (bf16[768,768]{1,0:T(8,128)(2,1)}, bf16[768,768]{1,0:T(8,128)(2,1)}, u32[]{:S(2)}, u32[]{:S(2)}) collective-permute-start(bf16[768,768]{1,0:T(8,128)(2,1)} %all-gather.5.cloned.1.call-done.weight_ref), channel_id=1, source_target_pairs={{0,1},{1,0},{2,3},{3,2},{4,5},{5,4},{6,7},{7,6},{8,9},{9,8},{10,11... | collective-permute-start | bytes 3538952 | tf_op jit(solution)/shard_map/ppermute | solution.py:457
  108.8 48.3 %collective-permute-start.9 = (bf16[768,768]{1,0:T(8,128)(2,1)S(1)}, bf16[768,768]{1,0:T(8,128)(2,1)}, u32[]{:S(2)}, u32[]{:S(2)}) collective-permute-start(bf16[768,768]{1,0:T(8,128)(2,1)S(1)} %copy-done.14), channel_id=1, source_target_pairs={{0,2},{1,3},{2,0},{3,1},{4,6},{5,7},{6,4},{7,5},{8,10},{9,11},{10,... | collective-permute-start | bytes 3538952 | tf_op jit(solution)/shard_map/ppermute | solution.py:457
  118.5 45.5 %collective-permute-start.16 = (bf16[768,768]{1,0:T(8,128)(2,1)}, bf16[768,768]{1,0:T(8,128)(2,1)}, u32[]{:S(2)}, u32[]{:S(2)}) collective-permute-start(bf16[768,768]{1,0:T(8,128)(2,1)} %all-gather.11.cloned.1.call-done), channel_id=1, source_target_pairs={{0,16},{16,0},{1,17},{17,1},{2,18},{18,2},{3,19},{19,3},{4,20},{20... | collective-permute-start | bytes 3538952 | tf_op jit(solution)/shard_map/ppermute | solution.py:461
  122.9 34.8 %collective-permute-start.8 = (bf16[768,384]{1,0:T(8,128)(2,1)}, bf16[768,384]{1,0:T(8,128)(2,1)}, u32[]{:S(2)}, u32[]{:S(2)}) collective-permute-start(bf16[768,384]{1,0:T(8,128)(2,1)} %slice.288), channel_id=1, source_target_pairs={{0,1},{1,0},{2,3},{3,2},{4,5},{5,4},{6,7},{7,6},{8,9},{9,8},{10,11... | collective-permute-start | bytes 1769480 | tf_op jit(solution)/shard_map/ppermute | solution.py:457
  157.0 432.9 %reduce-scatter.5.cloned.1.call-start = ((), (), s32[]{:S(2)}) async-start(), calls=%async_computation.8 | async-start | bytes 1474560 | tf_op jit(solution)/shard_map/reduce_scatter | solution.py:656
  166.9 29.1 %collective-permute-start.17 = (bf16[768,768]{1,0:T(8,128)(2,1)}, bf16[768,768]{1,0:T(8,128)(2,1)}, u32[]{:S(2)}, u32[]{:S(2)}) collective-permute-start(bf16[768,768]{1,0:T(8,128)(2,1)} %get-tuple-element.468.down_ref), channel_id=1, source_target_pairs={{0,2},{1,3},{2,0},{3,1},{4,6},{5,7},{6,4},{7,5},{8,10},{9,11},{10,... | collective-permute-start | bytes 3538952 | tf_op jit(solution)/shard_map/ppermute | solution.py:457
  180.5 40.0 %collective-permute-start.14 = (bf16[768,768]{1,0:T(8,128)(2,1)}, bf16[768,768]{1,0:T(8,128)(2,1)}, u32[]{:S(2)}, u32[]{:S(2)}) collective-permute-start(bf16[768,768]{1,0:T(8,128)(2,1)} %get-tuple-element.470.up_ref), channel_id=1, source_target_pairs={{0,2},{1,3},{2,0},{3,1},{4,6},{5,7},{6,4},{7,5},{8,10},{9,11},{10,... | collective-permute-start | bytes 3538952 | tf_op jit(solution)/shard_map/ppermute | solution.py:457
  188.1 44.9 %collective-permute-start.20 = (bf16[768,768]{1,0:T(8,128)(2,1)}, bf16[768,768]{1,0:T(8,128)(2,1)}, u32[]{:S(2)}, u32[]{:S(2)}) collective-permute-start(bf16[768,768]{1,0:T(8,128)(2,1)} %get-tuple-element.468.down_ref), channel_id=1, source_target_pairs={{0,1},{1,0},{2,3},{3,2},{4,5},{5,4},{6,7},{7,6},{8,9},{9,8},{10,11... | collective-permute-start | bytes 3538952 | tf_op jit(solution)/shard_map/ppermute | solution.py:457
  188.1 44.8 %collective-permute-start.19 = (bf16[768,768]{1,0:T(8,128)(2,1)}, bf16[768,768]{1,0:T(8,128)(2,1)}, u32[]{:S(2)}, u32[]{:S(2)}) collective-permute-start(bf16[768,768]{1,0:T(8,128)(2,1)} %get-tuple-element.470.up_ref), channel_id=1, source_target_pairs={{0,1},{1,0},{2,3},{3,2},{4,5},{5,4},{6,7},{7,6},{8,9},{9,8},{10,11... | collective-permute-start | bytes 3538952 | tf_op jit(solution)/shard_map/ppermute | solution.py:457
  196.0 48.9 %collective-permute-start.18 = (bf16[768,768]{1,0:T(8,128)(2,1)}, bf16[768,768]{1,0:T(8,128)(2,1)}, u32[]{:S(2)}, u32[]{:S(2)}) collective-permute-start(bf16[768,768]{1,0:T(8,128)(2,1)} %collective-permute-done.17.down_ref), channel_id=1, source_target_pairs={{0,1},{1,0},{2,3},{3,2},{4,5},{5,4},{6,7},{7,6},{8,9},{9,8},{10,11... | collective-permute-start | bytes 3538952 | tf_op jit(solution)/shard_map/ppermute | solution.py:457
  258.5 33.1 %collective-permute-start.26 = (bf16[768,768]{1,0:T(8,128)(2,1)}, bf16[768,768]{1,0:T(8,128)(2,1)}, u32[]{:S(2)}, u32[]{:S(2)}) collective-permute-start(bf16[768,768]{1,0:T(8,128)(2,1)} %all-gather.7.cloned.1.call-done.weight_ref), channel_id=1, source_target_pairs={{0,2},{1,3},{2,0},{3,1},{4,6},{5,7},{6,4},{7,5},{8,10},{9,11},{10,... | collective-permute-start | bytes 3538952 | tf_op jit(solution)/shard_map/ppermute | solution.py:457
  302.1 44.0 %collective-permute-start.32 = (bf16[768,768]{1,0:T(8,128)(2,1)}, bf16[768,768]{1,0:T(8,128)(2,1)}, u32[]{:S(2)}, u32[]{:S(2)}) collective-permute-start(bf16[768,768]{1,0:T(8,128)(2,1)} %get-tuple-element.237.down_ref), channel_id=1, source_target_pairs={{0,2},{1,3},{2,0},{3,1},{4,6},{5,7},{6,4},{7,5},{8,10},{9,11},{10,... | collective-permute-start | bytes 3538952 | tf_op jit(solution)/shard_map/ppermute | solution.py:457
  307.9 54.0 %collective-permute-start.35 = (bf16[768,768]{1,0:T(8,128)(2,1)}, bf16[768,768]{1,0:T(8,128)(2,1)}, u32[]{:S(2)}, u32[]{:S(2)}) collective-permute-start(bf16[768,768]{1,0:T(8,128)(2,1)} %get-tuple-element.237.down_ref), channel_id=1, source_target_pairs={{0,1},{1,0},{2,3},{3,2},{4,5},{5,4},{6,7},{7,6},{8,9},{9,8},{10,11... | collective-permute-start | bytes 3538952 | tf_op jit(solution)/shard_map/ppermute | solution.py:457
  312.3 55.1 %collective-permute-start.34 = (bf16[768,768]{1,0:T(8,128)(2,1)}, bf16[768,768]{1,0:T(8,128)(2,1)}, u32[]{:S(2)}, u32[]{:S(2)}) collective-permute-start(bf16[768,768]{1,0:T(8,128)(2,1)} %get-tuple-element.235.up_ref), channel_id=1, source_target_pairs={{0,1},{1,0},{2,3},{3,2},{4,5},{5,4},{6,7},{7,6},{8,9},{9,8},{10,11... | collective-permute-start | bytes 3538952 | tf_op jit(solution)/shard_map/ppermute | solution.py:457
  321.2 54.8 %collective-permute-start.31 = (bf16[768,768]{1,0:T(8,128)(2,1)}, bf16[768,768]{1,0:T(8,128)(2,1)}, u32[]{:S(2)}, u32[]{:S(2)}) collective-permute-start(bf16[768,768]{1,0:T(8,128)(2,1)} %collective-permute-done.30.up_ref), channel_id=1, source_target_pairs={{0,1},{1,0},{2,3},{3,2},{4,5},{5,4},{6,7},{7,6},{8,9},{9,8},{10,11... | collective-permute-start | bytes 3538952 | tf_op jit(solution)/shard_map/ppermute | solution.py:457
  346.1 30.0 %collective-permute-start.33 = (bf16[768,768]{1,0:T(8,128)(2,1)}, bf16[768,768]{1,0:T(8,128)(2,1)}, u32[]{:S(2)}, u32[]{:S(2)}) collective-permute-start(bf16[768,768]{1,0:T(8,128)(2,1)} %collective-permute-done.32.down_ref), channel_id=1, source_target_pairs={{0,1},{1,0},{2,3},{3,2},{4,5},{5,4},{6,7},{7,6},{8,9},{9,8},{10,11... | collective-permute-start | bytes 3538952 | tf_op jit(solution)/shard_map/ppermute | solution.py:457
  350.3 31.0 %collective-permute-start.24 = (bf16[384,768]{1,0:T(8,128)(2,1)}, bf16[384,768]{1,0:T(8,128)(2,1)}, u32[]{:S(2)}, u32[]{:S(2)}) collective-permute-start(bf16[384,768]{1,0:T(8,128)(2,1)} %get-tuple-element.472), channel_id=1, source_target_pairs={{16,0},{17,8},{18,4},{19,12},{20,2},{21,10},{22,6},{23,14},{24,1},... | collective-permute-start | bytes 1769480 | tf_op jit(solution)/shard_map/ppermute | solution.py:488
  388.6 42.7 %collective-permute-start.37 = (bf16[768,768]{1,0:T(8,128)(2,1)}, bf16[768,768]{1,0:T(8,128)(2,1)}, u32[]{:S(2)}, u32[]{:S(2)}) collective-permute-start(bf16[768,768]{1,0:T(8,128)(2,1)} %get-tuple-element.267), channel_id=1, source_target_pairs={{0,1},{1,0},{2,3},{3,2},{4,5},{5,4},{6,7},{7,6},{8,9},{9,8},{10,11... | collective-permute-start | bytes 3538952 | tf_op jit(solution)/shard_map/ppermute | solution.py:457
  389.1 42.2 %collective-permute-start.39 = (bf16[768,768]{1,0:T(8,128)(2,1)}, bf16[768,768]{1,0:T(8,128)(2,1)}, u32[]{:S(2)}, u32[]{:S(2)}) collective-permute-start(bf16[768,768]{1,0:T(8,128)(2,1)} %get-tuple-element.279), channel_id=1, source_target_pairs={{0,1},{1,0},{2,3},{3,2},{4,5},{5,4},{6,7},{7,6},{8,9},{9,8},{10,11... | collective-permute-start | bytes 3538952 | tf_op jit(solution)/shard_map/ppermute | solution.py:457
  422.4 40.1 %collective-permute-start.40 = (bf16[768,384]{1,0:T(8,128)(2,1)}, bf16[768,384]{1,0:T(8,128)(2,1)}, u32[]{:S(2)}, u32[]{:S(2)}) collective-permute-start(bf16[768,384]{1,0:T(8,128)(2,1)} %get-tuple-element.287), channel_id=1, source_target_pairs={{0,1},{1,0},{2,3},{3,2},{4,5},{5,4},{6,7},{7,6},{8,9},{9,8},{10,11... | collective-permute-start | bytes 1769480 | tf_op jit(solution)/shard_map/ppermute | solution.py:457
  430.7 32.2 %collective-permute-start.41 = (bf16[768,384]{1,0:T(8,128)(2,1)}, bf16[768,384]{1,0:T(8,128)(2,1)}, u32[]{:S(2)}, u32[]{:S(2)}) collective-permute-start(bf16[768,384]{1,0:T(8,128)(2,1)} %get-tuple-element.291), channel_id=1, source_target_pairs={{0,1},{1,0},{2,3},{3,2},{4,5},{5,4},{6,7},{7,6},{8,9},{9,8},{10,11... | collective-permute-start | bytes 1769480 | tf_op jit(solution)/shard_map/ppermute | solution.py:457
  430.8 50.1 %collective-permute-start.48 = (bf16[768,768]{1,0:T(8,128)(2,1)}, bf16[768,768]{1,0:T(8,128)(2,1)}, u32[]{:S(2)}, u32[]{:S(2)}) collective-permute-start(bf16[768,768]{1,0:T(8,128)(2,1)} %copy-done.102), channel_id=1, source_target_pairs={{0,1},{1,0},{2,3},{3,2},{4,5},{5,4},{6,7},{7,6},{8,9},{9,8},{10,11... | collective-permute-start | bytes 3538952 | tf_op jit(solution)/shard_map/ppermute | solution.py:457
  433.9 47.1 %collective-permute-start.49 = (bf16[768,768]{1,0:T(8,128)(2,1)}, bf16[768,768]{1,0:T(8,128)(2,1)}, u32[]{:S(2)}, u32[]{:S(2)}) collective-permute-start(bf16[768,768]{1,0:T(8,128)(2,1)} %add_convert_fusion.10), channel_id=1, source_target_pairs={{0,2},{1,3},{2,0},{3,1},{4,6},{5,7},{6,4},{7,5},{8,10},{9,11},{10,... | collective-permute-start | bytes 3538952 | tf_op jit(solution)/shard_map/ppermute | solution.py:457
  463.0 38.3 %collective-permute-start.45 = (bf16[768,768]{1,0:T(8,128)(2,1)}, bf16[768,768]{1,0:T(8,128)(2,1)S(1)}, u32[]{:S(2)}, u32[]{:S(2)}) collective-permute-start(bf16[768,768]{1,0:T(8,128)(2,1)} %get-tuple-element.321), channel_id=1, source_target_pairs={{0,1},{1,0},{2,3},{3,2},{4,5},{5,4},{6,7},{7,6},{8,9},{9,8},{10,11... | collective-permute-start | bytes 3538952 | tf_op jit(solution)/shard_map/ppermute | solution.py:457
  463.2 32.4 %collective-permute-start.46 = (bf16[768,768]{1,0:T(8,128)(2,1)}, bf16[768,768]{1,0:T(8,128)(2,1)S(1)}, u32[]{:S(2)}, u32[]{:S(2)}) collective-permute-start(bf16[768,768]{1,0:T(8,128)(2,1)} %add_convert_fusion.11), channel_id=1, source_target_pairs={{0,2},{1,3},{2,0},{3,1},{4,6},{5,7},{6,4},{7,5},{8,10},{9,11},{10,... | collective-permute-start | bytes 3538952 | tf_op jit(solution)/shard_map/ppermute | solution.py:457
  480.9 85.5 %collective-permute-start.59 = (bf16[768,768]{1,0:T(8,128)(2,1)}, bf16[768,768]{1,0:T(8,128)(2,1)}, u32[]{:S(2)}, u32[]{:S(2)}) collective-permute-start(bf16[768,768]{1,0:T(8,128)(2,1)} %get-tuple-element.374), channel_id=1, source_target_pairs={{0,1},{1,0},{2,3},{3,2},{4,5},{5,4},{6,7},{7,6},{8,9},{9,8},{10,11... | collective-permute-start | bytes 3538952 | tf_op jit(solution)/shard_map/ppermute | solution.py:457
  510.7 55.7 %collective-permute-start.60 = (bf16[768,768]{1,0:T(8,128)(2,1)}, bf16[768,768]{1,0:T(8,128)(2,1)}, u32[]{:S(2)}, u32[]{:S(2)}) collective-permute-start(bf16[768,768]{1,0:T(8,128)(2,1)} %add_convert_fusion.9), channel_id=1, source_target_pairs={{0,2},{1,3},{2,0},{3,1},{4,6},{5,7},{6,4},{7,5},{8,10},{9,11},{10,... | collective-permute-start | bytes 3538952 | tf_op jit(solution)/shard_map/ppermute | solution.py:457
  518.4 40.7 %collective-permute-start.51 = (bf16[768,768]{1,0:T(8,128)(2,1)}, bf16[768,768]{1,0:T(8,128)(2,1)}, u32[]{:S(2)}, u32[]{:S(2)}) collective-permute-start(bf16[768,768]{1,0:T(8,128)(2,1)} %get-tuple-element.335), channel_id=1, source_target_pairs={{0,1},{1,0},{2,3},{3,2},{4,5},{5,4},{6,7},{7,6},{8,9},{9,8},{10,11... | collective-permute-start | bytes 3538952 | tf_op jit(solution)/shard_map/ppermute | solution.py:457
  518.4 43.8 %collective-permute-start.53 = (bf16[768,768]{1,0:T(8,128)(2,1)}, bf16[768,768]{1,0:T(8,128)(2,1)}, u32[]{:S(2)}, u32[]{:S(2)}) collective-permute-start(bf16[768,768]{1,0:T(8,128)(2,1)} %get-tuple-element.347), channel_id=1, source_target_pairs={{0,1},{1,0},{2,3},{3,2},{4,5},{5,4},{6,7},{7,6},{8,9},{9,8},{10,11... | collective-permute-start | bytes 3538952 | tf_op jit(solution)/shard_map/ppermute | solution.py:457
  527.0 101.7 %collective-permute-start.76 = (bf16[768,768]{1,0:T(8,128)(2,1)}, bf16[768,768]{1,0:T(8,128)(2,1)}, u32[]{:S(2)}, u32[]{:S(2)}) collective-permute-start(bf16[768,768]{1,0:T(8,128)(2,1)} %get-tuple-element.323), channel_id=1, source_target_pairs={{0,1},{1,0},{2,3},{3,2},{4,5},{5,4},{6,7},{7,6},{8,9},{9,8},{10,11... | collective-permute-start | bytes 3538952 | tf_op jit(solution)/shard_map/ppermute | solution.py:457
  528.4 115.4 %reduce-scatter.7.cloned.1.call-start = ((), (), s32[]{:S(2)}) async-start(), calls=%async_computation.9 | async-start | bytes 983040 | tf_op jit(solution)/shard_map/reduce_scatter | solution.py:656
  559.1 49.7 %collective-permute-start.73 = (bf16[768,768]{1,0:T(8,128)(2,1)}, bf16[768,768]{1,0:T(8,128)(2,1)}, u32[]{:S(2)}, u32[]{:S(2)}) collective-permute-start(bf16[768,768]{1,0:T(8,128)(2,1)} %get-tuple-element.401), channel_id=1, source_target_pairs={{0,1},{1,0},{2,3},{3,2},{4,5},{5,4},{6,7},{7,6},{8,9},{9,8},{10,11... | collective-permute-start | bytes 3538952 | tf_op jit(solution)/shard_map/ppermute | solution.py:457
  562.2 46.5 %collective-permute-start.74 = (bf16[768,768]{1,0:T(8,128)(2,1)}, bf16[768,768]{1,0:T(8,128)(2,1)}, u32[]{:S(2)}, u32[]{:S(2)}) collective-permute-start(bf16[768,768]{1,0:T(8,128)(2,1)} %add_convert_fusion.6), channel_id=1, source_target_pairs={{0,2},{1,3},{2,0},{3,1},{4,6},{5,7},{6,4},{7,5},{8,10},{9,11},{10,... | collective-permute-start | bytes 3538952 | tf_op jit(solution)/shard_map/ppermute | solution.py:457
  599.3 84.4 %reduce-scatter.11.cloned.1.call-start = ((), (), s32[]{:S(2)}) async-start(), calls=%async_computation.11 | async-start | bytes 1474560 | tf_op jit(solution)/shard_map/reduce_scatter | solution.py:656
  628.6 37.1 %collective-permute-start.66 = (bf16[768,768]{1,0:T(8,128)(2,1)}, bf16[768,768]{1,0:T(8,128)(2,1)}, u32[]{:S(2)}, u32[]{:S(2)}) collective-permute-start(bf16[768,768]{1,0:T(8,128)(2,1)} %get-tuple-element.388), channel_id=1, source_target_pairs={{0,1},{1,0},{2,3},{3,2},{4,5},{5,4},{6,7},{7,6},{8,9},{9,8},{10,11... | collective-permute-start | bytes 3538952 | tf_op jit(solution)/shard_map/ppermute | solution.py:457
  632.7 33.0 %collective-permute-start.67 = (bf16[768,768]{1,0:T(8,128)(2,1)}, bf16[768,768]{1,0:T(8,128)(2,1)}, u32[]{:S(2)}, u32[]{:S(2)}) collective-permute-start(bf16[768,768]{1,0:T(8,128)(2,1)} %add_convert_fusion.4), channel_id=1, source_target_pairs={{0,2},{1,3},{2,0},{3,1},{4,6},{5,7},{6,4},{7,5},{8,10},{9,11},{10,... | collective-permute-start | bytes 3538952 | tf_op jit(solution)/shard_map/ppermute | solution.py:457
  650.2 77.4 %reduce-scatter.9.cloned.1.call-start = ((), (), s32[]{:S(2)}) async-start(), calls=%async_computation.10 | async-start | bytes 983040 | tf_op jit(solution)/shard_map/reduce_scatter | solution.py:656
  685.2 54.2 %collective-permute-start.65 = (bf16[384,768]{1,0:T(8,128)(2,1)S(1)}, bf16[384,768]{1,0:T(8,128)(2,1)}, u32[]{:S(2)}, u32[]{:S(2)}) collective-permute-start(bf16[384,768]{1,0:T(8,128)(2,1)S(1)} %copy-done.137), channel_id=1, source_target_pairs={{16,16},{17,24},{18,20},{19,28},{20,18},{21,26},{22,22},{23,30},{2... | collective-permute-start | bytes 1769480 | tf_op jit(solution)/shard_map/ppermute | solution.py:488
  686.6 54.0 %collective-permute-start.63 = (bf16[384,768]{1,0:T(8,128)(2,1)S(1)}, bf16[384,768]{1,0:T(8,128)(2,1)S(1)}, u32[]{:S(2)}, u32[]{:S(2)}) collective-permute-start(bf16[384,768]{1,0:T(8,128)(2,1)S(1)} %copy-done.137), channel_id=1, source_target_pairs={{0,16},{1,24},{2,20},{3,28},{4,18},{5,26},{6,22},{7,30},{8,17},{9,... | collective-permute-start | bytes 1769480 | tf_op jit(solution)/shard_map/ppermute | solution.py:488
  690.3 49.1 %collective-permute-start.64 = (bf16[384,768]{1,0:T(8,128)(2,1)S(1)}, bf16[384,768]{1,0:T(8,128)(2,1)}, u32[]{:S(2)}, u32[]{:S(2)}) collective-permute-start(bf16[384,768]{1,0:T(8,128)(2,1)S(1)} %copy-done.136), channel_id=1, source_target_pairs={{16,0},{17,8},{18,4},{19,12},{20,2},{21,10},{22,6},{23,14},{24,1},... | collective-permute-start | bytes 1769480 | tf_op jit(solution)/shard_map/ppermute | solution.py:488
  691.6 74.8 %collective-permute-start.62 = (bf16[384,768]{1,0:T(8,128)(2,1)S(1)}, bf16[384,768]{1,0:T(8,128)(2,1)}, u32[]{:S(2)}, u32[]{:S(2)}) collective-permute-start(bf16[384,768]{1,0:T(8,128)(2,1)S(1)} %copy-done.136), channel_id=1, source_target_pairs={{0,0},{1,8},{2,4},{3,12},{4,2},{5,10},{6,6},{7,14},{8,1},{9,9},{10... | collective-permute-start | bytes 1769480 | tf_op jit(solution)/shard_map/ppermute | solution.py:488
  740.6 30.6 %collective-permute-start.80 = (bf16[192,1536]{1,0:T(8,128)(2,1)S(1)}, bf16[192,1536]{1,0:T(8,128)(2,1)S(1)}, u32[]{:S(2)}, u32[]{:S(2)}) collective-permute-start(bf16[192,1536]{1,0:T(8,128)(2,1)S(1)} %pad_maximum_fusion.8.a_ref), channel_id=1, source_target_pairs={{0,1},{1,0},{2,3},{3,2},{4,5},{5,4},{6,7},{7,6},{8,9},{9,8},{10,11... | collective-permute-start | bytes 1769480 | tf_op jit(solution)/shard_map/ppermute | solution.py:457
  (210 other events, 1587.3 us)
Sparse Core Ops, SparseCore 0:
  23.2 56.9 all-gather.4
  82.3 36.1 all-gather.10
  120.7 29.5 all-gather.8
  157.2 28.7 all-gather.6
  528.5 30.2 reduce-scatter.4
  599.4 20.2 reduce-scatter.6
  650.4 26.1 reduce-scatter.10
  683.8 43.7 reduce-scatter.8

commit v6 on v5

--- a/solution.py
+++ b/solution.py
@@ -555,11 +555,17 @@
     own_down = after(own_down, own_up)
     proj_one = after(proj_one, own_down)
     own_up, own_down, proj_one = gathered(own_up), gathered(own_down), gathered(proj_one)
-    other_up, other_down = swap_sections(own_up), swap_sections(own_down)
 
     def head_weights(block):
         pieces = spread(block, across(block, 2))
         return pieces, jnp.concatenate(in_order([piece[:, 3 * wide:] for piece in pieces], quarter), 1)
+
+    def two_swapped(own, far):
+        return own, far, [swap_sections(own), swap_sections(far)]
+
+    def two_layers(own, far, others):
+        near, away = by_layer(own, others[0]), by_layer(far, others[1])
+        return (near[0], away[0]), (near[1], away[1])
 
     heads_by_layer = [head_weights(proj_zero), None]
     hidden_by_layer = [None, None]
@@ -600,49 +606,47 @@
             other_kv[p ^ 1] = across(own_qkv[p][:, :2 * wide], 1)
         outs, weights, inverses = {}, {}, {}
         late = {}
+        if layer == 0:
+            late["up_far"] = across(after(own_up, own_qkv[0]), 2)
         for step, p in enumerate(order):
-            own = own_qkv[p]
-            if layer == 0 and step == 3:
-                own = after(own, proj_one)
-            outs[p], weights[p], inverses[p] = attend(own, other_kv[p], key_bias, heads, frames)
+            outs[p], weights[p], inverses[p] = attend(own_qkv[p], other_kv[p], key_bias, heads, frames)
             if layer == 0 and step == 0:
-                late["up"] = by_layer(own_up, after(other_up, outs[p]))
-                late["up_far"] = across(late["up"][0], 2)
-            elif layer == 0 and step == 1:
-                late["down"] = by_layer(own_down, after(other_down, outs[p]))
-                late["down_far"] = across(late["down"][0], 2)
+                late["up"] = two_swapped(after(own_up, outs[p]), after(late["up_far"], outs[p]))
+                late["down_far"] = across(after(own_down, outs[p]), 2)
             elif layer == 0 and step == 2:
-                w_up = spread(late["up"][0], after(late["up_far"], outs[p]))
-                late["one_far"] = across(after(proj_one, outs[p]), 2)
+                late["down"] = two_swapped(own_down, after(late["down_far"], outs[p]))
             elif layer == 0 and step == 3:
-                w_down = spread(late["down"][0], after(late["down_far"], outs[p]))
-                hidden_by_layer[0] = (w_up, w_down)
-            elif layer == 1 and step == 0:
-                late["down_far"] = across(after(pending_one["down"], outs[p]), 2)
+                own, far, others = late["up"]
+                late["up"] = two_layers(own, far, [after(other, outs[p]) for other in others])
+                late["up_near"] = [across(piece, 1) for piece in late["up"][0]]
             elif layer == 1 and step == 1:
                 cot = after(edges_here, outs[p])
                 pending_one["cot"] = [transposed(cot[0], 1, 0), transposed(cot[1], 1, 1)]
-                w_up = spread(pending_one["up"], after(pending_one["up_far"], outs[p]))
-            elif layer == 1 and step == 3:
-                w_down = spread(pending_one["down"], after(late["down_far"], outs[p]))
-                hidden_by_layer[1] = (w_up, w_down)
-        attended, middle, normed_two = out_part(quarter, [outs[p] for p in range(QUARTERS)], w_out, x_low, vec)
+        skip = after(x_low, proj_one) if layer == 0 else x_low
+        attended, middle, normed_two = out_part(quarter, [outs[p] for p in range(QUARTERS)], w_out, skip, vec)
+        if layer == 0:
+            own, far, others = late["down"]
+            late["down"] = two_layers(own, far, [after(other, middle) for other in others])
+            late["down_near"] = [across(piece, 1) for piece in late["down"][0]]
+            late["one_far"] = across(after(proj_one, middle), 2)
+            hidden_by_layer[0] = [
+                [pieces[0], near[0], pieces[1], near[1]]
+                for pieces, near in ((late[name][0], late[name + "_near"]) for name in ("up", "down"))
+            ]
         w_up, w_down = hidden_by_layer[layer]
         bias_up = vec[8:].reshape(shards, QUARTERS, unit)
-        acts, slopes = [], []
+        acts, slopes = {}, {}
         result = middle + vec[7]
-        for p in range(QUARTERS):
+        for step, p in enumerate((0, 2, 1, 3)):
             bias = lax.dynamic_index_in_dim(bias_up, quarter ^ p, 1, keepdims=False).reshape(1, shards * unit)
-            act, slope, result = mlp_part(normed_two, w_up[p], bias, w_down[p], result)
-            acts.append(act)
-            slopes.append(slope)
-            if layer == 0 and p == 0:
-                far = after(late["one_far"], act)
-                pieces = spread(proj_one, far)
+            acts[p], slopes[p], result = mlp_part(normed_two, w_up[p], bias, w_down[p], result)
+            if layer == 0 and step == 1:
+                pieces = spread(proj_one, after(late["one_far"], acts[p]))
                 w_out_one = jnp.concatenate(in_order([piece[:, 3 * wide:] for piece in pieces], quarter), 1)
                 heads_by_layer[1] = (pieces, w_out_one)
-                pending_one["up"], pending_one["down"] = late["up"][1], late["down"][1]
-                pending_one["up_far"] = across(after(pending_one["up"], far), 2)
+            elif layer == 0 and step == 2:
+                ones = [[after(piece, acts[p]) for piece in late[name][1]] for name in ("up", "down")]
+                hidden_by_layer[1] = [[a, across(a, 1), b, across(b, 1)] for a, b in ones]
         kept = (x_low, normed, own_qkv, other_kv, weights, inverses, attended, middle, normed_two, acts, slopes)
         return result.astype(BF16), kept
 
@@ -655,10 +659,14 @@
             bit *= 2
         return lax.psum_scatter(block, "shard", scatter_dimension=0, tiled=True)
 
-    def half_sum(block):
+    def half_parts(block):
         cut = block.shape[1] // 2
         left, right = block[:, :cut], block[:, cut:]
-        return low_sum(jnp.where(first, left, right), swap_sections(jnp.where(first, right, left)))
+        return jnp.where(first, left, right), jnp.where(first, right, left)
+
+    def half_sum(block):
+        kept_half, sent = half_parts(block)
+        return low_sum(kept_half, swap_sections(sent))
 
     def backward(cot, layer, kept, above):
         (proj, w_out), (w_up, w_down), vec = heads_by_layer[layer], hidden_by_layer[layer], vec_by_layer[layer]
@@ -680,16 +688,21 @@
         if above is not None:
             far = after(above["far_proj"], mid_rows)
             above["half"] = half_sum(above["finish"](far))
-        far_down = low_sum(g_down[2], after(near_down[2], mid_rows))
+
+        def chip_halves(grads, near, token):
+            return [half_parts(low_sum(grads[p], after(near[p], token))) for p in (0, 2)]
+
+        down = chip_halves(g_down, near_down, mid_rows)
+        up = None
         results = {}
         for step, p in enumerate(order):
             head = d_heads[p]
             if step == 1:
-                head = after(head, far_down)
-                far_down = across(far_down, 2)
+                head = after(head, *[sent for _, sent in down])
+                down = [(kept_half, swap_sections(sent)) for kept_half, sent in down]
             elif step == 2:
-                head = after(head, far_up)
-                far_up = across(far_up, 2)
+                head = after(head, *[sent for _, sent in up])
+                up = [(kept_half, swap_sections(sent)) for kept_half, sent in up]
                 if above is not None:
                     half = after(above["half"], results[order[1]][0])
                     above["proj"] = scattered(jnp.concatenate([half, above["vec"]], 1))
@@ -697,10 +710,14 @@
                 head = after(head, above["mlp"])
             results[p] = attend_back(own_qkv[p], other_kv[p], weights[p], inverses[p], head, heads, frames)
             if step == 0:
-                far_up = low_sum(g_up[2], after(near_up[2], results[p][0]))
-        last = results[order[3]][0]
+                up = chip_halves(g_up, near_up, results[p][0])
+            elif step == 2:
+                down = [low_sum(a, after(b, results[p][0])) for a, b in down]
+                down[1] = across(down[1], 2)
+            elif step == 3:
+                up = [low_sum(a, after(b, results[p][0])) for a, b in up]
+                up[1] = across(up[1], 2)
         from_other = {p: across(results[p ^ 1][2], 1) for p in range(QUARTERS)}
-        half_down = half_sum(low_sum(g_down[0], near_down[0], after(far_down, last)))
         g_proj, sums_in, near_proj = {}, {}, {}
         d_normed = jnp.zeros(normed.shape, F32)
         for p in order:
@@ -715,7 +732,8 @@
             cut = block.shape[0] // 2
             block = block[:cut] + across(block[cut:].astype(BF16), bit).astype(F32)
             bit //= 2
-        half_up = half_sum(low_sum(g_up[0], near_up[0], after(far_up, d_normed)))
+        half_down = low_sum(down[0], after(down[1], d_normed))
+        half_up = low_sum(up[0], after(up[1], d_normed))
         if layer == 1:
             far_proj = low_sum(g_proj[2], after(near_proj[2], block))
         else:

time: 792 us -> 902 us (1.14)
  waiting for transfers between devices: 242 us -> 300 us
  local copies, waits for them, and re-layouts: 75.3 us -> 96.4 us
  other arithmetic: 68.2 us -> 87 us
    ppermute x12 -> x18, waiting for transfers between devices: 33.1 us -> 118 us  [swap_sections(): return lax.ppermute(block, 'section', [(0, 1), (1, 0)])]
    ppermute x62 -> x60, waiting for transfers between devices: 141 us -> 105 us  [across(): return lax.ppermute(block, 'replica', [(i, i ^ bit) for i in range(count)])]
    unnamed x340 -> x378, local copies, waits for them, and re-layouts: 44.2 us -> 54.9 us
    ppermute x12 -> x18, starting transfers between devices: 21.7 us -> 30.9 us  [swap_sections(): return lax.ppermute(block, 'section', [(0, 1), (1, 0)])]
    convert_element_type x19 -> x23, other arithmetic: 27.2 us -> 31.9 us  [low_sum(): return total.astype(BF16)]
    ppermute x62 -> x60, starting transfers between devices: 93.5 us -> 88.9 us  [across(): return lax.ppermute(block, 'replica', [(i, i ^ bit) for i in range(count)])]
  transfers between devices with their start and end apart: 91 -> 95, of which waited for: 23 -> 24; matrix products, arithmetic and copies ran while one was open for 14% -> 16% of each run, Pallas kernels for 28% -> 25%
where the time goes in v6:
time: 902 us; the launch traced here: 890 us
  waiting for transfers between devices  300 us (33%)
  Pallas kernels  233 us (26%)
  starting transfers between devices  139 us (15%)
  local copies, waits for them, and re-layouts  96.4 us (11%)
  other arithmetic  87 us (10%)
  matrix products  18.1 us (2%)
  between operations  16.6 us (2%)
    ppermute x18, waiting for transfers between devices, swap_sections(): return lax.ppermute(block, 'section', [(0, 1), (1, 0)])  118 us
    ppermute x60, waiting for transfers between devices, across(): return lax.ppermute(block, 'replica', [(i, i ^ bit) for i in range(count)])  105 us
    ppermute x60, starting transfers between devices, across(): return lax.ppermute(block, 'replica', [(i, i ^ bit) for i in range(count)])  88.9 us
    pallas_call x8, Pallas kernels, attend_back(): pl.pallas_call(functools.partial(attend_back_kernel, heads=heads, frames=...  64.3 us
    unnamed x378, local copies, waits for them, and re-layouts  54.9 us
    pallas_call x8, Pallas kernels, attend(): pl.pallas_call(functools.partial(attend_kernel, heads=heads, frames=frame...  51.4 us
    pallas_call x8, Pallas kernels, mlp_back_part(): pl.pallas_call(mlp_back_kernel, grid=(columns // tile,), in_specs=[whole,...  42.3 us
    all_gather x4, waiting for transfers between devices, gathered(): return lax.all_gather(block, 'shard', axis=0, tiled=True)  40.8 us
  transfers between devices with their start and end apart: 95, of which 24 were waited for; matrix products, arithmetic and copies ran while one was open for 16% of the time, Pallas kernels for 25%

profile of v6, /device:TPU:0, one launch (start us, length us, event | category | flops | bytes accessed | tf_op | source)
XLA Modules:
  0.0 890.3 jit_solution(10032536496152197214)
XLA Ops:
  15.1 7.0 collective-permute-done.4
  24.2 5.9 collective-permute-start
  47.1 49.3 %collective-permute-start.2 = (bf16[384,768]{1,0:T(8,128)(2,1)S(1)}, bf16[384,768]{1,0:T(8,128)(2,1)S(1)}, u32[]{:S(2)}, u32[]{:S(2)}) collective-permute-start(bf16[384,768]{1,0:T(8,128)(2,1)S(1)} %get-tuple-element.232.x_ref), channel_id=1, source_target_pairs={{0,2},{1,3},{2,0},{3,1},{4,6},{5,7},{6,4},{7,5},{8,10},{9,11},{10,... | collective-permute-start | bytes 1769480 | tf_op jit(solution)/shard_map/ppermute | solution.py:457
  110.6 7.9 all-gather.9.cloned.1.call-done
  120.0 13.8 %collective-permute-done.9.weight_ref = bf16[768,768]{1,0:T(8,128)(2,1)} collective-permute-done((bf16[768,768]{1,0:T(8,128)(2,1)}, bf16[768,768]{1,0:T(8,128)(2,1)}, u32[]{:S(2)}, u32[]{:S(2)}) %collective-permute-start.9) | collective-permute-done | bytes 1179680 | tf_op jit(solution)/shard_map/ppermute | solution.py:457
  142.6 7.7 all-gather.7.cloned.1.call-done.weight_ref
  150.3 6.4 attend.8
  156.7 25.2 %all-gather.11.cloned.1.call-done = bf16[768,768]{1,0:T(8,128)(2,1)} async-done(((bf16[192,768]{1,0:T(8,128)(2,1)}), bf16[768,768]{1,0:T(8,128)(2,1)}) %all-gather.11.cloned.1.call-update) | async-done | bytes 1179664 | tf_op jit(solution)/shard_map/all_gather | solution.py:542
  191.2 6.4 attend.9
  200.9 6.3 attend.11
  207.2 6.7 attend.10
  218.4 21.9 %collective-permute-done.19 = bf16[768,768]{1,0:T(8,128)(2,1)} collective-permute-done((bf16[768,768]{1,0:T(8,128)(2,1)}, bf16[768,768]{1,0:T(8,128)(2,1)}, u32[]{:S(2)}, u32[]{:S(2)}) %collective-permute-start.19) | collective-permute-done | bytes 1179680 | tf_op jit(solution)/shard_map/ppermute | solution.py:461
  244.5 21.0 %collective-permute-done.21 = bf16[768,768]{1,0:T(8,128)(2,1)} collective-permute-done((bf16[768,768]{1,0:T(8,128)(2,1)}, bf16[768,768]{1,0:T(8,128)(2,1)}, u32[]{:S(2)}, u32[]{:S(2)}) %collective-permute-start.21) | collective-permute-done | bytes 1179680 | tf_op jit(solution)/shard_map/ppermute | solution.py:461
  269.3 20.9 %collective-permute-done.17 = bf16[768,768]{1,0:T(8,128)(2,1)S(1)} collective-permute-done((bf16[768,768]{1,0:T(8,128)(2,1)}, bf16[768,768]{1,0:T(8,128)(2,1)S(1)}, u32[]{:S(2)}, u32[]{:S(2)}) %collective-permute-start.17) | collective-permute-done | bytes 1179680 | tf_op jit(solution)/shard_map/ppermute | solution.py:461
  343.8 10.7 %collective-permute-done.23 = bf16[384,768]{1,0:T(8,128)(2,1)S(1)} collective-permute-done((bf16[384,768]{1,0:T(8,128)(2,1)S(1)}, bf16[384,768]{1,0:T(8,128)(2,1)S(1)}, u32[]{:S(2)}, u32[]{:S(2)}) %collective-permute-start.23) | collective-permute-done | bytes 589856 | tf_op jit(solution)/shard_map/ppermute | solution.py:457
  370.9 6.3 attend.12
  377.2 6.6 attend.13
  384.3 6.3 attend.14
  394.4 6.4 attend.15
  426.2 6.1 mlp_back_part.8
  432.3 5.7 mlp_back_part.9
  458.5 8.0 attend_back.10
  466.6 7.8 attend_back.8
  485.0 8.0 attend_back.11
  496.9 8.2 attend_back.9
  505.6 5.4 collective-permute-start.51
  530.0 8.2 collective-permute-start.45
  540.1 10.5 %collective-permute-done.48 = bf16[768,384]{1,0:T(8,128)(2,1)S(1)} collective-permute-done((bf16[768,384]{1,0:T(8,128)(2,1)S(1)}, bf16[768,384]{1,0:T(8,128)(2,1)S(1)}, u32[]{:S(2)}, u32[]{:S(2)}) %collective-permute-start.48) | collective-permute-done | bytes 589856 | tf_op jit(solution)/shard_map/ppermute | solution.py:461
  550.8 8.2 collective-permute-start.49
  565.1 11.1 %collective-permute-done.49 = bf16[768,384]{1,0:T(8,128)(2,1)S(1)} collective-permute-done((bf16[768,384]{1,0:T(8,128)(2,1)S(1)}, bf16[768,384]{1,0:T(8,128)(2,1)S(1)}, u32[]{:S(2)}, u32[]{:S(2)}) %collective-permute-start.49) | collective-permute-done | bytes 589856 | tf_op jit(solution)/shard_map/ppermute | solution.py:457
  580.4 6.0 mlp_back_part.12
  586.5 5.8 mlp_back_part.13
  601.4 4.7 mlp_back_part.14
  607.2 4.8 mlp_back_part.15
  620.8 8.0 attend_back.14
  644.7 12.2 %collective-permute-done.64 = bf16[768,768]{1,0:T(8,128)(2,1)S(1)} collective-permute-done((bf16[768,768]{1,0:T(8,128)(2,1)}, bf16[768,768]{1,0:T(8,128)(2,1)S(1)}, u32[]{:S(2)}, u32[]{:S(2)}) %collective-permute-start.64) | collective-permute-done | bytes 1179680 | tf_op jit(solution)/shard_map/ppermute | solution.py:457
  658.6 8.1 attend_back.15
  669.9 7.9 attend_back.13
  681.0 8.4 attend_back.12
  689.4 9.4 %collective-permute-done.65 = bf16[768,384]{1,0:T(8,128)(2,1)S(1)} collective-permute-done((bf16[768,384]{1,0:T(8,128)(2,1)}, bf16[768,384]{1,0:T(8,128)(2,1)S(1)}, u32[]{:S(2)}, u32[]{:S(2)}) %collective-permute-start.65) | collective-permute-done | bytes 589856 | tf_op jit(solution)/shard_map/ppermute | solution.py:461
  728.4 8.1 collective-permute-done.82
  743.4 5.6 collective-permute-done.61
  753.8 20.2 %collective-permute-done.71 = bf16[768,768]{1,0:T(8,128)(2,1)} collective-permute-done((bf16[768,768]{1,0:T(8,128)(2,1)}, bf16[768,768]{1,0:T(8,128)(2,1)}, u32[]{:S(2)}, u32[]{:S(2)}) %collective-permute-start.71) | collective-permute-done | bytes 1179680 | tf_op jit(solution)/shard_map/ppermute | solution.py:457
  778.2 12.9 %collective-permute-done.72 = bf16[768,384]{1,0:T(8,128)(2,1)S(1)} collective-permute-done((bf16[768,384]{1,0:T(8,128)(2,1)S(1)}, bf16[768,384]{1,0:T(8,128)(2,1)S(1)}, u32[]{:S(2)}, u32[]{:S(2)}) %collective-permute-start.72) | collective-permute-done | bytes 589856 | tf_op jit(solution)/shard_map/ppermute | solution.py:461
  802.0 35.4 %reduce-scatter.9.cloned.1.call-done = bf16[192,512]{1,0:T(8,128)(2,1)} async-done(((bf16[768,512]{1,0:T(8,128)(2,1)}), bf16[192,512]{1,0:T(8,128)(2,1)}) %reduce-scatter.9.cloned.1.call-update) | async-done | bytes 196624 | tf_op jit(solution)/shard_map/reduce_scatter | solution.py:660
  843.1 10.7 %collective-permute-done.73 = bf16[192,512]{1,0:T(8,128)(2,1)S(1)} collective-permute-done((bf16[192,512]{1,0:T(8,128)(2,1)S(1)}, bf16[192,512]{1,0:T(8,128)(2,1)S(1)}, u32[]{:S(2)}, u32[]{:S(2)}) %collective-permute-start.73) | collective-permute-done | bytes 196640 | tf_op jit(solution)/shard_map/ppermute | solution.py:461
  857.8 12.3 %collective-permute-done.85.c_ref = bf16[192,1536]{1,0:T(8,128)(2,1)S(1)} collective-permute-done((bf16[192,1536]{1,0:T(8,128)(2,1)S(1)}, bf16[192,1536]{1,0:T(8,128)(2,1)S(1)}, u32[]{:S(2)}, u32[]{:S(2)}) %collective-permute-start.85) | collective-permute-done | bytes 589856 | tf_op jit(solution)/shard_map/ppermute | solution.py:457
  870.1 5.7 collective-permute-done.75.c_ref
  (736 shorter events, 357.6 us)
Async XLA Ops:
  7.2 97.3 %all-gather.5.cloned.1.call-start = ((), (), s32[]{:S(2)}) async-start(), calls=%async_computation.4 | async-start | bytes 1474560 | tf_op jit(solution)/shard_map/all_gather | solution.py:542
  23.1 95.4 %all-gather.9.cloned.1.call-start = ((), (), s32[]{:S(2)}) async-start(), calls=%async_computation.6 | async-start | bytes 1474560 | tf_op jit(solution)/shard_map/all_gather | solution.py:542
  41.8 108.5 %all-gather.7.cloned.1.call-start = ((), (), s32[]{:S(2)}) async-start(), calls=%async_computation.5 | async-start | bytes 1474560 | tf_op jit(solution)/shard_map/all_gather | solution.py:542
  42.6 139.3 %all-gather.11.cloned.1.call-start = ((), (), s32[]{:S(2)}) async-start(), calls=%async_computation.7 | async-start | bytes 1474560 | tf_op jit(solution)/shard_map/all_gather | solution.py:542
  42.7 53.6 %collective-permute-start.3 = (f32[12,768]{1,0:T(8,128)S(1)}, f32[12,768]{1,0:T(8,128)S(1)}, u32[]{:S(2)}, u32[]{:S(2)}) collective-permute-start(f32[12,768]{1,0:T(8,128)S(1)} %bitcast.65), channel_id=1, source_target_pairs={{0,16},{16,0},{1,17},{17,1},{2,18},{18,2},{3,19},{19,3},{4,20},{20... | collective-permute-start | bytes 110600 | tf_op jit(solution)/shard_map/ppermute | solution.py:461
  45.1 92.4 %collective-permute-start.7 = (f32[1,1536]{1,0:T(1,128)}, f32[1,1536]{1,0:T(1,128)}, u32[]{:S(2)}, u32[]{:S(2)}) collective-permute-start(f32[1,1536]{1,0:T(1,128)} %fusion.44), channel_id=1, source_target_pairs={{0,0},{16,16},{1,8},{17,24},{2,4},{18,20},{3,12},{19,28},{4,2},{20... | collective-permute-start | bytes 18440 | tf_op jit(solution)/shard_map/ppermute | solution.py:488
  47.1 57.1 %collective-permute-start.2 = (bf16[384,768]{1,0:T(8,128)(2,1)S(1)}, bf16[384,768]{1,0:T(8,128)(2,1)S(1)}, u32[]{:S(2)}, u32[]{:S(2)}) collective-permute-start(bf16[384,768]{1,0:T(8,128)(2,1)S(1)} %get-tuple-element.232.x_ref), channel_id=1, source_target_pairs={{0,2},{1,3},{2,0},{3,1},{4,6},{5,7},{6,4},{7,5},{8,10},{9,11},{10,... | collective-permute-start | bytes 1769480 | tf_op jit(solution)/shard_map/ppermute | solution.py:457
  100.0 580.9 %reduce-scatter.5.cloned.1.call-start = ((), (), s32[]{:S(2)}) async-start(), calls=%async_computation.8 | async-start | bytes 1474560 | tf_op jit(solution)/shard_map/reduce_scatter | solution.py:660
  118.5 67.3 %collective-permute-start.13 = (bf16[768,768]{1,0:T(8,128)(2,1)}, bf16[768,768]{1,0:T(8,128)(2,1)}, u32[]{:S(2)}, u32[]{:S(2)}) collective-permute-start(bf16[768,768]{1,0:T(8,128)(2,1)} %all-gather.9.cloned.1.call-done), channel_id=1, source_target_pairs={{0,2},{1,3},{2,0},{3,1},{4,6},{5,7},{6,4},{7,5},{8,10},{9,11},{10,... | collective-permute-start | bytes 3538952 | tf_op jit(solution)/shard_map/ppermute | solution.py:457
  133.8 53.5 %collective-permute-start.10 = (bf16[768,768]{1,0:T(8,128)(2,1)}, bf16[768,768]{1,0:T(8,128)(2,1)}, u32[]{:S(2)}, u32[]{:S(2)}) collective-permute-start(bf16[768,768]{1,0:T(8,128)(2,1)} %collective-permute-done.9.weight_ref), channel_id=1, source_target_pairs={{0,1},{1,0},{2,3},{3,2},{4,5},{5,4},{6,7},{7,6},{8,9},{9,8},{10,11... | collective-permute-start | bytes 3538952 | tf_op jit(solution)/shard_map/ppermute | solution.py:457
  142.1 49.1 %collective-permute-start.8 = (bf16[768,384]{1,0:T(8,128)(2,1)}, bf16[768,384]{1,0:T(8,128)(2,1)}, u32[]{:S(2)}, u32[]{:S(2)}) collective-permute-start(bf16[768,384]{1,0:T(8,128)(2,1)} %slice.320), channel_id=1, source_target_pairs={{0,1},{1,0},{2,3},{3,2},{4,5},{5,4},{6,7},{7,6},{8,9},{9,8},{10,11... | collective-permute-start | bytes 1769480 | tf_op jit(solution)/shard_map/ppermute | solution.py:457
  187.3 52.9 %collective-permute-start.19 = (bf16[768,768]{1,0:T(8,128)(2,1)}, bf16[768,768]{1,0:T(8,128)(2,1)}, u32[]{:S(2)}, u32[]{:S(2)}) collective-permute-start(bf16[768,768]{1,0:T(8,128)(2,1)} %all-gather.9.cloned.1.call-done), channel_id=1, source_target_pairs={{0,16},{16,0},{1,17},{17,1},{2,18},{18,2},{3,19},{19,3},{4,20},{20... | collective-permute-start | bytes 3538952 | tf_op jit(solution)/shard_map/ppermute | solution.py:461
  199.4 66.1 %collective-permute-start.21 = (bf16[768,768]{1,0:T(8,128)(2,1)}, bf16[768,768]{1,0:T(8,128)(2,1)}, u32[]{:S(2)}, u32[]{:S(2)}) collective-permute-start(bf16[768,768]{1,0:T(8,128)(2,1)} %all-gather.11.cloned.1.call-done), channel_id=1, source_target_pairs={{0,16},{16,0},{1,17},{17,1},{2,18},{18,2},{3,19},{19,3},{4,20},{20... | collective-permute-start | bytes 3538952 | tf_op jit(solution)/shard_map/ppermute | solution.py:461
  214.0 76.2 %collective-permute-start.17 = (bf16[768,768]{1,0:T(8,128)(2,1)}, bf16[768,768]{1,0:T(8,128)(2,1)S(1)}, u32[]{:S(2)}, u32[]{:S(2)}) collective-permute-start(bf16[768,768]{1,0:T(8,128)(2,1)} %collective-permute-done.16), channel_id=1, source_target_pairs={{0,16},{16,0},{1,17},{17,1},{2,18},{18,2},{3,19},{19,3},{4,20},{20... | collective-permute-start | bytes 3538952 | tf_op jit(solution)/shard_map/ppermute | solution.py:461
  218.3 115.8 %collective-permute-start.15 = (bf16[768,768]{1,0:T(8,128)(2,1)}, bf16[768,768]{1,0:T(8,128)(2,1)}, u32[]{:S(2)}, u32[]{:S(2)}) collective-permute-start(bf16[768,768]{1,0:T(8,128)(2,1)} %get-tuple-element.508.up_ref), channel_id=1, source_target_pairs={{0,1},{1,0},{2,3},{3,2},{4,5},{5,4},{6,7},{7,6},{8,9},{9,8},{10,11... | collective-permute-start | bytes 3538952 | tf_op jit(solution)/shard_map/ppermute | solution.py:457
  243.4 71.8 %collective-permute-start.20 = (bf16[768,768]{1,0:T(8,128)(2,1)}, bf16[768,768]{1,0:T(8,128)(2,1)}, u32[]{:S(2)}, u32[]{:S(2)}) collective-permute-start(bf16[768,768]{1,0:T(8,128)(2,1)} %get-tuple-element.504.up_ref), channel_id=1, source_target_pairs={{0,1},{1,0},{2,3},{3,2},{4,5},{5,4},{6,7},{7,6},{8,9},{9,8},{10,11... | collective-permute-start | bytes 3538952 | tf_op jit(solution)/shard_map/ppermute | solution.py:457
  265.5 49.2 %collective-permute-start.28 = (bf16[768,768]{1,0:T(8,128)(2,1)}, bf16[768,768]{1,0:T(8,128)(2,1)}, u32[]{:S(2)}, u32[]{:S(2)}) collective-permute-start(bf16[768,768]{1,0:T(8,128)(2,1)} %all-gather.7.cloned.1.call-done.weight_ref), channel_id=1, source_target_pairs={{0,2},{1,3},{2,0},{3,1},{4,6},{5,7},{6,4},{7,5},{8,10},{9,11},{10,... | collective-permute-start | bytes 3538952 | tf_op jit(solution)/shard_map/ppermute | solution.py:457
  269.3 55.8 %collective-permute-start.22 = (bf16[768,768]{1,0:T(8,128)(2,1)}, bf16[768,768]{1,0:T(8,128)(2,1)}, u32[]{:S(2)}, u32[]{:S(2)}) collective-permute-start(bf16[768,768]{1,0:T(8,128)(2,1)} %get-tuple-element.502.down_ref), channel_id=1, source_target_pairs={{0,1},{1,0},{2,3},{3,2},{4,5},{5,4},{6,7},{7,6},{8,9},{9,8},{10,11... | collective-permute-start | bytes 3538952 | tf_op jit(solution)/shard_map/ppermute | solution.py:457
  293.1 41.1 %collective-permute-start.18 = (bf16[768,768]{1,0:T(8,128)(2,1)}, bf16[768,768]{1,0:T(8,128)(2,1)}, u32[]{:S(2)}, u32[]{:S(2)}) collective-permute-start(bf16[768,768]{1,0:T(8,128)(2,1)} %get-tuple-element.506.down_ref), channel_id=1, source_target_pairs={{0,1},{1,0},{2,3},{3,2},{4,5},{5,4},{6,7},{7,6},{8,9},{9,8},{10,11... | collective-permute-start | bytes 3538952 | tf_op jit(solution)/shard_map/ppermute | solution.py:457
  339.7 80.1 %collective-permute-start.32 = (bf16[768,768]{1,0:T(8,128)(2,1)}, bf16[768,768]{1,0:T(8,128)(2,1)}, u32[]{:S(2)}, u32[]{:S(2)}) collective-permute-start(bf16[768,768]{1,0:T(8,128)(2,1)} %get-tuple-element.258.up_ref), channel_id=1, source_target_pairs={{0,1},{1,0},{2,3},{3,2},{4,5},{5,4},{6,7},{7,6},{8,9},{9,8},{10,11... | collective-permute-start | bytes 3538952 | tf_op jit(solution)/shard_map/ppermute | solution.py:457
  340.1 65.8 %collective-permute-start.34 = (bf16[768,768]{1,0:T(8,128)(2,1)}, bf16[768,768]{1,0:T(8,128)(2,1)}, u32[]{:S(2)}, u32[]{:S(2)}) collective-permute-start(bf16[768,768]{1,0:T(8,128)(2,1)} %get-tuple-element.260.up_ref), channel_id=1, source_target_pairs={{0,1},{1,0},{2,3},{3,2},{4,5},{5,4},{6,7},{7,6},{8,9},{9,8},{10,11... | collective-permute-start | bytes 3538952 | tf_op jit(solution)/shard_map/ppermute | solution.py:457
  370.4 45.1 %collective-permute-start.35 = (bf16[768,768]{1,0:T(8,128)(2,1)}, bf16[768,768]{1,0:T(8,128)(2,1)}, u32[]{:S(2)}, u32[]{:S(2)}) collective-permute-start(bf16[768,768]{1,0:T(8,128)(2,1)} %get-tuple-element.261.down_ref), channel_id=1, source_target_pairs={{0,1},{1,0},{2,3},{3,2},{4,5},{5,4},{6,7},{7,6},{8,9},{9,8},{10,11... | collective-permute-start | bytes 3538952 | tf_op jit(solution)/shard_map/ppermute | solution.py:457
  383.8 36.0 %collective-permute-start.33 = (bf16[768,768]{1,0:T(8,128)(2,1)}, bf16[768,768]{1,0:T(8,128)(2,1)}, u32[]{:S(2)}, u32[]{:S(2)}) collective-permute-start(bf16[768,768]{1,0:T(8,128)(2,1)} %get-tuple-element.259.down_ref), channel_id=1, source_target_pairs={{0,1},{1,0},{2,3},{3,2},{4,5},{5,4},{6,7},{7,6},{8,9},{9,8},{10,11... | collective-permute-start | bytes 3538952 | tf_op jit(solution)/shard_map/ppermute | solution.py:457
  438.0 36.3 %collective-permute-start.37 = (bf16[768,768]{1,0:T(8,128)(2,1)}, bf16[768,768]{1,0:T(8,128)(2,1)}, u32[]{:S(2)}, u32[]{:S(2)}) collective-permute-start(bf16[768,768]{1,0:T(8,128)(2,1)} %get-tuple-element.290), channel_id=1, source_target_pairs={{0,1},{1,0},{2,3},{3,2},{4,5},{5,4},{6,7},{7,6},{8,9},{9,8},{10,11... | collective-permute-start | bytes 3538952 | tf_op jit(solution)/shard_map/ppermute | solution.py:457
  438.1 36.7 %collective-permute-start.38 = (bf16[768,768]{1,0:T(8,128)(2,1)}, bf16[768,768]{1,0:T(8,128)(2,1)}, u32[]{:S(2)}, u32[]{:S(2)}) collective-permute-start(bf16[768,768]{1,0:T(8,128)(2,1)} %get-tuple-element.294), channel_id=1, source_target_pairs={{0,1},{1,0},{2,3},{3,2},{4,5},{5,4},{6,7},{7,6},{8,9},{9,8},{10,11... | collective-permute-start | bytes 3538952 | tf_op jit(solution)/shard_map/ppermute | solution.py:457
  438.6 36.2 %collective-permute-start.40 = (bf16[768,768]{1,0:T(8,128)(2,1)}, bf16[768,768]{1,0:T(8,128)(2,1)}, u32[]{:S(2)}, u32[]{:S(2)}) collective-permute-start(bf16[768,768]{1,0:T(8,128)(2,1)} %get-tuple-element.305), channel_id=1, source_target_pairs={{0,1},{1,0},{2,3},{3,2},{4,5},{5,4},{6,7},{7,6},{8,9},{9,8},{10,11... | collective-permute-start | bytes 3538952 | tf_op jit(solution)/shard_map/ppermute | solution.py:457
  439.2 42.0 %collective-permute-start.41 = (bf16[768,768]{1,0:T(8,128)(2,1)}, bf16[768,768]{1,0:T(8,128)(2,1)}, u32[]{:S(2)}, u32[]{:S(2)}) collective-permute-start(bf16[768,768]{1,0:T(8,128)(2,1)} %get-tuple-element.312), channel_id=1, source_target_pairs={{0,1},{1,0},{2,3},{3,2},{4,5},{5,4},{6,7},{7,6},{8,9},{9,8},{10,11... | collective-permute-start | bytes 3538952 | tf_op jit(solution)/shard_map/ppermute | solution.py:457
  466.5 56.3 %collective-permute-start.42 = (bf16[768,384]{1,0:T(8,128)(2,1)}, bf16[768,384]{1,0:T(8,128)(2,1)}, u32[]{:S(2)}, u32[]{:S(2)}) collective-permute-start(bf16[768,384]{1,0:T(8,128)(2,1)} %get-tuple-element.316), channel_id=1, source_target_pairs={{0,1},{1,0},{2,3},{3,2},{4,5},{5,4},{6,7},{7,6},{8,9},{9,8},{10,11... | collective-permute-start | bytes 1769480 | tf_op jit(solution)/shard_map/ppermute | solution.py:457
  474.3 42.2 %collective-permute-start.43 = (bf16[768,384]{1,0:T(8,128)(2,1)}, bf16[768,384]{1,0:T(8,128)(2,1)}, u32[]{:S(2)}, u32[]{:S(2)}) collective-permute-start(bf16[768,384]{1,0:T(8,128)(2,1)} %get-tuple-element.320), channel_id=1, source_target_pairs={{0,1},{1,0},{2,3},{3,2},{4,5},{5,4},{6,7},{7,6},{8,9},{9,8},{10,11... | collective-permute-start | bytes 1769480 | tf_op jit(solution)/shard_map/ppermute | solution.py:457
  510.9 48.4 %collective-permute-start.50 = (bf16[768,384]{1,0:T(8,128)(2,1)}, bf16[768,384]{1,0:T(8,128)(2,1)S(1)}, u32[]{:S(2)}, u32[]{:S(2)}) collective-permute-start(bf16[768,384]{1,0:T(8,128)(2,1)} %broadcast_select_fusion.15), channel_id=1, source_target_pairs={{0,16},{16,0},{1,17},{17,1},{2,18},{18,2},{3,19},{19,3},{4,20},{20... | collective-permute-start | bytes 1769480 | tf_op jit(solution)/shard_map/ppermute | solution.py:461
  522.9 40.1 %collective-permute-start.47 = (bf16[768,384]{1,0:T(8,128)(2,1)S(1)}, bf16[768,384]{1,0:T(8,128)(2,1)S(1)}, u32[]{:S(2)}, u32[]{:S(2)}) collective-permute-start(bf16[768,384]{1,0:T(8,128)(2,1)S(1)} %copy-done.153), channel_id=1, source_target_pairs={{0,16},{16,0},{1,17},{17,1},{2,18},{18,2},{3,19},{19,3},{4,20},{20... | collective-permute-start | bytes 1769480 | tf_op jit(solution)/shard_map/ppermute | solution.py:461
  563.0 103.8 %collective-permute-start.63 = (bf16[768,768]{1,0:T(8,128)(2,1)}, bf16[768,768]{1,0:T(8,128)(2,1)}, u32[]{:S(2)}, u32[]{:S(2)}) collective-permute-start(bf16[768,768]{1,0:T(8,128)(2,1)} %get-tuple-element.407), channel_id=1, source_target_pairs={{0,1},{1,0},{2,3},{3,2},{4,5},{5,4},{6,7},{7,6},{8,9},{9,8},{10,11... | collective-permute-start | bytes 3538952 | tf_op jit(solution)/shard_map/ppermute | solution.py:457
  586.4 42.3 %collective-permute-start.54 = (bf16[768,768]{1,0:T(8,128)(2,1)}, bf16[768,768]{1,0:T(8,128)(2,1)}, u32[]{:S(2)}, u32[]{:S(2)}) collective-permute-start(bf16[768,768]{1,0:T(8,128)(2,1)} %get-tuple-element.367), channel_id=1, source_target_pairs={{0,1},{1,0},{2,3},{3,2},{4,5},{5,4},{6,7},{7,6},{8,9},{9,8},{10,11... | collective-permute-start | bytes 3538952 | tf_op jit(solution)/shard_map/ppermute | solution.py:457
  592.2 39.9 %collective-permute-start.53 = (bf16[768,768]{1,0:T(8,128)(2,1)}, bf16[768,768]{1,0:T(8,128)(2,1)}, u32[]{:S(2)}, u32[]{:S(2)}) collective-permute-start(bf16[768,768]{1,0:T(8,128)(2,1)} %get-tuple-element.363), channel_id=1, source_target_pairs={{0,1},{1,0},{2,3},{3,2},{4,5},{5,4},{6,7},{7,6},{8,9},{9,8},{10,11... | collective-permute-start | bytes 3538952 | tf_op jit(solution)/shard_map/ppermute | solution.py:457
  592.8 39.4 %collective-permute-start.57 = (bf16[768,768]{1,0:T(8,128)(2,1)}, bf16[768,768]{1,0:T(8,128)(2,1)}, u32[]{:S(2)}, u32[]{:S(2)}) collective-permute-start(bf16[768,768]{1,0:T(8,128)(2,1)} %get-tuple-element.384), channel_id=1, source_target_pairs={{0,1},{1,0},{2,3},{3,2},{4,5},{5,4},{6,7},{7,6},{8,9},{9,8},{10,11... | collective-permute-start | bytes 3538952 | tf_op jit(solution)/shard_map/ppermute | solution.py:457
  594.2 45.1 %collective-permute-start.56 = (bf16[768,768]{1,0:T(8,128)(2,1)}, bf16[768,768]{1,0:T(8,128)(2,1)}, u32[]{:S(2)}, u32[]{:S(2)}) collective-permute-start(bf16[768,768]{1,0:T(8,128)(2,1)} %get-tuple-element.351), channel_id=1, source_target_pairs={{0,1},{1,0},{2,3},{3,2},{4,5},{5,4},{6,7},{7,6},{8,9},{9,8},{10,11... | collective-permute-start | bytes 3538952 | tf_op jit(solution)/shard_map/ppermute | solution.py:457
  595.8 155.7 %reduce-scatter.7.cloned.1.call-start = ((), (), s32[]{:S(2)}) async-start(), calls=%async_computation.9 | async-start | bytes 983040 | tf_op jit(solution)/shard_map/reduce_scatter | solution.py:660
  633.0 44.8 %collective-permute-start.78 = (bf16[768,384]{1,0:T(8,128)(2,1)}, bf16[768,384]{1,0:T(8,128)(2,1)}, u32[]{:S(2)}, u32[]{:S(2)}) collective-permute-start(bf16[768,384]{1,0:T(8,128)(2,1)} %broadcast_select_fusion.12), channel_id=1, source_target_pairs={{0,16},{16,0},{1,17},{17,1},{2,18},{18,2},{3,19},{19,3},{4,20},{20... | collective-permute-start | bytes 1769480 | tf_op jit(solution)/shard_map/ppermute | solution.py:461
  640.2 64.3 %collective-permute-start.81 = (bf16[768,384]{1,0:T(8,128)(2,1)}, bf16[768,384]{1,0:T(8,128)(2,1)}, u32[]{:S(2)}, u32[]{:S(2)}) collective-permute-start(bf16[768,384]{1,0:T(8,128)(2,1)} %broadcast_select_fusion.10), channel_id=1, source_target_pairs={{0,16},{16,0},{1,17},{17,1},{2,18},{18,2},{3,19},{19,3},{4,20},{20... | collective-permute-start | bytes 1769480 | tf_op jit(solution)/shard_map/ppermute | solution.py:461
  643.7 63.5 %collective-permute-start.80 = (bf16[768,384]{1,0:T(8,128)(2,1)}, bf16[768,384]{1,0:T(8,128)(2,1)}, u32[]{:S(2)}, u32[]{:S(2)}) collective-permute-start(bf16[768,384]{1,0:T(8,128)(2,1)} %broadcast_select_fusion.11), channel_id=1, source_target_pairs={{0,16},{16,0},{1,17},{17,1},{2,18},{18,2},{3,19},{19,3},{4,20},{20... | collective-permute-start | bytes 1769480 | tf_op jit(solution)/shard_map/ppermute | solution.py:461
  657.0 50.4 %collective-permute-start.77 = (bf16[768,384]{1,0:T(8,128)(2,1)}, bf16[768,384]{1,0:T(8,128)(2,1)}, u32[]{:S(2)}, u32[]{:S(2)}) collective-permute-start(bf16[768,384]{1,0:T(8,128)(2,1)} %broadcast_select_fusion.13), channel_id=1, source_target_pairs={{0,16},{16,0},{1,17},{17,1},{2,18},{18,2},{3,19},{19,3},{4,20},{20... | collective-permute-start | bytes 1769480 | tf_op jit(solution)/shard_map/ppermute | solution.py:461
  711.3 81.1 %reduce-scatter.11.cloned.1.call-start = ((), (), s32[]{:S(2)}) async-start(), calls=%async_computation.11 | async-start | bytes 1474560 | tf_op jit(solution)/shard_map/reduce_scatter | solution.py:660
  728.4 45.6 %collective-permute-start.70 = (bf16[768,768]{1,0:T(8,128)(2,1)}, bf16[768,768]{1,0:T(8,128)(2,1)}, u32[]{:S(2)}, u32[]{:S(2)}) collective-permute-start(bf16[768,768]{1,0:T(8,128)(2,1)} %get-tuple-element.421), channel_id=1, source_target_pairs={{0,1},{1,0},{2,3},{3,2},{4,5},{5,4},{6,7},{7,6},{8,9},{9,8},{10,11... | collective-permute-start | bytes 3538952 | tf_op jit(solution)/shard_map/ppermute | solution.py:457
  753.7 83.7 %reduce-scatter.9.cloned.1.call-start = ((), (), s32[]{:S(2)}) async-start(), calls=%async_computation.10 | async-start | bytes 983040 | tf_op jit(solution)/shard_map/reduce_scatter | solution.py:660
  795.1 58.8 %collective-permute-start.69 = (bf16[384,768]{1,0:T(8,128)(2,1)S(1)}, bf16[384,768]{1,0:T(8,128)(2,1)}, u32[]{:S(2)}, u32[]{:S(2)}) collective-permute-start(bf16[384,768]{1,0:T(8,128)(2,1)S(1)} %copy-done.152), channel_id=1, source_target_pairs={{16,16},{17,24},{18,20},{19,28},{20,18},{21,26},{22,22},{23,30},{2... | collective-permute-start | bytes 1769480 | tf_op jit(solution)/shard_map/ppermute | solution.py:488
  796.6 60.6 %collective-permute-start.67 = (bf16[384,768]{1,0:T(8,128)(2,1)S(1)}, bf16[384,768]{1,0:T(8,128)(2,1)S(1)}, u32[]{:S(2)}, u32[]{:S(2)}) collective-permute-start(bf16[384,768]{1,0:T(8,128)(2,1)S(1)} %copy-done.152), channel_id=1, source_target_pairs={{0,16},{1,24},{2,20},{3,28},{4,18},{5,26},{6,22},{7,30},{8,17},{9,... | collective-permute-start | bytes 1769480 | tf_op jit(solution)/shard_map/ppermute | solution.py:488
  799.0 57.1 %collective-permute-start.68 = (bf16[384,768]{1,0:T(8,128)(2,1)S(1)}, bf16[384,768]{1,0:T(8,128)(2,1)}, u32[]{:S(2)}, u32[]{:S(2)}) collective-permute-start(bf16[384,768]{1,0:T(8,128)(2,1)S(1)} %copy-done.151), channel_id=1, source_target_pairs={{16,0},{17,8},{18,4},{19,12},{20,2},{21,10},{22,6},{23,14},{24,1},... | collective-permute-start | bytes 1769480 | tf_op jit(solution)/shard_map/ppermute | solution.py:488
  800.3 75.5 %collective-permute-start.66 = (bf16[384,768]{1,0:T(8,128)(2,1)S(1)}, bf16[384,768]{1,0:T(8,128)(2,1)}, u32[]{:S(2)}, u32[]{:S(2)}) collective-permute-start(bf16[384,768]{1,0:T(8,128)(2,1)S(1)} %copy-done.151), channel_id=1, source_target_pairs={{0,0},{1,8},{2,4},{3,12},{4,2},{5,10},{6,6},{7,14},{8,1},{9,9},{10... | collective-permute-start | bytes 1769480 | tf_op jit(solution)/shard_map/ppermute | solution.py:488
  (233 other events, 1967.7 us)
Sparse Core Ops, SparseCore 0:
  23.2 56.9 all-gather.4
  82.3 36.1 all-gather.8
  120.7 29.5 all-gather.6
  152.3 29.5 all-gather.10
  595.9 27.7 reduce-scatter.4
  711.4 21.3 reduce-scatter.6
  753.8 27.2 reduce-scatter.10
  792.5 44.9 reduce-scatter.8

commit v7 on v5

--- a/solution.py
+++ b/solution.py
@@ -555,7 +555,7 @@
     own_down = after(own_down, own_up)
     proj_one = after(proj_one, own_down)
     own_up, own_down, proj_one = gathered(own_up), gathered(own_down), gathered(proj_one)
-    other_up, other_down = swap_sections(own_up), swap_sections(own_down)
+    other_up = swap_sections(own_up)
 
     def head_weights(block):
         pieces = spread(block, across(block, 2))
@@ -608,10 +608,10 @@
             if layer == 0 and step == 0:
                 late["up"] = by_layer(own_up, after(other_up, outs[p]))
                 late["up_far"] = across(late["up"][0], 2)
-            elif layer == 0 and step == 1:
+                other_down = swap_sections(after(own_down, outs[p]))
+            elif layer == 0 and step == 2:
                 late["down"] = by_layer(own_down, after(other_down, outs[p]))
                 late["down_far"] = across(late["down"][0], 2)
-            elif layer == 0 and step == 2:
                 w_up = spread(late["up"][0], after(late["up_far"], outs[p]))
                 late["one_far"] = across(after(proj_one, outs[p]), 2)
             elif layer == 0 and step == 3:
@@ -633,6 +633,8 @@
         result = middle + vec[7]
         for p in range(QUARTERS):
             bias = lax.dynamic_index_in_dim(bias_up, quarter ^ p, 1, keepdims=False).reshape(1, shards * unit)
+            if layer == 0 and p == QUARTERS - 1:
+                result = after(result, late["one_far"])
             act, slope, result = mlp_part(normed_two, w_up[p], bias, w_down[p], result)
             acts.append(act)
             slopes.append(slope)
@@ -689,7 +691,8 @@
                 far_down = across(far_down, 2)
             elif step == 2:
                 head = after(head, far_up)
-                far_up = across(far_up, 2)
+                if layer == 0:
+                    far_up = across(far_up, 2)
                 if above is not None:
                     half = after(above["half"], results[order[1]][0])
                     above["proj"] = scattered(jnp.concatenate([half, above["vec"]], 1))
@@ -715,6 +718,8 @@
             cut = block.shape[0] // 2
             block = block[:cut] + across(block[cut:].astype(BF16), bit).astype(F32)
             bit //= 2
+        if layer == 1:
+            far_up = across(after(far_up, block), 2)
         half_up = half_sum(low_sum(g_up[0], near_up[0], after(far_up, d_normed)))
         if layer == 1:
             far_proj = low_sum(g_proj[2], after(near_proj[2], block))
@@ -743,12 +748,14 @@
     g_zero, zero = backward(g_one, 0, kept_zero, one)
     y_one = after(y_one, g_one)
     out_slots = [transposed(y_one, 0, 1), transposed(y_one, 1, 1)]
+    g_zero = after(g_zero, *out_slots)
     back_slots = [transposed(g_zero, 0, 0), transposed(g_zero, 1, 0)]
     edges_out = jnp.stack([jnp.where(first, b, o) for b, o in zip(back_slots, out_slots)])
     mlp_one, proj_one = one["mlp"], one["proj"]
     mlp_zero = scattered(jnp.concatenate([after(half, g_zero) for half in zero["halves"]], 1))
     far = after(zero["far_proj"], g_zero)
-    proj_zero = scattered(jnp.concatenate([half_sum(zero["finish"](far)), zero["vec"]], 1))
+    proj_zero = jnp.concatenate([half_sum(zero["finish"](far)), zero["vec"]], 1)
+    proj_zero = scattered(after(proj_zero, *back_slots))
 
     def exchanged(zero, one):
         return jnp.where(first, zero, one), swap_sections(jnp.where(first, one, zero))
@@ -762,10 +769,12 @@
         return parts
 
     part = jnp.concatenate(joined(*exchanged(mlp_zero, mlp_one)), 1)
+    far = across(part, 2)
     f_down, f_up = placed_parts(
-        functools.partial(place_mlp_kernel, shards=shards), quarter, spread(part, across(part, 2)),
+        functools.partial(place_mlp_kernel, shards=shards), quarter, spread(part, far),
         [mlp_down.shape[1:], mlp_up.shape[1:]],
     )
+    proj_zero = after(proj_zero, far)
     own, other = exchanged(proj_zero, proj_one)
     cut = width // 2
     part = jnp.concatenate(

time: 792 us -> 793 us (level)
  starting transfers between devices: 135 us -> 149 us
  local copies, waits for them, and re-layouts: 75.3 us -> 66 us
    ppermute x12, waiting for transfers between devices: 33.1 us -> 89.7 us  [swap_sections(): return lax.ppermute(block, 'section', [(0, 1), (1, 0)])]
    ppermute x62, waiting for transfers between devices: 141 us -> 110 us  [across(): return lax.ppermute(block, 'replica', [(i, i ^ bit) for i in range(count)])]
    all_gather x4, waiting for transfers between devices: 33.5 us -> 7.24 us  [gathered(): return lax.all_gather(block, 'shard', axis=0, tiled=True)]
    reduce_scatter x4, waiting for transfers between devices: 34.5 us -> 11.2 us  [scattered(): return lax.psum_scatter(block, 'shard', scatter_dimension=0, tiled=True)]
    ppermute x12, starting transfers between devices: 21.7 us -> 41.8 us  [swap_sections(): return lax.ppermute(block, 'section', [(0, 1), (1, 0)])]
    ppermute x9, waiting for transfers between devices: 0.02 us -> 18.3 us  [transposed(): return lax.ppermute(block, AXES, route)]
    unnamed x340 -> x370, local copies, waits for them, and re-layouts: 44.2 us -> 38.7 us
  transfers between devices with their start and end apart: 91 -> 91, of which waited for: 23 -> 21; matrix products, arithmetic and copies ran while one was open for 14% -> 13% of each run, Pallas kernels for 28% -> 28%
where the time goes in v7:
time: 793 us; the launch traced here: 782 us
  waiting for transfers between devices  237 us (30%)
  Pallas kernels  230 us (29%)
  starting transfers between devices  149 us (19%)
  local copies, waits for them, and re-layouts  66 us (8%)
  other arithmetic  63.9 us (8%)
  matrix products  19.2 us (2%)
  between operations  16.9 us (2%)
    ppermute x62, waiting for transfers between devices, across(): return lax.ppermute(block, 'replica', [(i, i ^ bit) for i in range(count)])  110 us
    ppermute x12, waiting for transfers between devices, swap_sections(): return lax.ppermute(block, 'section', [(0, 1), (1, 0)])  89.7 us
    ppermute x62, starting transfers between devices, across(): return lax.ppermute(block, 'replica', [(i, i ^ bit) for i in range(count)])  88.8 us
    pallas_call x8, Pallas kernels, attend_back(): pl.pallas_call(functools.partial(attend_back_kernel, heads=heads, frames=...  64 us
    pallas_call x8, Pallas kernels, attend(): pl.pallas_call(functools.partial(attend_kernel, heads=heads, frames=frame...  51.6 us
    ppermute x12, starting transfers between devices, swap_sections(): return lax.ppermute(block, 'section', [(0, 1), (1, 0)])  41.8 us
    pallas_call x8, Pallas kernels, mlp_back_part(): pl.pallas_call(mlp_back_kernel, grid=(columns // tile,), in_specs=[whole,...  40.8 us
    unnamed x370, local copies, waits for them, and re-layouts  38.7 us
  transfers between devices with their start and end apart: 91, of which 21 were waited for; matrix products, arithmetic and copies ran while one was open for 13% of the time, Pallas kernels for 28%

profile of v7, /device:TPU:0, one launch (start us, length us, event | category | flops | bytes accessed | tf_op | source)
XLA Modules:
  0.0 782.1 jit_solution(9102802167139840148)
XLA Ops:
  15.1 7.0 collective-permute-done.4
  24.2 5.9 collective-permute-start
  45.2 54.1 %collective-permute-start.2 = (bf16[384,768]{1,0:T(8,128)(2,1)S(1)}, bf16[384,768]{1,0:T(8,128)(2,1)S(1)}, u32[]{:S(2)}, u32[]{:S(2)}) collective-permute-start(bf16[384,768]{1,0:T(8,128)(2,1)S(1)} %get-tuple-element.467.x_ref), channel_id=1, source_target_pairs={{0,2},{1,3},{2,0},{3,1},{4,6},{5,7},{6,4},{7,5},{8,10},{9,11},{10,... | collective-permute-start | bytes 1769480 | tf_op jit(solution)/shard_map/ppermute | solution.py:457
  101.9 10.1 %collective-permute-done.2 = bf16[384,768]{1,0:T(8,128)(2,1)S(1)} collective-permute-done((bf16[384,768]{1,0:T(8,128)(2,1)S(1)}, bf16[384,768]{1,0:T(8,128)(2,1)S(1)}, u32[]{:S(2)}, u32[]{:S(2)}) %collective-permute-start.2) | collective-permute-done | bytes 589856 | tf_op jit(solution)/shard_map/ppermute | solution.py:457
  119.9 12.7 %collective-permute-done.9.weight_ref = bf16[768,768]{1,0:T(8,128)(2,1)} collective-permute-done((bf16[768,768]{1,0:T(8,128)(2,1)}, bf16[768,768]{1,0:T(8,128)(2,1)}, u32[]{:S(2)}, u32[]{:S(2)}) %collective-permute-start.9) | collective-permute-done | bytes 1179680 | tf_op jit(solution)/shard_map/ppermute | solution.py:457
  140.2 6.3 attend.8
  162.8 6.5 attend.10
  169.3 8.4 %collective-permute-done.16 = bf16[768,768]{1,0:T(8,128)(2,1)} collective-permute-done((bf16[768,768]{1,0:T(8,128)(2,1)}, bf16[768,768]{1,0:T(8,128)(2,1)}, u32[]{:S(2)}, u32[]{:S(2)}) %collective-permute-start.16) | collective-permute-done | bytes 1179680 | tf_op jit(solution)/shard_map/ppermute | solution.py:461
  186.1 6.3 attend.11
  192.6 21.3 %collective-permute-done.17.down_ref = bf16[768,768]{1,0:T(8,128)(2,1)} collective-permute-done((bf16[768,768]{1,0:T(8,128)(2,1)}, bf16[768,768]{1,0:T(8,128)(2,1)}, u32[]{:S(2)}, u32[]{:S(2)}) %collective-permute-start.17) | collective-permute-done | bytes 1179680 | tf_op jit(solution)/shard_map/ppermute | solution.py:457
  215.3 6.6 attend.9
  250.5 14.3 %collective-permute-done.22 = bf16[384,768]{1,0:T(8,128)(2,1)S(1)} collective-permute-done((bf16[384,768]{1,0:T(8,128)(2,1)S(1)}, bf16[384,768]{1,0:T(8,128)(2,1)S(1)}, u32[]{:S(2)}, u32[]{:S(2)}) %collective-permute-start.22) | collective-permute-done | bytes 589856 | tf_op jit(solution)/shard_map/ppermute | solution.py:457
  280.0 6.8 attend.13
  295.9 6.3 attend.12
  305.9 6.4 attend.15
  312.3 17.4 %collective-permute-done.32.down_ref = bf16[768,768]{1,0:T(8,128)(2,1)} collective-permute-done((bf16[768,768]{1,0:T(8,128)(2,1)}, bf16[768,768]{1,0:T(8,128)(2,1)}, u32[]{:S(2)}, u32[]{:S(2)}) %collective-permute-start.32) | collective-permute-done | bytes 1179680 | tf_op jit(solution)/shard_map/ppermute | solution.py:457
  335.4 6.3 attend.14
  365.7 6.1 mlp_back_part.8
  372.4 4.7 mlp_back_part.9
  379.1 4.7 mlp_back_part.10
  385.9 4.7 mlp_back_part.11
  396.8 8.0 %attend_back.10 = (bf16[384,192]{1,0:T(8,128)(2,1)}, bf16[768,384]{1,0:T(8,128)(2,1)}, bf16[768,384]{1,0:T(8,128)(2,1)}) custom-call(bf16[768,576]{1,0:T(8,128)(2,1)} %copy-done.157, bf16[768,384]{1,0:T(8,128)(2,1)} %collective-permute-done.29.other_ref, bf16[3,1536,384]{2,1,0:T(8,128)(2,1)} %get-tuple-element.288.exp_ref, ...), custom_call_target="tpu_custom_call" | custom-call | flops 3623878656 | bytes 3538944 | tf_op jit(solution)/shard_map/attend_back/pallas_call | solution.py:157
  405.3 7.9 %attend_back.8 = (bf16[384,192]{1,0:T(8,128)(2,1)}, bf16[768,384]{1,0:T(8,128)(2,1)}, bf16[768,384]{1,0:T(8,128)(2,1)}) custom-call(bf16[768,576]{1,0:T(8,128)(2,1)} %add_convert_fusion.14.own_ref, bf16[768,384]{1,0:T(8,128)(2,1)} %collective-permute-done.26.other_ref, bf16[3,1536,384]{2,1,0:T(8,128)(2,1)} %get-tuple-element.267.exp_ref, ...), custom_call_target="tpu_custom_call" | custom-call | flops 3623878656 | bytes 3538944 | tf_op jit(solution)/shard_map/attend_back/pallas_call | solution.py:157
  415.8 8.2 %attend_back.11 = (bf16[384,192]{1,0:T(8,128)(2,1)}, bf16[768,384]{1,0:T(8,128)(2,1)}, bf16[768,384]{1,0:T(8,128)(2,1)}) custom-call(bf16[768,576]{1,0:T(8,128)(2,1)} %copy-done.155, bf16[768,384]{1,0:T(8,128)(2,1)} %collective-permute-done.28.other_ref, bf16[3,1536,384]{2,1,0:T(8,128)(2,1)} %get-tuple-element.283.exp_ref, ...), custom_call_target="tpu_custom_call" | custom-call | flops 3623878656 | bytes 3538944 | tf_op jit(solution)/shard_map/attend_back/pallas_call | solution.py:157
  427.1 7.9 %attend_back.9 = (bf16[384,192]{1,0:T(8,128)(2,1)}, bf16[768,384]{1,0:T(8,128)(2,1)}, bf16[768,384]{1,0:T(8,128)(2,1)}) custom-call(bf16[768,576]{1,0:T(8,128)(2,1)} %copy-done.154, bf16[768,384]{1,0:T(8,128)(2,1)} %copy-done.180, bf16[3,1536,384]{2,1,0:T(8,128)(2,1)} %get-tuple-element.271.exp_ref, f32[3,384]{1,0:T(4,128)} %get-tuple-element.272.inv_ref, ...), custom_call_target="tpu_custom_call" | custom-call | flops 3623878656 | bytes 3538944 | tf_op jit(solution)/shard_map/attend_back/pallas_call | solution.py:157
  437.0 8.9 %collective-permute-start.46 = (bf16[768,768]{1,0:T(8,128)(2,1)}, bf16[768,768]{1,0:T(8,128)(2,1)S(1)}, u32[]{:S(2)}, u32[]{:S(2)}) collective-permute-start(bf16[768,768]{1,0:T(8,128)(2,1)} %add_convert_fusion.11), channel_id=1, source_target_pairs={{0,2},{1,3},{2,0},{3,1},{4,6},{5,7},{6,4},{7,5},{8,10},{9,11},{10,... | collective-permute-start | bytes 3538952 | tf_op jit(solution)/shard_map/ppermute | solution.py:457
  465.0 20.4 %collective-permute-done.43 = bf16[384,768]{1,0:T(8,128)(2,1)S(1)} collective-permute-done((bf16[384,768]{1,0:T(8,128)(2,1)S(1)}, bf16[384,768]{1,0:T(8,128)(2,1)S(1)}, u32[]{:S(2)}, u32[]{:S(2)}) %collective-permute-start.43) | collective-permute-done | bytes 589856 | tf_op jit(solution)/shard_map/ppermute | solution.py:457
  488.9 5.8 collective-permute-start.47
  496.1 11.9 %collective-permute-done.47 = bf16[768,384]{1,0:T(8,128)(2,1)S(1)} collective-permute-done((bf16[768,384]{1,0:T(8,128)(2,1)S(1)}, bf16[768,384]{1,0:T(8,128)(2,1)S(1)}, u32[]{:S(2)}, u32[]{:S(2)}) %collective-permute-start.47) | collective-permute-done | bytes 589856 | tf_op jit(solution)/shard_map/ppermute | solution.py:461
  509.8 5.7 collective-permute-done.49
  516.0 5.8 collective-permute-start.50
  521.8 5.9 mlp_back_part.12
  528.2 5.3 mlp_back_part.13
  534.6 4.8 mlp_back_part.14
  541.5 4.7 mlp_back_part.15
  551.0 8.2 %attend_back.14 = (bf16[384,192]{1,0:T(8,128)(2,1)}, bf16[768,384]{1,0:T(8,128)(2,1)}, bf16[768,384]{1,0:T(8,128)(2,1)}) custom-call(bf16[768,576]{1,0:T(8,128)(2,1)} %copy-done.153, bf16[768,384]{1,0:T(8,128)(2,1)} %collective-permute-done.12.other_ref, bf16[3,1536,384]{2,1,0:T(8,128)(2,1)} %get-tuple-element.357.exp_ref, ...), custom_call_target="tpu_custom_call" | custom-call | flops 3623878656 | bytes 3538944 | tf_op jit(solution)/shard_map/attend_back/pallas_call | solution.py:157
  566.5 7.9 %attend_back.15 = (bf16[384,192]{1,0:T(8,128)(2,1)}, bf16[768,384]{1,0:T(8,128)(2,1)}, bf16[768,384]{1,0:T(8,128)(2,1)}) custom-call(bf16[768,576]{1,0:T(8,128)(2,1)} %add_convert_fusion.17.own_ref, bf16[768,384]{1,0:T(8,128)(2,1)} %copy-done.179, bf16[3,1536,384]{2,1,0:T(8,128)(2,1)} %get-tuple-element.352.exp_ref, f32[3,384]{1,0:T(4,128)} %get-tuple-element.353.inv_ref, ...), custom_call_target="tpu_custom_call" | custom-call | flops 3623878656 | bytes 3538944 | tf_op jit(solution)/shard_map/attend_back/pallas_call | solution.py:157
  579.1 8.1 %attend_back.13 = (bf16[384,192]{1,0:T(8,128)(2,1)}, bf16[768,384]{1,0:T(8,128)(2,1)}, bf16[768,384]{1,0:T(8,128)(2,1)}) custom-call(bf16[768,576]{1,0:T(8,128)(2,1)} %copy-done.151, bf16[768,384]{1,0:T(8,128)(2,1)} %collective-permute-done.8.other_ref, bf16[3,1536,384]{2,1,0:T(8,128)(2,1)} %get-tuple-element.340.exp_ref, ...), custom_call_target="tpu_custom_call" | custom-call | flops 3623878656 | bytes 3538944 | tf_op jit(solution)/shard_map/attend_back/pallas_call | solution.py:157
  595.5 7.9 %attend_back.12 = (bf16[384,192]{1,0:T(8,128)(2,1)}, bf16[768,384]{1,0:T(8,128)(2,1)}, bf16[768,384]{1,0:T(8,128)(2,1)}) custom-call(bf16[768,576]{1,0:T(8,128)(2,1)} %add_convert_fusion.19.own_ref, bf16[768,384]{1,0:T(8,128)(2,1)} %collective-permute-done.6.other_ref, bf16[3,1536,384]{2,1,0:T(8,128)(2,1)} %get-tuple-element.325.exp_ref, ...), custom_call_target="tpu_custom_call" | custom-call | flops 3623878656 | bytes 3538944 | tf_op jit(solution)/shard_map/attend_back/pallas_call | solution.py:157
  635.9 20.6 %collective-permute-done.71 = bf16[768,384]{1,0:T(8,128)(2,1)S(1)} collective-permute-done((bf16[768,384]{1,0:T(8,128)(2,1)S(1)}, bf16[768,384]{1,0:T(8,128)(2,1)S(1)}, u32[]{:S(2)}, u32[]{:S(2)}) %collective-permute-start.71) | collective-permute-done | bytes 589856 | tf_op jit(solution)/shard_map/ppermute | solution.py:461
  656.7 7.9 %collective-permute-start.74 = (bf16[768,384]{1,0:T(8,128)(2,1)}, bf16[768,384]{1,0:T(8,128)(2,1)}, u32[]{:S(2)}, u32[]{:S(2)}) collective-permute-start(bf16[768,384]{1,0:T(8,128)(2,1)} %broadcast_select_fusion.4), channel_id=1, source_target_pairs={{0,16},{16,0},{1,17},{17,1},{2,18},{18,2},{3,19},{19,3},{4,20},{20... | collective-permute-start | bytes 1769480 | tf_op jit(solution)/shard_map/ppermute | solution.py:461
  667.1 11.6 %collective-permute-done.74 = bf16[768,384]{1,0:T(8,128)(2,1)} collective-permute-done((bf16[768,384]{1,0:T(8,128)(2,1)}, bf16[768,384]{1,0:T(8,128)(2,1)}, u32[]{:S(2)}, u32[]{:S(2)}) %collective-permute-start.74) | collective-permute-done | bytes 589856 | tf_op jit(solution)/shard_map/ppermute | solution.py:461
  684.6 7.7 collective-permute-start.68
  694.9 19.4 %collective-permute-done.68 = bf16[768,384]{1,0:T(8,128)(2,1)S(1)} collective-permute-done((bf16[768,384]{1,0:T(8,128)(2,1)S(1)}, bf16[768,384]{1,0:T(8,128)(2,1)S(1)}, u32[]{:S(2)}, u32[]{:S(2)}) %collective-permute-start.68) | collective-permute-done | bytes 589856 | tf_op jit(solution)/shard_map/ppermute | solution.py:461
  715.4 18.3 %collective-permute-done.65 = bf16[384,768]{1,0:T(8,128)(2,1)S(1)} collective-permute-done((bf16[384,768]{1,0:T(8,128)(2,1)S(1)}, bf16[384,768]{1,0:T(8,128)(2,1)S(1)}, u32[]{:S(2)}, u32[]{:S(2)}) %collective-permute-start.65) | collective-permute-done | bytes 589856 | tf_op jit(solution)/shard_map/ppermute | solution.py:488
  734.9 6.7 collective-permute-done.75
  743.2 11.1 %reduce-scatter.9.cloned.1.call-done = bf16[192,512]{1,0:T(8,128)(2,1)} async-done(((bf16[768,512]{1,0:T(8,128)(2,1)}), bf16[192,512]{1,0:T(8,128)(2,1)}) %reduce-scatter.9.cloned.1.call-update) | async-done | bytes 196624 | tf_op jit(solution)/shard_map/reduce_scatter | solution.py:658
  763.3 5.2 collective-permute-done.79.c_ref
  (710 shorter events, 290.8 us)
Async XLA Ops:
  7.2 93.2 %all-gather.5.cloned.1.call-start = ((), (), s32[]{:S(2)}) async-start(), calls=%async_computation.4 | async-start | bytes 1474560 | tf_op jit(solution)/shard_map/all_gather | solution.py:542
  23.1 94.9 %all-gather.9.cloned.1.call-start = ((), (), s32[]{:S(2)}) async-start(), calls=%async_computation.6 | async-start | bytes 1474560 | tf_op jit(solution)/shard_map/all_gather | solution.py:542
  41.7 108.5 %all-gather.11.cloned.1.call-start = ((), (), s32[]{:S(2)}) async-start(), calls=%async_computation.7 | async-start | bytes 1474560 | tf_op jit(solution)/shard_map/all_gather | solution.py:542
  41.8 57.6 %collective-permute-start.3 = (f32[12,768]{1,0:T(8,128)S(1)}, f32[12,768]{1,0:T(8,128)S(1)}, u32[]{:S(2)}, u32[]{:S(2)}) collective-permute-start(f32[12,768]{1,0:T(8,128)S(1)} %bitcast.65), channel_id=1, source_target_pairs={{0,16},{16,0},{1,17},{17,1},{2,18},{18,2},{3,19},{19,3},{4,20},{20... | collective-permute-start | bytes 110600 | tf_op jit(solution)/shard_map/ppermute | solution.py:461
  45.2 66.7 %collective-permute-start.2 = (bf16[384,768]{1,0:T(8,128)(2,1)S(1)}, bf16[384,768]{1,0:T(8,128)(2,1)S(1)}, u32[]{:S(2)}, u32[]{:S(2)}) collective-permute-start(bf16[384,768]{1,0:T(8,128)(2,1)S(1)} %get-tuple-element.467.x_ref), channel_id=1, source_target_pairs={{0,2},{1,3},{2,0},{3,1},{4,6},{5,7},{6,4},{7,5},{8,10},{9,11},{10,... | collective-permute-start | bytes 1769480 | tf_op jit(solution)/shard_map/ppermute | solution.py:457
  100.4 32.2 %collective-permute-start.5 = (bf16[768,768]{1,0:T(8,128)(2,1)}, bf16[768,768]{1,0:T(8,128)(2,1)S(1)}, u32[]{:S(2)}, u32[]{:S(2)}) collective-permute-start(bf16[768,768]{1,0:T(8,128)(2,1)} %all-gather.5.cloned.1.call-done.weight_ref), channel_id=1, source_target_pairs={{0,1},{1,0},{2,3},{3,2},{4,5},{5,4},{6,7},{7,6},{8,9},{9,8},{10,11... | collective-permute-start | bytes 3538952 | tf_op jit(solution)/shard_map/ppermute | solution.py:457
  100.4 32.2 %collective-permute-start.9 = (bf16[768,768]{1,0:T(8,128)(2,1)}, bf16[768,768]{1,0:T(8,128)(2,1)}, u32[]{:S(2)}, u32[]{:S(2)}) collective-permute-start(bf16[768,768]{1,0:T(8,128)(2,1)} %all-gather.5.cloned.1.call-done.weight_ref), channel_id=1, source_target_pairs={{0,2},{1,3},{2,0},{3,1},{4,6},{5,7},{6,4},{7,5},{8,10},{9,11},{10,... | collective-permute-start | bytes 3538952 | tf_op jit(solution)/shard_map/ppermute | solution.py:457
  101.4 84.2 %all-gather.7.cloned.1.call-start = ((), (), s32[]{:S(2)}) async-start(), calls=%async_computation.5 | async-start | bytes 1474560 | tf_op jit(solution)/shard_map/all_gather | solution.py:542
  118.0 40.0 %collective-permute-start.13 = (bf16[768,768]{1,0:T(8,128)(2,1)}, bf16[768,768]{1,0:T(8,128)(2,1)}, u32[]{:S(2)}, u32[]{:S(2)}) collective-permute-start(bf16[768,768]{1,0:T(8,128)(2,1)} %all-gather.9.cloned.1.call-done), channel_id=1, source_target_pairs={{0,16},{16,0},{1,17},{17,1},{2,18},{18,2},{3,19},{19,3},{4,20},{20... | collective-permute-start | bytes 3538952 | tf_op jit(solution)/shard_map/ppermute | solution.py:461
  151.9 443.6 %reduce-scatter.5.cloned.1.call-start = ((), (), s32[]{:S(2)}) async-start(), calls=%async_computation.8 | async-start | bytes 1474560 | tf_op jit(solution)/shard_map/reduce_scatter | solution.py:658
  160.4 32.0 %collective-permute-start.14 = (bf16[768,768]{1,0:T(8,128)(2,1)S(1)}, bf16[768,768]{1,0:T(8,128)(2,1)}, u32[]{:S(2)}, u32[]{:S(2)}) collective-permute-start(bf16[768,768]{1,0:T(8,128)(2,1)S(1)} %get-tuple-element.482.up_ref), channel_id=1, source_target_pairs={{0,2},{1,3},{2,0},{3,1},{4,6},{5,7},{6,4},{7,5},{8,10},{9,11},{10,... | collective-permute-start | bytes 3538952 | tf_op jit(solution)/shard_map/ppermute | solution.py:457
  180.6 33.3 %collective-permute-start.17 = (bf16[768,768]{1,0:T(8,128)(2,1)}, bf16[768,768]{1,0:T(8,128)(2,1)}, u32[]{:S(2)}, u32[]{:S(2)}) collective-permute-start(bf16[768,768]{1,0:T(8,128)(2,1)} %get-tuple-element.480.down_ref), channel_id=1, source_target_pairs={{0,2},{1,3},{2,0},{3,1},{4,6},{5,7},{6,4},{7,5},{8,10},{9,11},{10,... | collective-permute-start | bytes 3538952 | tf_op jit(solution)/shard_map/ppermute | solution.py:457
  183.8 31.5 %collective-permute-start.8 = (bf16[768,384]{1,0:T(8,128)(2,1)}, bf16[768,384]{1,0:T(8,128)(2,1)}, u32[]{:S(2)}, u32[]{:S(2)}) collective-permute-start(bf16[768,384]{1,0:T(8,128)(2,1)} %slice.288), channel_id=1, source_target_pairs={{0,1},{1,0},{2,3},{3,2},{4,5},{5,4},{6,7},{7,6},{8,9},{9,8},{10,11... | collective-permute-start | bytes 1769480 | tf_op jit(solution)/shard_map/ppermute | solution.py:457
  185.6 47.6 %collective-permute-start.19 = (bf16[768,768]{1,0:T(8,128)(2,1)S(1)}, bf16[768,768]{1,0:T(8,128)(2,1)}, u32[]{:S(2)}, u32[]{:S(2)}) collective-permute-start(bf16[768,768]{1,0:T(8,128)(2,1)S(1)} %get-tuple-element.482.up_ref), channel_id=1, source_target_pairs={{0,1},{1,0},{2,3},{3,2},{4,5},{5,4},{6,7},{7,6},{8,9},{9,8},{10,11... | collective-permute-start | bytes 3538952 | tf_op jit(solution)/shard_map/ppermute | solution.py:457
  185.6 47.5 %collective-permute-start.20 = (bf16[768,768]{1,0:T(8,128)(2,1)}, bf16[768,768]{1,0:T(8,128)(2,1)S(1)}, u32[]{:S(2)}, u32[]{:S(2)}) collective-permute-start(bf16[768,768]{1,0:T(8,128)(2,1)} %get-tuple-element.480.down_ref), channel_id=1, source_target_pairs={{0,1},{1,0},{2,3},{3,2},{4,5},{5,4},{6,7},{7,6},{8,9},{9,8},{10,11... | collective-permute-start | bytes 3538952 | tf_op jit(solution)/shard_map/ppermute | solution.py:457
  192.4 51.1 %collective-permute-start.15 = (bf16[768,768]{1,0:T(8,128)(2,1)}, bf16[768,768]{1,0:T(8,128)(2,1)S(1)}, u32[]{:S(2)}, u32[]{:S(2)}) collective-permute-start(bf16[768,768]{1,0:T(8,128)(2,1)} %collective-permute-done.14.up_ref), channel_id=1, source_target_pairs={{0,1},{1,0},{2,3},{3,2},{4,5},{5,4},{6,7},{7,6},{8,9},{9,8},{10,11... | collective-permute-start | bytes 3538952 | tf_op jit(solution)/shard_map/ppermute | solution.py:457
  213.9 29.7 %collective-permute-start.21 = (bf16[768,768]{1,0:T(8,128)(2,1)}, bf16[768,768]{1,0:T(8,128)(2,1)}, u32[]{:S(2)}, u32[]{:S(2)}) collective-permute-start(bf16[768,768]{1,0:T(8,128)(2,1)} %all-gather.7.cloned.1.call-done.weight_ref), channel_id=1, source_target_pairs={{0,2},{1,3},{2,0},{3,1},{4,6},{5,7},{6,4},{7,5},{8,10},{9,11},{10,... | collective-permute-start | bytes 3538952 | tf_op jit(solution)/shard_map/ppermute | solution.py:457
  286.8 42.9 %collective-permute-start.32 = (bf16[768,768]{1,0:T(8,128)(2,1)}, bf16[768,768]{1,0:T(8,128)(2,1)}, u32[]{:S(2)}, u32[]{:S(2)}) collective-permute-start(bf16[768,768]{1,0:T(8,128)(2,1)} %get-tuple-element.245.down_ref), channel_id=1, source_target_pairs={{0,2},{1,3},{2,0},{3,1},{4,6},{5,7},{6,4},{7,5},{8,10},{9,11},{10,... | collective-permute-start | bytes 3538952 | tf_op jit(solution)/shard_map/ppermute | solution.py:457
  291.7 53.8 %collective-permute-start.34 = (bf16[768,768]{1,0:T(8,128)(2,1)}, bf16[768,768]{1,0:T(8,128)(2,1)}, u32[]{:S(2)}, u32[]{:S(2)}) collective-permute-start(bf16[768,768]{1,0:T(8,128)(2,1)} %get-tuple-element.243.up_ref), channel_id=1, source_target_pairs={{0,1},{1,0},{2,3},{3,2},{4,5},{5,4},{6,7},{7,6},{8,9},{9,8},{10,11... | collective-permute-start | bytes 3538952 | tf_op jit(solution)/shard_map/ppermute | solution.py:457
  295.1 55.6 %collective-permute-start.35 = (bf16[768,768]{1,0:T(8,128)(2,1)}, bf16[768,768]{1,0:T(8,128)(2,1)}, u32[]{:S(2)}, u32[]{:S(2)}) collective-permute-start(bf16[768,768]{1,0:T(8,128)(2,1)} %get-tuple-element.245.down_ref), channel_id=1, source_target_pairs={{0,1},{1,0},{2,3},{3,2},{4,5},{5,4},{6,7},{7,6},{8,9},{9,8},{10,11... | collective-permute-start | bytes 3538952 | tf_op jit(solution)/shard_map/ppermute | solution.py:457
  305.4 53.9 %collective-permute-start.31 = (bf16[768,768]{1,0:T(8,128)(2,1)}, bf16[768,768]{1,0:T(8,128)(2,1)}, u32[]{:S(2)}, u32[]{:S(2)}) collective-permute-start(bf16[768,768]{1,0:T(8,128)(2,1)} %collective-permute-done.30.up_ref), channel_id=1, source_target_pairs={{0,1},{1,0},{2,3},{3,2},{4,5},{5,4},{6,7},{7,6},{8,9},{9,8},{10,11... | collective-permute-start | bytes 3538952 | tf_op jit(solution)/shard_map/ppermute | solution.py:457
  334.0 30.5 %collective-permute-start.25 = (bf16[384,768]{1,0:T(8,128)(2,1)}, bf16[384,768]{1,0:T(8,128)(2,1)}, u32[]{:S(2)}, u32[]{:S(2)}) collective-permute-start(bf16[384,768]{1,0:T(8,128)(2,1)} %get-tuple-element.484), channel_id=1, source_target_pairs={{16,0},{17,8},{18,4},{19,12},{20,2},{21,10},{22,6},{23,14},{24,1},... | collective-permute-start | bytes 1769480 | tf_op jit(solution)/shard_map/ppermute | solution.py:488
  371.8 41.4 %collective-permute-start.37 = (bf16[768,768]{1,0:T(8,128)(2,1)}, bf16[768,768]{1,0:T(8,128)(2,1)}, u32[]{:S(2)}, u32[]{:S(2)}) collective-permute-start(bf16[768,768]{1,0:T(8,128)(2,1)} %get-tuple-element.275), channel_id=1, source_target_pairs={{0,1},{1,0},{2,3},{3,2},{4,5},{5,4},{6,7},{7,6},{8,9},{9,8},{10,11... | collective-permute-start | bytes 3538952 | tf_op jit(solution)/shard_map/ppermute | solution.py:457
  372.3 40.9 %collective-permute-start.39 = (bf16[768,768]{1,0:T(8,128)(2,1)}, bf16[768,768]{1,0:T(8,128)(2,1)}, u32[]{:S(2)}, u32[]{:S(2)}) collective-permute-start(bf16[768,768]{1,0:T(8,128)(2,1)} %get-tuple-element.287), channel_id=1, source_target_pairs={{0,1},{1,0},{2,3},{3,2},{4,5},{5,4},{6,7},{7,6},{8,9},{9,8},{10,11... | collective-permute-start | bytes 3538952 | tf_op jit(solution)/shard_map/ppermute | solution.py:457
  404.8 51.0 %collective-permute-start.40 = (bf16[768,384]{1,0:T(8,128)(2,1)}, bf16[768,384]{1,0:T(8,128)(2,1)}, u32[]{:S(2)}, u32[]{:S(2)}) collective-permute-start(bf16[768,384]{1,0:T(8,128)(2,1)} %get-tuple-element.295), channel_id=1, source_target_pairs={{0,1},{1,0},{2,3},{3,2},{4,5},{5,4},{6,7},{7,6},{8,9},{9,8},{10,11... | collective-permute-start | bytes 1769480 | tf_op jit(solution)/shard_map/ppermute | solution.py:457
  413.1 38.4 %collective-permute-start.41 = (bf16[768,384]{1,0:T(8,128)(2,1)}, bf16[768,384]{1,0:T(8,128)(2,1)}, u32[]{:S(2)}, u32[]{:S(2)}) collective-permute-start(bf16[768,384]{1,0:T(8,128)(2,1)} %get-tuple-element.299), channel_id=1, source_target_pairs={{0,1},{1,0},{2,3},{3,2},{4,5},{5,4},{6,7},{7,6},{8,9},{9,8},{10,11... | collective-permute-start | bytes 1769480 | tf_op jit(solution)/shard_map/ppermute | solution.py:457
  435.8 52.6 %collective-permute-start.45 = (bf16[768,768]{1,0:T(8,128)(2,1)}, bf16[768,768]{1,0:T(8,128)(2,1)S(1)}, u32[]{:S(2)}, u32[]{:S(2)}) collective-permute-start(bf16[768,768]{1,0:T(8,128)(2,1)} %copy-done.112), channel_id=1, source_target_pairs={{0,1},{1,0},{2,3},{3,2},{4,5},{5,4},{6,7},{7,6},{8,9},{9,8},{10,11... | collective-permute-start | bytes 3538952 | tf_op jit(solution)/shard_map/ppermute | solution.py:457
  437.0 49.0 %collective-permute-start.46 = (bf16[768,768]{1,0:T(8,128)(2,1)}, bf16[768,768]{1,0:T(8,128)(2,1)S(1)}, u32[]{:S(2)}, u32[]{:S(2)}) collective-permute-start(bf16[768,768]{1,0:T(8,128)(2,1)} %add_convert_fusion.11), channel_id=1, source_target_pairs={{0,2},{1,3},{2,0},{3,1},{4,6},{5,7},{6,4},{7,5},{8,10},{9,11},{10,... | collective-permute-start | bytes 3538952 | tf_op jit(solution)/shard_map/ppermute | solution.py:457
  464.4 51.0 %collective-permute-start.48 = (bf16[768,768]{1,0:T(8,128)(2,1)S(1)}, bf16[768,768]{1,0:T(8,128)(2,1)S(1)}, u32[]{:S(2)}, u32[]{:S(2)}) collective-permute-start(bf16[768,768]{1,0:T(8,128)(2,1)S(1)} %copy-done.110), channel_id=1, source_target_pairs={{0,1},{1,0},{2,3},{3,2},{4,5},{5,4},{6,7},{7,6},{8,9},{9,8},{10,11... | collective-permute-start | bytes 3538952 | tf_op jit(solution)/shard_map/ppermute | solution.py:457
  464.6 43.6 %collective-permute-start.44 = (bf16[768,768]{1,0:T(8,128)(2,1)S(1)}, bf16[768,768]{1,0:T(8,128)(2,1)S(1)}, u32[]{:S(2)}, u32[]{:S(2)}) collective-permute-start(bf16[768,768]{1,0:T(8,128)(2,1)S(1)} %get-tuple-element.310), channel_id=1, source_target_pairs={{0,1},{1,0},{2,3},{3,2},{4,5},{5,4},{6,7},{7,6},{8,9},{9,8},{10,11... | collective-permute-start | bytes 3538952 | tf_op jit(solution)/shard_map/ppermute | solution.py:457
  485.4 89.1 %collective-permute-start.59 = (bf16[768,768]{1,0:T(8,128)(2,1)}, bf16[768,768]{1,0:T(8,128)(2,1)}, u32[]{:S(2)}, u32[]{:S(2)}) collective-permute-start(bf16[768,768]{1,0:T(8,128)(2,1)} %get-tuple-element.383), channel_id=1, source_target_pairs={{0,1},{1,0},{2,3},{3,2},{4,5},{5,4},{6,7},{7,6},{8,9},{9,8},{10,11... | collective-permute-start | bytes 3538952 | tf_op jit(solution)/shard_map/ppermute | solution.py:457
  509.5 64.9 %collective-permute-start.60 = (bf16[768,768]{1,0:T(8,128)(2,1)}, bf16[768,768]{1,0:T(8,128)(2,1)}, u32[]{:S(2)}, u32[]{:S(2)}) collective-permute-start(bf16[768,768]{1,0:T(8,128)(2,1)} %add_convert_fusion.9), channel_id=1, source_target_pairs={{0,2},{1,3},{2,0},{3,1},{4,6},{5,7},{6,4},{7,5},{8,10},{9,11},{10,... | collective-permute-start | bytes 3538952 | tf_op jit(solution)/shard_map/ppermute | solution.py:457
  516.0 32.7 %collective-permute-start.50 = (bf16[768,384]{1,0:T(8,128)(2,1)S(1)}, bf16[768,384]{1,0:T(8,128)(2,1)S(1)}, u32[]{:S(2)}, u32[]{:S(2)}) collective-permute-start(bf16[768,384]{1,0:T(8,128)(2,1)S(1)} %broadcast_select_fusion.8), channel_id=1, source_target_pairs={{0,16},{16,0},{1,17},{17,1},{2,18},{18,2},{3,19},{19,3},{4,20},{20... | collective-permute-start | bytes 1769480 | tf_op jit(solution)/shard_map/ppermute | solution.py:461
  527.7 31.5 %collective-permute-start.51 = (bf16[768,768]{1,0:T(8,128)(2,1)}, bf16[768,768]{1,0:T(8,128)(2,1)}, u32[]{:S(2)}, u32[]{:S(2)}) collective-permute-start(bf16[768,768]{1,0:T(8,128)(2,1)} %get-tuple-element.344), channel_id=1, source_target_pairs={{0,1},{1,0},{2,3},{3,2},{4,5},{5,4},{6,7},{7,6},{8,9},{9,8},{10,11... | collective-permute-start | bytes 3538952 | tf_op jit(solution)/shard_map/ppermute | solution.py:457
  527.7 35.9 %collective-permute-start.53 = (bf16[768,768]{1,0:T(8,128)(2,1)}, bf16[768,768]{1,0:T(8,128)(2,1)}, u32[]{:S(2)}, u32[]{:S(2)}) collective-permute-start(bf16[768,768]{1,0:T(8,128)(2,1)} %get-tuple-element.356), channel_id=1, source_target_pairs={{0,1},{1,0},{2,3},{3,2},{4,5},{5,4},{6,7},{7,6},{8,9},{9,8},{10,11... | collective-permute-start | bytes 3538952 | tf_op jit(solution)/shard_map/ppermute | solution.py:457
  548.7 57.8 %collective-permute-start.69 = (bf16[768,768]{1,0:T(8,128)(2,1)}, bf16[768,768]{1,0:T(8,128)(2,1)}, u32[]{:S(2)}, u32[]{:S(2)}) collective-permute-start(bf16[768,768]{1,0:T(8,128)(2,1)} %get-tuple-element.410), channel_id=1, source_target_pairs={{0,1},{1,0},{2,3},{3,2},{4,5},{5,4},{6,7},{7,6},{8,9},{9,8},{10,11... | collective-permute-start | bytes 3538952 | tf_op jit(solution)/shard_map/ppermute | solution.py:457
  550.9 116.2 %reduce-scatter.7.cloned.1.call-start = ((), (), s32[]{:S(2)}) async-start(), calls=%async_computation.9 | async-start | bytes 983040 | tf_op jit(solution)/shard_map/reduce_scatter | solution.py:658
  561.8 44.4 %collective-permute-start.70 = (bf16[768,768]{1,0:T(8,128)(2,1)}, bf16[768,768]{1,0:T(8,128)(2,1)}, u32[]{:S(2)}, u32[]{:S(2)}) collective-permute-start(bf16[768,768]{1,0:T(8,128)(2,1)} %add_convert_fusion.6), channel_id=1, source_target_pairs={{0,2},{1,3},{2,0},{3,1},{4,6},{5,7},{6,4},{7,5},{8,10},{9,11},{10,... | collective-permute-start | bytes 3538952 | tf_op jit(solution)/shard_map/ppermute | solution.py:457
  566.2 62.2 %collective-permute-start.73 = (bf16[768,768]{1,0:T(8,128)(2,1)}, bf16[768,768]{1,0:T(8,128)(2,1)}, u32[]{:S(2)}, u32[]{:S(2)}) collective-permute-start(bf16[768,768]{1,0:T(8,128)(2,1)} %add_convert_fusion.5), channel_id=1, source_target_pairs={{0,2},{1,3},{2,0},{3,1},{4,6},{5,7},{6,4},{7,5},{8,10},{9,11},{10,... | collective-permute-start | bytes 3538952 | tf_op jit(solution)/shard_map/ppermute | solution.py:457
  595.3 30.0 %collective-permute-start.58 = (bf16[768,768]{1,0:T(8,128)(2,1)}, bf16[768,768]{1,0:T(8,128)(2,1)}, u32[]{:S(2)}, u32[]{:S(2)}) collective-permute-start(bf16[768,768]{1,0:T(8,128)(2,1)} %get-tuple-element.379), channel_id=1, source_target_pairs={{0,1},{1,0},{2,3},{3,2},{4,5},{5,4},{6,7},{7,6},{8,9},{9,8},{10,11... | collective-permute-start | bytes 3538952 | tf_op jit(solution)/shard_map/ppermute | solution.py:457
  606.0 127.8 %reduce-scatter.11.cloned.1.call-start = ((), (), s32[]{:S(2)}) async-start(), calls=%async_computation.11 | async-start | bytes 1474560 | tf_op jit(solution)/shard_map/reduce_scatter | solution.py:658
  615.0 52.1 %collective-permute-start.62 = (bf16[384,768]{1,0:T(8,128)(2,1)}, bf16[384,768]{1,0:T(8,128)(2,1)}, u32[]{:S(2)}, u32[]{:S(2)}) collective-permute-start(bf16[384,768]{1,0:T(8,128)(2,1)} %convert_element_type.277), channel_id=1, source_target_pairs={{0,16},{1,24},{2,20},{3,28},{4,18},{5,26},{6,22},{7,30},{8,17},{9,... | collective-permute-start | bytes 1769480 | tf_op jit(solution)/shard_map/ppermute | solution.py:488
  621.7 45.4 %collective-permute-start.63 = (bf16[384,768]{1,0:T(8,128)(2,1)}, bf16[384,768]{1,0:T(8,128)(2,1)}, u32[]{:S(2)}, u32[]{:S(2)}) collective-permute-start(bf16[384,768]{1,0:T(8,128)(2,1)} %convert_element_type.277), channel_id=1, source_target_pairs={{16,16},{17,24},{18,20},{19,28},{20,18},{21,26},{22,22},{23,30},{2... | collective-permute-start | bytes 1769480 | tf_op jit(solution)/shard_map/ppermute | solution.py:488
  625.3 31.2 %collective-permute-start.71 = (bf16[768,384]{1,0:T(8,128)(2,1)S(1)}, bf16[768,384]{1,0:T(8,128)(2,1)S(1)}, u32[]{:S(2)}, u32[]{:S(2)}) collective-permute-start(bf16[768,384]{1,0:T(8,128)(2,1)S(1)} %broadcast_select_fusion.5), channel_id=1, source_target_pairs={{0,16},{16,0},{1,17},{17,1},{2,18},{18,2},{3,19},{19,3},{4,20},{20... | collective-permute-start | bytes 1769480 | tf_op jit(solution)/shard_map/ppermute | solution.py:461
  631.1 50.1 %collective-permute-start.67 = (bf16[768,768]{1,0:T(8,128)(2,1)}, bf16[768,768]{1,0:T(8,128)(2,1)}, u32[]{:S(2)}, u32[]{:S(2)}) collective-permute-start(bf16[768,768]{1,0:T(8,128)(2,1)} %add_convert_fusion.4), channel_id=1, source_target_pairs={{0,2},{1,3},{2,0},{3,1},{4,6},{5,7},{6,4},{7,5},{8,10},{9,11},{10,... | collective-permute-start | bytes 3538952 | tf_op jit(solution)/shard_map/ppermute | solution.py:457
  681.1 73.2 %reduce-scatter.9.cloned.1.call-start = ((), (), s32[]{:S(2)}) async-start(), calls=%async_computation.10 | async-start | bytes 983040 | tf_op jit(solution)/shard_map/reduce_scatter | solution.py:658
  692.3 41.4 %collective-permute-start.65 = (bf16[384,768]{1,0:T(8,128)(2,1)S(1)}, bf16[384,768]{1,0:T(8,128)(2,1)S(1)}, u32[]{:S(2)}, u32[]{:S(2)}) collective-permute-start(bf16[384,768]{1,0:T(8,128)(2,1)S(1)} %copy-done.148), channel_id=1, source_target_pairs={{16,0},{17,8},{18,4},{19,12},{20,2},{21,10},{22,6},{23,14},{24,1},... | collective-permute-start | bytes 1769480 | tf_op jit(solution)/shard_map/ppermute | solution.py:488
  693.6 40.2 %collective-permute-start.64 = (bf16[384,768]{1,0:T(8,128)(2,1)S(1)}, bf16[384,768]{1,0:T(8,128)(2,1)S(1)}, u32[]{:S(2)}, u32[]{:S(2)}) collective-permute-start(bf16[384,768]{1,0:T(8,128)(2,1)S(1)} %copy-done.148), channel_id=1, source_target_pairs={{0,0},{1,8},{2,4},{3,12},{4,2},{5,10},{6,6},{7,14},{8,1},{9,9},{10... | collective-permute-start | bytes 1769480 | tf_op jit(solution)/shard_map/ppermute | solution.py:488
  (225 other events, 1967.3 us)
Sparse Core Ops, SparseCore 0:
  23.2 56.9 all-gather.4
  82.3 35.6 all-gather.8
  120.1 30.0 all-gather.10
  152.0 29.1 all-gather.6
  551.0 27.7 reduce-scatter.4
  606.1 31.0 reduce-scatter.6
  681.2 39.4 reduce-scatter.10
  733.9 20.3 reduce-scatter.8

commit v8 on v7

--- a/solution.py
+++ b/solution.py
@@ -691,8 +691,7 @@
                 far_down = across(far_down, 2)
             elif step == 2:
                 head = after(head, far_up)
-                if layer == 0:
-                    far_up = across(far_up, 2)
+                far_up = across(far_up, 2)
                 if above is not None:
                     half = after(above["half"], results[order[1]][0])
                     above["proj"] = scattered(jnp.concatenate([half, above["vec"]], 1))
@@ -718,8 +717,6 @@
             cut = block.shape[0] // 2
             block = block[:cut] + across(block[cut:].astype(BF16), bit).astype(F32)
             bit //= 2
-        if layer == 1:
-            far_up = across(after(far_up, block), 2)
         half_up = half_sum(low_sum(g_up[0], near_up[0], after(far_up, d_normed)))
         if layer == 1:
             far_proj = low_sum(g_proj[2], after(near_proj[2], block))

time: 793 us -> 773 us (0.975)
  waiting for transfers between devices: 237 us -> 200 us
  local copies, waits for them, and re-layouts: 66 us -> 77 us
  starting transfers between devices: 149 us -> 158 us
    ppermute x12, waiting for transfers between devices: 89.7 us -> 65.5 us  [swap_sections(): return lax.ppermute(block, 'section', [(0, 1), (1, 0)])]
    ppermute x62, waiting for transfers between devices: 110 us -> 101 us  [across(): return lax.ppermute(block, 'replica', [(i, i ^ bit) for i in range(count)])]
    unnamed x370 -> x356, local copies, waits for them, and re-layouts: 38.7 us -> 48.2 us
    ppermute x12, starting transfers between devices: 41.8 us -> 49.8 us  [swap_sections(): return lax.ppermute(block, 'section', [(0, 1), (1, 0)])]
  transfers between devices with their start and end apart: 91 -> 91, of which waited for: 21 -> 22; matrix products, arithmetic and copies ran while one was open for 13% -> 14% of each run, Pallas kernels for 28% -> 28%
where the time goes in v8:
time: 773 us; the launch traced here: 763 us
  Pallas kernels  228 us (29%)
  waiting for transfers between devices  200 us (26%)
  starting transfers between devices  158 us (20%)
  local copies, waits for them, and re-layouts  77 us (10%)
  other arithmetic  67 us (9%)
  between operations  16.7 us (2%)
  matrix products  15.8 us (2%)
    ppermute x62, waiting for transfers between devices, across(): return lax.ppermute(block, 'replica', [(i, i ^ bit) for i in range(count)])  101 us
    ppermute x62, starting transfers between devices, across(): return lax.ppermute(block, 'replica', [(i, i ^ bit) for i in range(count)])  89.6 us
    ppermute x12, waiting for transfers between devices, swap_sections(): return lax.ppermute(block, 'section', [(0, 1), (1, 0)])  65.5 us
    pallas_call x8, Pallas kernels, attend_back(): pl.pallas_call(functools.partial(attend_back_kernel, heads=heads, frames=...  63.9 us
    pallas_call x8, Pallas kernels, attend(): pl.pallas_call(functools.partial(attend_kernel, heads=heads, frames=frame...  51.7 us
    ppermute x12, starting transfers between devices, swap_sections(): return lax.ppermute(block, 'section', [(0, 1), (1, 0)])  49.8 us
    unnamed x356, local copies, waits for them, and re-layouts  48.2 us
    pallas_call x8, Pallas kernels, mlp_back_part(): pl.pallas_call(mlp_back_kernel, grid=(columns // tile,), in_specs=[whole,...  41.3 us
  transfers between devices with their start and end apart: 91, of which 22 were waited for; matrix products, arithmetic and copies ran while one was open for 14% of the time, Pallas kernels for 28%

profile of v8, /device:TPU:0, one launch (start us, length us, event | category | flops | bytes accessed | tf_op | source)
XLA Modules:
  0.0 762.9 jit_solution(7141750827656285445)
XLA Ops:
  15.1 7.0 collective-permute-done.4
  24.2 6.0 collective-permute-start
  45.3 54.1 %collective-permute-start.2 = (bf16[384,768]{1,0:T(8,128)(2,1)S(1)}, bf16[384,768]{1,0:T(8,128)(2,1)S(1)}, u32[]{:S(2)}, u32[]{:S(2)}) collective-permute-start(bf16[384,768]{1,0:T(8,128)(2,1)S(1)} %get-tuple-element.465.x_ref), channel_id=1, source_target_pairs={{0,2},{1,3},{2,0},{3,1},{4,6},{5,7},{6,4},{7,5},{8,10},{9,11},{10,... | collective-permute-start | bytes 1769480 | tf_op jit(solution)/shard_map/ppermute | solution.py:457
  101.9 9.5 %collective-permute-done.2 = bf16[384,768]{1,0:T(8,128)(2,1)S(1)} collective-permute-done((bf16[384,768]{1,0:T(8,128)(2,1)S(1)}, bf16[384,768]{1,0:T(8,128)(2,1)S(1)}, u32[]{:S(2)}, u32[]{:S(2)}) %collective-permute-start.2) | collective-permute-done | bytes 589856 | tf_op jit(solution)/shard_map/ppermute | solution.py:457
  113.7 4.7 all-gather.9.cloned.1.call-done
  119.9 12.7 %collective-permute-done.9.weight_ref = bf16[768,768]{1,0:T(8,128)(2,1)} collective-permute-done((bf16[768,768]{1,0:T(8,128)(2,1)}, bf16[768,768]{1,0:T(8,128)(2,1)}, u32[]{:S(2)}, u32[]{:S(2)}) %collective-permute-start.9) | collective-permute-done | bytes 1179680 | tf_op jit(solution)/shard_map/ppermute | solution.py:457
  140.2 6.3 attend.8
  163.2 6.5 attend.10
  169.7 8.0 %collective-permute-done.16 = bf16[768,768]{1,0:T(8,128)(2,1)} collective-permute-done((bf16[768,768]{1,0:T(8,128)(2,1)}, bf16[768,768]{1,0:T(8,128)(2,1)}, u32[]{:S(2)}, u32[]{:S(2)}) %collective-permute-start.16) | collective-permute-done | bytes 1179680 | tf_op jit(solution)/shard_map/ppermute | solution.py:461
  190.9 6.3 attend.11
  197.3 17.2 %collective-permute-done.17.down_ref = bf16[768,768]{1,0:T(8,128)(2,1)} collective-permute-done((bf16[768,768]{1,0:T(8,128)(2,1)}, bf16[768,768]{1,0:T(8,128)(2,1)}, u32[]{:S(2)}, u32[]{:S(2)}) %collective-permute-start.17) | collective-permute-done | bytes 1179680 | tf_op jit(solution)/shard_map/ppermute | solution.py:457
  216.0 6.6 attend.9
  253.8 12.4 %collective-permute-done.22 = bf16[384,768]{1,0:T(8,128)(2,1)S(1)} collective-permute-done((bf16[384,768]{1,0:T(8,128)(2,1)S(1)}, bf16[384,768]{1,0:T(8,128)(2,1)S(1)}, u32[]{:S(2)}, u32[]{:S(2)}) %collective-permute-start.22) | collective-permute-done | bytes 589856 | tf_op jit(solution)/shard_map/ppermute | solution.py:457
  276.8 6.8 attend.13
  290.6 6.3 attend.12
  297.5 6.5 attend.15
  304.0 12.5 %collective-permute-done.32.down_ref = bf16[768,768]{1,0:T(8,128)(2,1)} collective-permute-done((bf16[768,768]{1,0:T(8,128)(2,1)}, bf16[768,768]{1,0:T(8,128)(2,1)}, u32[]{:S(2)}, u32[]{:S(2)}) %collective-permute-start.32) | collective-permute-done | bytes 1179680 | tf_op jit(solution)/shard_map/ppermute | solution.py:457
  322.3 6.3 attend.14
  334.6 4.3 mlp_part.12
  354.0 6.1 mlp_back_part.8
  360.7 4.6 mlp_back_part.9
  367.4 4.6 mlp_back_part.10
  374.1 4.7 mlp_back_part.11
  386.4 8.0 %attend_back.10 = (bf16[384,192]{1,0:T(8,128)(2,1)}, bf16[768,384]{1,0:T(8,128)(2,1)}, bf16[768,384]{1,0:T(8,128)(2,1)}) custom-call(bf16[768,576]{1,0:T(8,128)(2,1)} %copy-done.151, bf16[768,384]{1,0:T(8,128)(2,1)} %collective-permute-done.29.other_ref, bf16[3,1536,384]{2,1,0:T(8,128)(2,1)} %get-tuple-element.287.exp_ref, ...), custom_call_target="tpu_custom_call" | custom-call | flops 3623878656 | bytes 3538944 | tf_op jit(solution)/shard_map/attend_back/pallas_call | solution.py:157
  394.9 7.8 %attend_back.8 = (bf16[384,192]{1,0:T(8,128)(2,1)}, bf16[768,384]{1,0:T(8,128)(2,1)}, bf16[768,384]{1,0:T(8,128)(2,1)}) custom-call(bf16[768,576]{1,0:T(8,128)(2,1)} %copy-done.150, bf16[768,384]{1,0:T(8,128)(2,1)} %collective-permute-done.26.other_ref, bf16[3,1536,384]{2,1,0:T(8,128)(2,1)} %get-tuple-element.266.exp_ref, ...), custom_call_target="tpu_custom_call" | custom-call | flops 3623878656 | bytes 3538944 | tf_op jit(solution)/shard_map/attend_back/pallas_call | solution.py:157
  406.1 7.6 collective-permute-start.49
  413.7 8.2 %attend_back.11 = (bf16[384,192]{1,0:T(8,128)(2,1)}, bf16[768,384]{1,0:T(8,128)(2,1)}, bf16[768,384]{1,0:T(8,128)(2,1)}) custom-call(bf16[768,576]{1,0:T(8,128)(2,1)} %copy-done.149, bf16[768,384]{1,0:T(8,128)(2,1)} %collective-permute-done.28.other_ref, bf16[3,1536,384]{2,1,0:T(8,128)(2,1)} %get-tuple-element.282.exp_ref, ...), custom_call_target="tpu_custom_call" | custom-call | flops 3623878656 | bytes 3538944 | tf_op jit(solution)/shard_map/attend_back/pallas_call | solution.py:157
  425.1 7.9 %attend_back.9 = (bf16[384,192]{1,0:T(8,128)(2,1)}, bf16[768,384]{1,0:T(8,128)(2,1)}, bf16[768,384]{1,0:T(8,128)(2,1)}) custom-call(bf16[768,576]{1,0:T(8,128)(2,1)} %copy-done.148, bf16[768,384]{1,0:T(8,128)(2,1)} %collective-permute-done.24.other_ref, bf16[3,1536,384]{2,1,0:T(8,128)(2,1)} %get-tuple-element.270.exp_ref, ...), custom_call_target="tpu_custom_call" | custom-call | flops 3623878656 | bytes 3538944 | tf_op jit(solution)/shard_map/attend_back/pallas_call | solution.py:157
  455.7 10.3 %collective-permute-done.46 = bf16[768,768]{1,0:T(8,128)(2,1)S(1)} collective-permute-done((bf16[768,768]{1,0:T(8,128)(2,1)}, bf16[768,768]{1,0:T(8,128)(2,1)S(1)}, u32[]{:S(2)}, u32[]{:S(2)}) %collective-permute-start.46) | collective-permute-done | bytes 1179680 | tf_op jit(solution)/shard_map/ppermute | solution.py:457
  466.0 5.7 collective-permute-start.50
  471.8 6.7 collective-permute-done.43
  479.6 5.8 collective-permute-start.47
  489.0 6.0 mlp_back_part.12
  500.6 5.7 mlp_back_part.13
  514.7 4.7 mlp_back_part.14
  519.5 4.7 mlp_back_part.15
  532.4 7.9 %attend_back.14 = (bf16[384,192]{1,0:T(8,128)(2,1)}, bf16[768,384]{1,0:T(8,128)(2,1)}, bf16[768,384]{1,0:T(8,128)(2,1)}) custom-call(bf16[768,576]{1,0:T(8,128)(2,1)} %copy-done.147, bf16[768,384]{1,0:T(8,128)(2,1)} %collective-permute-done.12.other_ref, bf16[3,1536,384]{2,1,0:T(8,128)(2,1)} %get-tuple-element.355.exp_ref, ...), custom_call_target="tpu_custom_call" | custom-call | flops 3623878656 | bytes 3538944 | tf_op jit(solution)/shard_map/attend_back/pallas_call | solution.py:157
  550.1 8.2 %attend_back.15 = (bf16[384,192]{1,0:T(8,128)(2,1)}, bf16[768,384]{1,0:T(8,128)(2,1)}, bf16[768,384]{1,0:T(8,128)(2,1)}) custom-call(bf16[768,576]{1,0:T(8,128)(2,1)} %add_convert_fusion.17.own_ref, bf16[768,384]{1,0:T(8,128)(2,1)} %copy-done.172, bf16[3,1536,384]{2,1,0:T(8,128)(2,1)} %get-tuple-element.350.exp_ref, f32[3,384]{1,0:T(4,128)} %get-tuple-element.351.inv_ref, ...), custom_call_target="tpu_custom_call" | custom-call | flops 3623878656 | bytes 3538944 | tf_op jit(solution)/shard_map/attend_back/pallas_call | solution.py:157
  558.3 7.8 %attend_back.13 = (bf16[384,192]{1,0:T(8,128)(2,1)}, bf16[768,384]{1,0:T(8,128)(2,1)}, bf16[768,384]{1,0:T(8,128)(2,1)}) custom-call(bf16[768,576]{1,0:T(8,128)(2,1)} %copy-done.145, bf16[768,384]{1,0:T(8,128)(2,1)} %collective-permute-done.8.other_ref, bf16[3,1536,384]{2,1,0:T(8,128)(2,1)} %get-tuple-element.338.exp_ref, ...), custom_call_target="tpu_custom_call" | custom-call | flops 3623878656 | bytes 3538944 | tf_op jit(solution)/shard_map/attend_back/pallas_call | solution.py:157
  567.2 8.1 %attend_back.12 = (bf16[384,192]{1,0:T(8,128)(2,1)}, bf16[768,384]{1,0:T(8,128)(2,1)}, bf16[768,384]{1,0:T(8,128)(2,1)}) custom-call(bf16[768,576]{1,0:T(8,128)(2,1)} %add_convert_fusion.19.own_ref, bf16[768,384]{1,0:T(8,128)(2,1)} %collective-permute-done.6.other_ref, bf16[3,1536,384]{2,1,0:T(8,128)(2,1)} %get-tuple-element.324.exp_ref, ...), custom_call_target="tpu_custom_call" | custom-call | flops 3623878656 | bytes 3538944 | tf_op jit(solution)/shard_map/attend_back/pallas_call | solution.py:157
  605.0 24.7 %collective-permute-start.71 = (bf16[768,384]{1,0:T(8,128)(2,1)S(1)}, bf16[768,384]{1,0:T(8,128)(2,1)S(1)}, u32[]{:S(2)}, u32[]{:S(2)}) collective-permute-start(bf16[768,384]{1,0:T(8,128)(2,1)S(1)} %broadcast_select_fusion.5), channel_id=1, source_target_pairs={{0,16},{16,0},{1,17},{17,1},{2,18},{18,2},{3,19},{19,3},{4,20},{20... | collective-permute-start | bytes 1769480 | tf_op jit(solution)/shard_map/ppermute | solution.py:461
  634.7 7.6 collective-permute-done.71
  650.5 5.9 collective-permute-done.74
  659.2 13.2 %collective-permute-done.67 = bf16[768,768]{1,0:T(8,128)(2,1)} collective-permute-done((bf16[768,768]{1,0:T(8,128)(2,1)}, bf16[768,768]{1,0:T(8,128)(2,1)}, u32[]{:S(2)}, u32[]{:S(2)}) %collective-permute-start.67) | collective-permute-done | bytes 1179680 | tf_op jit(solution)/shard_map/ppermute | solution.py:457
  677.8 22.5 %collective-permute-done.68 = bf16[768,384]{1,0:T(8,128)(2,1)S(1)} collective-permute-done((bf16[768,384]{1,0:T(8,128)(2,1)S(1)}, bf16[768,384]{1,0:T(8,128)(2,1)S(1)}, u32[]{:S(2)}, u32[]{:S(2)}) %collective-permute-start.68) | collective-permute-done | bytes 589856 | tf_op jit(solution)/shard_map/ppermute | solution.py:461
  701.5 14.3 %collective-permute-done.65 = bf16[384,768]{1,0:T(8,128)(2,1)} collective-permute-done((bf16[384,768]{1,0:T(8,128)(2,1)S(1)}, bf16[384,768]{1,0:T(8,128)(2,1)}, u32[]{:S(2)}, u32[]{:S(2)}) %collective-permute-start.65) | collective-permute-done | bytes 589856 | tf_op jit(solution)/shard_map/ppermute | solution.py:488
  716.9 6.7 collective-permute-done.75
  723.9 11.3 %reduce-scatter.9.cloned.1.call-done = bf16[192,512]{1,0:T(8,128)(2,1)} async-done(((bf16[768,512]{1,0:T(8,128)(2,1)}), bf16[192,512]{1,0:T(8,128)(2,1)}) %reduce-scatter.9.cloned.1.call-update) | async-done | bytes 196624 | tf_op jit(solution)/shard_map/reduce_scatter | solution.py:658
  (696 shorter events, 298.8 us)
Async XLA Ops:
  7.2 93.8 %all-gather.5.cloned.1.call-start = ((), (), s32[]{:S(2)}) async-start(), calls=%async_computation.4 | async-start | bytes 1474560 | tf_op jit(solution)/shard_map/all_gather | solution.py:542
  23.1 95.4 %all-gather.9.cloned.1.call-start = ((), (), s32[]{:S(2)}) async-start(), calls=%async_computation.6 | async-start | bytes 1474560 | tf_op jit(solution)/shard_map/all_gather | solution.py:542
  41.8 108.5 %all-gather.11.cloned.1.call-start = ((), (), s32[]{:S(2)}) async-start(), calls=%async_computation.7 | async-start | bytes 1474560 | tf_op jit(solution)/shard_map/all_gather | solution.py:542
  41.9 57.5 %collective-permute-start.3 = (f32[12,768]{1,0:T(8,128)S(1)}, f32[12,768]{1,0:T(8,128)S(1)}, u32[]{:S(2)}, u32[]{:S(2)}) collective-permute-start(f32[12,768]{1,0:T(8,128)S(1)} %bitcast.65), channel_id=1, source_target_pairs={{0,16},{16,0},{1,17},{17,1},{2,18},{18,2},{3,19},{19,3},{4,20},{20... | collective-permute-start | bytes 110600 | tf_op jit(solution)/shard_map/ppermute | solution.py:461
  45.3 66.1 %collective-permute-start.2 = (bf16[384,768]{1,0:T(8,128)(2,1)S(1)}, bf16[384,768]{1,0:T(8,128)(2,1)S(1)}, u32[]{:S(2)}, u32[]{:S(2)}) collective-permute-start(bf16[384,768]{1,0:T(8,128)(2,1)S(1)} %get-tuple-element.465.x_ref), channel_id=1, source_target_pairs={{0,2},{1,3},{2,0},{3,1},{4,6},{5,7},{6,4},{7,5},{8,10},{9,11},{10,... | collective-permute-start | bytes 1769480 | tf_op jit(solution)/shard_map/ppermute | solution.py:457
  101.0 31.6 %collective-permute-start.5 = (bf16[768,768]{1,0:T(8,128)(2,1)}, bf16[768,768]{1,0:T(8,128)(2,1)S(1)}, u32[]{:S(2)}, u32[]{:S(2)}) collective-permute-start(bf16[768,768]{1,0:T(8,128)(2,1)} %all-gather.5.cloned.1.call-done.weight_ref), channel_id=1, source_target_pairs={{0,1},{1,0},{2,3},{3,2},{4,5},{5,4},{6,7},{7,6},{8,9},{9,8},{10,11... | collective-permute-start | bytes 3538952 | tf_op jit(solution)/shard_map/ppermute | solution.py:457
  101.0 31.6 %collective-permute-start.9 = (bf16[768,768]{1,0:T(8,128)(2,1)}, bf16[768,768]{1,0:T(8,128)(2,1)}, u32[]{:S(2)}, u32[]{:S(2)}) collective-permute-start(bf16[768,768]{1,0:T(8,128)(2,1)} %all-gather.5.cloned.1.call-done.weight_ref), channel_id=1, source_target_pairs={{0,2},{1,3},{2,0},{3,1},{4,6},{5,7},{6,4},{7,5},{8,10},{9,11},{10,... | collective-permute-start | bytes 3538952 | tf_op jit(solution)/shard_map/ppermute | solution.py:457
  101.4 89.0 %all-gather.7.cloned.1.call-start = ((), (), s32[]{:S(2)}) async-start(), calls=%async_computation.5 | async-start | bytes 1474560 | tf_op jit(solution)/shard_map/all_gather | solution.py:542
  118.5 39.5 %collective-permute-start.13 = (bf16[768,768]{1,0:T(8,128)(2,1)}, bf16[768,768]{1,0:T(8,128)(2,1)}, u32[]{:S(2)}, u32[]{:S(2)}) collective-permute-start(bf16[768,768]{1,0:T(8,128)(2,1)} %all-gather.9.cloned.1.call-done), channel_id=1, source_target_pairs={{0,16},{16,0},{1,17},{17,1},{2,18},{18,2},{3,19},{19,3},{4,20},{20... | collective-permute-start | bytes 3538952 | tf_op jit(solution)/shard_map/ppermute | solution.py:461
  151.9 415.3 %reduce-scatter.5.cloned.1.call-start = ((), (), s32[]{:S(2)}) async-start(), calls=%async_computation.8 | async-start | bytes 1474560 | tf_op jit(solution)/shard_map/reduce_scatter | solution.py:658
  160.9 36.3 %collective-permute-start.14 = (bf16[768,768]{1,0:T(8,128)(2,1)}, bf16[768,768]{1,0:T(8,128)(2,1)}, u32[]{:S(2)}, u32[]{:S(2)}) collective-permute-start(bf16[768,768]{1,0:T(8,128)(2,1)} %get-tuple-element.480.up_ref), channel_id=1, source_target_pairs={{0,2},{1,3},{2,0},{3,1},{4,6},{5,7},{6,4},{7,5},{8,10},{9,11},{10,... | collective-permute-start | bytes 3538952 | tf_op jit(solution)/shard_map/ppermute | solution.py:457
  180.6 33.8 %collective-permute-start.17 = (bf16[768,768]{1,0:T(8,128)(2,1)}, bf16[768,768]{1,0:T(8,128)(2,1)}, u32[]{:S(2)}, u32[]{:S(2)}) collective-permute-start(bf16[768,768]{1,0:T(8,128)(2,1)} %get-tuple-element.478.down_ref), channel_id=1, source_target_pairs={{0,2},{1,3},{2,0},{3,1},{4,6},{5,7},{6,4},{7,5},{8,10},{9,11},{10,... | collective-permute-start | bytes 3538952 | tf_op jit(solution)/shard_map/ppermute | solution.py:457
  183.9 32.1 %collective-permute-start.8 = (bf16[768,384]{1,0:T(8,128)(2,1)}, bf16[768,384]{1,0:T(8,128)(2,1)}, u32[]{:S(2)}, u32[]{:S(2)}) collective-permute-start(bf16[768,384]{1,0:T(8,128)(2,1)} %slice.288), channel_id=1, source_target_pairs={{0,1},{1,0},{2,3},{3,2},{4,5},{5,4},{6,7},{7,6},{8,9},{9,8},{10,11... | collective-permute-start | bytes 1769480 | tf_op jit(solution)/shard_map/ppermute | solution.py:457
  190.3 43.2 %collective-permute-start.19 = (bf16[768,768]{1,0:T(8,128)(2,1)}, bf16[768,768]{1,0:T(8,128)(2,1)}, u32[]{:S(2)}, u32[]{:S(2)}) collective-permute-start(bf16[768,768]{1,0:T(8,128)(2,1)} %get-tuple-element.480.up_ref), channel_id=1, source_target_pairs={{0,1},{1,0},{2,3},{3,2},{4,5},{5,4},{6,7},{7,6},{8,9},{9,8},{10,11... | collective-permute-start | bytes 3538952 | tf_op jit(solution)/shard_map/ppermute | solution.py:457
  190.4 43.2 %collective-permute-start.20 = (bf16[768,768]{1,0:T(8,128)(2,1)}, bf16[768,768]{1,0:T(8,128)(2,1)}, u32[]{:S(2)}, u32[]{:S(2)}) collective-permute-start(bf16[768,768]{1,0:T(8,128)(2,1)} %get-tuple-element.478.down_ref), channel_id=1, source_target_pairs={{0,1},{1,0},{2,3},{3,2},{4,5},{5,4},{6,7},{7,6},{8,9},{9,8},{10,11... | collective-permute-start | bytes 3538952 | tf_op jit(solution)/shard_map/ppermute | solution.py:457
  197.2 48.3 %collective-permute-start.15 = (bf16[768,768]{1,0:T(8,128)(2,1)}, bf16[768,768]{1,0:T(8,128)(2,1)}, u32[]{:S(2)}, u32[]{:S(2)}) collective-permute-start(bf16[768,768]{1,0:T(8,128)(2,1)} %collective-permute-done.14.up_ref), channel_id=1, source_target_pairs={{0,1},{1,0},{2,3},{3,2},{4,5},{5,4},{6,7},{7,6},{8,9},{9,8},{10,11... | collective-permute-start | bytes 3538952 | tf_op jit(solution)/shard_map/ppermute | solution.py:457
  252.0 81.8 %collective-permute-start.34 = (bf16[768,768]{1,0:T(8,128)(2,1)}, bf16[768,768]{1,0:T(8,128)(2,1)}, u32[]{:S(2)}, u32[]{:S(2)}) collective-permute-start(bf16[768,768]{1,0:T(8,128)(2,1)} %get-tuple-element.242.up_ref), channel_id=1, source_target_pairs={{0,1},{1,0},{2,3},{3,2},{4,5},{5,4},{6,7},{7,6},{8,9},{9,8},{10,11... | collective-permute-start | bytes 3538952 | tf_op jit(solution)/shard_map/ppermute | solution.py:457
  252.5 44.4 %collective-permute-start.30 = (bf16[768,768]{1,0:T(8,128)(2,1)}, bf16[768,768]{1,0:T(8,128)(2,1)}, u32[]{:S(2)}, u32[]{:S(2)}) collective-permute-start(bf16[768,768]{1,0:T(8,128)(2,1)} %get-tuple-element.242.up_ref), channel_id=1, source_target_pairs={{0,2},{1,3},{2,0},{3,1},{4,6},{5,7},{6,4},{7,5},{8,10},{9,11},{10,... | collective-permute-start | bytes 3538952 | tf_op jit(solution)/shard_map/ppermute | solution.py:457
  283.6 32.8 %collective-permute-start.32 = (bf16[768,768]{1,0:T(8,128)(2,1)}, bf16[768,768]{1,0:T(8,128)(2,1)}, u32[]{:S(2)}, u32[]{:S(2)}) collective-permute-start(bf16[768,768]{1,0:T(8,128)(2,1)} %get-tuple-element.244.down_ref), channel_id=1, source_target_pairs={{0,2},{1,3},{2,0},{3,1},{4,6},{5,7},{6,4},{7,5},{8,10},{9,11},{10,... | collective-permute-start | bytes 3538952 | tf_op jit(solution)/shard_map/ppermute | solution.py:457
  290.6 48.3 %collective-permute-start.35 = (bf16[768,768]{1,0:T(8,128)(2,1)}, bf16[768,768]{1,0:T(8,128)(2,1)}, u32[]{:S(2)}, u32[]{:S(2)}) collective-permute-start(bf16[768,768]{1,0:T(8,128)(2,1)} %get-tuple-element.244.down_ref), channel_id=1, source_target_pairs={{0,1},{1,0},{2,3},{3,2},{4,5},{5,4},{6,7},{7,6},{8,9},{9,8},{10,11... | collective-permute-start | bytes 3538952 | tf_op jit(solution)/shard_map/ppermute | solution.py:457
  297.4 50.1 %collective-permute-start.31 = (bf16[768,768]{1,0:T(8,128)(2,1)}, bf16[768,768]{1,0:T(8,128)(2,1)}, u32[]{:S(2)}, u32[]{:S(2)}) collective-permute-start(bf16[768,768]{1,0:T(8,128)(2,1)} %collective-permute-done.30.up_ref), channel_id=1, source_target_pairs={{0,1},{1,0},{2,3},{3,2},{4,5},{5,4},{6,7},{7,6},{8,9},{9,8},{10,11... | collective-permute-start | bytes 3538952 | tf_op jit(solution)/shard_map/ppermute | solution.py:457
  316.4 31.1 %collective-permute-start.33 = (bf16[768,768]{1,0:T(8,128)(2,1)}, bf16[768,768]{1,0:T(8,128)(2,1)}, u32[]{:S(2)}, u32[]{:S(2)}) collective-permute-start(bf16[768,768]{1,0:T(8,128)(2,1)} %collective-permute-done.32.down_ref), channel_id=1, source_target_pairs={{0,1},{1,0},{2,3},{3,2},{4,5},{5,4},{6,7},{7,6},{8,9},{9,8},{10,11... | collective-permute-start | bytes 3538952 | tf_op jit(solution)/shard_map/ppermute | solution.py:457
  320.9 31.8 %collective-permute-start.25 = (bf16[384,768]{1,0:T(8,128)(2,1)}, bf16[384,768]{1,0:T(8,128)(2,1)}, u32[]{:S(2)}, u32[]{:S(2)}) collective-permute-start(bf16[384,768]{1,0:T(8,128)(2,1)} %get-tuple-element.482), channel_id=1, source_target_pairs={{16,0},{17,8},{18,4},{19,12},{20,2},{21,10},{22,6},{23,14},{24,1},... | collective-permute-start | bytes 1769480 | tf_op jit(solution)/shard_map/ppermute | solution.py:488
  360.1 43.1 %collective-permute-start.37 = (bf16[768,768]{1,0:T(8,128)(2,1)}, bf16[768,768]{1,0:T(8,128)(2,1)}, u32[]{:S(2)}, u32[]{:S(2)}) collective-permute-start(bf16[768,768]{1,0:T(8,128)(2,1)} %get-tuple-element.274), channel_id=1, source_target_pairs={{0,1},{1,0},{2,3},{3,2},{4,5},{5,4},{6,7},{7,6},{8,9},{9,8},{10,11... | collective-permute-start | bytes 3538952 | tf_op jit(solution)/shard_map/ppermute | solution.py:457
  360.6 42.6 %collective-permute-start.39 = (bf16[768,768]{1,0:T(8,128)(2,1)}, bf16[768,768]{1,0:T(8,128)(2,1)}, u32[]{:S(2)}, u32[]{:S(2)}) collective-permute-start(bf16[768,768]{1,0:T(8,128)(2,1)} %get-tuple-element.286), channel_id=1, source_target_pairs={{0,1},{1,0},{2,3},{3,2},{4,5},{5,4},{6,7},{7,6},{8,9},{9,8},{10,11... | collective-permute-start | bytes 3538952 | tf_op jit(solution)/shard_map/ppermute | solution.py:457
  394.5 49.5 %collective-permute-start.40 = (bf16[768,384]{1,0:T(8,128)(2,1)}, bf16[768,384]{1,0:T(8,128)(2,1)}, u32[]{:S(2)}, u32[]{:S(2)}) collective-permute-start(bf16[768,384]{1,0:T(8,128)(2,1)} %get-tuple-element.294), channel_id=1, source_target_pairs={{0,1},{1,0},{2,3},{3,2},{4,5},{5,4},{6,7},{7,6},{8,9},{9,8},{10,11... | collective-permute-start | bytes 1769480 | tf_op jit(solution)/shard_map/ppermute | solution.py:457
  402.7 50.5 %collective-permute-start.48 = (bf16[768,768]{1,0:T(8,128)(2,1)}, bf16[768,768]{1,0:T(8,128)(2,1)}, u32[]{:S(2)}, u32[]{:S(2)}) collective-permute-start(bf16[768,768]{1,0:T(8,128)(2,1)} %copy-done.108), channel_id=1, source_target_pairs={{0,1},{1,0},{2,3},{3,2},{4,5},{5,4},{6,7},{7,6},{8,9},{9,8},{10,11... | collective-permute-start | bytes 3538952 | tf_op jit(solution)/shard_map/ppermute | solution.py:457
  406.1 46.9 %collective-permute-start.49 = (bf16[768,768]{1,0:T(8,128)(2,1)}, bf16[768,768]{1,0:T(8,128)(2,1)}, u32[]{:S(2)}, u32[]{:S(2)}) collective-permute-start(bf16[768,768]{1,0:T(8,128)(2,1)} %add_convert_fusion.10), channel_id=1, source_target_pairs={{0,2},{1,3},{2,0},{3,1},{4,6},{5,7},{6,4},{7,5},{8,10},{9,11},{10,... | collective-permute-start | bytes 3538952 | tf_op jit(solution)/shard_map/ppermute | solution.py:457
  433.5 32.6 %collective-permute-start.46 = (bf16[768,768]{1,0:T(8,128)(2,1)}, bf16[768,768]{1,0:T(8,128)(2,1)S(1)}, u32[]{:S(2)}, u32[]{:S(2)}) collective-permute-start(bf16[768,768]{1,0:T(8,128)(2,1)} %add_convert_fusion.11), channel_id=1, source_target_pairs={{0,2},{1,3},{2,0},{3,1},{4,6},{5,7},{6,4},{7,5},{8,10},{9,11},{10,... | collective-permute-start | bytes 3538952 | tf_op jit(solution)/shard_map/ppermute | solution.py:457
  443.9 35.2 %collective-permute-start.45 = (bf16[768,768]{1,0:T(8,128)(2,1)S(1)}, bf16[768,768]{1,0:T(8,128)(2,1)S(1)}, u32[]{:S(2)}, u32[]{:S(2)}) collective-permute-start(bf16[768,768]{1,0:T(8,128)(2,1)S(1)} %copy-done.107), channel_id=1, source_target_pairs={{0,1},{1,0},{2,3},{3,2},{4,5},{5,4},{6,7},{7,6},{8,9},{9,8},{10,11... | collective-permute-start | bytes 3538952 | tf_op jit(solution)/shard_map/ppermute | solution.py:457
  453.0 34.0 %collective-permute-start.44 = (bf16[768,768]{1,0:T(8,128)(2,1)S(1)}, bf16[768,768]{1,0:T(8,128)(2,1)S(1)}, u32[]{:S(2)}, u32[]{:S(2)}) collective-permute-start(bf16[768,768]{1,0:T(8,128)(2,1)S(1)} %get-tuple-element.309), channel_id=1, source_target_pairs={{0,1},{1,0},{2,3},{3,2},{4,5},{5,4},{6,7},{7,6},{8,9},{9,8},{10,11... | collective-permute-start | bytes 3538952 | tf_op jit(solution)/shard_map/ppermute | solution.py:457
  453.2 92.9 %collective-permute-start.59 = (bf16[768,768]{1,0:T(8,128)(2,1)}, bf16[768,768]{1,0:T(8,128)(2,1)}, u32[]{:S(2)}, u32[]{:S(2)}) collective-permute-start(bf16[768,768]{1,0:T(8,128)(2,1)} %get-tuple-element.381), channel_id=1, source_target_pairs={{0,1},{1,0},{2,3},{3,2},{4,5},{5,4},{6,7},{7,6},{8,9},{9,8},{10,11... | collective-permute-start | bytes 3538952 | tf_op jit(solution)/shard_map/ppermute | solution.py:457
  495.0 45.2 %collective-permute-start.51 = (bf16[768,768]{1,0:T(8,128)(2,1)}, bf16[768,768]{1,0:T(8,128)(2,1)}, u32[]{:S(2)}, u32[]{:S(2)}) collective-permute-start(bf16[768,768]{1,0:T(8,128)(2,1)} %get-tuple-element.342), channel_id=1, source_target_pairs={{0,1},{1,0},{2,3},{3,2},{4,5},{5,4},{6,7},{7,6},{8,9},{9,8},{10,11... | collective-permute-start | bytes 3538952 | tf_op jit(solution)/shard_map/ppermute | solution.py:457
  499.0 47.2 %collective-permute-start.60 = (bf16[768,768]{1,0:T(8,128)(2,1)}, bf16[768,768]{1,0:T(8,128)(2,1)}, u32[]{:S(2)}, u32[]{:S(2)}) collective-permute-start(bf16[768,768]{1,0:T(8,128)(2,1)} %add_convert_fusion.9), channel_id=1, source_target_pairs={{0,2},{1,3},{2,0},{3,1},{4,6},{5,7},{6,4},{7,5},{8,10},{9,11},{10,... | collective-permute-start | bytes 3538952 | tf_op jit(solution)/shard_map/ppermute | solution.py:457
  500.6 42.3 %collective-permute-start.53 = (bf16[768,768]{1,0:T(8,128)(2,1)}, bf16[768,768]{1,0:T(8,128)(2,1)}, u32[]{:S(2)}, u32[]{:S(2)}) collective-permute-start(bf16[768,768]{1,0:T(8,128)(2,1)} %get-tuple-element.354), channel_id=1, source_target_pairs={{0,1},{1,0},{2,3},{3,2},{4,5},{5,4},{6,7},{7,6},{8,9},{9,8},{10,11... | collective-permute-start | bytes 3538952 | tf_op jit(solution)/shard_map/ppermute | solution.py:457
  507.4 122.2 %collective-permute-start.72 = (bf16[768,768]{1,0:T(8,128)(2,1)}, bf16[768,768]{1,0:T(8,128)(2,1)}, u32[]{:S(2)}, u32[]{:S(2)}) collective-permute-start(bf16[768,768]{1,0:T(8,128)(2,1)} %get-tuple-element.330), channel_id=1, source_target_pairs={{0,1},{1,0},{2,3},{3,2},{4,5},{5,4},{6,7},{7,6},{8,9},{9,8},{10,11... | collective-permute-start | bytes 3538952 | tf_op jit(solution)/shard_map/ppermute | solution.py:457
  509.1 141.4 %reduce-scatter.7.cloned.1.call-start = ((), (), s32[]{:S(2)}) async-start(), calls=%async_computation.9 | async-start | bytes 983040 | tf_op jit(solution)/shard_map/reduce_scatter | solution.py:658
  540.3 45.3 %collective-permute-start.69 = (bf16[768,768]{1,0:T(8,128)(2,1)}, bf16[768,768]{1,0:T(8,128)(2,1)}, u32[]{:S(2)}, u32[]{:S(2)}) collective-permute-start(bf16[768,768]{1,0:T(8,128)(2,1)} %get-tuple-element.408), channel_id=1, source_target_pairs={{0,1},{1,0},{2,3},{3,2},{4,5},{5,4},{6,7},{7,6},{8,9},{9,8},{10,11... | collective-permute-start | bytes 3538952 | tf_op jit(solution)/shard_map/ppermute | solution.py:457
  542.9 42.6 %collective-permute-start.70 = (bf16[768,768]{1,0:T(8,128)(2,1)}, bf16[768,768]{1,0:T(8,128)(2,1)}, u32[]{:S(2)}, u32[]{:S(2)}) collective-permute-start(bf16[768,768]{1,0:T(8,128)(2,1)} %add_convert_fusion.6), channel_id=1, source_target_pairs={{0,2},{1,3},{2,0},{3,1},{4,6},{5,7},{6,4},{7,5},{8,10},{9,11},{10,... | collective-permute-start | bytes 3538952 | tf_op jit(solution)/shard_map/ppermute | solution.py:457
  576.7 139.1 %reduce-scatter.11.cloned.1.call-start = ((), (), s32[]{:S(2)}) async-start(), calls=%async_computation.11 | async-start | bytes 1474560 | tf_op jit(solution)/shard_map/reduce_scatter | solution.py:658
  588.3 46.4 %collective-permute-start.58 = (bf16[768,768]{1,0:T(8,128)(2,1)S(1)}, bf16[768,768]{1,0:T(8,128)(2,1)S(1)}, u32[]{:S(2)}, u32[]{:S(2)}) collective-permute-start(bf16[768,768]{1,0:T(8,128)(2,1)S(1)} %get-tuple-element.377), channel_id=1, source_target_pairs={{0,1},{1,0},{2,3},{3,2},{4,5},{5,4},{6,7},{7,6},{8,9},{9,8},{10,11... | collective-permute-start | bytes 3538952 | tf_op jit(solution)/shard_map/ppermute | solution.py:457
  592.5 58.0 %collective-permute-start.62 = (bf16[384,768]{1,0:T(8,128)(2,1)}, bf16[384,768]{1,0:T(8,128)(2,1)}, u32[]{:S(2)}, u32[]{:S(2)}) collective-permute-start(bf16[384,768]{1,0:T(8,128)(2,1)} %convert_element_type.277), channel_id=1, source_target_pairs={{0,16},{1,24},{2,20},{3,28},{4,18},{5,26},{6,22},{7,30},{8,17},{9,... | collective-permute-start | bytes 1769480 | tf_op jit(solution)/shard_map/ppermute | solution.py:488
  599.1 51.4 %collective-permute-start.63 = (bf16[384,768]{1,0:T(8,128)(2,1)}, bf16[384,768]{1,0:T(8,128)(2,1)}, u32[]{:S(2)}, u32[]{:S(2)}) collective-permute-start(bf16[384,768]{1,0:T(8,128)(2,1)} %convert_element_type.277), channel_id=1, source_target_pairs={{16,16},{17,24},{18,20},{19,28},{20,18},{21,26},{22,22},{23,30},{2... | collective-permute-start | bytes 1769480 | tf_op jit(solution)/shard_map/ppermute | solution.py:488
  605.0 37.3 %collective-permute-start.71 = (bf16[768,384]{1,0:T(8,128)(2,1)S(1)}, bf16[768,384]{1,0:T(8,128)(2,1)S(1)}, u32[]{:S(2)}, u32[]{:S(2)}) collective-permute-start(bf16[768,384]{1,0:T(8,128)(2,1)S(1)} %broadcast_select_fusion.5), channel_id=1, source_target_pairs={{0,16},{16,0},{1,17},{17,1},{2,18},{18,2},{3,19},{19,3},{4,20},{20... | collective-permute-start | bytes 1769480 | tf_op jit(solution)/shard_map/ppermute | solution.py:461
  634.7 37.7 %collective-permute-start.66 = (bf16[768,768]{1,0:T(8,128)(2,1)}, bf16[768,768]{1,0:T(8,128)(2,1)}, u32[]{:S(2)}, u32[]{:S(2)}) collective-permute-start(bf16[768,768]{1,0:T(8,128)(2,1)} %get-tuple-element.396), channel_id=1, source_target_pairs={{0,1},{1,0},{2,3},{3,2},{4,5},{5,4},{6,7},{7,6},{8,9},{9,8},{10,11... | collective-permute-start | bytes 3538952 | tf_op jit(solution)/shard_map/ppermute | solution.py:457
  659.1 76.0 %reduce-scatter.9.cloned.1.call-start = ((), (), s32[]{:S(2)}) async-start(), calls=%async_computation.10 | async-start | bytes 983040 | tf_op jit(solution)/shard_map/reduce_scatter | solution.py:658
  675.5 40.3 %collective-permute-start.65 = (bf16[384,768]{1,0:T(8,128)(2,1)S(1)}, bf16[384,768]{1,0:T(8,128)(2,1)}, u32[]{:S(2)}, u32[]{:S(2)}) collective-permute-start(bf16[384,768]{1,0:T(8,128)(2,1)S(1)} %copy-done.142), channel_id=1, source_target_pairs={{16,0},{17,8},{18,4},{19,12},{20,2},{21,10},{22,6},{23,14},{24,1},... | collective-permute-start | bytes 1769480 | tf_op jit(solution)/shard_map/ppermute | solution.py:488
  676.8 39.0 %collective-permute-start.64 = (bf16[384,768]{1,0:T(8,128)(2,1)S(1)}, bf16[384,768]{1,0:T(8,128)(2,1)S(1)}, u32[]{:S(2)}, u32[]{:S(2)}) collective-permute-start(bf16[384,768]{1,0:T(8,128)(2,1)S(1)} %copy-done.142), channel_id=1, source_target_pairs={{0,0},{1,8},{2,4},{3,12},{4,2},{5,10},{6,6},{7,14},{8,1},{9,9},{10... | collective-permute-start | bytes 1769480 | tf_op jit(solution)/shard_map/ppermute | solution.py:488
  (218 other events, 1780.8 us)
Sparse Core Ops, SparseCore 0:
  23.2 56.9 all-gather.4
  82.3 36.1 all-gather.8
  120.6 29.5 all-gather.10
  152.0 29.1 all-gather.6
  509.2 26.8 reduce-scatter.4
  576.8 21.3 reduce-scatter.6
  659.3 35.5 reduce-scatter.10
  715.9 19.1 reduce-scatter.8

commit v9 on v8

--- a/solution.py
+++ b/solution.py
@@ -696,7 +696,7 @@
                     half = after(above["half"], results[order[1]][0])
                     above["proj"] = scattered(jnp.concatenate([half, above["vec"]], 1))
             elif step == 3 and above is not None:
-                head = after(head, above["mlp"])
+                head = after(head, above["mlp"], *above["slots"])
             results[p] = attend_back(own_qkv[p], other_kv[p], weights[p], inverses[p], head, heads, frames)
             if step == 0:
                 far_up = low_sum(g_up[2], after(near_up[2], results[p][0]))
@@ -742,10 +742,10 @@
     y_one, kept_one = forward(x_one, 1)
     cot = [after(part, y_one) for part in pending_one["cot"]]
     g_one, one = backward(jnp.where(first, cot[0], cot[1]), 1, kept_one, None)
-    g_zero, zero = backward(g_one, 0, kept_zero, one)
     y_one = after(y_one, g_one)
     out_slots = [transposed(y_one, 0, 1), transposed(y_one, 1, 1)]
-    g_zero = after(g_zero, *out_slots)
+    one["slots"] = out_slots
+    g_zero, zero = backward(g_one, 0, kept_zero, one)
     back_slots = [transposed(g_zero, 0, 0), transposed(g_zero, 1, 0)]
     edges_out = jnp.stack([jnp.where(first, b, o) for b, o in zip(back_slots, out_slots)])
     mlp_one, proj_one = one["mlp"], one["proj"]

time: 773 us -> 755 us (0.977)
  starting transfers between devices: 158 us -> 137 us
    ppermute x12, starting transfers between devices: 49.8 us -> 28.8 us  [swap_sections(): return lax.ppermute(block, 'section', [(0, 1), (1, 0)])]
    ppermute x62, waiting for transfers between devices: 101 us -> 110 us  [across(): return lax.ppermute(block, 'replica', [(i, i ^ bit) for i in range(count)])]
  transfers between devices with their start and end apart: 91 -> 91, of which waited for: 22 -> 22; matrix products, arithmetic and copies ran while one was open for 14% -> 14% of each run, Pallas kernels for 28% -> 29%
where the time goes in v9:
time: 755 us; the launch traced here: 744 us
  Pallas kernels  228 us (30%)
  waiting for transfers between devices  202 us (27%)
  starting transfers between devices  137 us (18%)
  local copies, waits for them, and re-layouts  77.5 us (10%)
  other arithmetic  67.3 us (9%)
  between operations  16.8 us (2%)
  matrix products  15.8 us (2%)
    ppermute x62, waiting for transfers between devices, across(): return lax.ppermute(block, 'replica', [(i, i ^ bit) for i in range(count)])  110 us
    ppermute x62, starting transfers between devices, across(): return lax.ppermute(block, 'replica', [(i, i ^ bit) for i in range(count)])  88.3 us
    pallas_call x8, Pallas kernels, attend_back(): pl.pallas_call(functools.partial(attend_back_kernel, heads=heads, frames=...  63.2 us
    ppermute x12, waiting for transfers between devices, swap_sections(): return lax.ppermute(block, 'section', [(0, 1), (1, 0)])  62.1 us
    pallas_call x8, Pallas kernels, attend(): pl.pallas_call(functools.partial(attend_kernel, heads=heads, frames=frame...  51.8 us
    unnamed x356, local copies, waits for them, and re-layouts  48.8 us
    pallas_call x8, Pallas kernels, mlp_back_part(): pl.pallas_call(mlp_back_kernel, grid=(columns // tile,), in_specs=[whole,...  41.4 us
    pallas_call x8, Pallas kernels, mlp_part(): pl.pallas_call(mlp_kernel, grid=(columns // tile,), in_specs=[whole, pl.B...  34.3 us
  transfers between devices with their start and end apart: 91, of which 22 were waited for; matrix products, arithmetic and copies ran while one was open for 14% of the time, Pallas kernels for 29%

profile of v9, /device:TPU:0, one launch (start us, length us, event | category | flops | bytes accessed | tf_op | source)
XLA Modules:
  0.0 744.1 jit_solution(3225167163344550967)
XLA Ops:
  15.1 7.0 collective-permute-done.4
  24.2 6.0 collective-permute-start
  45.3 54.1 %collective-permute-start.2 = (bf16[384,768]{1,0:T(8,128)(2,1)S(1)}, bf16[384,768]{1,0:T(8,128)(2,1)S(1)}, u32[]{:S(2)}, u32[]{:S(2)}) collective-permute-start(bf16[384,768]{1,0:T(8,128)(2,1)S(1)} %get-tuple-element.463.x_ref), channel_id=1, source_target_pairs={{0,2},{1,3},{2,0},{3,1},{4,6},{5,7},{6,4},{7,5},{8,10},{9,11},{10,... | collective-permute-start | bytes 1769480 | tf_op jit(solution)/shard_map/ppermute | solution.py:457
  101.6 9.7 %collective-permute-done.2 = bf16[384,768]{1,0:T(8,128)(2,1)S(1)} collective-permute-done((bf16[384,768]{1,0:T(8,128)(2,1)S(1)}, bf16[384,768]{1,0:T(8,128)(2,1)S(1)}, u32[]{:S(2)}, u32[]{:S(2)}) %collective-permute-start.2) | collective-permute-done | bytes 589856 | tf_op jit(solution)/shard_map/ppermute | solution.py:457
  113.7 4.7 all-gather.9.cloned.1.call-done
  119.9 12.7 %collective-permute-done.9.weight_ref = bf16[768,768]{1,0:T(8,128)(2,1)} collective-permute-done((bf16[768,768]{1,0:T(8,128)(2,1)}, bf16[768,768]{1,0:T(8,128)(2,1)}, u32[]{:S(2)}, u32[]{:S(2)}) %collective-permute-start.9) | collective-permute-done | bytes 1179680 | tf_op jit(solution)/shard_map/ppermute | solution.py:457
  140.2 6.3 attend.8
  163.2 6.8 attend.10
  169.9 7.8 %collective-permute-done.16 = bf16[768,768]{1,0:T(8,128)(2,1)} collective-permute-done((bf16[768,768]{1,0:T(8,128)(2,1)}, bf16[768,768]{1,0:T(8,128)(2,1)}, u32[]{:S(2)}, u32[]{:S(2)}) %collective-permute-start.16) | collective-permute-done | bytes 1179680 | tf_op jit(solution)/shard_map/ppermute | solution.py:461
  190.9 6.3 attend.11
  197.3 17.2 %collective-permute-done.17.down_ref = bf16[768,768]{1,0:T(8,128)(2,1)} collective-permute-done((bf16[768,768]{1,0:T(8,128)(2,1)}, bf16[768,768]{1,0:T(8,128)(2,1)}, u32[]{:S(2)}, u32[]{:S(2)}) %collective-permute-start.17) | collective-permute-done | bytes 1179680 | tf_op jit(solution)/shard_map/ppermute | solution.py:457
  216.0 6.5 attend.9
  253.8 12.4 %collective-permute-done.22 = bf16[384,768]{1,0:T(8,128)(2,1)S(1)} collective-permute-done((bf16[384,768]{1,0:T(8,128)(2,1)S(1)}, bf16[384,768]{1,0:T(8,128)(2,1)S(1)}, u32[]{:S(2)}, u32[]{:S(2)}) %collective-permute-start.22) | collective-permute-done | bytes 589856 | tf_op jit(solution)/shard_map/ppermute | solution.py:457
  276.8 6.7 attend.13
  290.5 6.3 attend.12
  297.5 6.5 attend.15
  303.9 12.5 %collective-permute-done.32.down_ref = bf16[768,768]{1,0:T(8,128)(2,1)} collective-permute-done((bf16[768,768]{1,0:T(8,128)(2,1)}, bf16[768,768]{1,0:T(8,128)(2,1)}, u32[]{:S(2)}, u32[]{:S(2)}) %collective-permute-start.32) | collective-permute-done | bytes 1179680 | tf_op jit(solution)/shard_map/ppermute | solution.py:457
  322.3 6.3 attend.14
  334.6 4.3 mlp_part.12
  354.0 6.1 mlp_back_part.8
  360.7 4.6 mlp_back_part.9
  367.4 4.6 mlp_back_part.10
  374.1 4.7 mlp_back_part.11
  386.4 8.0 %attend_back.10 = (bf16[384,192]{1,0:T(8,128)(2,1)}, bf16[768,384]{1,0:T(8,128)(2,1)}, bf16[768,384]{1,0:T(8,128)(2,1)}) custom-call(bf16[768,576]{1,0:T(8,128)(2,1)} %copy-done.151, bf16[768,384]{1,0:T(8,128)(2,1)} %collective-permute-done.29.other_ref, bf16[3,1536,384]{2,1,0:T(8,128)(2,1)} %get-tuple-element.286.exp_ref, ...), custom_call_target="tpu_custom_call" | custom-call | flops 3623878656 | bytes 3538944 | tf_op jit(solution)/shard_map/attend_back/pallas_call | solution.py:157
  394.9 7.8 %attend_back.8 = (bf16[384,192]{1,0:T(8,128)(2,1)}, bf16[768,384]{1,0:T(8,128)(2,1)}, bf16[768,384]{1,0:T(8,128)(2,1)}) custom-call(bf16[768,576]{1,0:T(8,128)(2,1)} %copy-done.150, bf16[768,384]{1,0:T(8,128)(2,1)} %collective-permute-done.26.other_ref, bf16[3,1536,384]{2,1,0:T(8,128)(2,1)} %get-tuple-element.265.exp_ref, ...), custom_call_target="tpu_custom_call" | custom-call | flops 3623878656 | bytes 3538944 | tf_op jit(solution)/shard_map/attend_back/pallas_call | solution.py:157
  406.1 7.6 %collective-permute-start.49 = (bf16[768,768]{1,0:T(8,128)(2,1)}, bf16[768,768]{1,0:T(8,128)(2,1)}, u32[]{:S(2)}, u32[]{:S(2)}) collective-permute-start(bf16[768,768]{1,0:T(8,128)(2,1)} %add_convert_fusion.10), channel_id=1, source_target_pairs={{0,2},{1,3},{2,0},{3,1},{4,6},{5,7},{6,4},{7,5},{8,10},{9,11},{10,... | collective-permute-start | bytes 3538952 | tf_op jit(solution)/shard_map/ppermute | solution.py:457
  413.7 8.2 %attend_back.11 = (bf16[384,192]{1,0:T(8,128)(2,1)}, bf16[768,384]{1,0:T(8,128)(2,1)}, bf16[768,384]{1,0:T(8,128)(2,1)}) custom-call(bf16[768,576]{1,0:T(8,128)(2,1)} %copy-done.149, bf16[768,384]{1,0:T(8,128)(2,1)} %collective-permute-done.28.other_ref, bf16[3,1536,384]{2,1,0:T(8,128)(2,1)} %get-tuple-element.281.exp_ref, ...), custom_call_target="tpu_custom_call" | custom-call | flops 3623878656 | bytes 3538944 | tf_op jit(solution)/shard_map/attend_back/pallas_call | solution.py:157
  425.1 8.0 %attend_back.9 = (bf16[384,192]{1,0:T(8,128)(2,1)}, bf16[768,384]{1,0:T(8,128)(2,1)}, bf16[768,384]{1,0:T(8,128)(2,1)}) custom-call(bf16[768,576]{1,0:T(8,128)(2,1)} %copy-done.148, bf16[768,384]{1,0:T(8,128)(2,1)} %collective-permute-done.24.other_ref, bf16[3,1536,384]{2,1,0:T(8,128)(2,1)} %get-tuple-element.269.exp_ref, ...), custom_call_target="tpu_custom_call" | custom-call | flops 3623878656 | bytes 3538944 | tf_op jit(solution)/shard_map/attend_back/pallas_call | solution.py:157
  455.7 10.3 %collective-permute-done.46 = bf16[768,768]{1,0:T(8,128)(2,1)S(1)} collective-permute-done((bf16[768,768]{1,0:T(8,128)(2,1)}, bf16[768,768]{1,0:T(8,128)(2,1)S(1)}, u32[]{:S(2)}, u32[]{:S(2)}) %collective-permute-start.46) | collective-permute-done | bytes 1179680 | tf_op jit(solution)/shard_map/ppermute | solution.py:457
  466.1 5.7 collective-permute-start.50
  471.8 6.7 collective-permute-done.43
  479.6 5.8 collective-permute-start.47
  489.1 6.1 mlp_back_part.12
  500.7 5.7 mlp_back_part.13
  508.7 4.5 collective-permute-start.51
  518.7 4.7 mlp_back_part.14
  523.5 4.7 mlp_back_part.15
  536.3 7.8 %attend_back.14 = (bf16[384,192]{1,0:T(8,128)(2,1)}, bf16[768,384]{1,0:T(8,128)(2,1)}, bf16[768,384]{1,0:T(8,128)(2,1)}) custom-call(bf16[768,576]{1,0:T(8,128)(2,1)} %copy-done.147, bf16[768,384]{1,0:T(8,128)(2,1)} %collective-permute-done.12.other_ref, bf16[3,1536,384]{2,1,0:T(8,128)(2,1)} %get-tuple-element.355.exp_ref, ...), custom_call_target="tpu_custom_call" | custom-call | flops 3623878656 | bytes 3538944 | tf_op jit(solution)/shard_map/attend_back/pallas_call | solution.py:157
  556.4 7.8 %attend_back.13 = (bf16[384,192]{1,0:T(8,128)(2,1)}, bf16[768,384]{1,0:T(8,128)(2,1)}, bf16[768,384]{1,0:T(8,128)(2,1)}) custom-call(bf16[768,576]{1,0:T(8,128)(2,1)} %copy-done.145, bf16[768,384]{1,0:T(8,128)(2,1)} %collective-permute-done.8.other_ref, bf16[3,1536,384]{2,1,0:T(8,128)(2,1)} %get-tuple-element.338.exp_ref, ...), custom_call_target="tpu_custom_call" | custom-call | flops 3623878656 | bytes 3538944 | tf_op jit(solution)/shard_map/attend_back/pallas_call | solution.py:157
  564.2 7.8 %attend_back.15 = (bf16[384,192]{1,0:T(8,128)(2,1)}, bf16[768,384]{1,0:T(8,128)(2,1)}, bf16[768,384]{1,0:T(8,128)(2,1)}) custom-call(bf16[768,576]{1,0:T(8,128)(2,1)} %add_convert_fusion.17.own_ref, bf16[768,384]{1,0:T(8,128)(2,1)} %copy-done.172, bf16[3,1536,384]{2,1,0:T(8,128)(2,1)} %get-tuple-element.350.exp_ref, f32[3,384]{1,0:T(4,128)} %get-tuple-element.351.inv_ref, ...), custom_call_target="tpu_custom_call" | custom-call | flops 3623878656 | bytes 3538944 | tf_op jit(solution)/shard_map/attend_back/pallas_call | solution.py:157
  573.6 7.9 %attend_back.12 = (bf16[384,192]{1,0:T(8,128)(2,1)}, bf16[768,384]{1,0:T(8,128)(2,1)}, bf16[768,384]{1,0:T(8,128)(2,1)}) custom-call(bf16[768,576]{1,0:T(8,128)(2,1)} %add_convert_fusion.19.own_ref, bf16[768,384]{1,0:T(8,128)(2,1)} %collective-permute-done.6.other_ref, bf16[3,1536,384]{2,1,0:T(8,128)(2,1)} %get-tuple-element.323.exp_ref, ...), custom_call_target="tpu_custom_call" | custom-call | flops 3623878656 | bytes 3538944 | tf_op jit(solution)/shard_map/attend_back/pallas_call | solution.py:157
  606.3 5.7 collective-permute-done.73
  627.1 4.5 collective-permute-done.74
  634.8 14.9 %collective-permute-done.67 = bf16[768,768]{1,0:T(8,128)(2,1)} collective-permute-done((bf16[768,768]{1,0:T(8,128)(2,1)}, bf16[768,768]{1,0:T(8,128)(2,1)}, u32[]{:S(2)}, u32[]{:S(2)}) %collective-permute-start.67) | collective-permute-done | bytes 1179680 | tf_op jit(solution)/shard_map/ppermute | solution.py:457
  657.1 28.3 %collective-permute-done.68 = bf16[768,384]{1,0:T(8,128)(2,1)S(1)} collective-permute-done((bf16[768,384]{1,0:T(8,128)(2,1)S(1)}, bf16[768,384]{1,0:T(8,128)(2,1)S(1)}, u32[]{:S(2)}, u32[]{:S(2)}) %collective-permute-start.68) | collective-permute-done | bytes 589856 | tf_op jit(solution)/shard_map/ppermute | solution.py:461
  686.6 10.2 %collective-permute-done.65 = bf16[384,768]{1,0:T(8,128)(2,1)} collective-permute-done((bf16[384,768]{1,0:T(8,128)(2,1)S(1)}, bf16[384,768]{1,0:T(8,128)(2,1)}, u32[]{:S(2)}, u32[]{:S(2)}) %collective-permute-start.65) | collective-permute-done | bytes 589856 | tf_op jit(solution)/shard_map/ppermute | solution.py:488
  698.0 6.7 collective-permute-done.75
  704.9 11.3 %reduce-scatter.9.cloned.1.call-done = bf16[192,512]{1,0:T(8,128)(2,1)} async-done(((bf16[768,512]{1,0:T(8,128)(2,1)}), bf16[192,512]{1,0:T(8,128)(2,1)}) %reduce-scatter.9.cloned.1.call-update) | async-done | bytes 196624 | tf_op jit(solution)/shard_map/reduce_scatter | solution.py:658
  (696 shorter events, 300.1 us)
Async XLA Ops:
  7.2 93.8 %all-gather.5.cloned.1.call-start = ((), (), s32[]{:S(2)}) async-start(), calls=%async_computation.4 | async-start | bytes 1474560 | tf_op jit(solution)/shard_map/all_gather | solution.py:542
  23.1 95.4 %all-gather.9.cloned.1.call-start = ((), (), s32[]{:S(2)}) async-start(), calls=%async_computation.6 | async-start | bytes 1474560 | tf_op jit(solution)/shard_map/all_gather | solution.py:542
  41.8 108.5 %all-gather.11.cloned.1.call-start = ((), (), s32[]{:S(2)}) async-start(), calls=%async_computation.7 | async-start | bytes 1474560 | tf_op jit(solution)/shard_map/all_gather | solution.py:542
  41.9 57.5 %collective-permute-start.3 = (f32[12,768]{1,0:T(8,128)S(1)}, f32[12,768]{1,0:T(8,128)S(1)}, u32[]{:S(2)}, u32[]{:S(2)}) collective-permute-start(f32[12,768]{1,0:T(8,128)S(1)} %bitcast.65), channel_id=1, source_target_pairs={{0,16},{16,0},{1,17},{17,1},{2,18},{18,2},{3,19},{19,3},{4,20},{20... | collective-permute-start | bytes 110600 | tf_op jit(solution)/shard_map/ppermute | solution.py:461
  45.3 66.1 %collective-permute-start.2 = (bf16[384,768]{1,0:T(8,128)(2,1)S(1)}, bf16[384,768]{1,0:T(8,128)(2,1)S(1)}, u32[]{:S(2)}, u32[]{:S(2)}) collective-permute-start(bf16[384,768]{1,0:T(8,128)(2,1)S(1)} %get-tuple-element.463.x_ref), channel_id=1, source_target_pairs={{0,2},{1,3},{2,0},{3,1},{4,6},{5,7},{6,4},{7,5},{8,10},{9,11},{10,... | collective-permute-start | bytes 1769480 | tf_op jit(solution)/shard_map/ppermute | solution.py:457
  101.0 31.6 %collective-permute-start.5 = (bf16[768,768]{1,0:T(8,128)(2,1)}, bf16[768,768]{1,0:T(8,128)(2,1)S(1)}, u32[]{:S(2)}, u32[]{:S(2)}) collective-permute-start(bf16[768,768]{1,0:T(8,128)(2,1)} %all-gather.5.cloned.1.call-done.weight_ref), channel_id=1, source_target_pairs={{0,1},{1,0},{2,3},{3,2},{4,5},{5,4},{6,7},{7,6},{8,9},{9,8},{10,11... | collective-permute-start | bytes 3538952 | tf_op jit(solution)/shard_map/ppermute | solution.py:457
  101.0 31.6 %collective-permute-start.9 = (bf16[768,768]{1,0:T(8,128)(2,1)}, bf16[768,768]{1,0:T(8,128)(2,1)}, u32[]{:S(2)}, u32[]{:S(2)}) collective-permute-start(bf16[768,768]{1,0:T(8,128)(2,1)} %all-gather.5.cloned.1.call-done.weight_ref), channel_id=1, source_target_pairs={{0,2},{1,3},{2,0},{3,1},{4,6},{5,7},{6,4},{7,5},{8,10},{9,11},{10,... | collective-permute-start | bytes 3538952 | tf_op jit(solution)/shard_map/ppermute | solution.py:457
  101.4 89.0 %all-gather.7.cloned.1.call-start = ((), (), s32[]{:S(2)}) async-start(), calls=%async_computation.5 | async-start | bytes 1474560 | tf_op jit(solution)/shard_map/all_gather | solution.py:542
  118.5 39.5 %collective-permute-start.13 = (bf16[768,768]{1,0:T(8,128)(2,1)}, bf16[768,768]{1,0:T(8,128)(2,1)}, u32[]{:S(2)}, u32[]{:S(2)}) collective-permute-start(bf16[768,768]{1,0:T(8,128)(2,1)} %all-gather.9.cloned.1.call-done), channel_id=1, source_target_pairs={{0,16},{16,0},{1,17},{17,1},{2,18},{18,2},{3,19},{19,3},{4,20},{20... | collective-permute-start | bytes 3538952 | tf_op jit(solution)/shard_map/ppermute | solution.py:461
  151.9 421.7 %reduce-scatter.5.cloned.1.call-start = ((), (), s32[]{:S(2)}) async-start(), calls=%async_computation.8 | async-start | bytes 1474560 | tf_op jit(solution)/shard_map/reduce_scatter | solution.py:658
  160.9 36.3 %collective-permute-start.14 = (bf16[768,768]{1,0:T(8,128)(2,1)}, bf16[768,768]{1,0:T(8,128)(2,1)}, u32[]{:S(2)}, u32[]{:S(2)}) collective-permute-start(bf16[768,768]{1,0:T(8,128)(2,1)} %get-tuple-element.478.up_ref), channel_id=1, source_target_pairs={{0,2},{1,3},{2,0},{3,1},{4,6},{5,7},{6,4},{7,5},{8,10},{9,11},{10,... | collective-permute-start | bytes 3538952 | tf_op jit(solution)/shard_map/ppermute | solution.py:457
  180.6 33.8 %collective-permute-start.17 = (bf16[768,768]{1,0:T(8,128)(2,1)}, bf16[768,768]{1,0:T(8,128)(2,1)}, u32[]{:S(2)}, u32[]{:S(2)}) collective-permute-start(bf16[768,768]{1,0:T(8,128)(2,1)} %get-tuple-element.476.down_ref), channel_id=1, source_target_pairs={{0,2},{1,3},{2,0},{3,1},{4,6},{5,7},{6,4},{7,5},{8,10},{9,11},{10,... | collective-permute-start | bytes 3538952 | tf_op jit(solution)/shard_map/ppermute | solution.py:457
  183.9 32.1 %collective-permute-start.8 = (bf16[768,384]{1,0:T(8,128)(2,1)}, bf16[768,384]{1,0:T(8,128)(2,1)}, u32[]{:S(2)}, u32[]{:S(2)}) collective-permute-start(bf16[768,384]{1,0:T(8,128)(2,1)} %slice.288), channel_id=1, source_target_pairs={{0,1},{1,0},{2,3},{3,2},{4,5},{5,4},{6,7},{7,6},{8,9},{9,8},{10,11... | collective-permute-start | bytes 1769480 | tf_op jit(solution)/shard_map/ppermute | solution.py:457
  190.3 43.2 %collective-permute-start.19 = (bf16[768,768]{1,0:T(8,128)(2,1)}, bf16[768,768]{1,0:T(8,128)(2,1)}, u32[]{:S(2)}, u32[]{:S(2)}) collective-permute-start(bf16[768,768]{1,0:T(8,128)(2,1)} %get-tuple-element.478.up_ref), channel_id=1, source_target_pairs={{0,1},{1,0},{2,3},{3,2},{4,5},{5,4},{6,7},{7,6},{8,9},{9,8},{10,11... | collective-permute-start | bytes 3538952 | tf_op jit(solution)/shard_map/ppermute | solution.py:457
  190.4 43.1 %collective-permute-start.20 = (bf16[768,768]{1,0:T(8,128)(2,1)}, bf16[768,768]{1,0:T(8,128)(2,1)}, u32[]{:S(2)}, u32[]{:S(2)}) collective-permute-start(bf16[768,768]{1,0:T(8,128)(2,1)} %get-tuple-element.476.down_ref), channel_id=1, source_target_pairs={{0,1},{1,0},{2,3},{3,2},{4,5},{5,4},{6,7},{7,6},{8,9},{9,8},{10,11... | collective-permute-start | bytes 3538952 | tf_op jit(solution)/shard_map/ppermute | solution.py:457
  197.2 48.3 %collective-permute-start.15 = (bf16[768,768]{1,0:T(8,128)(2,1)}, bf16[768,768]{1,0:T(8,128)(2,1)}, u32[]{:S(2)}, u32[]{:S(2)}) collective-permute-start(bf16[768,768]{1,0:T(8,128)(2,1)} %collective-permute-done.14.up_ref), channel_id=1, source_target_pairs={{0,1},{1,0},{2,3},{3,2},{4,5},{5,4},{6,7},{7,6},{8,9},{9,8},{10,11... | collective-permute-start | bytes 3538952 | tf_op jit(solution)/shard_map/ppermute | solution.py:457
  214.5 31.0 %collective-permute-start.21 = (bf16[768,768]{1,0:T(8,128)(2,1)}, bf16[768,768]{1,0:T(8,128)(2,1)}, u32[]{:S(2)}, u32[]{:S(2)}) collective-permute-start(bf16[768,768]{1,0:T(8,128)(2,1)} %all-gather.7.cloned.1.call-done.weight_ref), channel_id=1, source_target_pairs={{0,2},{1,3},{2,0},{3,1},{4,6},{5,7},{6,4},{7,5},{8,10},{9,11},{10,... | collective-permute-start | bytes 3538952 | tf_op jit(solution)/shard_map/ppermute | solution.py:457
  252.0 81.8 %collective-permute-start.34 = (bf16[768,768]{1,0:T(8,128)(2,1)}, bf16[768,768]{1,0:T(8,128)(2,1)}, u32[]{:S(2)}, u32[]{:S(2)}) collective-permute-start(bf16[768,768]{1,0:T(8,128)(2,1)} %get-tuple-element.241.up_ref), channel_id=1, source_target_pairs={{0,1},{1,0},{2,3},{3,2},{4,5},{5,4},{6,7},{7,6},{8,9},{9,8},{10,11... | collective-permute-start | bytes 3538952 | tf_op jit(solution)/shard_map/ppermute | solution.py:457
  252.5 44.4 %collective-permute-start.30 = (bf16[768,768]{1,0:T(8,128)(2,1)}, bf16[768,768]{1,0:T(8,128)(2,1)}, u32[]{:S(2)}, u32[]{:S(2)}) collective-permute-start(bf16[768,768]{1,0:T(8,128)(2,1)} %get-tuple-element.241.up_ref), channel_id=1, source_target_pairs={{0,2},{1,3},{2,0},{3,1},{4,6},{5,7},{6,4},{7,5},{8,10},{9,11},{10,... | collective-permute-start | bytes 3538952 | tf_op jit(solution)/shard_map/ppermute | solution.py:457
  283.6 32.8 %collective-permute-start.32 = (bf16[768,768]{1,0:T(8,128)(2,1)}, bf16[768,768]{1,0:T(8,128)(2,1)}, u32[]{:S(2)}, u32[]{:S(2)}) collective-permute-start(bf16[768,768]{1,0:T(8,128)(2,1)} %get-tuple-element.243.down_ref), channel_id=1, source_target_pairs={{0,2},{1,3},{2,0},{3,1},{4,6},{5,7},{6,4},{7,5},{8,10},{9,11},{10,... | collective-permute-start | bytes 3538952 | tf_op jit(solution)/shard_map/ppermute | solution.py:457
  290.5 48.4 %collective-permute-start.35 = (bf16[768,768]{1,0:T(8,128)(2,1)}, bf16[768,768]{1,0:T(8,128)(2,1)}, u32[]{:S(2)}, u32[]{:S(2)}) collective-permute-start(bf16[768,768]{1,0:T(8,128)(2,1)} %get-tuple-element.243.down_ref), channel_id=1, source_target_pairs={{0,1},{1,0},{2,3},{3,2},{4,5},{5,4},{6,7},{7,6},{8,9},{9,8},{10,11... | collective-permute-start | bytes 3538952 | tf_op jit(solution)/shard_map/ppermute | solution.py:457
  297.4 50.1 %collective-permute-start.31 = (bf16[768,768]{1,0:T(8,128)(2,1)}, bf16[768,768]{1,0:T(8,128)(2,1)}, u32[]{:S(2)}, u32[]{:S(2)}) collective-permute-start(bf16[768,768]{1,0:T(8,128)(2,1)} %collective-permute-done.30.up_ref), channel_id=1, source_target_pairs={{0,1},{1,0},{2,3},{3,2},{4,5},{5,4},{6,7},{7,6},{8,9},{9,8},{10,11... | collective-permute-start | bytes 3538952 | tf_op jit(solution)/shard_map/ppermute | solution.py:457
  316.4 31.1 %collective-permute-start.33 = (bf16[768,768]{1,0:T(8,128)(2,1)}, bf16[768,768]{1,0:T(8,128)(2,1)}, u32[]{:S(2)}, u32[]{:S(2)}) collective-permute-start(bf16[768,768]{1,0:T(8,128)(2,1)} %collective-permute-done.32.down_ref), channel_id=1, source_target_pairs={{0,1},{1,0},{2,3},{3,2},{4,5},{5,4},{6,7},{7,6},{8,9},{9,8},{10,11... | collective-permute-start | bytes 3538952 | tf_op jit(solution)/shard_map/ppermute | solution.py:457
  320.9 31.8 %collective-permute-start.25 = (bf16[384,768]{1,0:T(8,128)(2,1)}, bf16[384,768]{1,0:T(8,128)(2,1)}, u32[]{:S(2)}, u32[]{:S(2)}) collective-permute-start(bf16[384,768]{1,0:T(8,128)(2,1)} %get-tuple-element.480), channel_id=1, source_target_pairs={{16,0},{17,8},{18,4},{19,12},{20,2},{21,10},{22,6},{23,14},{24,1},... | collective-permute-start | bytes 1769480 | tf_op jit(solution)/shard_map/ppermute | solution.py:488
  360.1 43.1 %collective-permute-start.37 = (bf16[768,768]{1,0:T(8,128)(2,1)}, bf16[768,768]{1,0:T(8,128)(2,1)}, u32[]{:S(2)}, u32[]{:S(2)}) collective-permute-start(bf16[768,768]{1,0:T(8,128)(2,1)} %get-tuple-element.273), channel_id=1, source_target_pairs={{0,1},{1,0},{2,3},{3,2},{4,5},{5,4},{6,7},{7,6},{8,9},{9,8},{10,11... | collective-permute-start | bytes 3538952 | tf_op jit(solution)/shard_map/ppermute | solution.py:457
  360.6 42.6 %collective-permute-start.39 = (bf16[768,768]{1,0:T(8,128)(2,1)}, bf16[768,768]{1,0:T(8,128)(2,1)}, u32[]{:S(2)}, u32[]{:S(2)}) collective-permute-start(bf16[768,768]{1,0:T(8,128)(2,1)} %get-tuple-element.285), channel_id=1, source_target_pairs={{0,1},{1,0},{2,3},{3,2},{4,5},{5,4},{6,7},{7,6},{8,9},{9,8},{10,11... | collective-permute-start | bytes 3538952 | tf_op jit(solution)/shard_map/ppermute | solution.py:457
  394.5 49.5 %collective-permute-start.40 = (bf16[768,384]{1,0:T(8,128)(2,1)}, bf16[768,384]{1,0:T(8,128)(2,1)}, u32[]{:S(2)}, u32[]{:S(2)}) collective-permute-start(bf16[768,384]{1,0:T(8,128)(2,1)} %get-tuple-element.293), channel_id=1, source_target_pairs={{0,1},{1,0},{2,3},{3,2},{4,5},{5,4},{6,7},{7,6},{8,9},{9,8},{10,11... | collective-permute-start | bytes 1769480 | tf_op jit(solution)/shard_map/ppermute | solution.py:457
  402.7 50.5 %collective-permute-start.48 = (bf16[768,768]{1,0:T(8,128)(2,1)}, bf16[768,768]{1,0:T(8,128)(2,1)}, u32[]{:S(2)}, u32[]{:S(2)}) collective-permute-start(bf16[768,768]{1,0:T(8,128)(2,1)} %copy-done.108), channel_id=1, source_target_pairs={{0,1},{1,0},{2,3},{3,2},{4,5},{5,4},{6,7},{7,6},{8,9},{9,8},{10,11... | collective-permute-start | bytes 3538952 | tf_op jit(solution)/shard_map/ppermute | solution.py:457
  406.1 46.9 %collective-permute-start.49 = (bf16[768,768]{1,0:T(8,128)(2,1)}, bf16[768,768]{1,0:T(8,128)(2,1)}, u32[]{:S(2)}, u32[]{:S(2)}) collective-permute-start(bf16[768,768]{1,0:T(8,128)(2,1)} %add_convert_fusion.10), channel_id=1, source_target_pairs={{0,2},{1,3},{2,0},{3,1},{4,6},{5,7},{6,4},{7,5},{8,10},{9,11},{10,... | collective-permute-start | bytes 3538952 | tf_op jit(solution)/shard_map/ppermute | solution.py:457
  433.5 32.6 %collective-permute-start.46 = (bf16[768,768]{1,0:T(8,128)(2,1)}, bf16[768,768]{1,0:T(8,128)(2,1)S(1)}, u32[]{:S(2)}, u32[]{:S(2)}) collective-permute-start(bf16[768,768]{1,0:T(8,128)(2,1)} %add_convert_fusion.11), channel_id=1, source_target_pairs={{0,2},{1,3},{2,0},{3,1},{4,6},{5,7},{6,4},{7,5},{8,10},{9,11},{10,... | collective-permute-start | bytes 3538952 | tf_op jit(solution)/shard_map/ppermute | solution.py:457
  444.0 35.1 %collective-permute-start.45 = (bf16[768,768]{1,0:T(8,128)(2,1)S(1)}, bf16[768,768]{1,0:T(8,128)(2,1)S(1)}, u32[]{:S(2)}, u32[]{:S(2)}) collective-permute-start(bf16[768,768]{1,0:T(8,128)(2,1)S(1)} %copy-done.107), channel_id=1, source_target_pairs={{0,1},{1,0},{2,3},{3,2},{4,5},{5,4},{6,7},{7,6},{8,9},{9,8},{10,11... | collective-permute-start | bytes 3538952 | tf_op jit(solution)/shard_map/ppermute | solution.py:457
  453.1 34.0 %collective-permute-start.44 = (bf16[768,768]{1,0:T(8,128)(2,1)S(1)}, bf16[768,768]{1,0:T(8,128)(2,1)S(1)}, u32[]{:S(2)}, u32[]{:S(2)}) collective-permute-start(bf16[768,768]{1,0:T(8,128)(2,1)S(1)} %get-tuple-element.308), channel_id=1, source_target_pairs={{0,1},{1,0},{2,3},{3,2},{4,5},{5,4},{6,7},{7,6},{8,9},{9,8},{10,11... | collective-permute-start | bytes 3538952 | tf_op jit(solution)/shard_map/ppermute | solution.py:457
  453.3 98.8 %collective-permute-start.61 = (bf16[768,768]{1,0:T(8,128)(2,1)}, bf16[768,768]{1,0:T(8,128)(2,1)}, u32[]{:S(2)}, u32[]{:S(2)}) collective-permute-start(bf16[768,768]{1,0:T(8,128)(2,1)} %get-tuple-element.381), channel_id=1, source_target_pairs={{0,1},{1,0},{2,3},{3,2},{4,5},{5,4},{6,7},{7,6},{8,9},{9,8},{10,11... | collective-permute-start | bytes 3538952 | tf_op jit(solution)/shard_map/ppermute | solution.py:457
  495.1 49.1 %collective-permute-start.53 = (bf16[768,768]{1,0:T(8,128)(2,1)}, bf16[768,768]{1,0:T(8,128)(2,1)}, u32[]{:S(2)}, u32[]{:S(2)}) collective-permute-start(bf16[768,768]{1,0:T(8,128)(2,1)} %get-tuple-element.342), channel_id=1, source_target_pairs={{0,1},{1,0},{2,3},{3,2},{4,5},{5,4},{6,7},{7,6},{8,9},{9,8},{10,11... | collective-permute-start | bytes 3538952 | tf_op jit(solution)/shard_map/ppermute | solution.py:457
  499.0 52.1 %collective-permute-start.62 = (bf16[768,768]{1,0:T(8,128)(2,1)}, bf16[768,768]{1,0:T(8,128)(2,1)}, u32[]{:S(2)}, u32[]{:S(2)}) collective-permute-start(bf16[768,768]{1,0:T(8,128)(2,1)} %add_convert_fusion.9), channel_id=1, source_target_pairs={{0,2},{1,3},{2,0},{3,1},{4,6},{5,7},{6,4},{7,5},{8,10},{9,11},{10,... | collective-permute-start | bytes 3538952 | tf_op jit(solution)/shard_map/ppermute | solution.py:457
  500.6 47.8 %collective-permute-start.55 = (bf16[768,768]{1,0:T(8,128)(2,1)}, bf16[768,768]{1,0:T(8,128)(2,1)}, u32[]{:S(2)}, u32[]{:S(2)}) collective-permute-start(bf16[768,768]{1,0:T(8,128)(2,1)} %get-tuple-element.354), channel_id=1, source_target_pairs={{0,1},{1,0},{2,3},{3,2},{4,5},{5,4},{6,7},{7,6},{8,9},{9,8},{10,11... | collective-permute-start | bytes 3538952 | tf_op jit(solution)/shard_map/ppermute | solution.py:457
  508.6 118.5 %reduce-scatter.7.cloned.1.call-start = ((), (), s32[]{:S(2)}) async-start(), calls=%async_computation.9 | async-start | bytes 983040 | tf_op jit(solution)/shard_map/reduce_scatter | solution.py:658
  508.7 64.7 %collective-permute-start.51 = (bf16[384,768]{1,0:T(8,128)(2,1)}, bf16[384,768]{1,0:T(8,128)(2,1)}, u32[]{:S(2)}, u32[]{:S(2)}) collective-permute-start(bf16[384,768]{1,0:T(8,128)(2,1)} %convert_element_type.277), channel_id=1, source_target_pairs={{0,16},{1,24},{2,20},{3,28},{4,18},{5,26},{6,22},{7,30},{8,17},{9,... | collective-permute-start | bytes 1769480 | tf_op jit(solution)/shard_map/ppermute | solution.py:488
  548.4 43.9 %collective-permute-start.69 = (bf16[768,768]{1,0:T(8,128)(2,1)}, bf16[768,768]{1,0:T(8,128)(2,1)}, u32[]{:S(2)}, u32[]{:S(2)}) collective-permute-start(bf16[768,768]{1,0:T(8,128)(2,1)} %get-tuple-element.406), channel_id=1, source_target_pairs={{0,1},{1,0},{2,3},{3,2},{4,5},{5,4},{6,7},{7,6},{8,9},{9,8},{10,11... | collective-permute-start | bytes 3538952 | tf_op jit(solution)/shard_map/ppermute | solution.py:457
  551.1 41.0 %collective-permute-start.70 = (bf16[768,768]{1,0:T(8,128)(2,1)}, bf16[768,768]{1,0:T(8,128)(2,1)}, u32[]{:S(2)}, u32[]{:S(2)}) collective-permute-start(bf16[768,768]{1,0:T(8,128)(2,1)} %add_convert_fusion.6), channel_id=1, source_target_pairs={{0,2},{1,3},{2,0},{3,1},{4,6},{5,7},{6,4},{7,5},{8,10},{9,11},{10,... | collective-permute-start | bytes 3538952 | tf_op jit(solution)/shard_map/ppermute | solution.py:457
  573.3 38.7 %collective-permute-start.72 = (bf16[768,768]{1,0:T(8,128)(2,1)}, bf16[768,768]{1,0:T(8,128)(2,1)}, u32[]{:S(2)}, u32[]{:S(2)}) collective-permute-start(bf16[768,768]{1,0:T(8,128)(2,1)} %get-tuple-element.329), channel_id=1, source_target_pairs={{0,1},{1,0},{2,3},{3,2},{4,5},{5,4},{6,7},{7,6},{8,9},{9,8},{10,11... | collective-permute-start | bytes 3538952 | tf_op jit(solution)/shard_map/ppermute | solution.py:457
  582.7 114.2 %reduce-scatter.11.cloned.1.call-start = ((), (), s32[]{:S(2)}) async-start(), calls=%async_computation.11 | async-start | bytes 1474560 | tf_op jit(solution)/shard_map/reduce_scatter | solution.py:658
  612.0 37.7 %collective-permute-start.66 = (bf16[768,768]{1,0:T(8,128)(2,1)}, bf16[768,768]{1,0:T(8,128)(2,1)}, u32[]{:S(2)}, u32[]{:S(2)}) collective-permute-start(bf16[768,768]{1,0:T(8,128)(2,1)} %get-tuple-element.394), channel_id=1, source_target_pairs={{0,1},{1,0},{2,3},{3,2},{4,5},{5,4},{6,7},{7,6},{8,9},{9,8},{10,11... | collective-permute-start | bytes 3538952 | tf_op jit(solution)/shard_map/ppermute | solution.py:457
  618.7 31.0 %collective-permute-start.67 = (bf16[768,768]{1,0:T(8,128)(2,1)}, bf16[768,768]{1,0:T(8,128)(2,1)}, u32[]{:S(2)}, u32[]{:S(2)}) collective-permute-start(bf16[768,768]{1,0:T(8,128)(2,1)} %add_convert_fusion.4), channel_id=1, source_target_pairs={{0,2},{1,3},{2,0},{3,1},{4,6},{5,7},{6,4},{7,5},{8,10},{9,11},{10,... | collective-permute-start | bytes 3538952 | tf_op jit(solution)/shard_map/ppermute | solution.py:457
  634.5 81.7 %reduce-scatter.9.cloned.1.call-start = ((), (), s32[]{:S(2)}) async-start(), calls=%async_computation.10 | async-start | bytes 983040 | tf_op jit(solution)/shard_map/reduce_scatter | solution.py:658
  652.0 33.4 %collective-permute-start.68 = (bf16[768,384]{1,0:T(8,128)(2,1)S(1)}, bf16[768,384]{1,0:T(8,128)(2,1)S(1)}, u32[]{:S(2)}, u32[]{:S(2)}) collective-permute-start(bf16[768,384]{1,0:T(8,128)(2,1)S(1)} %broadcast_select_fusion.6), channel_id=1, source_target_pairs={{0,16},{16,0},{1,17},{17,1},{2,18},{18,2},{3,19},{19,3},{4,20},{20... | collective-permute-start | bytes 1769480 | tf_op jit(solution)/shard_map/ppermute | solution.py:461
  654.7 42.1 %collective-permute-start.65 = (bf16[384,768]{1,0:T(8,128)(2,1)S(1)}, bf16[384,768]{1,0:T(8,128)(2,1)}, u32[]{:S(2)}, u32[]{:S(2)}) collective-permute-start(bf16[384,768]{1,0:T(8,128)(2,1)S(1)} %copy-done.142), channel_id=1, source_target_pairs={{16,0},{17,8},{18,4},{19,12},{20,2},{21,10},{22,6},{23,14},{24,1},... | collective-permute-start | bytes 1769480 | tf_op jit(solution)/shard_map/ppermute | solution.py:488
  656.0 40.8 %collective-permute-start.64 = (bf16[384,768]{1,0:T(8,128)(2,1)S(1)}, bf16[384,768]{1,0:T(8,128)(2,1)S(1)}, u32[]{:S(2)}, u32[]{:S(2)}) collective-permute-start(bf16[384,768]{1,0:T(8,128)(2,1)S(1)} %copy-done.142), channel_id=1, source_target_pairs={{0,0},{1,8},{2,4},{3,12},{4,2},{5,10},{6,6},{7,14},{8,1},{9,9},{10... | collective-permute-start | bytes 1769480 | tf_op jit(solution)/shard_map/ppermute | solution.py:488
  (218 other events, 1723.2 us)
Sparse Core Ops, SparseCore 0:
  23.2 56.9 all-gather.4
  82.3 36.1 all-gather.8
  120.6 29.5 all-gather.10
  152.0 29.1 all-gather.6
  508.7 43.0 reduce-scatter.4
  582.8 22.0 reduce-scatter.6
  634.6 29.3 reduce-scatter.10
  697.0 19.1 reduce-scatter.8
